TPU v7x, 512 devices: a whole 4x4x16 slice. The times are simulated.
512 devices in a mesh: replica: 8 (over x, core), shard: 64 (over y, z).
Axes of the slice: x: 4, y: 4, z: 16, core: 2. Of those that a mesh axis runs over, the one named last changes fastest.
Arguments:
- grads: bfloat16 [8, 128, 512, 512], P('replica', None, 'shard')
- block_slot: int32 [128], replicated, may hold values from 0 to 255, as said below
- left_stat: float32 [256, 512, 512], P('shard', 'replica'), may hold values from 0 to 2
- right_stat: float32 [256, 512, 512], P('shard', 'replica'), may hold values from 0 to 2
- left_root: bfloat16 [256, 512, 512], P('shard', 'replica'), as said below
- right_root: bfloat16 [256, 512, 512], P('shard', 'replica'), as said below
Outputs:
- update: bfloat16 [128, 512, 512], P(None, 'shard')
- left_new: float32 [256, 512, 512], P('shard', 'replica')
- right_new: float32 [256, 512, 512], P('shard', 'replica')
Inputs may be any that keep to these rules, and one draw needn't show every extreme that they name: `block_slot`: slot k belongs to index k // 4 of shard. No two blocks share a slot; some index of shard owns 4 blocks. `left_root`: every slot's matrix is exactly symmetric. `right_root`: every slot's matrix is exactly symmetric.
All inputs are finite; a program needn't handle non-finite values.
Results may differ from a plain program's by a relative error of at most 0.02.
Values may be sent and summed in bfloat16 or wider, within the bound.
No kernel may reach another device: no remote copies, remote signals or barrier semaphores. Data moves between devices by JAX's collectives and lax.ppermute only.
A program may use at most 64 MiB of HBM per device.

v0:
```python
import jax
import jax.numpy as jnp
from jax import lax
from jax.sharding import PartitionSpec as P

STAT_DECAY = 0.9
NORM_EPS = 1e-12


def local(grads, block_slot, left_stat, right_stat, left_root, right_root):
    shard_count = lax.axis_size("shard")
    replica_count = lax.axis_size("replica")
    replica_pos = lax.axis_index("replica")
    capacity = left_stat.shape[0]
    block_count = grads.shape[1]
    shard_rows = grads.shape[2]
    width = grads.shape[3]
    own_width = width // replica_count
    slot_total = capacity * shard_count
    slot_index = block_slot % capacity * shard_count + block_slot // capacity
    matches = slot_index[None, :] == jnp.arange(slot_total, dtype=jnp.int32)[:, None]
    block_of_slot = jnp.sum(
        jnp.where(matches, jnp.arange(block_count, dtype=jnp.int32)[None, :], 0), axis=1
    )
    occupied = jnp.any(matches, axis=1)
    grad_rows = grads[0].reshape(block_count, shard_rows * width)
    outgoing = jnp.where(
        occupied[:, None], jnp.take(grad_rows, block_of_slot, axis=0), jnp.zeros((), jnp.bfloat16)
    )
    outgoing = outgoing.reshape(capacity, shard_count, shard_rows * width)
    incoming = lax.all_to_all(outgoing, "shard", split_axis=1, concat_axis=1, tiled=True)
    summed = lax.psum(
        incoming.reshape(capacity, width, width).astype(jnp.float32).astype(jnp.bfloat16), "replica"
    )
    grad_cols = lax.dynamic_slice_in_dim(summed, replica_pos * own_width, own_width, 2)
    grad_sq = jnp.sum(jnp.square(summed.astype(jnp.float32)), axis=(1, 2))
    own_rows = lax.dynamic_slice_in_dim(summed, replica_pos * own_width, own_width, 1)
    left_term = jnp.einsum("cib,cjb->cij", own_rows, summed, preferred_element_type=jnp.float32)
    right_term = jnp.einsum("cbi,cbj->cij", grad_cols, summed, preferred_element_type=jnp.float32)
    left_new = STAT_DECAY * left_stat + (1.0 - STAT_DECAY) * left_term
    right_new = STAT_DECAY * right_stat + (1.0 - STAT_DECAY) * right_term
    shaped = jnp.einsum(
        "cbj,cij->cbi", summed, right_root, preferred_element_type=jnp.float32
    ).astype(jnp.bfloat16)
    direction = jnp.einsum(
        "cnd,cne->cde",
        lax.all_gather(left_root, "replica", axis=1, tiled=True),
        shaped,
        preferred_element_type=jnp.float32,
    )
    dir_sq = lax.psum(jnp.sum(jnp.square(direction), axis=(1, 2)), "replica")
    ratio = jnp.sqrt(grad_sq) / jnp.sqrt(dir_sq + NORM_EPS)
    step_update = (-direction * ratio[:, None, None]).astype(jnp.bfloat16)
    returning = lax.all_to_all(
        step_update.reshape(capacity, shard_count, shard_rows * own_width),
        "shard",
        split_axis=1,
        concat_axis=1,
        tiled=True,
    )
    mine = jnp.take(returning.reshape(slot_total, shard_rows * own_width), slot_index, axis=0)
    mine = mine.reshape(block_count, shard_rows, own_width)
    update = lax.all_gather(mine, "replica", axis=2, tiled=True)
    return (update, left_new, right_new)


def solution(mesh):
    in_specs = (
        P("replica", None, "shard", None),
        P(),
        P("shard", "replica", None),
        P("shard", "replica", None),
        P("shard", "replica", None),
        P("shard", "replica", None),
    )
    out_specs = (P(None, "shard", None), P("shard", "replica", None), P("shard", "replica", None))
    return jax.shard_map(local, mesh=mesh, in_specs=in_specs, out_specs=out_specs, check_vma=False)
```

profile of v0, /device:TPU:1, one launch (start us, length us, event | category | flops | bytes accessed | tf_op | source)
XLA Modules:
  0.0 303.0 jit_solution(3582523850558164963)
XLA Ops:
  7.2 0.0 copy-start
  7.2 0.7 compare_and_fusion.1
  7.9 0.1 select_reduce_fusion
  8.0 0.1 fusion.7
  8.1 0.1 reduce_sum.32
  8.2 1.6 copy.43
  9.9 0.1 copy.33
  10.0 0.1 broadcast_in_dim.54
  10.1 0.1 copy.32
  10.2 1.8 gather_fusion
  12.0 4.1 %fusion = bf16[4,64,4096]{2,0,1:T(4,128)(2,1)} fusion(bf16[4,64,4096]{2,1,0:T(8,128)(2,1)S(1)} %bitcast.16, pred[4,64]{0,1:T(8,128)(4,1)S(1)} %copy.33, pred[4,64]{0,1:T(8,128)(4,1)S(1)} %copy.32), kind=kLoop, calls=%fused_computation.4 | loop fusion | flops 2097152 | bytes 4194816 | tf_op jit(solution)/shard_map/jit(_where)/select_n | solution.py:27
  16.1 19.3 %all-to-all-start = ((bf16[4,64,4096]{2,0,1:T(4,128)(2,1)}), bf16[4,64,4096]{2,0,1:T(4,128)(2,1)S(1)}, u32[]{:S(2)}, u32[]{:S(2)}) async-start(bf16[4,64,4096]{2,0,1:T(4,128)(2,1)} %fusion), calls=%async_computation | async-start | bytes 4194304 | tf_op jit(solution)/shard_map/all_to_all | solution.py:31
  35.4 0.0 all-gather.3.cloned.1.call-start
  35.4 0.7 all-gather.3.cloned.1.call-update
  36.1 0.0 all-reduce.2.cloned.1.call-start
  36.2 94.0 %all-to-all-done = bf16[4,64,4096]{2,0,1:T(4,128)(2,1)S(1)} async-done(((bf16[4,64,4096]{2,0,1:T(4,128)(2,1)}), bf16[4,64,4096]{2,0,1:T(4,128)(2,1)S(1)}, u32[]{:S(2)}, u32[]{:S(2)}) %all-to-all-start) | async-done | bytes 2097184 | tf_op jit(solution)/shard_map/all_to_all | solution.py:31
  130.2 2.5 copy.35
  132.7 4.2 %reshape.60 = bf16[4,512,512]{2,1,0:T(8,128)(2,1)} reshape(bf16[4,64,4096]{2,1,0:T(8,128)(2,1)} %copy.35) | data formatting | bytes 4194304 | tf_op jit(solution)/shard_map/reshape | solution.py:33
  136.8 0.0 all-reduce.2.cloned.1.call-update
  136.9 0.0 all-gather.3.cloned.1.call-done
  136.9 76.2 %all-reduce.2.cloned.1.call-done = bf16[4,512,512]{2,1,0:T(8,128)(2,1)} async-done(((bf16[4,512,512]{2,1,0:T(8,128)(2,1)}), bf16[4,512,512]{2,1,0:T(8,128)(2,1)}) %all-reduce.2.cloned.1.call-update) | async-done | bytes 2097168 | tf_op jit(solution)/shard_map/psum | solution.py:32
  213.1 0.0 copy-done
  213.1 0.0 copy-start.1
  213.1 3.6 %multiply_reduce_fusion.1 = (f32[4]{0:T(128)S(1)}, f32[4,64,512]{2,1,0:T(8,128)S(1)}) fusion(bf16[4,512,512]{2,1,0:T(8,128)(2,1)} %all-gather.3.cloned.1.call-done, bf16[4,512,512]{2,1,0:T(8,128)(2,1)} %all-reduce.2.cloned.1.call-done, bf16[4,64,512]{2,1,0:T(8,128)(2,1)S(1)} %copy-done), kind=kOutput, calls=%fused_computation.13 | convolution fusion | flops 268828672 | bytes 4980752 | tf_op jit(solution)/shard_map/cnd,cne->cde/dot_general | solution.py:45
  216.7 14.2 %psum.15 = f32[4]{0:T(128)S(1)} all-reduce(f32[4]{0:T(128)S(1)} %get-tuple-element.17), channel_id=1, replica_groups=mesh['replica'=8,'shard'=64] {'replica'}, use_global_device_ids=true, to_apply=%region_5.6 | all-reduce | flops 4 | bytes 32 | tf_op jit(solution)/shard_map/psum | solution.py:51
  230.9 0.0 copy-done.1
  230.9 0.6 multiply_reduce_fusion
  231.5 0.1 fusion.5
  231.7 0.3 copy.36
  231.9 0.3 reshape.61
  232.3 0.9 copy.37
  233.2 0.0 copy-start.2
  233.2 15.5 %all-to-all-start.1 = ((bf16[4,64,512]{2,0,1:T(4,128)(2,1)}), bf16[4,64,512]{2,0,1:T(4,128)(2,1)S(1)}, u32[]{:S(2)}, u32[]{:S(2)}) async-start(bf16[4,64,512]{2,0,1:T(4,128)(2,1)} %copy.37), calls=%async_computation.1 | async-start | bytes 524288 | tf_op jit(solution)/shard_map/all_to_all | solution.py:54
  248.7 0.0 all-gather.5.cloned.1.call-start
  248.8 17.7 %all-to-all-done.1 = bf16[4,64,512]{2,0,1:T(4,128)(2,1)S(1)} async-done(((bf16[4,64,512]{2,0,1:T(4,128)(2,1)}), bf16[4,64,512]{2,0,1:T(4,128)(2,1)S(1)}, u32[]{:S(2)}, u32[]{:S(2)}) %all-to-all-start.1) | async-done | bytes 262176 | tf_op jit(solution)/shard_map/all_to_all | solution.py:54
  266.5 0.8 gather_fusion.1
  267.4 0.1 copy.39
  267.5 0.7 broadcast_select_fusion
  268.2 0.0 copy-start.3
  268.2 0.0 all-gather.5.cloned.1.call-update
  268.2 0.0 copy-done.2
  268.2 1.5 fusion.1
  269.7 0.0 copy-done.3
  269.7 1.6 fusion.2
  271.2 22.6 %all-gather.5.cloned.1.call-done = bf16[128,8,512]{0,2,1:T(8,128)(2,1)} async-done(((bf16[128,8,64]{0,2,1:T(8,128)(2,1)}), bf16[128,8,512]{0,2,1:T(8,128)(2,1)}) %all-gather.5.cloned.1.call-update) | async-done | bytes 1048592 | tf_op jit(solution)/shard_map/all_gather | solution.py:63
  293.8 2.6 copy.41
  (7 shorter events, 0.1 us)
Async XLA Ops:
  7.2 206.0 %copy-start = (bf16[4,64,512]{2,1,0:T(8,128)(2,1)S(1)}, bf16[4,64,512]{2,1,0:T(8,128)(2,1)}, u32[]{:S(2)}) copy-start(bf16[4,64,512]{2,1,0:T(8,128)(2,1)} %param.11) | copy-start | bytes 786436
  16.1 114.1 %all-to-all-start = ((bf16[4,64,4096]{2,0,1:T(4,128)(2,1)}), bf16[4,64,4096]{2,0,1:T(4,128)(2,1)S(1)}, u32[]{:S(2)}, u32[]{:S(2)}) async-start(bf16[4,64,4096]{2,0,1:T(4,128)(2,1)} %fusion), calls=%async_computation | async-start | bytes 4194304 | tf_op jit(solution)/shard_map/all_to_all | solution.py:31
  35.4 101.5 %all-gather.3.cloned.1.call-start = ((), (), s32[]{:S(2)}) async-start(), calls=%async_computation.3 | async-start | bytes 2359296 | tf_op jit(solution)/shard_map/all_gather | solution.py:47
  36.1 177.0 %all-reduce.2.cloned.1.call-start = ((), (), s32[]{:S(2)}) async-start(), calls=%async_computation.2 | async-start | bytes 4194304 | tf_op jit(solution)/shard_map/psum | solution.py:32
  213.1 17.8 %copy-start.1 = (bf16[4,512,512]{2,1,0:T(8,128)(2,1)S(1)}, bf16[4,512,512]{2,1,0:T(8,128)(2,1)}, u32[]{:S(2)}) copy-start(bf16[4,512,512]{2,1,0:T(8,128)(2,1)} %all-reduce.2.cloned.1.call-done) | copy-start | bytes 6291460
  233.2 35.1 %copy-start.2 = (f32[4,64,512]{2,1,0:T(8,128)S(1)}, f32[4,64,512]{2,1,0:T(8,128)}, u32[]{:S(2)}) copy-start(f32[4,64,512]{2,1,0:T(8,128)} %param.9) | copy-start | bytes 1572868
  233.2 33.3 %all-to-all-start.1 = ((bf16[4,64,512]{2,0,1:T(4,128)(2,1)}), bf16[4,64,512]{2,0,1:T(4,128)(2,1)S(1)}, u32[]{:S(2)}, u32[]{:S(2)}) async-start(bf16[4,64,512]{2,0,1:T(4,128)(2,1)} %copy.37), calls=%async_computation.1 | async-start | bytes 524288 | tf_op jit(solution)/shard_map/all_to_all | solution.py:54
  248.7 45.1 %all-gather.5.cloned.1.call-start = ((), (), s32[]{:S(2)}) async-start(), calls=%async_computation.4 | async-start | bytes 1179648 | tf_op jit(solution)/shard_map/all_gather | solution.py:63
  268.2 1.5 copy-start.3
Sparse Core Ops, SparseCore 0:
  38.4 34.3 all-gather.2
  137.0 76.0 all-reduce.1
  268.3 25.4 all-gather.4
where the time goes:
time: 303 us
  waiting for transfers between devices  211 us (70%)
  starting transfers between devices  34.9 us (12%)
  local copies, waits for them, and re-layouts  15.7 us (5%)
  blocking collectives  14.2 us (5%)
  between operations  13.9 us (5%)
  matrix products  6.61 us (2%)
  other arithmetic  6.47 us (2%)
    all_to_all x1, waiting for transfers between devices, local(): lax.all_to_all(outgoing, 'shard', split_axis=1, concat_axis=1, tiled=True)  94 us
    psum x1, waiting for transfers between devices, local(): lax.psum(incoming.reshape(capacity, width, width).astype(jnp.float32).ast...  76.2 us
    all_gather x1, waiting for transfers between devices, local(): update = lax.all_gather(mine, 'replica', axis=2, tiled=True)  22.6 us
    all_to_all x1, starting transfers between devices, local(): lax.all_to_all(outgoing, 'shard', split_axis=1, concat_axis=1, tiled=True)  19.3 us
    all_to_all x1, waiting for transfers between devices, local(): lax.all_to_all(step_update.reshape(capacity, shard_count, shard_rows * ow...  17.7 us
    all_to_all x1, starting transfers between devices, local(): lax.all_to_all(step_update.reshape(capacity, shard_count, shard_rows * ow...  15.5 us
    psum x1, blocking collectives, local(): dir_sq = lax.psum(jnp.sum(jnp.square(direction), axis=(1, 2)), 'replica')  14.2 us
  transfers between devices with their start and end apart: 5, of which 4 were waited for; matrix products, arithmetic and copies ran while one was open for 3% of the time, Pallas kernels for 0%

commit v1 on v0

v1 whole, which is shorter than its diff:
```python
import functools

import jax
import jax.numpy as jnp
from jax import lax
from jax.experimental import pallas as pl
from jax.experimental.pallas import tpu as pltpu
from jax.sharding import Mesh, PartitionSpec as P

STAT_DECAY = 0.9
NORM_EPS = 1e-12
F32 = jnp.float32
BF16 = jnp.bfloat16
VMEM_SPEC = pl.BlockSpec(memory_space=pltpu.VMEM)
SMEM_SPEC = pl.BlockSpec(memory_space=pltpu.SMEM)
PARAMS = pltpu.CompilerParams(vmem_limit_bytes=32 * 1024 * 1024)


def dot(a, b, dims):
    return lax.dot_general(a, b, (dims, ((), ())), preferred_element_type=F32)


def pair_sum_kernel(order, core, own, other, out):
    chips, depth = out.shape[0], out.shape[1]
    width = out.shape[3]
    cols = pl.ds(pl.multiple_of(core[0] * width, 128), width)

    def body(i, carry):
        for x in range(chips):
            block = order[i * chips + x]
            mine = own[block, :, cols].astype(F32)
            out[x, i] = (mine + other[block].astype(F32)).astype(BF16)
        return carry

    lax.fori_loop(0, depth, body, 0, unroll=4)


def chip_sum_kernel(place, parts, out, total):
    depth = parts.shape[1]
    acc = parts[0].astype(F32)
    for x in range(1, parts.shape[0]):
        acc = acc + parts[x].astype(F32)
    total[0:depth] = acc.astype(BF16)
    total[depth] = jnp.zeros(total.shape[1:], BF16)

    def body(o, carry):
        out[o] = total[place[o]]
        return carry

    lax.fori_loop(0, out.shape[0], body, 0, unroll=8)


def direction_kernel(info, own, other, left, right, out):
    core = info[0]
    half = own.shape[1]
    groups = left.shape[0]
    size = groups * left.shape[2]
    slot = info[1]
    left_mat = left[:, slot].reshape(size, size)
    g_own = own[...]
    g_other = other[...]
    grad_sq = jnp.sum(jnp.square(g_own.astype(F32))) + jnp.sum(jnp.square(g_other.astype(F32)))

    def columns(h):
        cols = pl.ds(pl.multiple_of(h * half, 128), half)
        upper = right[pl.ds(core * (groups // 2), groups // 2), slot, :, cols].reshape(half, half)
        lower = right[pl.ds((1 - core) * (groups // 2), groups // 2), slot, :, cols].reshape(half, half)
        shaped = dot(g_own, upper, ((1,), (0,))) + dot(g_other, lower, ((1,), (0,)))
        return dot(left_mat, shaped.astype(BF16), ((1,), (0,)))

    far = columns(1 - core)
    dir_sq = jnp.sum(jnp.square(far))
    near = columns(core)
    dir_sq = dir_sq + jnp.sum(jnp.square(near))
    grad_sq = jnp.full((1, 1), grad_sq, F32)
    dir_sq = jnp.full((1, 1), dir_sq, F32)
    ratio = jnp.sqrt(grad_sq) / jnp.sqrt(dir_sq + NORM_EPS)
    out[...] = (-near * ratio).astype(BF16)


def stats_kernel(info, chip_of_slot, grads, left, right, left_out, right_out):
    x, core = info[0], info[1]
    rows = left.shape[1]
    half = grads.shape[2]
    row_at = pl.multiple_of((2 * x + core) * rows, 16)
    col_at = pl.multiple_of((x % 2) * 2 * rows, 128)
    for j in range(left.shape[0]):
        chip = chip_of_slot[j]

        @pl.when(chip >= 0)
        def _():
            g0 = grads[2 * chip]
            g1 = grads[2 * chip + 1]
            r0 = grads[2 * chip, pl.ds(row_at, rows)]
            r1 = grads[2 * chip + 1, pl.ds(row_at, rows)]
            term = dot(r0, g0, ((1,), (1,))) + dot(r1, g1, ((1,), (1,)))
            left_out[j] = STAT_DECAY * left[j] + (1.0 - STAT_DECAY) * term
            cols = grads[2 * chip + x // 2, :, pl.ds(col_at, 2 * rows)]
            for h, g in ((0, g0), (1, g1)):
                prod = dot(cols, g, ((0,), (0,)))
                term = jnp.where(core == 0, prod[:rows], prod[rows:])
                at = pl.ds(h * half, half)
                right_out[j, :, at] = STAT_DECAY * right[j, :, at] + (1.0 - STAT_DECAY) * term

        @pl.when(chip < 0)
        def _():
            left_out[j] = STAT_DECAY * left[j]
            right_out[j] = STAT_DECAY * right[j]


def compact_kernel(owner, rows, out):
    def body(i, carry):
        block = rows[owner[i]]
        for x in range(out.shape[0]):
            out[x, i] = block
        return carry

    lax.fori_loop(0, out.shape[1], body, 0, unroll=4)


def place_kernel(rank, core, own, other, out):
    chips = own.shape[0]
    width = own.shape[3]
    near = pl.ds(pl.multiple_of(core[0] * width, 128), width)
    far = pl.ds(pl.multiple_of((1 - core[0]) * width, 128), width)

    def body(b, carry):
        x = rank[b] % chips
        i = rank[b] // chips
        out[b, :, near] = own[x, i]
        out[b, :, far] = other[x, i]
        return carry

    lax.fori_loop(0, out.shape[0], body, 0, unroll=4)


def call(kernel, out_shape, in_specs, scratch=()):
    multi = isinstance(out_shape, (tuple, list))
    return pl.pallas_call(
        kernel,
        out_shape=out_shape,
        in_specs=in_specs,
        out_specs=tuple(VMEM_SPEC for _ in out_shape) if multi else VMEM_SPEC,
        scratch_shapes=list(scratch),
        compiler_params=PARAMS,
    )


def exchange(value, axis):
    return lax.all_to_all(value, axis, 0, 0, tiled=True)


def swap_cores(value):
    return lax.ppermute(value, "core", [(0, 1), (1, 0)])


def local(grads, block_slot, left_stat, right_stat, left_root, right_root):
    grads = grads[0]
    chips = lax.axis_size("x")
    x = lax.axis_index("x")
    core = lax.axis_index("core")
    me = lax.axis_index("y") * lax.axis_size("z") + lax.axis_index("z")
    owners = lax.axis_size("y") * lax.axis_size("z")
    capacity = left_stat.shape[0]
    blocks, shard_rows, width = grads.shape
    half = width // 2
    depth = blocks // chips
    core1 = core.reshape(1)

    left_all = lax.all_gather(left_root, ("x", "core"), axis=0)
    right_all = lax.all_gather(right_root, ("x", "core"), axis=0)

    sent = lax.dynamic_slice_in_dim(grads, (1 - core) * half, half, 2)
    other = swap_cores(sent)

    rank = jnp.sum((block_slot[None, :] < block_slot[:, None]).astype(jnp.int32), axis=1)
    ids = jnp.arange(blocks, dtype=jnp.int32)
    at_rank = (rank[None, :] == ids[:, None]).astype(jnp.int32)
    order = jnp.sum(at_rank * ids[None, :], axis=1)
    slots = jnp.sum(at_rank * block_slot[None, :], axis=1)
    owner_of = slots // capacity
    mine = slots.reshape(depth, chips)
    mine = jnp.sum(jnp.where(jnp.arange(chips)[None, :] == x, mine, 0), axis=1)
    owner_here = mine // capacity
    hits = owner_here[None, :] == jnp.arange(owners, dtype=jnp.int32)[:, None]
    place = jnp.sum(jnp.where(hits, jnp.arange(depth, dtype=jnp.int32)[None, :] - depth, 0), axis=1) + depth
    slot_here = jnp.sum(jnp.where(owner_here == me, mine % capacity, 0))
    local_slot = jnp.arange(capacity, dtype=jnp.int32) + me * capacity
    chip_of_slot = jnp.sum(
        jnp.where(slots[None, :] == local_slot[:, None], ids[None, :] % chips + 1, 0), axis=1
    ) - 1

    parts = call(
        pair_sum_kernel,
        jax.ShapeDtypeStruct((chips, depth, shard_rows, half), BF16),
        [SMEM_SPEC, SMEM_SPEC, VMEM_SPEC, VMEM_SPEC],
    )(order, core1, grads, other)
    parts = exchange(parts, "x")
    outgoing = call(
        chip_sum_kernel,
        jax.ShapeDtypeStruct((owners, shard_rows, half), BF16),
        [SMEM_SPEC, VMEM_SPEC],
        [pltpu.VMEM((depth + 1, shard_rows, half), BF16)],
    )(place, parts)
    own = exchange(outgoing, ("y", "z")).reshape(width, half)
    far = swap_cores(own)
    grads_all = lax.all_gather(own, ("x", "core"), axis=0)

    update = call(
        direction_kernel,
        jax.ShapeDtypeStruct((width, half), BF16),
        [SMEM_SPEC] + [VMEM_SPEC] * 4,
    )(jnp.stack([core, slot_here]), own, far, left_all, right_all)

    rows = exchange(update.reshape(owners, shard_rows, half), ("y", "z"))
    packed = call(
        compact_kernel,
        jax.ShapeDtypeStruct((chips, depth, shard_rows, half), BF16),
        [SMEM_SPEC, VMEM_SPEC],
    )(owner_here, rows)
    near = exchange(packed, "x")
    near, grads_all = lax.optimization_barrier((near, grads_all))
    beyond = swap_cores(near)
    left_new, right_new = call(
        stats_kernel,
        (jax.ShapeDtypeStruct(left_stat.shape, F32), jax.ShapeDtypeStruct(right_stat.shape, F32)),
        [SMEM_SPEC, SMEM_SPEC] + [VMEM_SPEC] * 3,
    )(jnp.stack([x, core]), chip_of_slot, grads_all, left_stat, right_stat)
    result = call(
        place_kernel,
        jax.ShapeDtypeStruct((blocks, shard_rows, width), BF16),
        [SMEM_SPEC, SMEM_SPEC, VMEM_SPEC, VMEM_SPEC],
    )(rank, core1, near, beyond)
    return (result, left_new, right_new)


def solution(mesh):
    fine = Mesh(mesh.devices.reshape(4, 2, 4, 16), ("x", "core", "y", "z"))
    replica, shard = ("x", "core"), ("y", "z")
    in_specs = (
        P(replica, None, shard, None),
        P(),
        P(shard, replica, None),
        P(shard, replica, None),
        P(shard, replica, None),
        P(shard, replica, None),
    )
    out_specs = (P(None, shard, None), P(shard, replica, None), P(shard, replica, None))
    return jax.shard_map(local, mesh=fine, in_specs=in_specs, out_specs=out_specs, check_vma=False)
```

time: 303 us -> 157 us (0.52)
  waiting for transfers between devices: 211 us -> 27.5 us
  blocking collectives: 14.2 us -> 66.9 us
  Pallas kernels: 0 us -> 10.9 us
  local copies, waits for them, and re-layouts: 15.7 us -> 6.92 us
  starting transfers between devices: 34.9 us -> 26.4 us
  matrix products: 6.61 us -> 0 us
    all_to_all x2, waiting for transfers between devices: 112 us -> 15.8 us  [exchange(): return lax.all_to_all(value, axis, 0, 0, tiled=True)]
    psum x1 -> x0, waiting for transfers between devices: 76.2 us -> none  [local(): lax.psum(incoming.reshape(capacity, width, width).astype(jnp.float32).ast...]
    all_to_all x0 -> x2, blocking collectives: none -> 66.9 us  [exchange(): return lax.all_to_all(value, axis, 0, 0, tiled=True)]
    all_to_all x2, starting transfers between devices: 34.8 us -> 6.94 us  [exchange(): return lax.all_to_all(value, axis, 0, 0, tiled=True)]
    ppermute x0 -> x3, starting transfers between devices: none -> 19.3 us  [swap_cores(): return lax.ppermute(value, 'core', [(0, 1), (1, 0)])]
    psum x1 -> x0, blocking collectives: 14.2 us -> none  [local(): dir_sq = lax.psum(jnp.sum(jnp.square(direction), axis=(1, 2)), 'replica')]
    all_gather x2 -> x3, waiting for transfers between devices: 22.6 us -> 9.67 us  [the longest x1 9.66 us: local(): right_all = lax.all_gather(right_root, ('x', 'core'), axis=0)]
    pallas_call x0 -> x6, Pallas kernels: none -> 10.9 us  [the longest x1 2.75 us: local(): call(stats_kernel, (jax.ShapeDtypeStruct(left_stat.shape, F32), jax.Shape...]
  transfers between devices with their start and end apart: 5 -> 8, of which waited for: 4 -> 4; matrix products, arithmetic and copies ran while one was open for 3% -> 3% of each run, Pallas kernels for 0% -> 5%
where the time goes in v1:
time: 157 us; the launch traced here: 156 us
  blocking collectives  66.9 us (43%)
  waiting for transfers between devices  27.5 us (18%)
  starting transfers between devices  26.4 us (17%)
  between operations  13.9 us (9%)
  Pallas kernels  10.9 us (7%)
  local copies, waits for them, and re-layouts  6.92 us (4%)
  other arithmetic  3.52 us (2%)
    all_to_all x2, blocking collectives, exchange(): return lax.all_to_all(value, axis, 0, 0, tiled=True)  66.9 us
    ppermute x3, starting transfers between devices, swap_cores(): return lax.ppermute(value, 'core', [(0, 1), (1, 0)])  19.3 us
    all_to_all x2, waiting for transfers between devices, exchange(): return lax.all_to_all(value, axis, 0, 0, tiled=True)  15.8 us
    all_gather x1, waiting for transfers between devices, local(): right_all = lax.all_gather(right_root, ('x', 'core'), axis=0)  9.66 us
    all_to_all x2, starting transfers between devices, exchange(): return lax.all_to_all(value, axis, 0, 0, tiled=True)  6.94 us
    unnamed x14, local copies, waits for them, and re-layouts  5.73 us
  transfers between devices with their start and end apart: 8, of which 4 were waited for; matrix products, arithmetic and copies ran while one was open for 3% of the time, Pallas kernels for 5%

profile of v1, /device:TPU:1, one launch (start us, length us, event | category | flops | bytes accessed | tf_op | source)
XLA Modules:
  0.0 156.1 jit_solution(995962781959393568)
XLA Ops:
  7.2 0.0 copy-start.1
  7.2 0.0 all-gather.8.cloned.1.call-start
  7.2 0.7 all-gather.8.cloned.1.call-update
  7.9 0.0 all-gather.10.cloned.1.call-start
  8.0 0.7 all-gather.10.cloned.1.call-update
  8.7 1.1 dynamic-slice_bitcast_fusion
  9.7 8.8 %collective-permute-start = (bf16[128,8,256]{2,1,0:T(8,128)(2,1)S(1)}, bf16[128,8,256]{2,1,0:T(8,128)(2,1)S(1)}, u32[]{:S(2)}, u32[]{:S(2)}) collective-permute-start(bf16[128,8,256]{2,1,0:T(8,128)(2,1)S(1)} %dynamic-slice_bitcast_fusion), channel_id=1, source_target_pairs={{0,64},{64,0},{1,65},{65,1},{2,66},{66,2},{3,67},{67,3},{4,68},{68... | collective-permute-start | bytes 1572872 | tf_op jit(solution)/shard_map/ppermute | solution.py:154
  18.5 0.9 convert_reduce_fusion.rank
  19.5 0.8 select_reduce_fusion
  20.2 0.1 reshape.72
  20.4 0.1 select_reduce_fusion.3
  20.5 0.0 collective-permute-done.other
  20.5 0.0 copy-done.1
  20.5 1.7 %shard_map.85 = bf16[4,32,8,256]{3,2,1,0:T(8,128)(2,1)} custom-call(s32[128]{0:T(128)S(1)} %get-tuple-element.11.order, s32[1]{0:T(128)} %bitcast.core, bf16[128,8,512]{2,1,0:T(8,128)(2,1)S(1)} %bitcast.14, bf16[128,8,256]{2,1,0:T(8,128)(2,1)S(1)} %collective-permute-done.other), custom_call_target="tpu_custom_call" | custom-call | tf_op jit(solution)/shard_map/pallas_call | solution.py:193
  22.1 3.5 %all-to-all-start = ((bf16[4,32,8,256]{3,2,1,0:T(8,128)(2,1)}), bf16[4,32,8,256]{3,2,1,0:T(8,128)(2,1)S(1)}, u32[]{:S(2)}, u32[]{:S(2)}) async-start(bf16[4,32,8,256]{3,2,1,0:T(8,128)(2,1)} %shard_map.85), calls=%async_computation | async-start | bytes 1048576 | tf_op jit(solution)/shard_map/all_to_all | solution.py:150
  25.6 0.0 all-gather.6.cloned.1.call-start
  25.7 0.6 fusion.1
  26.3 0.1 select_reduce_fusion.2
  26.4 8.8 %all-to-all-done.parts = bf16[4,32,8,256]{3,2,1,0:T(8,128)(2,1)S(1)} async-done(((bf16[4,32,8,256]{3,2,1,0:T(8,128)(2,1)}), bf16[4,32,8,256]{3,2,1,0:T(8,128)(2,1)S(1)}, u32[]{:S(2)}, u32[]{:S(2)}) %all-to-all-start) | async-done | bytes 524320 | tf_op jit(solution)/shard_map/all_to_all | solution.py:150
  35.2 0.7 shard_map.86
  35.9 31.8 %all_to_all.20 = bf16[64,8,256]{2,1,0:T(8,128)(2,1)} all-to-all(bf16[64,8,256]{2,1,0:T(8,128)(2,1)S(1)} %shard_map.86), channel_id=1, replica_groups=mesh['x'=4,'core'=2,'y'=4,'z'=16] {'y','z'}, dimensions={0} | all-to-all | bytes 524288 | tf_op jit(solution)/shard_map/all_to_all | solution.py:150
  67.8 0.0 all-gather.6.cloned.1.call-update
  67.8 5.3 %collective-permute-start.1 = (bf16[512,256]{1,0:T(8,128)(2,1)}, bf16[512,256]{1,0:T(8,128)(2,1)S(1)}, u32[]{:S(2)}, u32[]{:S(2)}) collective-permute-start(bf16[512,256]{1,0:T(8,128)(2,1)} %bitcast.12), channel_id=1, source_target_pairs={{0,64},{64,0},{1,65},{65,1},{2,66},{66,2},{3,67},{67,3},{4,68},{68... | collective-permute-start | bytes 786440 | tf_op jit(solution)/shard_map/ppermute | solution.py:154
  73.1 0.7 pad_add_fusion.info
  73.8 0.6 collective-permute-done.1.other
  74.4 0.0 all-gather.8.cloned.1.call-done
  74.4 9.7 %all-gather.10.cloned.1.call-done = bf16[32,64,512]{2,1,0:T(8,128)(2,1)} async-done(((bf16[4,64,512]{2,1,0:T(8,128)(2,1)}), bf16[32,64,512]{2,1,0:T(8,128)(2,1)}) %all-gather.10.cloned.1.call-update) | async-done | bytes 2097168 | tf_op jit(solution)/shard_map/all_gather | solution.py:171
  84.1 0.0 copy-start
  84.1 0.9 copy-done
  85.1 1.6 %copy-done.2 = bf16[32,64,512]{2,1,0:T(8,128)(2,1)S(1)} copy-done((bf16[32,64,512]{2,1,0:T(8,128)(2,1)S(1)}, bf16[32,64,512]{2,1,0:T(8,128)(2,1)}, u32[]{:S(2)}) %copy-start.2) | copy-done | bytes 2097176
  86.6 1.6 %copy-done.3 = bf16[32,64,512]{2,1,0:T(8,128)(2,1)S(1)} copy-done((bf16[32,64,512]{2,1,0:T(8,128)(2,1)S(1)}, bf16[32,64,512]{2,1,0:T(8,128)(2,1)}, u32[]{:S(2)}) %copy-start.3) | copy-done | bytes 2097176
  88.2 1.8 %shard_map.87 = bf16[512,256]{1,0:T(8,128)(2,1)S(1)} custom-call(s32[2]{0:T(128)S(1)} %pad_add_fusion.info, bf16[512,256]{1,0:T(8,128)(2,1)S(1)} %bitcast.13, bf16[512,256]{1,0:T(8,128)(2,1)S(1)} %collective-permute-done.1.other, bf16[8,4,64,512]{3,2,1,0:T(8,128)(2,1)S(1)} %bitcast.15, bf16[8,4,64,512]{3,2,1,0:T(8,128)(2,1)S(1)} %bitcast.16), custom_call_target="tpu_custom_call" | custom-call | tf_op jit(solution)/shard_map/pallas_call | solution.py:209
  90.0 0.0 copy-start.5
  90.0 0.0 copy-start.6
  90.0 35.1 %all_to_all.21.rows = bf16[64,8,256]{2,1,0:T(8,128)(2,1)S(1)} all-to-all(bf16[64,8,256]{2,1,0:T(8,128)(2,1)S(1)} %bitcast.17), channel_id=1, replica_groups=mesh['x'=4,'core'=2,'y'=4,'z'=16] {'y','z'}, dimensions={0} | all-to-all | bytes 524288 | tf_op jit(solution)/shard_map/all_to_all | solution.py:150
  125.1 1.4 shard_map.88
  126.5 3.5 %all-to-all-start.3 = ((bf16[4,32,8,256]{3,2,1,0:T(8,128)(2,1)}), bf16[4,32,8,256]{3,2,1,0:T(8,128)(2,1)S(1)}, u32[]{:S(2)}, u32[]{:S(2)}) async-start(bf16[4,32,8,256]{3,2,1,0:T(8,128)(2,1)} %shard_map.88), calls=%async_computation.3 | async-start | bytes 1048576 | tf_op jit(solution)/shard_map/all_to_all | solution.py:150
  130.0 7.0 %all-to-all-done.3.own = bf16[4,32,8,256]{3,2,1,0:T(8,128)(2,1)S(1)} async-done(((bf16[4,32,8,256]{3,2,1,0:T(8,128)(2,1)}), bf16[4,32,8,256]{3,2,1,0:T(8,128)(2,1)S(1)}, u32[]{:S(2)}, u32[]{:S(2)}) %all-to-all-start.3) | async-done | bytes 524320 | tf_op jit(solution)/shard_map/all_to_all | solution.py:150
  137.1 5.3 %collective-permute-start.2 = (bf16[4,32,8,256]{3,2,1,0:T(8,128)(2,1)S(1)}, bf16[4,32,8,256]{3,2,1,0:T(8,128)(2,1)S(1)}, u32[]{:S(2)}, u32[]{:S(2)}) collective-permute-start(bf16[4,32,8,256]{3,2,1,0:T(8,128)(2,1)S(1)} %all-to-all-done.3.own), channel_id=1, source_target_pairs={{0,64},{64,0},{1,65},{65,1},{2,66},{66,2},{3,67},{67,3},{4,68},{68... | collective-permute-start | bytes 1572872 | tf_op jit(solution)/shard_map/ppermute | solution.py:154
  142.3 0.1 pad_add_fusion.1.info
  142.4 0.2 select_reduce_fusion.4
  142.6 0.0 copy-done.5
  142.6 0.0 copy-done.6
  142.6 0.0 copy-start.4
  142.6 1.6 %copy-done.4 = bf16[8,512,256]{2,1,0:T(8,128)(2,1)S(1)} copy-done((bf16[8,512,256]{2,1,0:T(8,128)(2,1)S(1)}, bf16[8,512,256]{2,1,0:T(8,128)(2,1)}, u32[]{:S(2)}) %copy-start.4) | copy-done | bytes 2097176
  144.2 2.7 %shard_map.90 = (f32[4,64,512]{2,1,0:T(8,128)}, f32[4,64,512]{2,1,0:T(8,128)}) custom-call(s32[2]{0:T(128)S(1)} %pad_add_fusion.1.info, s32[4]{0:T(128)S(1)} %broadcast_add_fusion.chip_of_slot, bf16[8,512,256]{2,1,0:T(8,128)(2,1)S(1)} %copy-done.4, f32[4,64,512]{2,1,0:T(8,128)S(1)} %copy-done.5, f32[4,64,512]{2,1,0:T(8,128)S(1)} %copy-done.6), custom_call_target="tpu_custom_call" | custom-call | tf_op jit(solution)/shard_map/pallas_call | solution.py:224
  147.0 0.0 collective-permute-done.2.other
  147.0 2.6 %shard_map.89 = bf16[128,8,512]{2,1,0:T(8,128)(2,1)} custom-call(s32[128]{0:T(128)S(1)} %convert_reduce_fusion.rank, s32[1]{0:T(128)} %bitcast.core, bf16[4,32,8,256]{3,2,1,0:T(8,128)(2,1)S(1)} %all-to-all-done.3.own, bf16[4,32,8,256]{3,2,1,0:T(8,128)(2,1)S(1)} %collective-permute-done.2.other), custom_call_target="tpu_custom_call" | custom-call | tf_op jit(solution)/shard_map/pallas_call | solution.py:229
  (8 shorter events, 0.0 us)
Async XLA Ops:
  7.2 13.3 %copy-start.1 = (bf16[1,128,8,512]{3,2,1,0:T(8,128)(2,1)S(1)}, bf16[1,128,8,512]{3,2,1,0:T(8,128)(2,1)}, u32[]{:S(2)}) copy-start(bf16[1,128,8,512]{3,2,1,0:T(8,128)(2,1)} %param.6) | copy-start | bytes 3145732
  7.2 67.3 %all-gather.8.cloned.1.call-start = ((), (), s32[]{:S(2)}) async-start(), calls=%async_computation.5 | async-start | bytes 2359296 | tf_op jit(solution)/shard_map/all_gather | solution.py:170
  7.9 76.2 %all-gather.10.cloned.1.call-start = ((), (), s32[]{:S(2)}) async-start(), calls=%async_computation.6 | async-start | bytes 2359296 | tf_op jit(solution)/shard_map/all_gather | solution.py:171
  9.7 10.7 %collective-permute-start = (bf16[128,8,256]{2,1,0:T(8,128)(2,1)S(1)}, bf16[128,8,256]{2,1,0:T(8,128)(2,1)S(1)}, u32[]{:S(2)}, u32[]{:S(2)}) collective-permute-start(bf16[128,8,256]{2,1,0:T(8,128)(2,1)S(1)} %dynamic-slice_bitcast_fusion), channel_id=1, source_target_pairs={{0,64},{64,0},{1,65},{65,1},{2,66},{66,2},{3,67},{67,3},{4,68},{68... | collective-permute-start | bytes 1572872 | tf_op jit(solution)/shard_map/ppermute | solution.py:154
  22.1 13.1 %all-to-all-start = ((bf16[4,32,8,256]{3,2,1,0:T(8,128)(2,1)}), bf16[4,32,8,256]{3,2,1,0:T(8,128)(2,1)S(1)}, u32[]{:S(2)}, u32[]{:S(2)}) async-start(bf16[4,32,8,256]{3,2,1,0:T(8,128)(2,1)} %shard_map.85), calls=%async_computation | async-start | bytes 1048576 | tf_op jit(solution)/shard_map/all_to_all | solution.py:150
  25.6 111.4 %all-gather.6.cloned.1.call-start = ((), (), s32[]{:S(2)}) async-start(), calls=%async_computation.4 | async-start | bytes 2359296 | tf_op jit(solution)/shard_map/all_gather | solution.py:207
  67.8 6.6 %collective-permute-start.1 = (bf16[512,256]{1,0:T(8,128)(2,1)}, bf16[512,256]{1,0:T(8,128)(2,1)S(1)}, u32[]{:S(2)}, u32[]{:S(2)}) collective-permute-start(bf16[512,256]{1,0:T(8,128)(2,1)} %bitcast.12), channel_id=1, source_target_pairs={{0,64},{64,0},{1,65},{65,1},{2,66},{66,2},{3,67},{67,3},{4,68},{68... | collective-permute-start | bytes 786440 | tf_op jit(solution)/shard_map/ppermute | solution.py:154
  84.1 0.9 copy-start
  85.1 1.6 %copy-start.2 = (bf16[32,64,512]{2,1,0:T(8,128)(2,1)S(1)}, bf16[32,64,512]{2,1,0:T(8,128)(2,1)}, u32[]{:S(2)}) copy-start(bf16[32,64,512]{2,1,0:T(8,128)(2,1)} %all-gather.8.cloned.1.call-done) | copy-start | bytes 6291460
  86.6 1.6 %copy-start.3 = (bf16[32,64,512]{2,1,0:T(8,128)(2,1)S(1)}, bf16[32,64,512]{2,1,0:T(8,128)(2,1)}, u32[]{:S(2)}) copy-start(bf16[32,64,512]{2,1,0:T(8,128)(2,1)} %all-gather.10.cloned.1.call-done) | copy-start | bytes 6291460
  90.0 52.6 %copy-start.5 = (f32[4,64,512]{2,1,0:T(8,128)S(1)}, f32[4,64,512]{2,1,0:T(8,128)}, u32[]{:S(2)}) copy-start(f32[4,64,512]{2,1,0:T(8,128)} %left.1) | copy-start | bytes 1572868
  90.0 52.6 %copy-start.6 = (f32[4,64,512]{2,1,0:T(8,128)S(1)}, f32[4,64,512]{2,1,0:T(8,128)}, u32[]{:S(2)}) copy-start(f32[4,64,512]{2,1,0:T(8,128)} %right.1) | copy-start | bytes 1572868
  126.5 10.5 %all-to-all-start.3 = ((bf16[4,32,8,256]{3,2,1,0:T(8,128)(2,1)}), bf16[4,32,8,256]{3,2,1,0:T(8,128)(2,1)S(1)}, u32[]{:S(2)}, u32[]{:S(2)}) async-start(bf16[4,32,8,256]{3,2,1,0:T(8,128)(2,1)} %shard_map.88), calls=%async_computation.3 | async-start | bytes 1048576 | tf_op jit(solution)/shard_map/all_to_all | solution.py:150
  137.1 9.9 %collective-permute-start.2 = (bf16[4,32,8,256]{3,2,1,0:T(8,128)(2,1)S(1)}, bf16[4,32,8,256]{3,2,1,0:T(8,128)(2,1)S(1)}, u32[]{:S(2)}, u32[]{:S(2)}) collective-permute-start(bf16[4,32,8,256]{3,2,1,0:T(8,128)(2,1)S(1)} %all-to-all-done.3.own), channel_id=1, source_target_pairs={{0,64},{64,0},{1,65},{65,1},{2,66},{66,2},{3,67},{67,3},{4,68},{68... | collective-permute-start | bytes 1572872 | tf_op jit(solution)/shard_map/ppermute | solution.py:154
  142.6 1.6 %copy-start.4 = (bf16[8,512,256]{2,1,0:T(8,128)(2,1)S(1)}, bf16[8,512,256]{2,1,0:T(8,128)(2,1)}, u32[]{:S(2)}) copy-start(bf16[8,512,256]{2,1,0:T(8,128)(2,1)} %all-gather.6.cloned.1.call-done.grads) | copy-start | bytes 6291460
Sparse Core Ops, SparseCore 0:
  10.2 38.5 all-gather.7
  50.9 33.1 all-gather.9
  86.3 33.1 all-gather.5

commit v2 on v1

v2 whole, which is shorter than its diff:
```python
import functools

import jax
import jax.numpy as jnp
from jax import lax
from jax.experimental import pallas as pl
from jax.experimental.pallas import tpu as pltpu
from jax.sharding import Mesh, PartitionSpec as P

STAT_DECAY = 0.9
NORM_EPS = 1e-12
F32 = jnp.float32
BF16 = jnp.bfloat16
VMEM_SPEC = pl.BlockSpec(memory_space=pltpu.VMEM)
HBM_SPEC = pl.BlockSpec(memory_space=pltpu.HBM)
SMEM_SPEC = pl.BlockSpec(memory_space=pltpu.SMEM)
PARAMS = pltpu.CompilerParams(vmem_limit_bytes=32 * 1024 * 1024)


def dot(a, b, dims):
    return lax.dot_general(a, b, (dims, ((), ())), preferred_element_type=F32)


def split_kernel(core_ref, grads, left_root, right_root, kept, sent, roots, sems):
    core = core_ref[0]
    width = kept.shape[2]
    capacity = left_root.shape[0]
    near = pl.ds(pl.multiple_of(core * width, 128), width)
    far = pl.ds(pl.multiple_of((1 - core) * width, 128), width)
    copies = [
        pltpu.make_async_copy(grads.at[:, :, far], sent, sems.at[0]),
        pltpu.make_async_copy(grads.at[:, :, near], kept, sems.at[1]),
        pltpu.make_async_copy(left_root, roots.at[pl.ds(0, capacity)], sems.at[2]),
        pltpu.make_async_copy(right_root, roots.at[pl.ds(capacity, capacity)], sems.at[3]),
    ]
    for copy in copies:
        copy.start()
    for copy in copies:
        copy.wait()


def pair_sum_kernel(order, own, other, out):
    chips, depth = out.shape[:2]

    def body(i, carry):
        for x in range(chips):
            block = order[i * chips + x]
            out[x, i] = own[block] + other[block]
        return carry

    lax.fori_loop(0, depth, body, 0, unroll=4)


def chip_sum_kernel(at, table, parts, out, total):
    depth = parts.shape[1]
    acc = parts[0].astype(F32)
    for x in range(1, parts.shape[0]):
        acc = acc + parts[x].astype(F32)
    total[0:depth] = acc.astype(BF16)
    total[depth] = jnp.zeros(total.shape[1:], BF16)

    def body(o, carry):
        out[o] = total[table[at + o]]
        return carry

    lax.fori_loop(0, out.shape[0], body, 0, unroll=8)


def direction_kernel(at, table, own_hbm, other, roots, out, own, left, right, sems):
    core, slot = table[at], table[at + 1]
    capacity = roots.shape[1] // 2
    copies = [
        pltpu.make_async_copy(own_hbm, own, sems.at[0]),
        pltpu.make_async_copy(roots.at[:, capacity + slot], right, sems.at[1]),
        pltpu.make_async_copy(roots.at[:, slot], left, sems.at[2]),
    ]
    for copy in copies:
        copy.start()
    half = own.shape[1]
    groups, rows, size = left.shape
    copies[0].wait()
    g_own = own[...]
    g_other = other[...]
    grad_sq = jnp.sum(jnp.square(g_own.astype(F32))) + jnp.sum(jnp.square(g_other.astype(F32)))
    copies[1].wait()

    def shaped(h):
        cols = pl.ds(pl.multiple_of(h * half, 128), half)
        upper = right[pl.ds(core * (groups // 2), groups // 2), :, cols].reshape(half, half)
        lower = right[pl.ds((1 - core) * (groups // 2), groups // 2), :, cols].reshape(half, half)
        return (dot(g_own, upper, ((1,), (0,))) + dot(g_other, lower, ((1,), (0,)))).astype(BF16)

    shaped_far = shaped(1 - core)
    shaped_near = shaped(core)
    copies[2].wait()
    left_mat = left[...].reshape(size, size)
    dir_sq = jnp.sum(jnp.square(dot(left_mat, shaped_far, ((1,), (0,)))))
    near = dot(left_mat, shaped_near, ((1,), (0,)))
    dir_sq = dir_sq + jnp.sum(jnp.square(near))
    grad_sq = jnp.full((1, 1), grad_sq, F32)
    dir_sq = jnp.full((1, 1), dir_sq, F32)
    ratio = jnp.sqrt(grad_sq) / jnp.sqrt(dir_sq + NORM_EPS)
    out[...] = (-near * ratio).astype(BF16)


def stats_kernel(at, table, grads_hbm, left, right, left_hbm, right_hbm, grads, left_out, right_out, sems, out_sems):
    core, x = table[at], table[at + 2]
    capacity, rows, _ = left.shape
    half = grads.shape[3]
    loads = [
        pltpu.make_async_copy(grads_hbm.at[table[at + 3 + capacity + j]], grads.at[j], sems.at[j])
        for j in range(capacity)
    ]
    stores = []
    for load in loads:
        load.start()
    for j in range(capacity):
        full = table[at + 3 + j] > 0
        loads[j].wait()

        @pl.when(full)
        def _():
            g0 = grads[j, 0]
            g1 = grads[j, 1]
            own = pl.ds(pl.multiple_of((2 * x + core) * rows, 16), rows)
            term = dot(grads[j, 0, own], g0, ((1,), (1,))) + dot(grads[j, 1, own], g1, ((1,), (1,)))
            left_out[j] = STAT_DECAY * left[j] + (1.0 - STAT_DECAY) * term
            cols = grads[j, x // 2, :, pl.ds(pl.multiple_of((x % 2) * 2 * rows, 128), 2 * rows)]
            for h, g in ((0, g0), (1, g1)):
                prod = dot(cols, g, ((0,), (0,)))
                term = jnp.where(core == 0, prod[:rows], prod[rows:])
                at_cols = pl.ds(h * half, half)
                right_out[j, :, at_cols] = STAT_DECAY * right[j, :, at_cols] + (1.0 - STAT_DECAY) * term

        @pl.when(jnp.logical_not(full))
        def _():
            left_out[j] = STAT_DECAY * left[j]
            right_out[j] = STAT_DECAY * right[j]

        stores.append(pltpu.make_async_copy(left_out.at[j], left_hbm.at[j], out_sems.at[0, j]))
        stores.append(pltpu.make_async_copy(right_out.at[j], right_hbm.at[j], out_sems.at[1, j]))
        stores[-2].start()
        stores[-1].start()
    for store in stores:
        store.wait()


def compact_kernel(at, table, rows, out):
    def body(i, carry):
        block = rows[table[at + i]]
        for x in range(out.shape[0]):
            out[x, i] = block
        return carry

    lax.fori_loop(0, out.shape[1], body, 0, unroll=8)


def place_kernel(at, core_at, table, own, other, out):
    width = own.shape[2]
    core = table[core_at]
    near = pl.ds(pl.multiple_of(core * width, 128), width)
    far = pl.ds(pl.multiple_of((1 - core) * width, 128), width)
    first = pl.program_id(0) * out.shape[0]

    def body(b, carry):
        source = table[at + first + b]
        out[b, :, near] = own[source]
        out[b, :, far] = other[source]
        return carry

    lax.fori_loop(0, out.shape[0], body, 0, unroll=8)


def call(kernel, out_shape, in_specs, scratch=()):
    return pl.pallas_call(
        kernel,
        out_shape=out_shape,
        in_specs=in_specs,
        out_specs=VMEM_SPEC,
        scratch_shapes=list(scratch),
        compiler_params=PARAMS,
    )


def exchange(value, axis):
    return lax.all_to_all(value, axis, 0, 0, tiled=True)


def in_hbm(value):
    return pltpu.with_memory_space_constraint(value, pltpu.HBM)


def swap_cores(value):
    return lax.ppermute(value, "core", [(0, 1), (1, 0)])


def local(grads, block_slot, left_stat, right_stat, left_root, right_root):
    grads = grads[0]
    chips = lax.axis_size("x")
    x = lax.axis_index("x")
    core = lax.axis_index("core")
    owners = lax.axis_size("y") * lax.axis_size("z")
    me = lax.axis_index("y") * lax.axis_size("z") + lax.axis_index("z")
    capacity, stat_rows, _ = left_stat.shape
    blocks, shard_rows, width = grads.shape
    half = width // 2
    depth = blocks // chips

    kept, sent, roots = pl.pallas_call(
        split_kernel,
        out_shape=[
            jax.ShapeDtypeStruct((blocks, shard_rows, half), BF16),
            jax.ShapeDtypeStruct((blocks, shard_rows, half), BF16),
            jax.ShapeDtypeStruct((2 * capacity, stat_rows, width), BF16),
        ],
        in_specs=[SMEM_SPEC, HBM_SPEC, HBM_SPEC, HBM_SPEC],
        out_specs=[VMEM_SPEC, VMEM_SPEC, HBM_SPEC],
        scratch_shapes=[pltpu.SemaphoreType.DMA((4,))],
        compiler_params=PARAMS,
    )(core.reshape(1), in_hbm(grads), in_hbm(left_root), in_hbm(right_root))
    other = swap_cores(sent)
    roots = lax.all_gather(roots, ("x", "core"), axis=0)

    ids = jnp.arange(blocks, dtype=jnp.int32)
    rank = jnp.sum((block_slot[None, :] < block_slot[:, None]).astype(jnp.int32), axis=1)
    order = jnp.sum(jnp.where(rank[None, :] == ids[:, None], ids[None, :], 0), axis=1)
    owner = block_slot // capacity
    here = rank % chips == x
    spot = rank // chips
    owner_ids = jnp.arange(owners, dtype=jnp.int32)
    hits = here[None, :] & (owner[None, :] == owner_ids[:, None])
    place = jnp.sum(jnp.where(hits, spot[None, :] - depth, 0), axis=1) + depth
    hits = here[None, :] & (spot[None, :] == ids[:depth, None])
    owner_here = jnp.sum(jnp.where(hits, owner[None, :], 0), axis=1)
    slot_here = jnp.sum(jnp.where(here & (owner == me), block_slot % capacity, 0))
    mine = block_slot[None, :] == me * capacity + ids[:capacity, None]
    full = jnp.sum(mine.astype(jnp.int32), axis=1)
    chip_of_slot = jnp.sum(jnp.where(mine, rank[None, :] % chips, 0), axis=1)
    source = (rank % chips) * depth + spot
    info = jnp.stack([core, slot_here, x])
    table = jnp.concatenate([source, place, owner_here, info, full, chip_of_slot])
    at_place = blocks
    at_owner = at_place + owners
    at_info = at_owner + depth

    parts = call(
        pair_sum_kernel,
        jax.ShapeDtypeStruct((chips, depth, shard_rows, half), BF16),
        [SMEM_SPEC, VMEM_SPEC, VMEM_SPEC],
    )(order, kept, other)
    parts = exchange(parts, "x")
    outgoing = call(
        functools.partial(chip_sum_kernel, at_place),
        jax.ShapeDtypeStruct((owners, shard_rows, half), BF16),
        [SMEM_SPEC, VMEM_SPEC],
        [pltpu.VMEM((depth + 1, shard_rows, half), BF16)],
    )(table, parts)
    own = exchange(outgoing, ("y", "z")).reshape(width, half)
    far = swap_cores(own)
    grads_all = lax.all_gather(own, ("x", "core"), axis=0)

    update = call(
        functools.partial(direction_kernel, at_info),
        jax.ShapeDtypeStruct((width, half), BF16),
        [SMEM_SPEC, HBM_SPEC, VMEM_SPEC, HBM_SPEC],
        [
            pltpu.VMEM((width, half), BF16),
            pltpu.VMEM((width // stat_rows, stat_rows, width), BF16),
            pltpu.VMEM((width // stat_rows, stat_rows, width), BF16),
            pltpu.SemaphoreType.DMA((3,)),
        ],
    )(table, in_hbm(own), far, in_hbm(roots))

    rows = exchange(update.reshape(owners, shard_rows, half), ("y", "z"))
    packed = call(
        functools.partial(compact_kernel, at_owner),
        jax.ShapeDtypeStruct((chips, depth, shard_rows, half), BF16),
        [SMEM_SPEC, VMEM_SPEC],
    )(table, rows)
    packed, grads_all = lax.optimization_barrier((packed, grads_all))
    near = exchange(packed, "x").reshape(blocks, shard_rows, half)
    beyond = swap_cores(near)

    left_new, right_new = pl.pallas_call(
        functools.partial(stats_kernel, at_info),
        out_shape=[jax.ShapeDtypeStruct(left_stat.shape, F32), jax.ShapeDtypeStruct(right_stat.shape, F32)],
        in_specs=[SMEM_SPEC, HBM_SPEC, VMEM_SPEC, VMEM_SPEC],
        out_specs=[HBM_SPEC, HBM_SPEC],
        scratch_shapes=[
            pltpu.VMEM((capacity, 2, width, half), BF16),
            pltpu.VMEM(left_stat.shape, F32),
            pltpu.VMEM(right_stat.shape, F32),
            pltpu.SemaphoreType.DMA((capacity,)),
            pltpu.SemaphoreType.DMA((2, capacity)),
        ],
        compiler_params=PARAMS,
        cost_estimate=pl.CostEstimate(flops=400_000_000, bytes_accessed=6_000_000, transcendentals=0),
    )(table, in_hbm(grads_all.reshape(chips, 2, width, half)), left_stat, right_stat)

    steps = 4
    whole = pl.BlockSpec((blocks, shard_rows, half), lambda i, table: (0, 0, 0))
    result = pl.pallas_call(
        functools.partial(place_kernel, 0, at_info),
        out_shape=jax.ShapeDtypeStruct((blocks, shard_rows, width), BF16),
        grid_spec=pltpu.PrefetchScalarGridSpec(
            num_scalar_prefetch=1,
            grid=(steps,),
            in_specs=[whole, whole],
            out_specs=pl.BlockSpec((blocks // steps, shard_rows, width), lambda i, table: (i, 0, 0)),
        ),
        compiler_params=PARAMS,
    )(table, near, beyond)
    return (result, left_new, right_new)


def solution(mesh):
    fine = Mesh(mesh.devices.reshape(4, 2, 4, 16), ("x", "core", "y", "z"))
    replica, shard = ("x", "core"), ("y", "z")
    in_specs = (
        P(replica, None, shard, None),
        P(),
        P(shard, replica, None),
        P(shard, replica, None),
        P(shard, replica, None),
        P(shard, replica, None),
    )
    out_specs = (P(None, shard, None), P(shard, replica, None), P(shard, replica, None))
    return jax.shard_map(local, mesh=fine, in_specs=in_specs, out_specs=out_specs, check_vma=False)
```

time: 157 us -> 147 us (0.936)
  waiting for transfers between devices: 27.5 us -> 9.89 us
  Pallas kernels: 10.9 us -> 28.4 us
  local copies, waits for them, and re-layouts: 6.92 us -> 0.71 us
  starting transfers between devices: 26.4 us -> 22.8 us
    pallas_call x5 -> x6, Pallas kernels: 9.26 us -> 26.8 us  [the longest x1 17 us: local(): pl.pallas_call(split_kernel, out_shape=[jax.ShapeDtypeStruct((blocks, sha...]
    all_gather x2 -> x1, waiting for transfers between devices: 9.66 us -> 0.01 us  [local(): roots = lax.all_gather(roots, ('x', 'core'), axis=0)]
    all_to_all x2 -> x1, waiting for transfers between devices: 15.8 us -> 8.47 us  [exchange(): return lax.all_to_all(value, axis, 0, 0, tiled=True)]
    unnamed x14 -> x6, local copies, waits for them, and re-layouts: 5.73 us -> 0.02 us
    all_to_all x2 -> x1, starting transfers between devices: 6.94 us -> 3.47 us  [exchange(): return lax.all_to_all(value, axis, 0, 0, tiled=True)]
    all_to_all x2 -> x3, blocking collectives: 66.9 us -> 67.2 us  [exchange(): return lax.all_to_all(value, axis, 0, 0, tiled=True)]
  transfers between devices with their start and end apart: 8 -> 6, of which waited for: 4 -> 2; matrix products, arithmetic and copies ran while one was open for 3% -> 2% of each run, Pallas kernels for 5% -> 6%
where the time goes in v2:
time: 147 us; the launch traced here: 146 us
  blocking collectives  67.2 us (46%)
  Pallas kernels  28.4 us (19%)
  starting transfers between devices  22.8 us (16%)
  between operations  14.2 us (10%)
  waiting for transfers between devices  9.89 us (7%)
  other arithmetic  2.85 us (2%)
    all_to_all x3, blocking collectives, exchange(): return lax.all_to_all(value, axis, 0, 0, tiled=True)  67.2 us
    ppermute x3, starting transfers between devices, swap_cores(): return lax.ppermute(value, 'core', [(0, 1), (1, 0)])  19.3 us
    pallas_call x1, Pallas kernels, local(): pl.pallas_call(split_kernel, out_shape=[jax.ShapeDtypeStruct((blocks, sha...  17 us
    all_to_all x1, waiting for transfers between devices, exchange(): return lax.all_to_all(value, axis, 0, 0, tiled=True)  8.47 us
    all_to_all x1, starting transfers between devices, exchange(): return lax.all_to_all(value, axis, 0, 0, tiled=True)  3.47 us
    pallas_call x1, Pallas kernels, local(): pl.pallas_call(functools.partial(stats_kernel, at_info), out_shape=[jax.S...  3.31 us
  transfers between devices with their start and end apart: 6, of which 2 were waited for; matrix products, arithmetic and copies ran while one was open for 2% of the time, Pallas kernels for 6%

profile of v2, /device:TPU:1, one launch (start us, length us, event | category | flops | bytes accessed | tf_op | source)
XLA Modules:
  0.0 146.1 jit_solution(16720321195751754357)
XLA Ops:
  7.2 0.0 copy-start.2
  7.2 0.0 all-gather.6.cloned.1.call-start
  7.2 17.0 %shard_map.85 = (bf16[128,8,256]{2,1,0:T(8,128)(2,1)S(1)}, bf16[128,8,256]{2,1,0:T(8,128)(2,1)S(1)}, bf16[8,64,512]{2,1,0:T(8,128)(2,1)}) custom-call(s32[1]{0:T(128)} %bitcast.core_ref, bf16[128,8,512]{2,1,0:T(8,128)(2,1)} %bitcast.19, bf16[4,64,512]{2,1,0:T(8,128)(2,1)} %left_root.1, bf16[4,64,512]{2,1,0:T(8,128)(2,1)} %right_root.1), custom_call_target="tpu_custom_call" | custom-call | tf_op jit(solution)/shard_map/pallas_call | solution.py:209
  24.3 0.0 all-gather.6.cloned.1.call-update
  24.3 8.8 %collective-permute-start = (bf16[128,8,256]{2,1,0:T(8,128)(2,1)S(1)}, bf16[128,8,256]{2,1,0:T(8,128)(2,1)S(1)}, u32[]{:S(2)}, u32[]{:S(2)}) collective-permute-start(bf16[128,8,256]{2,1,0:T(8,128)(2,1)S(1)} %get-tuple-element.11), channel_id=1, source_target_pairs={{0,64},{64,0},{1,65},{65,1},{2,66},{66,2},{3,67},{67,3},{4,68},{68... | collective-permute-start | bytes 1572872 | tf_op jit(solution)/shard_map/ppermute | solution.py:194
  33.1 0.9 convert_reduce_fusion
  34.0 0.1 select_reduce_fusion.order
  34.1 1.3 fusion.3
  35.5 0.1 select_reduce_fusion.1
  35.6 0.0 collective-permute-done.other
  35.6 1.6 %shard_map.86 = bf16[4,32,8,256]{3,2,1,0:T(8,128)(2,1)} custom-call(s32[128]{0:T(128)S(1)} %select_reduce_fusion.order, bf16[128,8,256]{2,1,0:T(8,128)(2,1)S(1)} %get-tuple-element.10.own, bf16[128,8,256]{2,1,0:T(8,128)(2,1)S(1)} %collective-permute-done.other), custom_call_target="tpu_custom_call" | custom-call | tf_op jit(solution)/shard_map/pallas_call | solution.py:246
  37.2 3.5 %all-to-all-start = ((bf16[4,32,8,256]{3,2,1,0:T(8,128)(2,1)}), bf16[4,32,8,256]{3,2,1,0:T(8,128)(2,1)S(1)}, u32[]{:S(2)}, u32[]{:S(2)}) async-start(bf16[4,32,8,256]{3,2,1,0:T(8,128)(2,1)} %shard_map.86), calls=%async_computation | async-start | bytes 1048576 | tf_op jit(solution)/shard_map/all_to_all | solution.py:186
  40.6 0.0 all-gather.4.cloned.1.call-start
  40.7 0.0 copy-done.2
  40.7 0.2 fusion.2
  40.9 0.2 select_reduce_fusion.2
  41.1 0.7 concatenate.3.table
  41.8 8.5 %all-to-all-done.parts = bf16[4,32,8,256]{3,2,1,0:T(8,128)(2,1)S(1)} async-done(((bf16[4,32,8,256]{3,2,1,0:T(8,128)(2,1)}), bf16[4,32,8,256]{3,2,1,0:T(8,128)(2,1)S(1)}, u32[]{:S(2)}, u32[]{:S(2)}) %all-to-all-start) | async-done | bytes 524320 | tf_op jit(solution)/shard_map/all_to_all | solution.py:186
  50.2 0.7 shard_map.87
  51.0 0.0 copy-start
  51.0 0.0 copy-start.1
  51.0 32.0 %all_to_all.20 = bf16[64,8,256]{2,1,0:T(8,128)(2,1)} all-to-all(bf16[64,8,256]{2,1,0:T(8,128)(2,1)S(1)} %shard_map.87), channel_id=1, replica_groups=mesh['x'=4,'core'=2,'y'=4,'z'=16] {'y','z'}, dimensions={0} | all-to-all | bytes 524288 | tf_op jit(solution)/shard_map/all_to_all | solution.py:186
  83.0 0.0 all-gather.4.cloned.1.call-update
  83.0 5.3 %collective-permute-start.1 = (bf16[512,256]{1,0:T(8,128)(2,1)}, bf16[512,256]{1,0:T(8,128)(2,1)S(1)}, u32[]{:S(2)}, u32[]{:S(2)}) collective-permute-start(bf16[512,256]{1,0:T(8,128)(2,1)} %bitcast.16), channel_id=1, source_target_pairs={{0,64},{64,0},{1,65},{65,1},{2,66},{66,2},{3,67},{67,3},{4,68},{68... | collective-permute-start | bytes 786440 | tf_op jit(solution)/shard_map/ppermute | solution.py:194
  88.3 1.4 collective-permute-done.1.other
  89.6 0.0 all-gather.6.cloned.1.call-done
  89.6 2.9 %shard_map.88 = bf16[512,256]{1,0:T(8,128)(2,1)S(1)} custom-call(s32[235]{0:T(256)S(1)} %concatenate.3.table, bf16[512,256]{1,0:T(8,128)(2,1)} %bitcast.17, bf16[512,256]{1,0:T(8,128)(2,1)S(1)} %collective-permute-done.1.other, bf16[8,8,64,512]{3,2,1,0:T(8,128)(2,1)} %bitcast.14), custom_call_target="tpu_custom_call" | custom-call | tf_op jit(solution)/shard_map/pallas_call | solution.py:262
  92.5 25.8 %all_to_all.21.rows = bf16[64,8,256]{2,1,0:T(8,128)(2,1)S(1)} all-to-all(bf16[64,8,256]{2,1,0:T(8,128)(2,1)S(1)} %bitcast.13), channel_id=1, replica_groups=mesh['x'=4,'core'=2,'y'=4,'z'=16] {'y','z'}, dimensions={0} | all-to-all | bytes 524288 | tf_op jit(solution)/shard_map/all_to_all | solution.py:186
  118.3 0.6 shard_map.89
  118.9 0.0 all-gather.4.cloned.1.call-done
  118.9 9.5 %all_to_all.22 = bf16[4,32,8,256]{3,2,1,0:T(8,128)(2,1)S(1)} all-to-all(bf16[4,32,8,256]{3,2,1,0:T(8,128)(2,1)S(1)} %shard_map.89), channel_id=1, replica_groups=mesh['x'=4,'core'=2,'y'=4,'z'=16] {'x'}, dimensions={0} | all-to-all | bytes 1048576 | tf_op jit(solution)/shard_map/all_to_all | solution.py:186
  128.4 5.2 %collective-permute-start.2 = (bf16[128,8,256]{2,1,0:T(8,128)(2,1)S(1)}, bf16[128,8,256]{2,1,0:T(8,128)(2,1)S(1)}, u32[]{:S(2)}, u32[]{:S(2)}) collective-permute-start(bf16[128,8,256]{2,1,0:T(8,128)(2,1)S(1)} %bitcast.11), channel_id=1, source_target_pairs={{0,64},{64,0},{1,65},{65,1},{2,66},{66,2},{3,67},{67,3},{4,68},{68... | collective-permute-start | bytes 1572872 | tf_op jit(solution)/shard_map/ppermute | solution.py:194
  133.7 0.0 copy-done
  133.7 0.0 copy-done.1
  133.7 3.3 %shard_map.91 = (f32[4,64,512]{2,1,0:T(8,128)}, f32[4,64,512]{2,1,0:T(8,128)}) custom-call(s32[235]{0:T(256)S(1)} %concatenate.3.table, bf16[4,2,512,256]{3,2,1,0:T(8,128)(2,1)} %bitcast.18, f32[4,64,512]{2,1,0:T(8,128)S(1)} %copy-done, f32[4,64,512]{2,1,0:T(8,128)S(1)} %copy-done.1), custom_call_target="tpu_custom_call" | custom-call | flops 400000000 | bytes 6000000 | tf_op jit(solution)/shard_map/pallas_call | solution.py:284
  137.0 0.0 collective-permute-done.2.other
  137.0 2.2 %shard_map.90 = bf16[128,8,512]{2,1,0:T(8,128)(2,1)} custom-call(s32[235]{0:T(256)S(1)} %concatenate.3.table, bf16[128,8,256]{2,1,0:T(8,128)(2,1)S(1)} %bitcast.12, bf16[128,8,256]{2,1,0:T(8,128)(2,1)S(1)} %collective-permute-done.2.other), custom_call_target="tpu_custom_call" | custom-call | tf_op jit(solution)/shard_map/pallas_call | solution.py:302
  (5 shorter events, 0.0 us)
Async XLA Ops:
  7.2 33.5 %copy-start.2 = (s32[128]{0:T(128)S(1)}, s32[128]{0:T(128)}, u32[]{:S(2)}) copy-start(s32[128]{0:T(128)} %param.7) | copy-start | bytes 1540
  7.2 82.5 %all-gather.6.cloned.1.call-start = ((), (), s32[]{:S(2)}) async-start(), calls=%async_computation.5 | async-start | bytes 4718592 | tf_op jit(solution)/shard_map/all_gather | solution.py:222
  24.3 11.3 %collective-permute-start = (bf16[128,8,256]{2,1,0:T(8,128)(2,1)S(1)}, bf16[128,8,256]{2,1,0:T(8,128)(2,1)S(1)}, u32[]{:S(2)}, u32[]{:S(2)}) collective-permute-start(bf16[128,8,256]{2,1,0:T(8,128)(2,1)S(1)} %get-tuple-element.11), channel_id=1, source_target_pairs={{0,64},{64,0},{1,65},{65,1},{2,66},{66,2},{3,67},{67,3},{4,68},{68... | collective-permute-start | bytes 1572872 | tf_op jit(solution)/shard_map/ppermute | solution.py:194
  37.2 13.1 %all-to-all-start = ((bf16[4,32,8,256]{3,2,1,0:T(8,128)(2,1)}), bf16[4,32,8,256]{3,2,1,0:T(8,128)(2,1)S(1)}, u32[]{:S(2)}, u32[]{:S(2)}) async-start(bf16[4,32,8,256]{3,2,1,0:T(8,128)(2,1)} %shard_map.86), calls=%async_computation | async-start | bytes 1048576 | tf_op jit(solution)/shard_map/all_to_all | solution.py:186
  40.6 78.3 %all-gather.4.cloned.1.call-start = ((), (), s32[]{:S(2)}) async-start(), calls=%async_computation.4 | async-start | bytes 2359296 | tf_op jit(solution)/shard_map/all_gather | solution.py:260
  51.0 82.7 %copy-start = (f32[4,64,512]{2,1,0:T(8,128)S(1)}, f32[4,64,512]{2,1,0:T(8,128)}, u32[]{:S(2)}) copy-start(f32[4,64,512]{2,1,0:T(8,128)} %left.1) | copy-start | bytes 1572868
  51.0 82.7 %copy-start.1 = (f32[4,64,512]{2,1,0:T(8,128)S(1)}, f32[4,64,512]{2,1,0:T(8,128)}, u32[]{:S(2)}) copy-start(f32[4,64,512]{2,1,0:T(8,128)} %right.1) | copy-start | bytes 1572868
  83.0 6.6 %collective-permute-start.1 = (bf16[512,256]{1,0:T(8,128)(2,1)}, bf16[512,256]{1,0:T(8,128)(2,1)S(1)}, u32[]{:S(2)}, u32[]{:S(2)}) collective-permute-start(bf16[512,256]{1,0:T(8,128)(2,1)} %bitcast.16), channel_id=1, source_target_pairs={{0,64},{64,0},{1,65},{65,1},{2,66},{66,2},{3,67},{67,3},{4,68},{68... | collective-permute-start | bytes 786440 | tf_op jit(solution)/shard_map/ppermute | solution.py:194
  128.4 8.6 %collective-permute-start.2 = (bf16[128,8,256]{2,1,0:T(8,128)(2,1)S(1)}, bf16[128,8,256]{2,1,0:T(8,128)(2,1)S(1)}, u32[]{:S(2)}, u32[]{:S(2)}) collective-permute-start(bf16[128,8,256]{2,1,0:T(8,128)(2,1)S(1)} %bitcast.11), channel_id=1, source_target_pairs={{0,64},{64,0},{1,65},{65,1},{2,66},{66,2},{3,67},{67,3},{4,68},{68... | collective-permute-start | bytes 1572872 | tf_op jit(solution)/shard_map/ppermute | solution.py:194
Sparse Core Ops, SparseCore 0:
  24.4 45.4 all-gather.5
  83.1 26.2 all-gather.3

commit v3 on v2

v3 whole, which is shorter than its diff:
```python
import functools

import jax
import jax.numpy as jnp
from jax import lax
from jax.experimental import pallas as pl
from jax.experimental.pallas import tpu as pltpu
from jax.sharding import Mesh, PartitionSpec as P

STAT_DECAY = 0.9
NORM_EPS = 1e-12
F32 = jnp.float32
BF16 = jnp.bfloat16
VMEM_SPEC = pl.BlockSpec(memory_space=pltpu.VMEM)
HBM_SPEC = pl.BlockSpec(memory_space=pltpu.HBM)
SMEM_SPEC = pl.BlockSpec(memory_space=pltpu.SMEM)
PARAMS = pltpu.CompilerParams(vmem_limit_bytes=32 * 1024 * 1024)


def dot(a, b, dims):
    return lax.dot_general(a, b, (dims, ((), ())), preferred_element_type=F32)


ORDER, SOURCE, PLACE, OWNER, SLOT, FULL, CHIP, WHERE = range(8)


def fill_table(slots, core, x, me, capacity, chips, table):
    blocks = slots.shape[1]
    square = (blocks, blocks)
    cap_bits, chip_bits = capacity.bit_length() - 1, chips.bit_length() - 1
    depth = blocks // chips
    lane = lax.broadcasted_iota(jnp.int32, square, 1)
    sublane = lax.broadcasted_iota(jnp.int32, square, 0)
    across = jnp.broadcast_to(slots[...], square)
    slot = across.T

    def total(mask, value):
        return jnp.sum(jnp.where(mask, value, 0), axis=0, keepdims=True)

    rank_row = total(slot < across, 1)
    rank = jnp.broadcast_to(rank_row, square).T
    here = (rank & (chips - 1)) == x
    spot = rank >> chip_bits
    owner = slot >> cap_bits
    local_slot = slot == me * capacity + lane
    table[pl.ds(ORDER, 1)] = total(rank == lane, sublane)
    table[pl.ds(SOURCE, 1)] = (rank_row & (chips - 1)) * depth + (rank_row >> chip_bits)
    table[pl.ds(PLACE, 1)] = total(here & (owner == lane), spot - depth) + depth
    table[pl.ds(OWNER, 1)] = total(here & (spot == lane), owner)
    table[pl.ds(SLOT, 1)] = total(here & (owner == me), slot & (capacity - 1))
    table[pl.ds(FULL, 1)] = total(local_slot, 1)
    table[pl.ds(CHIP, 1)] = total(local_slot, rank & (chips - 1))
    row = lax.broadcasted_iota(jnp.int32, (1, blocks), 1)
    table[pl.ds(WHERE, 1)] = jnp.where(row == 0, core, x)


def split_kernel(chips, core_ref, x_ref, me_ref, slots, grads, left_root, right_root, kept, sent, roots, table, held, sems):
    core = core_ref[0]
    width = kept.shape[2]
    capacity = left_root.shape[0]
    near = pl.ds(pl.multiple_of(core * width, 128), width)
    far = pl.ds(pl.multiple_of((1 - core) * width, 128), width)
    loads = [
        pltpu.make_async_copy(left_root, held.at[pl.ds(0, capacity)], sems.at[0]),
        pltpu.make_async_copy(right_root, held.at[pl.ds(capacity, capacity)], sems.at[1]),
        pltpu.make_async_copy(grads.at[:, :, far], sent, sems.at[2]),
        pltpu.make_async_copy(grads.at[:, :, near], kept, sems.at[3]),
    ]
    store = pltpu.make_async_copy(held, roots, sems.at[4])
    for load in loads:
        load.start()
    loads[0].wait()
    loads[1].wait()
    store.start()
    fill_table(slots, core, x_ref[0], me_ref[0], capacity, chips, table)
    loads[2].wait()
    loads[3].wait()
    store.wait()


def pair_sum_kernel(table, own, other, out):
    chips, depth = out.shape[:2]

    def body(i, carry):
        for x in range(chips):
            block = table[ORDER, i * chips + x]
            out[x, i] = own[block] + other[block]
        return carry

    lax.fori_loop(0, depth, body, 0, unroll=8)


def chip_sum_kernel(table, parts, out, total):
    depth = parts.shape[1]
    acc = parts[0].astype(F32)
    for x in range(1, parts.shape[0]):
        acc = acc + parts[x].astype(F32)
    total[0:depth] = acc.astype(BF16)
    total[depth] = jnp.zeros(total.shape[1:], BF16)

    def body(o, carry):
        out[o] = total[table[PLACE, o]]
        return carry

    lax.fori_loop(0, out.shape[0], body, 0, unroll=8)


def near_kernel(table, own_hbm, roots, partial, left, lower, grad_sq, own, upper, sems):
    core, slot = table[WHERE, 0], table[SLOT, 0]
    capacity = roots.shape[1] // 2
    groups = upper.shape[0]
    half = own.shape[1]
    loads = [
        pltpu.make_async_copy(own_hbm, own, sems.at[0]),
        pltpu.make_async_copy(roots.at[pl.ds(core * groups, groups), capacity + slot], upper, sems.at[1]),
        pltpu.make_async_copy(roots.at[pl.ds((1 - core) * groups, groups), capacity + slot], lower, sems.at[2]),
        pltpu.make_async_copy(roots.at[:, slot], left, sems.at[3]),
    ]
    for load in loads:
        load.start()
    loads[0].wait()
    grad = own[...]
    grad_sq[...] = jnp.full(grad_sq.shape, jnp.sum(jnp.square(grad.astype(F32))), F32)
    loads[1].wait()
    partial[...] = dot(grad, upper[...].reshape(half, 2 * half), ((1,), (0,)))
    loads[2].wait()
    loads[3].wait()


def direction_kernel(table, other, partial, left, lower, grad_sq_near, out):
    core = table[WHERE, 0]
    half = other.shape[1]
    size = 2 * half
    grad = other[...]
    grad_sq = grad_sq_near[0:1, 0:1] + jnp.full((1, 1), jnp.sum(jnp.square(grad.astype(F32))), F32)
    left_mat = left[...].reshape(size, size)

    def columns(h):
        cols = pl.ds(pl.multiple_of(h * half, 128), half)
        shaped = partial[:, cols] + dot(grad, lower[:, :, cols].reshape(half, half), ((1,), (0,)))
        return dot(left_mat, shaped.astype(BF16), ((1,), (0,)))

    dir_sq = jnp.sum(jnp.square(columns(1 - core)))
    near = columns(core)
    dir_sq = jnp.full((1, 1), dir_sq + jnp.sum(jnp.square(near)), F32)
    ratio = jnp.sqrt(grad_sq) / jnp.sqrt(dir_sq + NORM_EPS)
    out[...] = (-near * ratio).astype(BF16)


def stats_kernel(table, grads_hbm, left, right, left_hbm, right_hbm, grads, left_out, right_out, sems, out_sems):
    core, x = table[WHERE, 0], table[WHERE, 1]
    capacity, rows, _ = left.shape
    half = grads.shape[3]
    loads = [
        pltpu.make_async_copy(grads_hbm.at[table[CHIP, j]], grads.at[j], sems.at[j]) for j in range(capacity)
    ]
    stores = []
    for load in loads:
        load.start()
    for j in range(capacity):
        full = table[FULL, j] > 0
        loads[j].wait()

        @pl.when(full)
        def _():
            g0 = grads[j, 0]
            g1 = grads[j, 1]
            own = pl.ds(pl.multiple_of((2 * x + core) * rows, 16), rows)
            term = dot(grads[j, 0, own], g0, ((1,), (1,))) + dot(grads[j, 1, own], g1, ((1,), (1,)))
            left_out[j] = STAT_DECAY * left[j] + (1.0 - STAT_DECAY) * term
            cols = grads[j, x // 2, :, pl.ds(pl.multiple_of((x % 2) * 2 * rows, 128), 2 * rows)]
            for h, g in ((0, g0), (1, g1)):
                prod = dot(cols, g, ((0,), (0,)))
                term = jnp.where(core == 0, prod[:rows], prod[rows:])
                at_cols = pl.ds(h * half, half)
                right_out[j, :, at_cols] = STAT_DECAY * right[j, :, at_cols] + (1.0 - STAT_DECAY) * term

        @pl.when(jnp.logical_not(full))
        def _():
            left_out[j] = STAT_DECAY * left[j]
            right_out[j] = STAT_DECAY * right[j]

        stores.append(pltpu.make_async_copy(left_out.at[j], left_hbm.at[j], out_sems.at[0, j]))
        stores.append(pltpu.make_async_copy(right_out.at[j], right_hbm.at[j], out_sems.at[1, j]))
        stores[-2].start()
        stores[-1].start()
    for store in stores:
        store.wait()


def compact_kernel(table, rows, out):
    def body(i, carry):
        block = rows[table[OWNER, i]]
        for x in range(out.shape[0]):
            out[x, i] = block
        return carry

    lax.fori_loop(0, out.shape[1], body, 0, unroll=8)


def place_half(core, table, rows, out_hbm, ordered, sems):
    steps = sems.shape[0]
    step = rows.shape[0] // steps
    width = rows.shape[2]
    cols = pl.ds(pl.multiple_of(core * width, 128), width)
    stores = []
    for i in range(steps):

        def body(b, carry):
            ordered[i * step + b] = rows[table[SOURCE, i * step + b]]
            return carry

        lax.fori_loop(0, step, body, 0, unroll=8)
        part = pl.ds(i * step, step)
        stores.append(pltpu.make_async_copy(ordered.at[part], out_hbm.at[part, :, cols], sems.at[i]))
        stores[-1].start()
    for store in stores:
        store.wait()


def place_near_kernel(table, rows, out_hbm, ordered, sems):
    place_half(table[WHERE, 0], table, rows, out_hbm, ordered, sems)


def place_far_kernel(table, rows, begun, out_hbm, ordered, sems):
    del begun
    place_half(1 - table[WHERE, 0], table, rows, out_hbm, ordered, sems)


def call(kernel, out_shape, in_specs, scratch=()):
    return pl.pallas_call(
        kernel,
        out_shape=out_shape,
        in_specs=in_specs,
        out_specs=VMEM_SPEC,
        scratch_shapes=list(scratch),
        compiler_params=PARAMS,
    )


def exchange(value, axis):
    return lax.all_to_all(value, axis, 0, 0, tiled=True)


def in_hbm(value):
    return pltpu.with_memory_space_constraint(value, pltpu.HBM)


def swap_cores(value):
    return lax.ppermute(value, "core", [(0, 1), (1, 0)])


def local(grads, block_slot, left_stat, right_stat, left_root, right_root):
    grads = grads[0]
    chips = lax.axis_size("x")
    x = lax.axis_index("x")
    core = lax.axis_index("core")
    owners = lax.axis_size("y") * lax.axis_size("z")
    me = lax.axis_index("y") * lax.axis_size("z") + lax.axis_index("z")
    capacity, stat_rows, _ = left_stat.shape
    blocks, shard_rows, width = grads.shape
    half = width // 2
    depth = blocks // chips

    kept, sent, roots, table = pl.pallas_call(
        functools.partial(split_kernel, chips),
        out_shape=[
            jax.ShapeDtypeStruct((blocks, shard_rows, half), BF16),
            jax.ShapeDtypeStruct((blocks, shard_rows, half), BF16),
            jax.ShapeDtypeStruct((2 * capacity, stat_rows, width), BF16),
            jax.ShapeDtypeStruct((8, blocks), jnp.int32),
        ],
        in_specs=[SMEM_SPEC] * 3 + [VMEM_SPEC] + [HBM_SPEC] * 3,
        out_specs=[VMEM_SPEC, VMEM_SPEC, HBM_SPEC, VMEM_SPEC],
        scratch_shapes=[
            pltpu.VMEM((2 * capacity, stat_rows, width), BF16),
            pltpu.SemaphoreType.DMA((5,)),
        ],
        compiler_params=PARAMS,
    )(
        core.reshape(1),
        x.reshape(1),
        me.reshape(1),
        block_slot.reshape(1, blocks),
        in_hbm(grads),
        in_hbm(left_root),
        in_hbm(right_root),
    )
    other = swap_cores(sent)
    roots = lax.all_gather(roots, ("x", "core"), axis=0)

    parts = call(
        pair_sum_kernel,
        jax.ShapeDtypeStruct((chips, depth, shard_rows, half), BF16),
        [SMEM_SPEC, VMEM_SPEC, VMEM_SPEC],
    )(table, kept, other)
    parts = exchange(parts, "x")
    outgoing = call(
        chip_sum_kernel,
        jax.ShapeDtypeStruct((owners, shard_rows, half), BF16),
        [SMEM_SPEC, VMEM_SPEC],
        [pltpu.VMEM((depth + 1, shard_rows, half), BF16)],
    )(table, parts)
    own = exchange(outgoing, ("y", "z")).reshape(width, half)
    far = swap_cores(own)
    grads_all = lax.all_gather(own, ("x", "core"), axis=0)

    groups = width // stat_rows
    partial, left, lower, grad_sq = pl.pallas_call(
        near_kernel,
        out_shape=[
            jax.ShapeDtypeStruct((width, width), F32),
            jax.ShapeDtypeStruct((groups, stat_rows, width), BF16),
            jax.ShapeDtypeStruct((groups // 2, stat_rows, width), BF16),
            jax.ShapeDtypeStruct((8, 128), F32),
        ],
        in_specs=[SMEM_SPEC, HBM_SPEC, HBM_SPEC],
        out_specs=[VMEM_SPEC] * 4,
        scratch_shapes=[
            pltpu.VMEM((width, half), BF16),
            pltpu.VMEM((groups // 2, stat_rows, width), BF16),
            pltpu.SemaphoreType.DMA((4,)),
        ],
        compiler_params=PARAMS,
        cost_estimate=pl.CostEstimate(flops=270_000_000, bytes_accessed=4_000_000, transcendentals=0),
    )(table, in_hbm(own), in_hbm(roots))
    update = call(
        direction_kernel,
        jax.ShapeDtypeStruct((width, half), BF16),
        [SMEM_SPEC] + [VMEM_SPEC] * 5,
    )(table, far, partial, left, lower, grad_sq)

    rows = exchange(update.reshape(owners, shard_rows, half), ("y", "z"))
    packed = call(
        compact_kernel,
        jax.ShapeDtypeStruct((chips, depth, shard_rows, half), BF16),
        [SMEM_SPEC, VMEM_SPEC],
    )(table, rows)
    packed, grads_all = lax.optimization_barrier((packed, grads_all))
    near = exchange(packed, "x").reshape(blocks, shard_rows, half)

    left_new, right_new = pl.pallas_call(
        stats_kernel,
        out_shape=[jax.ShapeDtypeStruct(left_stat.shape, F32), jax.ShapeDtypeStruct(right_stat.shape, F32)],
        in_specs=[SMEM_SPEC, HBM_SPEC, VMEM_SPEC, VMEM_SPEC],
        out_specs=[HBM_SPEC, HBM_SPEC],
        scratch_shapes=[
            pltpu.VMEM((capacity, 2, width, half), BF16),
            pltpu.VMEM(left_stat.shape, F32),
            pltpu.VMEM(right_stat.shape, F32),
            pltpu.SemaphoreType.DMA((capacity,)),
            pltpu.SemaphoreType.DMA((2, capacity)),
        ],
        compiler_params=PARAMS,
        cost_estimate=pl.CostEstimate(flops=400_000_000, bytes_accessed=6_000_000, transcendentals=0),
    )(table, in_hbm(grads_all.reshape(chips, 2, width, half)), left_stat, right_stat)

    near, left_new, right_new = lax.optimization_barrier((near, left_new, right_new))
    beyond = swap_cores(near)
    scratch = [pltpu.VMEM((blocks, shard_rows, half), BF16), pltpu.SemaphoreType.DMA((4,))]
    begun = pl.pallas_call(
        place_near_kernel,
        out_shape=jax.ShapeDtypeStruct((blocks, shard_rows, width), BF16),
        in_specs=[SMEM_SPEC, VMEM_SPEC],
        out_specs=HBM_SPEC,
        scratch_shapes=scratch,
        compiler_params=PARAMS,
        cost_estimate=pl.CostEstimate(flops=0, bytes_accessed=4_000_000, transcendentals=0),
    )(table, near)
    result = pl.pallas_call(
        place_far_kernel,
        out_shape=jax.ShapeDtypeStruct((blocks, shard_rows, width), BF16),
        in_specs=[SMEM_SPEC, VMEM_SPEC, HBM_SPEC],
        out_specs=HBM_SPEC,
        scratch_shapes=scratch,
        input_output_aliases={2: 0},
        compiler_params=PARAMS,
    )(table, beyond, begun)
    return (result, left_new, right_new)


def solution(mesh):
    fine = Mesh(mesh.devices.reshape(4, 2, 4, 16), ("x", "core", "y", "z"))
    replica, shard = ("x", "core"), ("y", "z")
    in_specs = (
        P(replica, None, shard, None),
        P(),
        P(shard, replica, None),
        P(shard, replica, None),
        P(shard, replica, None),
        P(shard, replica, None),
    )
    out_specs = (P(None, shard, None), P(shard, replica, None), P(shard, replica, None))
    return jax.shard_map(local, mesh=fine, in_specs=in_specs, out_specs=out_specs, check_vma=False)
```

time: 147 us -> 129 us (0.88)
  Pallas kernels: 28.4 us -> 15.4 us
  waiting for transfers between devices: 9.89 us -> 5.57 us
  other arithmetic: 2.85 us -> 0 us
  blocking collectives: 67.2 us -> 69.4 us
    pallas_call x6 -> x8, Pallas kernels: 26.8 us -> 14.6 us  [the longest x1 3.37 us: local(): pl.pallas_call(stats_kernel, out_shape=[jax.ShapeDtypeStruct(left_stat.sh...]
    all_to_all x1, waiting for transfers between devices: 8.47 us -> 3.99 us  [exchange(): return lax.all_to_all(value, axis, 0, 0, tiled=True)]
    reduce_sum x6 -> x0, other arithmetic: 2.83 us -> none  [the longest x1 1.34 us: local(): jnp.sum(jnp.where(here & (owner == me), block_slot % capacity, 0))]
    all_to_all x3, blocking collectives: 67.2 us -> 69.4 us  [exchange(): return lax.all_to_all(value, axis, 0, 0, tiled=True)]
  transfers between devices with their start and end apart: 6 -> 6, of which waited for: 2 -> 2; matrix products, arithmetic and copies ran while one was open for 2% -> 0% of each run, Pallas kernels for 6% -> 9%
where the time goes in v3:
time: 129 us; the launch traced here: 128 us
  blocking collectives  69.4 us (54%)
  starting transfers between devices  23.2 us (18%)
  Pallas kernels  15.4 us (12%)
  between operations  14.2 us (11%)
  waiting for transfers between devices  5.57 us (4%)
    all_to_all x3, blocking collectives, exchange(): return lax.all_to_all(value, axis, 0, 0, tiled=True)  69.4 us
    ppermute x3, starting transfers between devices, swap_cores(): return lax.ppermute(value, 'core', [(0, 1), (1, 0)])  19.7 us
    all_to_all x1, waiting for transfers between devices, exchange(): return lax.all_to_all(value, axis, 0, 0, tiled=True)  3.99 us
    all_to_all x1, starting transfers between devices, exchange(): return lax.all_to_all(value, axis, 0, 0, tiled=True)  3.47 us
    pallas_call x1, Pallas kernels, local(): pl.pallas_call(stats_kernel, out_shape=[jax.ShapeDtypeStruct(left_stat.sh...  3.37 us
  transfers between devices with their start and end apart: 6, of which 2 were waited for; matrix products, arithmetic and copies ran while one was open for 0% of the time, Pallas kernels for 9%

profile of v3, /device:TPU:1, one launch (start us, length us, event | category | flops | bytes accessed | tf_op | source)
XLA Modules:
  0.0 128.5 jit_solution(4203931994509815215)
XLA Ops:
  7.2 0.0 all-gather.6.cloned.1.call-start
  7.2 0.0 copy-start.2
  7.2 0.6 copy-done.2
  7.9 1.9 %shard_map.85 = (bf16[128,8,256]{2,1,0:T(8,128)(2,1)S(1)}, bf16[128,8,256]{2,1,0:T(8,128)(2,1)S(1)}, bf16[8,64,512]{2,1,0:T(8,128)(2,1)}, s32[8,128]{1,0:T(8,128)S(1)}) custom-call(s32[1]{0:T(128)} %bitcast.core_ref, s32[1]{0:T(128)} %bitcast.1.x_ref, s32[1]{0:T(128)} %bitcast.2.me_ref, s32[1,128]{1,0:T(1,128)S(1)} %bitcast.14, ...), custom_call_target="tpu_custom_call" | custom-call | tf_op jit(solution)/shard_map/pallas_call | solution.py:265
  9.7 0.0 all-gather.6.cloned.1.call-update
  9.8 0.0 all-gather.4.cloned.1.call-start
  9.8 8.8 %collective-permute-start = (bf16[128,8,256]{2,1,0:T(8,128)(2,1)S(1)}, bf16[128,8,256]{2,1,0:T(8,128)(2,1)S(1)}, u32[]{:S(2)}, u32[]{:S(2)}) collective-permute-start(bf16[128,8,256]{2,1,0:T(8,128)(2,1)S(1)} %get-tuple-element.20), channel_id=1, source_target_pairs={{0,64},{64,0},{1,65},{65,1},{2,66},{66,2},{3,67},{67,3},{4,68},{68... | collective-permute-start | bytes 1572872 | tf_op jit(solution)/shard_map/ppermute | solution.py:250
  18.6 1.5 %collective-permute-done.other = bf16[128,8,256]{2,1,0:T(8,128)(2,1)S(1)} collective-permute-done((bf16[128,8,256]{2,1,0:T(8,128)(2,1)S(1)}, bf16[128,8,256]{2,1,0:T(8,128)(2,1)S(1)}, u32[]{:S(2)}, u32[]{:S(2)}) %collective-permute-start) | collective-permute-done | bytes 524320 | tf_op jit(solution)/shard_map/ppermute | solution.py:250
  20.1 0.8 shard_map.86
  20.9 11.6 %all_to_all.20.parts = bf16[4,32,8,256]{3,2,1,0:T(8,128)(2,1)S(1)} all-to-all(bf16[4,32,8,256]{3,2,1,0:T(8,128)(2,1)S(1)} %shard_map.86), channel_id=1, replica_groups=mesh['x'=4,'core'=2,'y'=4,'z'=16] {'x'}, dimensions={0} | all-to-all | bytes 1048576 | tf_op jit(solution)/shard_map/all_to_all | solution.py:242
  32.6 0.9 shard_map.87
  33.4 31.7 %all_to_all.21 = bf16[64,8,256]{2,1,0:T(8,128)(2,1)} all-to-all(bf16[64,8,256]{2,1,0:T(8,128)(2,1)S(1)} %shard_map.87), channel_id=1, replica_groups=mesh['x'=4,'core'=2,'y'=4,'z'=16] {'y','z'}, dimensions={0} | all-to-all | bytes 524288 | tf_op jit(solution)/shard_map/all_to_all | solution.py:242
  65.1 0.0 all-gather.4.cloned.1.call-update
  65.1 6.0 %collective-permute-start.1 = (bf16[512,256]{1,0:T(8,128)(2,1)}, bf16[512,256]{1,0:T(8,128)(2,1)S(1)}, u32[]{:S(2)}, u32[]{:S(2)}) collective-permute-start(bf16[512,256]{1,0:T(8,128)(2,1)} %bitcast.17), channel_id=1, source_target_pairs={{0,64},{64,0},{1,65},{65,1},{2,66},{66,2},{3,67},{67,3},{4,68},{68... | collective-permute-start | bytes 786440 | tf_op jit(solution)/shard_map/ppermute | solution.py:250
  71.1 0.0 all-gather.6.cloned.1.call-done
  71.1 0.0 copy-start
  71.1 0.0 copy-start.1
  71.2 2.1 %shard_map.88 = (f32[512,512]{1,0:T(8,128)S(1)}, bf16[8,64,512]{2,1,0:T(8,128)(2,1)S(1)}, bf16[4,64,512]{2,1,0:T(8,128)(2,1)S(1)}, f32[8,128]{1,0:T(8,128)S(1)}) custom-call(s32[8,128]{1,0:T(8,128)S(1)} %get-tuple-element.18.table, bf16[512,256]{1,0:T(8,128)(2,1)} %bitcast.18, bf16[8,8,64,512]{3,2,1,0:T(8,128)(2,1)} %bitcast.15), custom_call_target="tpu_custom_call" | custom-call | flops 270000000 | bytes 4000000 | tf_op jit(solution)/shard_map/pallas_call | solution.py:309
  73.3 0.0 collective-permute-done.1.other
  73.3 1.5 %shard_map.89 = bf16[512,256]{1,0:T(8,128)(2,1)S(1)} custom-call(s32[8,128]{1,0:T(8,128)S(1)} %get-tuple-element.18.table, bf16[512,256]{1,0:T(8,128)(2,1)S(1)} %collective-permute-done.1.other, f32[512,512]{1,0:T(8,128)S(1)} %get-tuple-element.22.partial, bf16[8,64,512]{2,1,0:T(8,128)(2,1)S(1)} %get-tuple-element.23.left, ...), custom_call_target="tpu_custom_call" | custom-call | tf_op jit(solution)/shard_map/pallas_call | solution.py:327
  74.8 26.1 %all_to_all.22.rows = bf16[64,8,256]{2,1,0:T(8,128)(2,1)S(1)} all-to-all(bf16[64,8,256]{2,1,0:T(8,128)(2,1)S(1)} %bitcast.13), channel_id=1, replica_groups=mesh['x'=4,'core'=2,'y'=4,'z'=16] {'y','z'}, dimensions={0} | all-to-all | bytes 524288 | tf_op jit(solution)/shard_map/all_to_all | solution.py:242
  100.9 1.5 %shard_map.90 = bf16[4,32,8,256]{3,2,1,0:T(8,128)(2,1)} custom-call(s32[8,128]{1,0:T(8,128)S(1)} %get-tuple-element.18.table, bf16[64,8,256]{2,1,0:T(8,128)(2,1)S(1)} %all_to_all.22.rows), custom_call_target="tpu_custom_call" | custom-call | tf_op jit(solution)/shard_map/pallas_call | solution.py:334
  102.4 0.0 all-gather.4.cloned.1.call-done
  102.4 3.5 %all-to-all-start.3 = ((bf16[4,32,8,256]{3,2,1,0:T(8,128)(2,1)}), bf16[4,32,8,256]{3,2,1,0:T(8,128)(2,1)S(1)}, u32[]{:S(2)}, u32[]{:S(2)}) async-start(bf16[4,32,8,256]{3,2,1,0:T(8,128)(2,1)} %shard_map.90), calls=%async_computation.3 | async-start | bytes 1048576 | tf_op jit(solution)/shard_map/all_to_all | solution.py:242
  105.9 0.0 copy-done
  105.9 0.0 copy-done.1
  105.9 3.4 %shard_map.91 = (f32[4,64,512]{2,1,0:T(8,128)}, f32[4,64,512]{2,1,0:T(8,128)}) custom-call(s32[8,128]{1,0:T(8,128)S(1)} %get-tuple-element.18.table, bf16[4,2,512,256]{3,2,1,0:T(8,128)(2,1)} %bitcast.19, f32[4,64,512]{2,1,0:T(8,128)S(1)} %copy-done, f32[4,64,512]{2,1,0:T(8,128)S(1)} %copy-done.1), custom_call_target="tpu_custom_call" | custom-call | flops 400000000 | bytes 6000000 | tf_op jit(solution)/shard_map/pallas_call | solution.py:342
  109.3 4.0 %all-to-all-done.3 = bf16[4,32,8,256]{3,2,1,0:T(8,128)(2,1)S(1)} async-done(((bf16[4,32,8,256]{3,2,1,0:T(8,128)(2,1)}), bf16[4,32,8,256]{3,2,1,0:T(8,128)(2,1)S(1)}, u32[]{:S(2)}, u32[]{:S(2)}) %all-to-all-start.3) | async-done | bytes 524320 | tf_op jit(solution)/shard_map/all_to_all | solution.py:242
  113.2 4.9 %collective-permute-start.2 = (bf16[128,8,256]{2,1,0:T(8,128)(2,1)S(1)}, bf16[128,8,256]{2,1,0:T(8,128)(2,1)S(1)}, u32[]{:S(2)}, u32[]{:S(2)}) collective-permute-start(bf16[128,8,256]{2,1,0:T(8,128)(2,1)S(1)} %bitcast.11), channel_id=1, source_target_pairs={{0,64},{64,0},{1,65},{65,1},{2,66},{66,2},{3,67},{67,3},{4,68},{68... | collective-permute-start | bytes 1572872 | tf_op jit(solution)/shard_map/ppermute | solution.py:250
  118.2 1.7 %shard_map.92.begun = bf16[128,8,512]{2,1,0:T(8,128)(2,1)} custom-call(s32[8,128]{1,0:T(8,128)S(1)} %get-tuple-element.18.table, bf16[128,8,256]{2,1,0:T(8,128)(2,1)S(1)} %bitcast.12), custom_call_target="tpu_custom_call" | custom-call | bytes 4000000 | tf_op jit(solution)/shard_map/pallas_call | solution.py:361
  119.9 0.0 collective-permute-done.2.rows
  119.9 1.7 %shard_map.93 = bf16[128,8,512]{2,1,0:T(8,128)(2,1)} custom-call(s32[8,128]{1,0:T(8,128)S(1)} %get-tuple-element.18.table, bf16[128,8,256]{2,1,0:T(8,128)(2,1)S(1)} %collective-permute-done.2.rows, bf16[128,8,512]{2,1,0:T(8,128)(2,1)} %shard_map.92.begun), custom_call_target="tpu_custom_call", output_to_operand_aliasing={{}: (2, {})} | custom-call | tf_op jit(solution)/shard_map/pallas_call | solution.py:370
Async XLA Ops:
  7.2 64.0 %all-gather.6.cloned.1.call-start = ((), (), s32[]{:S(2)}) async-start(), calls=%async_computation.5 | async-start | bytes 4718592 | tf_op jit(solution)/shard_map/all_gather | solution.py:290
  7.2 0.7 copy-start.2
  9.8 92.6 %all-gather.4.cloned.1.call-start = ((), (), s32[]{:S(2)}) async-start(), calls=%async_computation.4 | async-start | bytes 2359296 | tf_op jit(solution)/shard_map/all_gather | solution.py:306
  9.8 10.3 %collective-permute-start = (bf16[128,8,256]{2,1,0:T(8,128)(2,1)S(1)}, bf16[128,8,256]{2,1,0:T(8,128)(2,1)S(1)}, u32[]{:S(2)}, u32[]{:S(2)}) collective-permute-start(bf16[128,8,256]{2,1,0:T(8,128)(2,1)S(1)} %get-tuple-element.20), channel_id=1, source_target_pairs={{0,64},{64,0},{1,65},{65,1},{2,66},{66,2},{3,67},{67,3},{4,68},{68... | collective-permute-start | bytes 1572872 | tf_op jit(solution)/shard_map/ppermute | solution.py:250
  65.1 8.2 %collective-permute-start.1 = (bf16[512,256]{1,0:T(8,128)(2,1)}, bf16[512,256]{1,0:T(8,128)(2,1)S(1)}, u32[]{:S(2)}, u32[]{:S(2)}) collective-permute-start(bf16[512,256]{1,0:T(8,128)(2,1)} %bitcast.17), channel_id=1, source_target_pairs={{0,64},{64,0},{1,65},{65,1},{2,66},{66,2},{3,67},{67,3},{4,68},{68... | collective-permute-start | bytes 786440 | tf_op jit(solution)/shard_map/ppermute | solution.py:250
  71.1 34.7 %copy-start = (f32[4,64,512]{2,1,0:T(8,128)S(1)}, f32[4,64,512]{2,1,0:T(8,128)}, u32[]{:S(2)}) copy-start(f32[4,64,512]{2,1,0:T(8,128)} %left.1) | copy-start | bytes 1572868
  71.1 34.7 %copy-start.1 = (f32[4,64,512]{2,1,0:T(8,128)S(1)}, f32[4,64,512]{2,1,0:T(8,128)}, u32[]{:S(2)}) copy-start(f32[4,64,512]{2,1,0:T(8,128)} %right.1) | copy-start | bytes 1572868
  102.4 10.9 %all-to-all-start.3 = ((bf16[4,32,8,256]{3,2,1,0:T(8,128)(2,1)}), bf16[4,32,8,256]{3,2,1,0:T(8,128)(2,1)S(1)}, u32[]{:S(2)}, u32[]{:S(2)}) async-start(bf16[4,32,8,256]{3,2,1,0:T(8,128)(2,1)} %shard_map.90), calls=%async_computation.3 | async-start | bytes 1048576 | tf_op jit(solution)/shard_map/all_to_all | solution.py:242
  113.2 6.6 %collective-permute-start.2 = (bf16[128,8,256]{2,1,0:T(8,128)(2,1)S(1)}, bf16[128,8,256]{2,1,0:T(8,128)(2,1)S(1)}, u32[]{:S(2)}, u32[]{:S(2)}) collective-permute-start(bf16[128,8,256]{2,1,0:T(8,128)(2,1)S(1)} %bitcast.11), channel_id=1, source_target_pairs={{0,64},{64,0},{1,65},{65,1},{2,66},{66,2},{3,67},{67,3},{4,68},{68... | collective-permute-start | bytes 1572872 | tf_op jit(solution)/shard_map/ppermute | solution.py:250
Sparse Core Ops, SparseCore 0:
  10.7 45.4 all-gather.5
  65.2 26.9 all-gather.3

commit v4 on v3

v4 whole, which is shorter than its diff:
```python
import functools

import jax
import jax.numpy as jnp
from jax import lax
from jax.experimental import pallas as pl
from jax.experimental.pallas import tpu as pltpu
from jax.sharding import Mesh, PartitionSpec as P

STAT_DECAY = 0.9
NORM_EPS = 1e-12
F32 = jnp.float32
BF16 = jnp.bfloat16
VMEM_SPEC = pl.BlockSpec(memory_space=pltpu.VMEM)
HBM_SPEC = pl.BlockSpec(memory_space=pltpu.HBM)
SMEM_SPEC = pl.BlockSpec(memory_space=pltpu.SMEM)
PARAMS = pltpu.CompilerParams(vmem_limit_bytes=32 * 1024 * 1024)


def dot(a, b, dims):
    return lax.dot_general(a, b, (dims, ((), ())), preferred_element_type=F32)


ORDER, SOURCE, PLACE, OWNER, SLOT, FULL, CHIP, WHERE = range(8)


def fill_table(slots, core, x, me, capacity, chips, table):
    blocks = slots.shape[1]
    square = (blocks, blocks)
    cap_bits, chip_bits = capacity.bit_length() - 1, chips.bit_length() - 1
    depth = blocks // chips
    lane = lax.broadcasted_iota(jnp.int32, square, 1)
    sublane = lax.broadcasted_iota(jnp.int32, square, 0)
    across = jnp.broadcast_to(slots[...], square)
    slot = across.T

    def total(mask, value):
        return jnp.sum(jnp.where(mask, value, 0), axis=0, keepdims=True)

    rank_row = total(slot < across, 1)
    rank = jnp.broadcast_to(rank_row, square).T
    chip = rank & (chips - 1)
    spot = rank >> chip_bits
    owner = slot >> cap_bits
    local_slot = slot == me * capacity + lane
    table[pl.ds(ORDER, 1)] = total(rank == lane, sublane)
    table[pl.ds(SOURCE, 1)] = (rank_row & (chips - 1)) * depth + (rank_row >> chip_bits)
    table[pl.ds(PLACE, 1)] = total((chip == x) & (owner == lane), spot - depth) + depth
    table[pl.ds(OWNER, 1)] = total((chip == x) & (spot == lane), owner)
    table[pl.ds(SLOT, 1)] = total((owner == me) & (chip == lane), slot & (capacity - 1))
    table[pl.ds(FULL, 1)] = total(local_slot, 1)
    table[pl.ds(CHIP, 1)] = total(local_slot, chip)
    row = lax.broadcasted_iota(jnp.int32, (1, blocks), 1)
    table[pl.ds(WHERE, 1)] = jnp.where(row == 0, core, x)


def send_kernel(core_ref, grads, sent, sem):
    width = sent.shape[2]
    far = pl.ds(pl.multiple_of((1 - core_ref[0]) * width, 128), width)
    load = pltpu.make_async_copy(grads.at[:, :, far], sent, sem)
    load.start()
    load.wait()


def keep_kernel(chips, capacity, core_ref, x_ref, me_ref, slots_hbm, grads, kept, table, slots, sems):
    core = core_ref[0]
    width = kept.shape[2]
    near = pl.ds(pl.multiple_of(core * width, 128), width)
    slots_load = pltpu.make_async_copy(slots_hbm, slots, sems.at[0])
    load = pltpu.make_async_copy(grads.at[:, :, near], kept, sems.at[1])
    slots_load.start()
    load.start()
    slots_load.wait()
    fill_table(slots, core, x_ref[0], me_ref[0], capacity, chips, table)
    load.wait()


def select_roots_kernel(table, left_root, right_root, *refs):
    pieces, sems = refs[:-1], refs[-1]
    chips = len(pieces)
    loads = []
    for k, piece in enumerate(pieces):
        slot = table[SLOT, lax.rem(table[WHERE, 1] + k, chips)]
        for side, root in enumerate((left_root, right_root)):
            loads.append(pltpu.make_async_copy(root.at[slot], piece.at[side], sems.at[k, side]))
            loads[-1].start()
    for load in loads:
        load.wait()


def order_roots_kernel(table, *refs):
    pieces, out = refs[:-1], refs[-1]
    chips = len(pieces)
    for k, piece in enumerate(pieces):
        out[lax.rem(table[WHERE, 1] + chips - k, chips)] = piece[...]


def merge_roots_kernel(table, mine, others, left, right):
    core = table[WHERE, 0]
    for x in range(mine.shape[0]):
        left[2 * x + core] = mine[x, 0]
        right[2 * x + core] = mine[x, 1]
        left[2 * x + 1 - core] = others[x, 0]
        right[2 * x + 1 - core] = others[x, 1]


def pair_sum_kernel(table, own, other, out):
    chips, depth = out.shape[:2]

    def body(i, carry):
        for x in range(chips):
            block = table[ORDER, i * chips + x]
            out[x, i] = own[block] + other[block]
        return carry

    lax.fori_loop(0, depth, body, 0, unroll=8)


def chip_sum_kernel(table, parts, out, total):
    depth = parts.shape[1]
    acc = parts[0].astype(F32)
    for x in range(1, parts.shape[0]):
        acc = acc + parts[x].astype(F32)
    total[0:depth] = acc.astype(BF16)
    total[depth] = jnp.zeros(total.shape[1:], BF16)

    def body(o, carry):
        out[o] = total[table[PLACE, o]]
        return carry

    lax.fori_loop(0, out.shape[0], body, 0, unroll=8)


def near_kernel(table, own, right, partial, grad_sq):
    core = table[WHERE, 0]
    half = own.shape[1]
    groups = right.shape[0] // 2
    grad = own[...]
    grad_sq[...] = jnp.full(grad_sq.shape, jnp.sum(jnp.square(grad.astype(F32))), F32)
    upper = right[pl.ds(core * groups, groups)].reshape(half, 2 * half)
    partial[...] = dot(grad, upper, ((1,), (0,)))


def direction_kernel(table, other, partial, left, right, grad_sq_near, out):
    core = table[WHERE, 0]
    half = other.shape[1]
    groups = right.shape[0] // 2
    size = 2 * half
    grad = other[...]
    grad_sq = grad_sq_near[0:1, 0:1] + jnp.full((1, 1), jnp.sum(jnp.square(grad.astype(F32))), F32)
    left_mat = left[...].reshape(size, size)

    def columns(h):
        cols = pl.ds(pl.multiple_of(h * half, 128), half)
        lower = right[pl.ds((1 - core) * groups, groups), :, cols].reshape(half, half)
        shaped = partial[:, cols] + dot(grad, lower, ((1,), (0,)))
        return dot(left_mat, shaped.astype(BF16), ((1,), (0,)))

    dir_sq = jnp.sum(jnp.square(columns(1 - core)))
    near = columns(core)
    dir_sq = jnp.full((1, 1), dir_sq + jnp.sum(jnp.square(near)), F32)
    ratio = jnp.sqrt(grad_sq) / jnp.sqrt(dir_sq + NORM_EPS)
    out[...] = (-near * ratio).astype(BF16)


def terms_kernel(table, own, other, *refs):
    pieces, grad = refs[:-1], refs[-1]
    core, x = table[WHERE, 0], table[WHERE, 1]
    chips = len(pieces)
    half = own.shape[1]
    rows = pieces[0].shape[1]
    grad[:, pl.ds(pl.multiple_of(core * half, 128), half)] = own[...]
    grad[:, pl.ds(pl.multiple_of((1 - core) * half, 128), half)] = other[...]
    whole = grad[...]
    for k, piece in enumerate(pieces):
        chip = lax.rem(x + k, chips)
        some = grad[pl.ds(pl.multiple_of((2 * chip + core) * rows, 16), rows)]
        piece[0] = dot(some, whole, ((1,), (1,))).astype(BF16)
        cols = grad[:, pl.ds(pl.multiple_of(chip * 2 * rows, 128), 2 * rows)]
        both = dot(cols, whole, ((0,), (0,)))
        piece[1] = jnp.where(core == 0, both[:rows], both[rows:]).astype(BF16)


def stats_kernel(table, *refs):
    pieces = refs[:-8]
    left_hbm, right_hbm, left_new_hbm, right_new_hbm, stats, results, sems, out_sems = refs[-8:]
    chips = len(pieces)
    capacity = left_hbm.shape[0]
    loads = []
    for j in range(capacity):
        for side, source in enumerate((left_hbm, right_hbm)):
            loads.append(pltpu.make_async_copy(source.at[j], stats.at[j, side], sems.at[j, side]))
            loads[-1].start()
    stores = []
    for j in range(capacity):
        full = table[FULL, j] > 0
        k = lax.rem(table[WHERE, 1] + chips - table[CHIP, j], chips)
        loads[2 * j].wait()
        loads[2 * j + 1].wait()
        for other, piece in enumerate(pieces):

            @pl.when(jnp.logical_and(full, k == other))
            def _():
                results[j] = STAT_DECAY * stats[j] + (1.0 - STAT_DECAY) * piece[...].astype(F32)

        @pl.when(jnp.logical_not(full))
        def _():
            results[j] = STAT_DECAY * stats[j]

        for side, target in enumerate((left_new_hbm, right_new_hbm)):
            stores.append(pltpu.make_async_copy(results.at[j, side], target.at[j], out_sems.at[j, side]))
            stores[-1].start()
    for store in stores:
        store.wait()


def compact_kernel(table, rows, out):
    def body(i, carry):
        block = rows[table[OWNER, i]]
        for x in range(out.shape[0]):
            out[x, i] = block
        return carry

    lax.fori_loop(0, out.shape[1], body, 0, unroll=8)


def place_half(core, table, rows, out_hbm, ordered, sems):
    steps = sems.shape[0]
    step = rows.shape[0] // steps
    width = rows.shape[2]
    cols = pl.ds(pl.multiple_of(core * width, 128), width)
    stores = []
    for i in range(steps):

        def body(b, carry):
            ordered[i * step + b] = rows[table[SOURCE, i * step + b]]
            return carry

        lax.fori_loop(0, step, body, 0, unroll=8)
        part = pl.ds(i * step, step)
        stores.append(pltpu.make_async_copy(ordered.at[part], out_hbm.at[part, :, cols], sems.at[i]))
        stores[-1].start()
    for store in stores:
        store.wait()


def place_near_kernel(table, rows, out_hbm, ordered, sems):
    place_half(table[WHERE, 0], table, rows, out_hbm, ordered, sems)


def place_far_kernel(table, rows, begun, out_hbm, ordered, sems):
    del begun
    place_half(1 - table[WHERE, 0], table, rows, out_hbm, ordered, sems)


def call(kernel, out_shape, in_specs, scratch=(), out_specs=None, cost=None, aliases=None):
    if out_specs is None:
        out_specs = [VMEM_SPEC] * len(out_shape) if isinstance(out_shape, list) else VMEM_SPEC
    if cost is not None:
        cost = pl.CostEstimate(flops=cost[0], bytes_accessed=cost[1], transcendentals=0)
    return pl.pallas_call(
        kernel,
        out_shape=out_shape,
        in_specs=in_specs,
        out_specs=out_specs,
        scratch_shapes=list(scratch),
        input_output_aliases=aliases or {},
        compiler_params=PARAMS,
        cost_estimate=cost,
    )


def exchange(value, axis):
    return lax.all_to_all(value, axis, 0, 0, tiled=True)


def in_hbm(value):
    return pltpu.with_memory_space_constraint(value, pltpu.HBM)


def turn(value, k):
    chips = lax.axis_size("x")
    return lax.ppermute(value, "x", [(i, (i + k) % chips) for i in range(chips)]) if k else value


def swap_cores(value):
    return lax.ppermute(value, "core", [(0, 1), (1, 0)])


def local(grads, block_slot, left_stat, right_stat, left_root, right_root):
    grads = grads[0]
    chips = lax.axis_size("x")
    x = lax.axis_index("x")
    core = lax.axis_index("core")
    owners = lax.axis_size("y") * lax.axis_size("z")
    me = lax.axis_index("y") * lax.axis_size("z") + lax.axis_index("z")
    capacity, stat_rows, _ = left_stat.shape
    blocks, shard_rows, width = grads.shape
    half = width // 2
    depth = blocks // chips

    piece = jax.ShapeDtypeStruct((2, stat_rows, width), BF16)
    groups = width // stat_rows
    half_rows = jax.ShapeDtypeStruct((blocks, shard_rows, half), BF16)
    grads = in_hbm(grads)

    sent = call(send_kernel, half_rows, [SMEM_SPEC, HBM_SPEC], [pltpu.SemaphoreType.DMA])(core.reshape(1), grads)
    sent, late_grads = lax.optimization_barrier((sent, grads))
    other = swap_cores(sent)
    kept, table = call(
        functools.partial(keep_kernel, chips, capacity),
        [half_rows, jax.ShapeDtypeStruct((8, blocks), jnp.int32)],
        [SMEM_SPEC] * 3 + [HBM_SPEC] * 2,
        [pltpu.VMEM((1, blocks), jnp.int32), pltpu.SemaphoreType.DMA((2,))],
        cost=(0, 4_000_000),
    )(core.reshape(1), x.reshape(1), me.reshape(1), in_hbm(block_slot.reshape(1, blocks)), in_hbm(late_grads))

    parts = call(
        pair_sum_kernel,
        jax.ShapeDtypeStruct((chips, depth, shard_rows, half), BF16),
        [SMEM_SPEC, VMEM_SPEC, VMEM_SPEC],
    )(table, kept, other)
    parts = exchange(parts, "x")
    outgoing = call(
        chip_sum_kernel,
        jax.ShapeDtypeStruct((owners, shard_rows, half), BF16),
        [SMEM_SPEC, VMEM_SPEC],
        [pltpu.VMEM((depth + 1, shard_rows, half), BF16)],
    )(table, parts)

    outgoing, late_table = lax.optimization_barrier((outgoing, table))
    own = exchange(outgoing, ("y", "z"))
    pieces = call(
        select_roots_kernel,
        [piece] * chips,
        [SMEM_SPEC, HBM_SPEC, HBM_SPEC],
        [pltpu.SemaphoreType.DMA((chips, 2))],
        cost=(0, 2_000_000),
    )(late_table, in_hbm(left_root), in_hbm(right_root))
    pieces = [turn(value, k) for k, value in enumerate(pieces)]
    mine = call(
        order_roots_kernel,
        jax.ShapeDtypeStruct((chips, 2, stat_rows, width), BF16),
        [SMEM_SPEC] + [VMEM_SPEC] * chips,
        cost=(0, 1_000_000),
    )(late_table, *pieces)
    others = swap_cores(mine)
    left, right = call(
        merge_roots_kernel,
        [jax.ShapeDtypeStruct((groups, stat_rows, width), BF16)] * 2,
        [SMEM_SPEC, VMEM_SPEC, VMEM_SPEC],
        cost=(0, 2_000_000),
    )(late_table, mine, others)
    own, left, right = lax.optimization_barrier((own, left, right))

    own = own.reshape(width, half)
    far = swap_cores(own)
    partial, grad_sq = call(
        near_kernel,
        [jax.ShapeDtypeStruct((width, width), F32), jax.ShapeDtypeStruct((8, 128), F32)],
        [SMEM_SPEC, VMEM_SPEC, VMEM_SPEC],
        cost=(270_000_000, 4_000_000),
    )(table, own, right)
    update = call(
        direction_kernel,
        jax.ShapeDtypeStruct((width, half), BF16),
        [SMEM_SPEC] + [VMEM_SPEC] * 5,
    )(table, far, partial, left, right, grad_sq)

    update, own, far = lax.optimization_barrier((update, own, far))
    rows = exchange(update.reshape(owners, shard_rows, half), ("y", "z"))
    pieces = call(
        terms_kernel,
        [piece] * chips,
        [SMEM_SPEC, VMEM_SPEC, VMEM_SPEC],
        [pltpu.VMEM((width, width), BF16)],
        cost=(800_000_000, 2_000_000),
    )(table, own, far)
    pieces = [turn(value, k) for k, value in enumerate(pieces)]
    stat = jax.ShapeDtypeStruct(left_stat.shape, F32)
    both_stats = (capacity, 2, stat_rows, width)
    left_new, right_new = call(
        stats_kernel,
        [stat, stat],
        [SMEM_SPEC] + [VMEM_SPEC] * chips + [HBM_SPEC] * 2,
        [
            pltpu.VMEM(both_stats, F32),
            pltpu.VMEM(both_stats, F32),
            pltpu.SemaphoreType.DMA((capacity, 2)),
            pltpu.SemaphoreType.DMA((capacity, 2)),
        ],
        [HBM_SPEC, HBM_SPEC],
        cost=(10_000_000, 5_000_000),
    )(table, *pieces, in_hbm(left_stat), in_hbm(right_stat))
    rows, left_new, right_new = lax.optimization_barrier((rows, left_new, right_new))

    packed = call(
        compact_kernel,
        jax.ShapeDtypeStruct((chips, depth, shard_rows, half), BF16),
        [SMEM_SPEC, VMEM_SPEC],
    )(table, rows)
    near = exchange(packed, "x").reshape(blocks, shard_rows, half)
    beyond = swap_cores(near)
    whole_rows = jax.ShapeDtypeStruct((blocks, shard_rows, width), BF16)
    scratch = [pltpu.VMEM((blocks, shard_rows, half), BF16), pltpu.SemaphoreType.DMA((4,))]
    begun = call(
        place_near_kernel, whole_rows, [SMEM_SPEC, VMEM_SPEC], scratch, HBM_SPEC, cost=(0, 4_000_000)
    )(table, near)
    result = call(
        place_far_kernel, whole_rows, [SMEM_SPEC, VMEM_SPEC, HBM_SPEC], scratch, HBM_SPEC, aliases={2: 0}
    )(table, beyond, begun)
    return (result, left_new, right_new)


def solution(mesh):
    fine = Mesh(mesh.devices.reshape(4, 2, 4, 16), ("x", "core", "y", "z"))
    replica, shard = ("x", "core"), ("y", "z")
    in_specs = (
        P(replica, None, shard, None),
        P(),
        P(shard, replica, None),
        P(shard, replica, None),
        P(shard, replica, None),
        P(shard, replica, None),
    )
    out_specs = (P(None, shard, None), P(shard, replica, None), P(shard, replica, None))
    return jax.shard_map(local, mesh=fine, in_specs=in_specs, out_specs=out_specs, check_vma=False)
```

time: 129 us -> 122 us (0.946)
  blocking collectives: 69.4 us -> 21.5 us
  starting transfers between devices: 23.2 us -> 67.6 us
  between operations: 14.2 us -> 0.85 us
  waiting for transfers between devices: 5.57 us -> 12.3 us
  Pallas kernels: 15.4 us -> 19.3 us
    all_to_all x3 -> x2, blocking collectives: 69.4 us -> 21.5 us  [exchange(): return lax.all_to_all(value, axis, 0, 0, tiled=True)]
    all_to_all x1 -> x2, starting transfers between devices: 3.47 us -> 28.7 us  [exchange(): return lax.all_to_all(value, axis, 0, 0, tiled=True)]
    ppermute x0 -> x6, starting transfers between devices: none -> 17.7 us  [turn(): lax.ppermute(value, 'x', [(i, (i + k) % chips) for i in range(chips)])]
    ppermute x0 -> x6, waiting for transfers between devices: none -> 7.75 us  [turn(): lax.ppermute(value, 'x', [(i, (i + k) % chips) for i in range(chips)])]
    pallas_call x5 -> x10, Pallas kernels: 10.8 us -> 14.1 us  [the longest x1 2.77 us: local(): call(stats_kernel, [stat, stat], [SMEM_SPEC] + [VMEM_SPEC] * chips + [HBM...]
    all_to_all x1 -> x2, waiting for transfers between devices: 3.99 us -> 2.41 us  [exchange(): return lax.all_to_all(value, axis, 0, 0, tiled=True)]
    ppermute x3 -> x4, starting transfers between devices: 19.7 us -> 21.1 us  [swap_cores(): return lax.ppermute(value, 'core', [(0, 1), (1, 0)])]
  transfers between devices with their start and end apart: 6 -> 12, of which waited for: 2 -> 8; matrix products, arithmetic and copies ran while one was open for 0% -> 0% of each run, Pallas kernels for 9% -> 9%
where the time goes in v4:
time: 122 us
  starting transfers between devices  67.6 us (55%)
  blocking collectives  21.5 us (18%)
  Pallas kernels  19.3 us (16%)
  waiting for transfers between devices  12.3 us (10%)
    all_to_all x2, starting transfers between devices, exchange(): return lax.all_to_all(value, axis, 0, 0, tiled=True)  28.7 us
    all_to_all x2, blocking collectives, exchange(): return lax.all_to_all(value, axis, 0, 0, tiled=True)  21.5 us
    ppermute x4, starting transfers between devices, swap_cores(): return lax.ppermute(value, 'core', [(0, 1), (1, 0)])  21.1 us
    ppermute x6, starting transfers between devices, turn(): lax.ppermute(value, 'x', [(i, (i + k) % chips) for i in range(chips)])  17.7 us
    ppermute x6, waiting for transfers between devices, turn(): lax.ppermute(value, 'x', [(i, (i + k) % chips) for i in range(chips)])  7.75 us
    pallas_call x1, Pallas kernels, local(): call(stats_kernel, [stat, stat], [SMEM_SPEC] + [VMEM_SPEC] * chips + [HBM...  2.77 us
  transfers between devices with their start and end apart: 12, of which 8 were waited for; matrix products, arithmetic and copies ran while one was open for 0% of the time, Pallas kernels for 9%

profile of v4, /device:TPU:1, one launch (start us, length us, event | category | flops | bytes accessed | tf_op | source)
XLA Modules:
  0.0 121.5 jit_solution(15950674883085493766)
XLA Ops:
  0.6 1.1 shard_map.85
  1.7 8.8 %collective-permute-start = (bf16[128,8,256]{2,1,0:T(8,128)(2,1)S(1)}, bf16[128,8,256]{2,1,0:T(8,128)(2,1)S(1)}, u32[]{:S(2)}, u32[]{:S(2)}) collective-permute-start(bf16[128,8,256]{2,1,0:T(8,128)(2,1)S(1)} %shard_map.85), channel_id=1, source_target_pairs={{0,64},{64,0},{1,65},{65,1},{2,66},{66,2},{3,67},{67,3},{4,68},{68... | collective-permute-start | bytes 1572872 | tf_op jit(solution)/shard_map/ppermute | solution.py:287
  10.5 1.1 shard_map.86
  11.6 0.4 collective-permute-done.other
  12.0 0.8 shard_map.87
  12.8 11.6 %all_to_all.20.parts = bf16[4,32,8,256]{3,2,1,0:T(8,128)(2,1)S(1)} all-to-all(bf16[4,32,8,256]{3,2,1,0:T(8,128)(2,1)S(1)} %shard_map.87), channel_id=1, replica_groups=mesh['x'=4,'core'=2,'y'=4,'z'=16] {'x'}, dimensions={0} | all-to-all | bytes 1048576 | tf_op jit(solution)/shard_map/all_to_all | solution.py:274
  24.4 1.6 %shard_map.88 = bf16[64,8,256]{2,1,0:T(8,128)(2,1)} custom-call(s32[8,128]{1,0:T(8,128)S(1)} %get-tuple-element.37.table, bf16[4,32,8,256]{3,2,1,0:T(8,128)(2,1)S(1)} %all_to_all.20.parts), custom_call_target="tpu_custom_call" | custom-call | tf_op jit(solution)/shard_map/pallas_call | solution.py:324
  26.0 13.9 %all-to-all-start.1 = ((bf16[64,8,256]{2,1,0:T(8,128)(2,1)}), bf16[64,8,256]{2,1,0:T(8,128)(2,1)S(1)}, u32[]{:S(2)}, u32[]{:S(2)}) async-start(bf16[64,8,256]{2,1,0:T(8,128)(2,1)} %shard_map.88), calls=%async_computation.1 | async-start | bytes 524288 | tf_op jit(solution)/shard_map/all_to_all | solution.py:274
  39.9 1.7 %shard_map.89 = (bf16[2,64,512]{2,1,0:T(8,128)(2,1)S(1)}, bf16[2,64,512]{2,1,0:T(8,128)(2,1)S(1)}, bf16[2,64,512]{2,1,0:T(8,128)(2,1)S(1)}, bf16[2,64,512]{2,1,0:T(8,128)(2,1)S(1)}) custom-call(s32[8,128]{1,0:T(8,128)S(1)} %get-tuple-element.37.table, bf16[4,64,512]{2,1,0:T(8,128)(2,1)} %left_root.1, bf16[4,64,512]{2,1,0:T(8,128)(2,1)} %right_root.1), custom_call_target="tpu_custom_call" | custom-call | bytes 2000000 | tf_op jit(solution)/shard_map/pallas_call | solution.py:333
  41.6 2.2 %collective-permute-start.1 = (bf16[2,64,512]{2,1,0:T(8,128)(2,1)S(1)}, bf16[2,64,512]{2,1,0:T(8,128)(2,1)S(1)}, u32[]{:S(2)}, u32[]{:S(2)}) collective-permute-start(bf16[2,64,512]{2,1,0:T(8,128)(2,1)S(1)} %get-tuple-element.39), channel_id=1, source_target_pairs={{0,128},{128,256},{256,384},{384,0},{1,129},{129,257},{257,385},{3... | collective-permute-start | bytes 393224 | tf_op jit(solution)/shard_map/ppermute | solution.py:283
  43.8 3.7 %collective-permute-start.2 = (bf16[2,64,512]{2,1,0:T(8,128)(2,1)S(1)}, bf16[2,64,512]{2,1,0:T(8,128)(2,1)S(1)}, u32[]{:S(2)}, u32[]{:S(2)}) collective-permute-start(bf16[2,64,512]{2,1,0:T(8,128)(2,1)S(1)} %get-tuple-element.40), channel_id=1, source_target_pairs={{0,256},{128,384},{256,0},{384,128},{1,257},{129,385},{257,1},{385... | collective-permute-start | bytes 393224 | tf_op jit(solution)/shard_map/ppermute | solution.py:283
  47.5 2.5 %collective-permute-start.3 = (bf16[2,64,512]{2,1,0:T(8,128)(2,1)S(1)}, bf16[2,64,512]{2,1,0:T(8,128)(2,1)S(1)}, u32[]{:S(2)}, u32[]{:S(2)}) collective-permute-start(bf16[2,64,512]{2,1,0:T(8,128)(2,1)S(1)} %get-tuple-element.41), channel_id=1, source_target_pairs={{0,384},{128,0},{256,128},{384,256},{1,385},{129,1},{257,129},{385... | collective-permute-start | bytes 393224 | tf_op jit(solution)/shard_map/ppermute | solution.py:283
  50.1 0.0 collective-permute-done.1.refs_1_
  50.1 2.1 %collective-permute-done.2.refs_2_ = bf16[2,64,512]{2,1,0:T(8,128)(2,1)S(1)} collective-permute-done((bf16[2,64,512]{2,1,0:T(8,128)(2,1)S(1)}, bf16[2,64,512]{2,1,0:T(8,128)(2,1)S(1)}, u32[]{:S(2)}, u32[]{:S(2)}) %collective-permute-start.2) | collective-permute-done | bytes 131104 | tf_op jit(solution)/shard_map/ppermute | solution.py:283
  52.2 2.2 %collective-permute-done.3.refs_3_ = bf16[2,64,512]{2,1,0:T(8,128)(2,1)S(1)} collective-permute-done((bf16[2,64,512]{2,1,0:T(8,128)(2,1)S(1)}, bf16[2,64,512]{2,1,0:T(8,128)(2,1)S(1)}, u32[]{:S(2)}, u32[]{:S(2)}) %collective-permute-start.3) | collective-permute-done | bytes 131104 | tf_op jit(solution)/shard_map/ppermute | solution.py:283
  54.4 0.6 shard_map.90.mine
  55.0 4.6 %collective-permute-start.4 = (bf16[4,2,64,512]{3,2,1,0:T(8,128)(2,1)S(1)}, bf16[4,2,64,512]{3,2,1,0:T(8,128)(2,1)S(1)}, u32[]{:S(2)}, u32[]{:S(2)}) collective-permute-start(bf16[4,2,64,512]{3,2,1,0:T(8,128)(2,1)S(1)} %shard_map.90.mine), channel_id=1, source_target_pairs={{0,64},{64,0},{1,65},{65,1},{2,66},{66,2},{3,67},{67,3},{4,68},{68... | collective-permute-start | bytes 1572872 | tf_op jit(solution)/shard_map/ppermute | solution.py:287
  59.6 1.5 %collective-permute-done.4.others = bf16[4,2,64,512]{3,2,1,0:T(8,128)(2,1)S(1)} collective-permute-done((bf16[4,2,64,512]{3,2,1,0:T(8,128)(2,1)S(1)}, bf16[4,2,64,512]{3,2,1,0:T(8,128)(2,1)S(1)}, u32[]{:S(2)}, u32[]{:S(2)}) %collective-permute-start.4) | collective-permute-done | bytes 524320 | tf_op jit(solution)/shard_map/ppermute | solution.py:287
  61.1 0.7 shard_map.91
  61.8 0.0 all-to-all-done.1
  61.8 2.3 %collective-permute-start.5 = (bf16[512,256]{1,0:T(8,128)(2,1)S(1)}, bf16[512,256]{1,0:T(8,128)(2,1)S(1)}, u32[]{:S(2)}, u32[]{:S(2)}) collective-permute-start(bf16[512,256]{1,0:T(8,128)(2,1)S(1)} %bitcast.10), channel_id=1, source_target_pairs={{0,64},{64,0},{1,65},{65,1},{2,66},{66,2},{3,67},{67,3},{4,68},{68... | collective-permute-start | bytes 786440 | tf_op jit(solution)/shard_map/ppermute | solution.py:287
  64.1 0.9 shard_map.92
  65.0 0.2 collective-permute-done.5.other
  65.3 2.2 %shard_map.93 = bf16[512,256]{1,0:T(8,128)(2,1)} custom-call(s32[8,128]{1,0:T(8,128)S(1)} %get-tuple-element.37.table, bf16[512,256]{1,0:T(8,128)(2,1)S(1)} %collective-permute-done.5.other, f32[512,512]{1,0:T(8,128)S(1)} %get-tuple-element.46.partial, bf16[8,64,512]{2,1,0:T(8,128)(2,1)S(1)} %get-tuple-element.47.left, ...), custom_call_target="tpu_custom_call" | custom-call | tf_op jit(solution)/shard_map/pallas_call | solution.py:364
  67.4 14.9 %all-to-all-start.2 = ((bf16[64,8,256]{2,1,0:T(8,128)(2,1)}), bf16[64,8,256]{2,1,0:T(8,128)(2,1)S(1)}, u32[]{:S(2)}, u32[]{:S(2)}) async-start(bf16[64,8,256]{2,1,0:T(8,128)(2,1)} %bitcast.6), calls=%async_computation.2 | async-start | bytes 524288 | tf_op jit(solution)/shard_map/all_to_all | solution.py:274
  82.3 1.8 %shard_map.94 = (bf16[2,64,512]{2,1,0:T(8,128)(2,1)S(1)}, bf16[2,64,512]{2,1,0:T(8,128)(2,1)S(1)}, bf16[2,64,512]{2,1,0:T(8,128)(2,1)S(1)}, bf16[2,64,512]{2,1,0:T(8,128)(2,1)S(1)}) custom-call(s32[8,128]{1,0:T(8,128)S(1)} %get-tuple-element.37.table, bf16[512,256]{1,0:T(8,128)(2,1)S(1)} %bitcast.12, bf16[512,256]{1,0:T(8,128)(2,1)S(1)} %collective-permute-done.5.other), custom_call_target="tpu_custom_call" | custom-call | flops 800000000 | bytes 2000000 | tf_op jit(solution)/shard_map/pallas_call | solution.py:372
  84.1 3.1 %collective-permute-start.6 = (bf16[2,64,512]{2,1,0:T(8,128)(2,1)S(1)}, bf16[2,64,512]{2,1,0:T(8,128)(2,1)S(1)}, u32[]{:S(2)}, u32[]{:S(2)}) collective-permute-start(bf16[2,64,512]{2,1,0:T(8,128)(2,1)S(1)} %get-tuple-element.53), channel_id=1, source_target_pairs={{0,128},{128,256},{256,384},{384,0},{1,129},{129,257},{257,385},{3... | collective-permute-start | bytes 393224 | tf_op jit(solution)/shard_map/ppermute | solution.py:283
  87.2 3.7 %collective-permute-start.7 = (bf16[2,64,512]{2,1,0:T(8,128)(2,1)S(1)}, bf16[2,64,512]{2,1,0:T(8,128)(2,1)S(1)}, u32[]{:S(2)}, u32[]{:S(2)}) collective-permute-start(bf16[2,64,512]{2,1,0:T(8,128)(2,1)S(1)} %get-tuple-element.54), channel_id=1, source_target_pairs={{0,256},{128,384},{256,0},{384,128},{1,257},{129,385},{257,1},{385... | collective-permute-start | bytes 393224 | tf_op jit(solution)/shard_map/ppermute | solution.py:283
  90.9 2.5 %collective-permute-start.8 = (bf16[2,64,512]{2,1,0:T(8,128)(2,1)S(1)}, bf16[2,64,512]{2,1,0:T(8,128)(2,1)S(1)}, u32[]{:S(2)}, u32[]{:S(2)}) collective-permute-start(bf16[2,64,512]{2,1,0:T(8,128)(2,1)S(1)} %get-tuple-element.55), channel_id=1, source_target_pairs={{0,384},{128,0},{256,128},{384,256},{1,385},{129,1},{257,129},{385... | collective-permute-start | bytes 393224 | tf_op jit(solution)/shard_map/ppermute | solution.py:283
  93.5 0.0 collective-permute-done.6.refs_1_
  93.5 1.3 %collective-permute-done.7.refs_2_ = bf16[2,64,512]{2,1,0:T(8,128)(2,1)S(1)} collective-permute-done((bf16[2,64,512]{2,1,0:T(8,128)(2,1)S(1)}, bf16[2,64,512]{2,1,0:T(8,128)(2,1)S(1)}, u32[]{:S(2)}, u32[]{:S(2)}) %collective-permute-start.7) | collective-permute-done | bytes 131104 | tf_op jit(solution)/shard_map/ppermute | solution.py:283
  94.7 2.2 %collective-permute-done.8.refs_3_ = bf16[2,64,512]{2,1,0:T(8,128)(2,1)S(1)} collective-permute-done((bf16[2,64,512]{2,1,0:T(8,128)(2,1)S(1)}, bf16[2,64,512]{2,1,0:T(8,128)(2,1)S(1)}, u32[]{:S(2)}, u32[]{:S(2)}) %collective-permute-start.8) | collective-permute-done | bytes 131104 | tf_op jit(solution)/shard_map/ppermute | solution.py:283
  96.9 2.8 %shard_map.95 = (f32[4,64,512]{2,1,0:T(8,128)}, f32[4,64,512]{2,1,0:T(8,128)}) custom-call(s32[8,128]{1,0:T(8,128)S(1)} %get-tuple-element.37.table, bf16[2,64,512]{2,1,0:T(8,128)(2,1)S(1)} %get-tuple-element.52.refs_0_, bf16[2,64,512]{2,1,0:T(8,128)(2,1)S(1)} %collective-permute-done.6.refs_1_, bf16[2,64,512]{2,1,0:T(8,128)(2,1)S(1)} %collective-permute-done.7.refs_2_, ...), custom_call_target="tpu_custom_call" | custom-call | flops 10000000 | bytes 5000000 | tf_op jit(solution)/shard_map/pallas_call | solution.py:382
  99.7 2.4 %all-to-all-done.2.rows = bf16[64,8,256]{2,1,0:T(8,128)(2,1)S(1)} async-done(((bf16[64,8,256]{2,1,0:T(8,128)(2,1)}), bf16[64,8,256]{2,1,0:T(8,128)(2,1)S(1)}, u32[]{:S(2)}, u32[]{:S(2)}) %all-to-all-start.2) | async-done | bytes 262176 | tf_op jit(solution)/shard_map/all_to_all | solution.py:274
  102.1 0.7 shard_map.96
  102.8 9.8 %all_to_all.21 = bf16[4,32,8,256]{3,2,1,0:T(8,128)(2,1)S(1)} all-to-all(bf16[4,32,8,256]{3,2,1,0:T(8,128)(2,1)S(1)} %shard_map.96), channel_id=1, replica_groups=mesh['x'=4,'core'=2,'y'=4,'z'=16] {'x'}, dimensions={0} | all-to-all | bytes 1048576 | tf_op jit(solution)/shard_map/all_to_all | solution.py:274
  112.7 5.4 %collective-permute-start.9 = (bf16[128,8,256]{2,1,0:T(8,128)(2,1)S(1)}, bf16[128,8,256]{2,1,0:T(8,128)(2,1)S(1)}, u32[]{:S(2)}, u32[]{:S(2)}) collective-permute-start(bf16[128,8,256]{2,1,0:T(8,128)(2,1)S(1)} %bitcast.8), channel_id=1, source_target_pairs={{0,64},{64,0},{1,65},{65,1},{2,66},{66,2},{3,67},{67,3},{4,68},{68... | collective-permute-start | bytes 1572872 | tf_op jit(solution)/shard_map/ppermute | solution.py:287
  118.1 1.7 %shard_map.97.begun = bf16[128,8,512]{2,1,0:T(8,128)(2,1)} custom-call(s32[8,128]{1,0:T(8,128)S(1)} %get-tuple-element.37.table, bf16[128,8,256]{2,1,0:T(8,128)(2,1)S(1)} %bitcast.9), custom_call_target="tpu_custom_call" | custom-call | bytes 4000000 | tf_op jit(solution)/shard_map/pallas_call | solution.py:406
  119.8 0.0 collective-permute-done.9.rows
  119.8 1.7 %shard_map.98 = bf16[128,8,512]{2,1,0:T(8,128)(2,1)} custom-call(s32[8,128]{1,0:T(8,128)S(1)} %get-tuple-element.37.table, bf16[128,8,256]{2,1,0:T(8,128)(2,1)S(1)} %collective-permute-done.9.rows, bf16[128,8,512]{2,1,0:T(8,128)(2,1)} %shard_map.97.begun), custom_call_target="tpu_custom_call", output_to_operand_aliasing={{}: (2, {})} | custom-call | tf_op jit(solution)/shard_map/pallas_call | solution.py:409
Async XLA Ops:
  1.7 10.3 %collective-permute-start = (bf16[128,8,256]{2,1,0:T(8,128)(2,1)S(1)}, bf16[128,8,256]{2,1,0:T(8,128)(2,1)S(1)}, u32[]{:S(2)}, u32[]{:S(2)}) collective-permute-start(bf16[128,8,256]{2,1,0:T(8,128)(2,1)S(1)} %shard_map.85), channel_id=1, source_target_pairs={{0,64},{64,0},{1,65},{65,1},{2,66},{66,2},{3,67},{67,3},{4,68},{68... | collective-permute-start | bytes 1572872 | tf_op jit(solution)/shard_map/ppermute | solution.py:287
  26.0 35.8 %all-to-all-start.1 = ((bf16[64,8,256]{2,1,0:T(8,128)(2,1)}), bf16[64,8,256]{2,1,0:T(8,128)(2,1)S(1)}, u32[]{:S(2)}, u32[]{:S(2)}) async-start(bf16[64,8,256]{2,1,0:T(8,128)(2,1)} %shard_map.88), calls=%async_computation.1 | async-start | bytes 524288 | tf_op jit(solution)/shard_map/all_to_all | solution.py:274
  41.6 8.4 %collective-permute-start.1 = (bf16[2,64,512]{2,1,0:T(8,128)(2,1)S(1)}, bf16[2,64,512]{2,1,0:T(8,128)(2,1)S(1)}, u32[]{:S(2)}, u32[]{:S(2)}) collective-permute-start(bf16[2,64,512]{2,1,0:T(8,128)(2,1)S(1)} %get-tuple-element.39), channel_id=1, source_target_pairs={{0,128},{128,256},{256,384},{384,0},{1,129},{129,257},{257,385},{3... | collective-permute-start | bytes 393224 | tf_op jit(solution)/shard_map/ppermute | solution.py:283
  43.8 8.4 %collective-permute-start.2 = (bf16[2,64,512]{2,1,0:T(8,128)(2,1)S(1)}, bf16[2,64,512]{2,1,0:T(8,128)(2,1)S(1)}, u32[]{:S(2)}, u32[]{:S(2)}) collective-permute-start(bf16[2,64,512]{2,1,0:T(8,128)(2,1)S(1)} %get-tuple-element.40), channel_id=1, source_target_pairs={{0,256},{128,384},{256,0},{384,128},{1,257},{129,385},{257,1},{385... | collective-permute-start | bytes 393224 | tf_op jit(solution)/shard_map/ppermute | solution.py:283
  47.5 6.8 %collective-permute-start.3 = (bf16[2,64,512]{2,1,0:T(8,128)(2,1)S(1)}, bf16[2,64,512]{2,1,0:T(8,128)(2,1)S(1)}, u32[]{:S(2)}, u32[]{:S(2)}) collective-permute-start(bf16[2,64,512]{2,1,0:T(8,128)(2,1)S(1)} %get-tuple-element.41), channel_id=1, source_target_pairs={{0,384},{128,0},{256,128},{384,256},{1,385},{129,1},{257,129},{385... | collective-permute-start | bytes 393224 | tf_op jit(solution)/shard_map/ppermute | solution.py:283
  55.0 6.1 %collective-permute-start.4 = (bf16[4,2,64,512]{3,2,1,0:T(8,128)(2,1)S(1)}, bf16[4,2,64,512]{3,2,1,0:T(8,128)(2,1)S(1)}, u32[]{:S(2)}, u32[]{:S(2)}) collective-permute-start(bf16[4,2,64,512]{3,2,1,0:T(8,128)(2,1)S(1)} %shard_map.90.mine), channel_id=1, source_target_pairs={{0,64},{64,0},{1,65},{65,1},{2,66},{66,2},{3,67},{67,3},{4,68},{68... | collective-permute-start | bytes 1572872 | tf_op jit(solution)/shard_map/ppermute | solution.py:287
  61.8 3.4 %collective-permute-start.5 = (bf16[512,256]{1,0:T(8,128)(2,1)S(1)}, bf16[512,256]{1,0:T(8,128)(2,1)S(1)}, u32[]{:S(2)}, u32[]{:S(2)}) collective-permute-start(bf16[512,256]{1,0:T(8,128)(2,1)S(1)} %bitcast.10), channel_id=1, source_target_pairs={{0,64},{64,0},{1,65},{65,1},{2,66},{66,2},{3,67},{67,3},{4,68},{68... | collective-permute-start | bytes 786440 | tf_op jit(solution)/shard_map/ppermute | solution.py:287
  67.4 34.7 %all-to-all-start.2 = ((bf16[64,8,256]{2,1,0:T(8,128)(2,1)}), bf16[64,8,256]{2,1,0:T(8,128)(2,1)S(1)}, u32[]{:S(2)}, u32[]{:S(2)}) async-start(bf16[64,8,256]{2,1,0:T(8,128)(2,1)} %bitcast.6), calls=%async_computation.2 | async-start | bytes 524288 | tf_op jit(solution)/shard_map/all_to_all | solution.py:274
  84.1 9.3 %collective-permute-start.6 = (bf16[2,64,512]{2,1,0:T(8,128)(2,1)S(1)}, bf16[2,64,512]{2,1,0:T(8,128)(2,1)S(1)}, u32[]{:S(2)}, u32[]{:S(2)}) collective-permute-start(bf16[2,64,512]{2,1,0:T(8,128)(2,1)S(1)} %get-tuple-element.53), channel_id=1, source_target_pairs={{0,128},{128,256},{256,384},{384,0},{1,129},{129,257},{257,385},{3... | collective-permute-start | bytes 393224 | tf_op jit(solution)/shard_map/ppermute | solution.py:283
  87.2 7.5 %collective-permute-start.7 = (bf16[2,64,512]{2,1,0:T(8,128)(2,1)S(1)}, bf16[2,64,512]{2,1,0:T(8,128)(2,1)S(1)}, u32[]{:S(2)}, u32[]{:S(2)}) collective-permute-start(bf16[2,64,512]{2,1,0:T(8,128)(2,1)S(1)} %get-tuple-element.54), channel_id=1, source_target_pairs={{0,256},{128,384},{256,0},{384,128},{1,257},{129,385},{257,1},{385... | collective-permute-start | bytes 393224 | tf_op jit(solution)/shard_map/ppermute | solution.py:283
  90.9 6.0 %collective-permute-start.8 = (bf16[2,64,512]{2,1,0:T(8,128)(2,1)S(1)}, bf16[2,64,512]{2,1,0:T(8,128)(2,1)S(1)}, u32[]{:S(2)}, u32[]{:S(2)}) collective-permute-start(bf16[2,64,512]{2,1,0:T(8,128)(2,1)S(1)} %get-tuple-element.55), channel_id=1, source_target_pairs={{0,384},{128,0},{256,128},{384,256},{1,385},{129,1},{257,129},{385... | collective-permute-start | bytes 393224 | tf_op jit(solution)/shard_map/ppermute | solution.py:283
  112.7 7.1 %collective-permute-start.9 = (bf16[128,8,256]{2,1,0:T(8,128)(2,1)S(1)}, bf16[128,8,256]{2,1,0:T(8,128)(2,1)S(1)}, u32[]{:S(2)}, u32[]{:S(2)}) collective-permute-start(bf16[128,8,256]{2,1,0:T(8,128)(2,1)S(1)} %bitcast.8), channel_id=1, source_target_pairs={{0,64},{64,0},{1,65},{65,1},{2,66},{66,2},{3,67},{67,3},{4,68},{68... | collective-permute-start | bytes 1572872 | tf_op jit(solution)/shard_map/ppermute | solution.py:287

commit v5 on v4

--- a/solution.py
+++ b/solution.py
@@ -54,12 +54,19 @@
     table[pl.ds(WHERE, 1)] = jnp.where(row == 0, core, x)
 
 
-def send_kernel(core_ref, grads, sent, sem):
+def send_kernel(core_ref, grads, left_root, right_root, sent, sems):
     width = sent.shape[2]
+    groups = grads.shape[0]
+    capacity = left_root.shape[0]
     far = pl.ds(pl.multiple_of((1 - core_ref[0]) * width, 128), width)
-    load = pltpu.make_async_copy(grads.at[:, :, far], sent, sem)
-    load.start()
-    load.wait()
+    loads = [pltpu.make_async_copy(grads.at[:, :, far], sent.at[pl.ds(0, groups)], sems.at[0])]
+    for i in range(4):
+        root = (left_root, right_root)[i // 2].at[:, :, pl.ds(i % 2 * width, width)]
+        loads.append(pltpu.make_async_copy(root, sent.at[pl.ds(groups + i * capacity, capacity)], sems.at[i + 1]))
+    for load in loads:
+        load.start()
+    for load in loads:
+        load.wait()
 
 
 def keep_kernel(chips, capacity, core_ref, x_ref, me_ref, slots_hbm, grads, kept, table, slots, sems):
@@ -75,33 +82,40 @@
     load.wait()
 
 
-def select_roots_kernel(table, left_root, right_root, *refs):
-    pieces, sems = refs[:-1], refs[-1]
-    chips = len(pieces)
+def select_roots_kernel(groups, table, other, left_root, right_root, beside, across, mine, sems):
+    core, x = table[WHERE, 0], table[WHERE, 1]
+    capacity = left_root.shape[0]
+    width = other.shape[2]
     loads = []
-    for k, piece in enumerate(pieces):
-        slot = table[SLOT, lax.rem(table[WHERE, 1] + k, chips)]
+    for i, (chip, out) in enumerate(((lax.rem(x + 1 + 2 * core, 4), beside), (x, mine), (lax.rem(x + 2, 4), across))):
+        slot = table[SLOT, chip]
+        target = across if i == 2 else out.at[core]
         for side, root in enumerate((left_root, right_root)):
-            loads.append(pltpu.make_async_copy(root.at[slot], piece.at[side], sems.at[k, side]))
+            loads.append(pltpu.make_async_copy(root.at[slot], target.at[side], sems.at[i, side]))
             loads[-1].start()
+    for chip, out in ((lax.rem(x + 1 + 2 * core, 4), beside), (x, mine)):
+        slot = table[SLOT, chip]
+        for i in range(4):
+            out[1 - core, i // 2, :, i % 2 * width : (i % 2 + 1) * width] = other[groups + i * capacity + slot]
     for load in loads:
         load.wait()
 
 
-def order_roots_kernel(table, *refs):
-    pieces, out = refs[:-1], refs[-1]
-    chips = len(pieces)
-    for k, piece in enumerate(pieces):
-        out[lax.rem(table[WHERE, 1] + chips - k, chips)] = piece[...]
-
-
-def merge_roots_kernel(table, mine, others, left, right):
-    core = table[WHERE, 0]
-    for x in range(mine.shape[0]):
-        left[2 * x + core] = mine[x, 0]
-        right[2 * x + core] = mine[x, 1]
-        left[2 * x + 1 - core] = others[x, 0]
-        right[2 * x + 1 - core] = others[x, 1]
+def stack_kernel(beside, across, out):
+    out[0:2] = beside[...]
+    out[2] = across[...]
+
+
+def merge_roots_kernel(table, mine, beside, across, others, left, right):
+    core, x = table[WHERE, 0], table[WHERE, 1]
+    near, far, opposite = lax.rem(x + 3 - 2 * core, 4), lax.rem(x + 1 + 2 * core, 4), lax.rem(x + 2, 4)
+    for side, out in enumerate((left, right)):
+        for parity in range(2):
+            out[2 * x + parity] = mine[parity, side]
+            out[2 * near + parity] = beside[parity, side]
+            out[2 * far + parity] = others[parity, side]
+        out[2 * opposite + core] = across[side]
+        out[2 * opposite + 1 - core] = others[2, side]
 
 
 def pair_sum_kernel(table, own, other, out):
@@ -114,6 +128,19 @@
         return carry
 
     lax.fori_loop(0, depth, body, 0, unroll=8)
+
+
+def store_in_steps(source, target, sems, dim, fill):
+    steps = sems.shape[0]
+    count = source.shape[dim] // steps
+    stores = []
+    for i in range(steps):
+        fill(i * count, count)
+        part = (slice(None),) * dim + (pl.ds(i * count, count),)
+        stores.append(pltpu.make_async_copy(source.at[part], target.at[part], sems.at[i]))
+        stores[-1].start()
+    for store in stores:
+        store.wait()
 
 
 def chip_sum_kernel(table, parts, out, total):
@@ -163,52 +190,51 @@
     out[...] = (-near * ratio).astype(BF16)
 
 
-def terms_kernel(table, own, other, *refs):
-    pieces, grad = refs[:-1], refs[-1]
+def terms_kernel(table, own, other, beside, across, mine, grad):
     core, x = table[WHERE, 0], table[WHERE, 1]
-    chips = len(pieces)
     half = own.shape[1]
-    rows = pieces[0].shape[1]
+    rows = mine.shape[1]
     grad[:, pl.ds(pl.multiple_of(core * half, 128), half)] = own[...]
     grad[:, pl.ds(pl.multiple_of((1 - core) * half, 128), half)] = other[...]
     whole = grad[...]
-    for k, piece in enumerate(pieces):
-        chip = lax.rem(x + k, chips)
-        some = grad[pl.ds(pl.multiple_of((2 * chip + core) * rows, 16), rows)]
-        piece[0] = dot(some, whole, ((1,), (1,))).astype(BF16)
-        cols = grad[:, pl.ds(pl.multiple_of(chip * 2 * rows, 128), 2 * rows)]
-        both = dot(cols, whole, ((0,), (0,)))
-        piece[1] = jnp.where(core == 0, both[:rows], both[rows:]).astype(BF16)
-
-
-def stats_kernel(table, *refs):
-    pieces = refs[:-8]
-    left_hbm, right_hbm, left_new_hbm, right_new_hbm, stats, results, sems, out_sems = refs[-8:]
-    chips = len(pieces)
-    capacity = left_hbm.shape[0]
-    loads = []
-    for j in range(capacity):
-        for side, source in enumerate((left_hbm, right_hbm)):
-            loads.append(pltpu.make_async_copy(source.at[j], stats.at[j, side], sems.at[j, side]))
-            loads[-1].start()
+
+    def of_chip(chip):
+        at = pl.ds(pl.multiple_of(chip * 2 * rows, 128), 2 * rows)
+        return dot(grad[at], whole, ((1,), (1,))), dot(grad[:, at], whole, ((0,), (0,)))
+
+    for side, term in enumerate(of_chip(lax.rem(x + 1 + 2 * core, 4))):
+        for parity in range(2):
+            beside[parity, side] = term[parity * rows : (parity + 1) * rows].astype(BF16)
+    for chip, out in ((lax.rem(x + 2, 4), across), (x, mine)):
+        for side, term in enumerate(of_chip(chip)):
+            out[side] = jnp.where(core == 0, term[:rows], term[rows:]).astype(BF16)
+
+
+def stats_kernel(table, mine, across, beside, passed, left, right, left_hbm, right_hbm, left_out, right_out, sems):
+    core, x = table[WHERE, 0], table[WHERE, 1]
     stores = []
-    for j in range(capacity):
+    for j in range(left.shape[0]):
         full = table[FULL, j] > 0
-        k = lax.rem(table[WHERE, 1] + chips - table[CHIP, j], chips)
-        loads[2 * j].wait()
-        loads[2 * j + 1].wait()
-        for other, piece in enumerate(pieces):
-
-            @pl.when(jnp.logical_and(full, k == other))
+        way = lax.rem(table[CHIP, j] + 4 - x, 4)
+
+        def add(here, term):
+            @pl.when(jnp.logical_and(full, here))
             def _():
-                results[j] = STAT_DECAY * stats[j] + (1.0 - STAT_DECAY) * piece[...].astype(F32)
+                left_out[j] = STAT_DECAY * left[j] + (1.0 - STAT_DECAY) * term(0).astype(F32)
+                right_out[j] = STAT_DECAY * right[j] + (1.0 - STAT_DECAY) * term(1).astype(F32)
+
+        add(way == 0, lambda side: mine[side])
+        add(way == 2, lambda side: across[side])
+        add(way == 3 - 2 * core, lambda side: beside[core, side])
+        add(way == 1 + 2 * core, lambda side: passed[side])
 
         @pl.when(jnp.logical_not(full))
         def _():
-            results[j] = STAT_DECAY * stats[j]
-
-        for side, target in enumerate((left_new_hbm, right_new_hbm)):
-            stores.append(pltpu.make_async_copy(results.at[j, side], target.at[j], out_sems.at[j, side]))
+            left_out[j] = STAT_DECAY * left[j]
+            right_out[j] = STAT_DECAY * right[j]
+
+        for side, (result, target) in enumerate(((left_out, left_hbm), (right_out, right_hbm))):
+            stores.append(pltpu.make_async_copy(result.at[j], target.at[j], sems.at[j, side]))
             stores[-1].start()
     for store in stores:
         store.wait()
@@ -225,23 +251,17 @@
 
 
 def place_half(core, table, rows, out_hbm, ordered, sems):
-    steps = sems.shape[0]
-    step = rows.shape[0] // steps
     width = rows.shape[2]
     cols = pl.ds(pl.multiple_of(core * width, 128), width)
-    stores = []
-    for i in range(steps):
-
+
+    def fill(first, count):
         def body(b, carry):
-            ordered[i * step + b] = rows[table[SOURCE, i * step + b]]
+            ordered[first + b] = rows[table[SOURCE, first + b]]
             return carry
 
-        lax.fori_loop(0, step, body, 0, unroll=8)
-        part = pl.ds(i * step, step)
-        stores.append(pltpu.make_async_copy(ordered.at[part], out_hbm.at[part, :, cols], sems.at[i]))
-        stores[-1].start()
-    for store in stores:
-        store.wait()
+        lax.fori_loop(0, count, body, 0, unroll=8)
+
+    store_in_steps(ordered, out_hbm.at[:, :, cols], sems, 0, fill)
 
 
 def place_near_kernel(table, rows, out_hbm, ordered, sems):
@@ -301,15 +321,21 @@
 
     piece = jax.ShapeDtypeStruct((2, stat_rows, width), BF16)
     groups = width // stat_rows
-    half_rows = jax.ShapeDtypeStruct((blocks, shard_rows, half), BF16)
-    grads = in_hbm(grads)
-
-    sent = call(send_kernel, half_rows, [SMEM_SPEC, HBM_SPEC], [pltpu.SemaphoreType.DMA])(core.reshape(1), grads)
+    grads = in_hbm(grads.reshape(-1, stat_rows, width))
+    left_root, right_root = in_hbm(left_root), in_hbm(right_root)
+    grad_groups = grads.shape[0]
+
+    sent = call(
+        send_kernel,
+        jax.ShapeDtypeStruct((grad_groups + 4 * capacity, stat_rows, half), BF16),
+        [SMEM_SPEC] + [HBM_SPEC] * 3,
+        [pltpu.SemaphoreType.DMA((5,))],
+    )(core.reshape(1), grads, left_root, right_root)
     sent, late_grads = lax.optimization_barrier((sent, grads))
     other = swap_cores(sent)
     kept, table = call(
         functools.partial(keep_kernel, chips, capacity),
-        [half_rows, jax.ShapeDtypeStruct((8, blocks), jnp.int32)],
+        [jax.ShapeDtypeStruct((grad_groups, stat_rows, half), BF16), jax.ShapeDtypeStruct((8, blocks), jnp.int32)],
         [SMEM_SPEC] * 3 + [HBM_SPEC] * 2,
         [pltpu.VMEM((1, blocks), jnp.int32), pltpu.SemaphoreType.DMA((2,))],
         cost=(0, 4_000_000),
@@ -319,7 +345,7 @@
         pair_sum_kernel,
         jax.ShapeDtypeStruct((chips, depth, shard_rows, half), BF16),
         [SMEM_SPEC, VMEM_SPEC, VMEM_SPEC],
-    )(table, kept, other)
+    )(table, kept.reshape(-1, shard_rows, half), other.reshape(-1, shard_rows, half))
     parts = exchange(parts, "x")
     outgoing = call(
         chip_sum_kernel,
@@ -328,30 +354,32 @@
         [pltpu.VMEM((depth + 1, shard_rows, half), BF16)],
     )(table, parts)
 
-    outgoing, late_table = lax.optimization_barrier((outgoing, table))
+    outgoing, late_other = lax.optimization_barrier((outgoing, other))
     own = exchange(outgoing, ("y", "z"))
-    pieces = call(
-        select_roots_kernel,
-        [piece] * chips,
-        [SMEM_SPEC, HBM_SPEC, HBM_SPEC],
-        [pltpu.SemaphoreType.DMA((chips, 2))],
+    both = jax.ShapeDtypeStruct((2, 2, stat_rows, width), BF16)
+    beside, across, mine = call(
+        functools.partial(select_roots_kernel, grad_groups),
+        [both, piece, both],
+        [SMEM_SPEC, VMEM_SPEC, HBM_SPEC, HBM_SPEC],
+        [pltpu.SemaphoreType.DMA((3, 2))],
         cost=(0, 2_000_000),
-    )(late_table, in_hbm(left_root), in_hbm(right_root))
-    pieces = [turn(value, k) for k, value in enumerate(pieces)]
-    mine = call(
-        order_roots_kernel,
-        jax.ShapeDtypeStruct((chips, 2, stat_rows, width), BF16),
-        [SMEM_SPEC] + [VMEM_SPEC] * chips,
+    )(table, late_other, left_root, right_root)
+    ways = [(2 * i, 2 * ((i + 1) % chips)) for i in range(chips)]
+    ways += [(2 * i + 1, 2 * ((i - 1) % chips) + 1) for i in range(chips)]
+    beside, across = lax.ppermute(beside, ("x", "core"), ways), turn(across, 2)
+    stacked = call(
+        stack_kernel,
+        jax.ShapeDtypeStruct((3, 2, stat_rows, width), BF16),
+        [VMEM_SPEC, VMEM_SPEC],
         cost=(0, 1_000_000),
-    )(late_table, *pieces)
-    others = swap_cores(mine)
+    )(beside, across)
+    others = swap_cores(stacked)
     left, right = call(
         merge_roots_kernel,
         [jax.ShapeDtypeStruct((groups, stat_rows, width), BF16)] * 2,
-        [SMEM_SPEC, VMEM_SPEC, VMEM_SPEC],
+        [SMEM_SPEC] + [VMEM_SPEC] * 4,
         cost=(0, 2_000_000),
-    )(late_table, mine, others)
-    own, left, right = lax.optimization_barrier((own, left, right))
+    )(table, mine, beside, across, others)
 
     own = own.reshape(width, half)
     far = swap_cores(own)
@@ -369,37 +397,37 @@
 
     update, own, far = lax.optimization_barrier((update, own, far))
     rows = exchange(update.reshape(owners, shard_rows, half), ("y", "z"))
-    pieces = call(
+    beside, across, mine = call(
         terms_kernel,
-        [piece] * chips,
+        [both, piece, piece],
         [SMEM_SPEC, VMEM_SPEC, VMEM_SPEC],
         [pltpu.VMEM((width, width), BF16)],
         cost=(800_000_000, 2_000_000),
     )(table, own, far)
-    pieces = [turn(value, k) for k, value in enumerate(pieces)]
-    stat = jax.ShapeDtypeStruct(left_stat.shape, F32)
-    both_stats = (capacity, 2, stat_rows, width)
-    left_new, right_new = call(
-        stats_kernel,
-        [stat, stat],
-        [SMEM_SPEC] + [VMEM_SPEC] * chips + [HBM_SPEC] * 2,
-        [
-            pltpu.VMEM(both_stats, F32),
-            pltpu.VMEM(both_stats, F32),
-            pltpu.SemaphoreType.DMA((capacity, 2)),
-            pltpu.SemaphoreType.DMA((capacity, 2)),
-        ],
-        [HBM_SPEC, HBM_SPEC],
-        cost=(10_000_000, 5_000_000),
-    )(table, *pieces, in_hbm(left_stat), in_hbm(right_stat))
-    rows, left_new, right_new = lax.optimization_barrier((rows, left_new, right_new))
-
+    across = turn(across, 2)
+    beside = lax.ppermute(beside, ("x", "core"), ways)
     packed = call(
         compact_kernel,
         jax.ShapeDtypeStruct((chips, depth, shard_rows, half), BF16),
         [SMEM_SPEC, VMEM_SPEC],
     )(table, rows)
+    packed, beside, across = lax.optimization_barrier((packed, beside, across))
     near = exchange(packed, "x").reshape(blocks, shard_rows, half)
+    passed = swap_cores(lax.dynamic_index_in_dim(beside, 1 - core, keepdims=False))
+    stat = jax.ShapeDtypeStruct(left_stat.shape, F32)
+    left_new, right_new = call(
+        stats_kernel,
+        [stat, stat],
+        [SMEM_SPEC] + [VMEM_SPEC] * 6,
+        [
+            pltpu.VMEM(left_stat.shape, F32),
+            pltpu.VMEM(right_stat.shape, F32),
+            pltpu.SemaphoreType.DMA((capacity, 2)),
+        ],
+        [HBM_SPEC, HBM_SPEC],
+        cost=(10_000_000, 5_000_000),
+    )(table, mine, across, beside, passed, left_stat, right_stat)
+    near, left_new, right_new = lax.optimization_barrier((near, left_new, right_new))
     beyond = swap_cores(near)
     whole_rows = jax.ShapeDtypeStruct((blocks, shard_rows, width), BF16)
     scratch = [pltpu.VMEM((blocks, shard_rows, half), BF16), pltpu.SemaphoreType.DMA((4,))]

time: 122 us -> 121 us (level)
  blocking collectives: 21.5 us -> 11.6 us
  waiting for transfers between devices: 12.3 us -> 20.9 us
    ppermute x6 -> x2, starting transfers between devices: 17.7 us -> 5.01 us  [turn(): lax.ppermute(value, 'x', [(i, (i + k) % chips) for i in range(chips)])]
    all_to_all x2 -> x3, waiting for transfers between devices: 2.41 us -> 12.9 us  [exchange(): return lax.all_to_all(value, axis, 0, 0, tiled=True)]
    all_to_all x2 -> x1, blocking collectives: 21.5 us -> 11.6 us  [exchange(): return lax.all_to_all(value, axis, 0, 0, tiled=True)]
    ppermute x4 -> x5, starting transfers between devices: 21.1 us -> 29.1 us  [swap_cores(): return lax.ppermute(value, 'core', [(0, 1), (1, 0)])]
    ppermute x0 -> x2, starting transfers between devices: none -> 5.66 us  [the longest x1 2.86 us: local(): beside = lax.ppermute(beside, ('x', 'core'), ways)]
    ppermute x6 -> x2, waiting for transfers between devices: 7.75 us -> 5.83 us  [turn(): lax.ppermute(value, 'x', [(i, (i + k) % chips) for i in range(chips)])]
    pallas_call x6, Pallas kernels: 9.09 us -> 7.24 us  [the longest x1 1.69 us: local(): call(stats_kernel, [stat, stat], [SMEM_SPEC] + [VMEM_SPEC] * 6, [pltpu.VM...]
    all_to_all x2 -> x3, starting transfers between devices: 28.7 us -> 28.4 us  [exchange(): return lax.all_to_all(value, axis, 0, 0, tiled=True)]
  transfers between devices with their start and end apart: 12 -> 12, of which waited for: 8 -> 4; matrix products, arithmetic and copies ran while one was open for 0% -> 0% of each run, Pallas kernels for 9% -> 9%
where the time goes in v5:
time: 121 us; the launch traced here: 120 us
  starting transfers between devices  68.2 us (56%)
  waiting for transfers between devices  20.9 us (17%)
  Pallas kernels  18.3 us (15%)
  blocking collectives  11.6 us (10%)
    ppermute x5, starting transfers between devices, swap_cores(): return lax.ppermute(value, 'core', [(0, 1), (1, 0)])  29.1 us
    all_to_all x3, starting transfers between devices, exchange(): return lax.all_to_all(value, axis, 0, 0, tiled=True)  28.4 us
    all_to_all x3, waiting for transfers between devices, exchange(): return lax.all_to_all(value, axis, 0, 0, tiled=True)  12.9 us
    all_to_all x1, blocking collectives, exchange(): return lax.all_to_all(value, axis, 0, 0, tiled=True)  11.6 us
    ppermute x2, waiting for transfers between devices, turn(): lax.ppermute(value, 'x', [(i, (i + k) % chips) for i in range(chips)])  5.83 us
    ppermute x2, starting transfers between devices, turn(): lax.ppermute(value, 'x', [(i, (i + k) % chips) for i in range(chips)])  5.01 us
    ppermute x1, starting transfers between devices, local(): beside = lax.ppermute(beside, ('x', 'core'), ways)  2.86 us
    ppermute x1, starting transfers between devices, local(): lax.ppermute(beside, ('x', 'core'), ways)  2.79 us
  transfers between devices with their start and end apart: 12, of which 4 were waited for; matrix products, arithmetic and copies ran while one was open for 0% of the time, Pallas kernels for 9%

profile of v5, /device:TPU:1, one launch (start us, length us, event | category | flops | bytes accessed | tf_op | source)
XLA Modules:
  0.0 119.8 jit_solution(6252239649155858048)
XLA Ops:
  0.6 1.2 %shard_map.85 = bf16[32,64,256]{2,1,0:T(8,128)(2,1)S(1)} custom-call(s32[1]{0:T(128)} %bitcast.core_ref, bf16[16,64,512]{2,1,0:T(8,128)(2,1)} %bitcast.19, bf16[4,64,512]{2,1,0:T(8,128)(2,1)} %left_root.3, bf16[4,64,512]{2,1,0:T(8,128)(2,1)} %right_root.3), custom_call_target="tpu_custom_call" | custom-call | tf_op jit(solution)/shard_map/pallas_call | solution.py:328
  1.9 8.8 %collective-permute-start = (bf16[32,64,256]{2,1,0:T(8,128)(2,1)S(1)}, bf16[32,64,256]{2,1,0:T(8,128)(2,1)S(1)}, u32[]{:S(2)}, u32[]{:S(2)}) collective-permute-start(bf16[32,64,256]{2,1,0:T(8,128)(2,1)S(1)} %shard_map.85), channel_id=1, source_target_pairs={{0,64},{64,0},{1,65},{65,1},{2,66},{66,2},{3,67},{67,3},{4,68},{68... | collective-permute-start | bytes 3145736 | tf_op jit(solution)/shard_map/ppermute | solution.py:307
  10.7 1.1 shard_map.86
  11.8 1.2 collective-permute-done.other
  12.9 0.8 shard_map.87
  13.7 11.6 %all_to_all.20.parts = bf16[4,32,8,256]{3,2,1,0:T(8,128)(2,1)S(1)} all-to-all(bf16[4,32,8,256]{3,2,1,0:T(8,128)(2,1)S(1)} %shard_map.87), channel_id=1, replica_groups=mesh['x'=4,'core'=2,'y'=4,'z'=16] {'x'}, dimensions={0} | all-to-all | bytes 1048576 | tf_op jit(solution)/shard_map/all_to_all | solution.py:294
  25.4 1.6 %shard_map.88 = bf16[64,8,256]{2,1,0:T(8,128)(2,1)} custom-call(s32[8,128]{1,0:T(8,128)S(1)} %get-tuple-element.31.table, bf16[4,32,8,256]{3,2,1,0:T(8,128)(2,1)S(1)} %all_to_all.20.parts), custom_call_target="tpu_custom_call" | custom-call | tf_op jit(solution)/shard_map/pallas_call | solution.py:350
  26.9 13.9 %all-to-all-start.1 = ((bf16[64,8,256]{2,1,0:T(8,128)(2,1)}), bf16[64,8,256]{2,1,0:T(8,128)(2,1)S(1)}, u32[]{:S(2)}, u32[]{:S(2)}) async-start(bf16[64,8,256]{2,1,0:T(8,128)(2,1)} %shard_map.88), calls=%async_computation.1 | async-start | bytes 524288 | tf_op jit(solution)/shard_map/all_to_all | solution.py:294
  40.8 1.7 %shard_map.89 = (bf16[2,2,64,512]{3,2,1,0:T(8,128)(2,1)S(1)}, bf16[2,64,512]{2,1,0:T(8,128)(2,1)S(1)}, bf16[2,2,64,512]{3,2,1,0:T(8,128)(2,1)S(1)}) custom-call(s32[8,128]{1,0:T(8,128)S(1)} %get-tuple-element.31.table, bf16[32,64,256]{2,1,0:T(8,128)(2,1)S(1)} %collective-permute-done.other, bf16[4,64,512]{2,1,0:T(8,128)(2,1)} %left_root.3, ...), custom_call_target="tpu_custom_call" | custom-call | bytes 2000000 | tf_op jit(solution)/shard_map/pallas_call | solution.py:360
  42.5 2.8 %collective-permute-start.2 = (bf16[2,2,64,512]{3,2,1,0:T(8,128)(2,1)S(1)}, bf16[2,2,64,512]{3,2,1,0:T(8,128)(2,1)S(1)}, u32[]{:S(2)}, u32[]{:S(2)}) collective-permute-start(bf16[2,2,64,512]{3,2,1,0:T(8,128)(2,1)S(1)} %get-tuple-element.37), channel_id=1, source_target_pairs={{0,128},{128,256},{256,384},{384,0},{64,448},{192,64},{320,192},{4... | collective-permute-start | bytes 786440 | tf_op jit(solution)/shard_map/ppermute | solution.py:369
  45.3 3.1 %collective-permute-start.3 = (bf16[2,64,512]{2,1,0:T(8,128)(2,1)S(1)}, bf16[2,64,512]{2,1,0:T(8,128)(2,1)S(1)}, u32[]{:S(2)}, u32[]{:S(2)}) collective-permute-start(bf16[2,64,512]{2,1,0:T(8,128)(2,1)S(1)} %get-tuple-element.38), channel_id=1, source_target_pairs={{0,256},{128,384},{256,0},{384,128},{1,257},{129,385},{257,1},{385... | collective-permute-start | bytes 393224 | tf_op jit(solution)/shard_map/ppermute | solution.py:303
  48.4 5.8 %collective-permute-done.3.across = bf16[2,64,512]{2,1,0:T(8,128)(2,1)S(1)} collective-permute-done((bf16[2,64,512]{2,1,0:T(8,128)(2,1)S(1)}, bf16[2,64,512]{2,1,0:T(8,128)(2,1)S(1)}, u32[]{:S(2)}, u32[]{:S(2)}) %collective-permute-start.3) | collective-permute-done | bytes 131104 | tf_op jit(solution)/shard_map/ppermute | solution.py:303
  54.2 0.0 collective-permute-done.2.beside
  54.2 4.6 %collective-permute-start.4 = (bf16[3,2,64,512]{3,2,1,0:T(8,128)(2,1)S(1)}, bf16[3,2,64,512]{3,2,1,0:T(8,128)(2,1)S(1)}, u32[]{:S(2)}, u32[]{:S(2)}) collective-permute-start(bf16[3,2,64,512]{3,2,1,0:T(8,128)(2,1)S(1)} %shard_map.90), channel_id=1, source_target_pairs={{0,64},{64,0},{1,65},{65,1},{2,66},{66,2},{3,67},{67,3},{4,68},{68... | collective-permute-start | bytes 1179656 | tf_op jit(solution)/shard_map/ppermute | solution.py:307
  58.8 0.0 all-to-all-done.1
  58.8 5.8 %collective-permute-start.1 = (bf16[512,256]{1,0:T(8,128)(2,1)S(1)}, bf16[512,256]{1,0:T(8,128)(2,1)S(1)}, u32[]{:S(2)}, u32[]{:S(2)}) collective-permute-start(bf16[512,256]{1,0:T(8,128)(2,1)S(1)} %bitcast.16), channel_id=1, source_target_pairs={{0,64},{64,0},{1,65},{65,1},{2,66},{66,2},{3,67},{67,3},{4,68},{68... | collective-permute-start | bytes 786440 | tf_op jit(solution)/shard_map/ppermute | solution.py:307
  64.7 0.0 collective-permute-done.4.others
  64.7 0.7 shard_map.91
  65.4 0.9 shard_map.92
  66.3 0.0 collective-permute-done.1.other
  66.3 2.2 %shard_map.93 = bf16[512,256]{1,0:T(8,128)(2,1)} custom-call(s32[8,128]{1,0:T(8,128)S(1)} %get-tuple-element.31.table, bf16[512,256]{1,0:T(8,128)(2,1)S(1)} %collective-permute-done.1.other, f32[512,512]{1,0:T(8,128)S(1)} %get-tuple-element.40.partial, bf16[8,64,512]{2,1,0:T(8,128)(2,1)S(1)} %get-tuple-element.41.left, ...), custom_call_target="tpu_custom_call" | custom-call | tf_op jit(solution)/shard_map/pallas_call | solution.py:392
  68.5 10.9 %all-to-all-start.2 = ((bf16[64,8,256]{2,1,0:T(8,128)(2,1)}), bf16[64,8,256]{2,1,0:T(8,128)(2,1)S(1)}, u32[]{:S(2)}, u32[]{:S(2)}) async-start(bf16[64,8,256]{2,1,0:T(8,128)(2,1)} %bitcast.8), calls=%async_computation.2 | async-start | bytes 524288 | tf_op jit(solution)/shard_map/all_to_all | solution.py:294
  79.4 1.5 %shard_map.95 = (bf16[2,2,64,512]{3,2,1,0:T(8,128)(2,1)S(1)}, bf16[2,64,512]{2,1,0:T(8,128)(2,1)S(1)}, bf16[2,64,512]{2,1,0:T(8,128)(2,1)S(1)}) custom-call(s32[8,128]{1,0:T(8,128)S(1)} %get-tuple-element.31.table, bf16[512,256]{1,0:T(8,128)(2,1)S(1)} %bitcast.18, bf16[512,256]{1,0:T(8,128)(2,1)S(1)} %collective-permute-done.1.other), custom_call_target="tpu_custom_call" | custom-call | flops 800000000 | bytes 2000000 | tf_op jit(solution)/shard_map/pallas_call | solution.py:400
  81.0 2.9 %collective-permute-start.5 = (bf16[2,2,64,512]{3,2,1,0:T(8,128)(2,1)S(1)}, bf16[2,2,64,512]{3,2,1,0:T(8,128)(2,1)S(1)}, u32[]{:S(2)}, u32[]{:S(2)}) collective-permute-start(bf16[2,2,64,512]{3,2,1,0:T(8,128)(2,1)S(1)} %get-tuple-element.46), channel_id=1, source_target_pairs={{0,128},{128,256},{256,384},{384,0},{64,448},{192,64},{320,192},{4... | collective-permute-start | bytes 786440 | tf_op jit(solution)/shard_map/ppermute | solution.py:408
  83.8 1.9 %collective-permute-start.6 = (bf16[2,64,512]{2,1,0:T(8,128)(2,1)S(1)}, bf16[2,64,512]{2,1,0:T(8,128)(2,1)S(1)}, u32[]{:S(2)}, u32[]{:S(2)}) collective-permute-start(bf16[2,64,512]{2,1,0:T(8,128)(2,1)S(1)} %get-tuple-element.47), channel_id=1, source_target_pairs={{0,256},{128,384},{256,0},{384,128},{1,257},{129,385},{257,1},{385... | collective-permute-start | bytes 393224 | tf_op jit(solution)/shard_map/ppermute | solution.py:303
  85.8 12.9 %all-to-all-done.2.rows = bf16[64,8,256]{2,1,0:T(8,128)(2,1)S(1)} async-done(((bf16[64,8,256]{2,1,0:T(8,128)(2,1)}), bf16[64,8,256]{2,1,0:T(8,128)(2,1)S(1)}, u32[]{:S(2)}, u32[]{:S(2)}) %all-to-all-start.2) | async-done | bytes 262176 | tf_op jit(solution)/shard_map/all_to_all | solution.py:294
  98.6 1.5 %shard_map.94 = bf16[4,32,8,256]{3,2,1,0:T(8,128)(2,1)} custom-call(s32[8,128]{1,0:T(8,128)S(1)} %get-tuple-element.31.table, bf16[64,8,256]{2,1,0:T(8,128)(2,1)S(1)} %all-to-all-done.2.rows), custom_call_target="tpu_custom_call" | custom-call | tf_op jit(solution)/shard_map/pallas_call | solution.py:409
  100.1 0.0 copy-start
  100.1 0.0 copy-start.1
  100.1 0.0 collective-permute-done.6.across
  100.1 0.0 collective-permute-done.5.beside
  100.1 3.6 %all-to-all-start.3 = ((bf16[4,32,8,256]{3,2,1,0:T(8,128)(2,1)}), bf16[4,32,8,256]{3,2,1,0:T(8,128)(2,1)S(1)}, u32[]{:S(2)}, u32[]{:S(2)}) async-start(bf16[4,32,8,256]{3,2,1,0:T(8,128)(2,1)} %shard_map.94), calls=%async_computation.3 | async-start | bytes 1048576 | tf_op jit(solution)/shard_map/all_to_all | solution.py:294
  103.8 4.6 %collective-permute-start.7 = (bf16[2,64,512]{2,1,0:T(8,128)(2,1)S(1)}, bf16[2,64,512]{2,1,0:T(8,128)(2,1)S(1)}, u32[]{:S(2)}, u32[]{:S(2)}) collective-permute-start(bf16[2,64,512]{2,1,0:T(8,128)(2,1)S(1)} %dynamic-slice_bitcast_fusion), channel_id=1, source_target_pairs={{0,64},{64,0},{1,65},{65,1},{2,66},{66,2},{3,67},{67,3},{4,68},{68... | collective-permute-start | bytes 393224 | tf_op jit(solution)/shard_map/ppermute | solution.py:307
  108.4 1.0 collective-permute-done.7.passed
  109.4 0.0 copy-done
  109.4 0.0 copy-done.1
  109.4 1.7 %shard_map.96 = (f32[4,64,512]{2,1,0:T(8,128)}, f32[4,64,512]{2,1,0:T(8,128)}) custom-call(s32[8,128]{1,0:T(8,128)S(1)} %get-tuple-element.31.table, bf16[2,64,512]{2,1,0:T(8,128)(2,1)S(1)} %get-tuple-element.49.mine, bf16[2,64,512]{2,1,0:T(8,128)(2,1)S(1)} %collective-permute-done.6.across, bf16[2,2,64,512]{3,2,1,0:T(8,128)(2,1)S(1)} %collective-permute-done.5.beside, ...), custom_call_target="tpu_custom_call" | custom-call | flops 10000000 | bytes 5000000 | tf_op jit(solution)/shard_map/pallas_call | solution.py:418
  111.1 0.0 all-to-all-done.3
  111.1 5.3 %collective-permute-start.8 = (bf16[128,8,256]{2,1,0:T(8,128)(2,1)S(1)}, bf16[128,8,256]{2,1,0:T(8,128)(2,1)S(1)}, u32[]{:S(2)}, u32[]{:S(2)}) collective-permute-start(bf16[128,8,256]{2,1,0:T(8,128)(2,1)S(1)} %bitcast.13), channel_id=1, source_target_pairs={{0,64},{64,0},{1,65},{65,1},{2,66},{66,2},{3,67},{67,3},{4,68},{68... | collective-permute-start | bytes 1572872 | tf_op jit(solution)/shard_map/ppermute | solution.py:307
  116.4 1.7 %shard_map.97.begun = bf16[128,8,512]{2,1,0:T(8,128)(2,1)} custom-call(s32[8,128]{1,0:T(8,128)S(1)} %get-tuple-element.31.table, bf16[128,8,256]{2,1,0:T(8,128)(2,1)S(1)} %bitcast.14), custom_call_target="tpu_custom_call" | custom-call | bytes 4000000 | tf_op jit(solution)/shard_map/pallas_call | solution.py:434
  118.1 0.0 collective-permute-done.8.rows
  118.1 1.7 %shard_map.98 = bf16[128,8,512]{2,1,0:T(8,128)(2,1)} custom-call(s32[8,128]{1,0:T(8,128)S(1)} %get-tuple-element.31.table, bf16[128,8,256]{2,1,0:T(8,128)(2,1)S(1)} %collective-permute-done.8.rows, bf16[128,8,512]{2,1,0:T(8,128)(2,1)} %shard_map.97.begun), custom_call_target="tpu_custom_call", output_to_operand_aliasing={{}: (2, {})} | custom-call | tf_op jit(solution)/shard_map/pallas_call | solution.py:437
  (2 shorter events, 0.0 us)
Async XLA Ops:
  1.9 11.1 %collective-permute-start = (bf16[32,64,256]{2,1,0:T(8,128)(2,1)S(1)}, bf16[32,64,256]{2,1,0:T(8,128)(2,1)S(1)}, u32[]{:S(2)}, u32[]{:S(2)}) collective-permute-start(bf16[32,64,256]{2,1,0:T(8,128)(2,1)S(1)} %shard_map.85), channel_id=1, source_target_pairs={{0,64},{64,0},{1,65},{65,1},{2,66},{66,2},{3,67},{67,3},{4,68},{68... | collective-permute-start | bytes 3145736 | tf_op jit(solution)/shard_map/ppermute | solution.py:307
  26.9 31.9 %all-to-all-start.1 = ((bf16[64,8,256]{2,1,0:T(8,128)(2,1)}), bf16[64,8,256]{2,1,0:T(8,128)(2,1)S(1)}, u32[]{:S(2)}, u32[]{:S(2)}) async-start(bf16[64,8,256]{2,1,0:T(8,128)(2,1)} %shard_map.88), calls=%async_computation.1 | async-start | bytes 524288 | tf_op jit(solution)/shard_map/all_to_all | solution.py:294
  42.5 11.7 %collective-permute-start.2 = (bf16[2,2,64,512]{3,2,1,0:T(8,128)(2,1)S(1)}, bf16[2,2,64,512]{3,2,1,0:T(8,128)(2,1)S(1)}, u32[]{:S(2)}, u32[]{:S(2)}) collective-permute-start(bf16[2,2,64,512]{3,2,1,0:T(8,128)(2,1)S(1)} %get-tuple-element.37), channel_id=1, source_target_pairs={{0,128},{128,256},{256,384},{384,0},{64,448},{192,64},{320,192},{4... | collective-permute-start | bytes 786440 | tf_op jit(solution)/shard_map/ppermute | solution.py:369
  45.3 8.9 %collective-permute-start.3 = (bf16[2,64,512]{2,1,0:T(8,128)(2,1)S(1)}, bf16[2,64,512]{2,1,0:T(8,128)(2,1)S(1)}, u32[]{:S(2)}, u32[]{:S(2)}) collective-permute-start(bf16[2,64,512]{2,1,0:T(8,128)(2,1)S(1)} %get-tuple-element.38), channel_id=1, source_target_pairs={{0,256},{128,384},{256,0},{384,128},{1,257},{129,385},{257,1},{385... | collective-permute-start | bytes 393224 | tf_op jit(solution)/shard_map/ppermute | solution.py:303
  54.2 10.4 %collective-permute-start.4 = (bf16[3,2,64,512]{3,2,1,0:T(8,128)(2,1)S(1)}, bf16[3,2,64,512]{3,2,1,0:T(8,128)(2,1)S(1)}, u32[]{:S(2)}, u32[]{:S(2)}) collective-permute-start(bf16[3,2,64,512]{3,2,1,0:T(8,128)(2,1)S(1)} %shard_map.90), channel_id=1, source_target_pairs={{0,64},{64,0},{1,65},{65,1},{2,66},{66,2},{3,67},{67,3},{4,68},{68... | collective-permute-start | bytes 1179656 | tf_op jit(solution)/shard_map/ppermute | solution.py:307
  58.8 7.5 %collective-permute-start.1 = (bf16[512,256]{1,0:T(8,128)(2,1)S(1)}, bf16[512,256]{1,0:T(8,128)(2,1)S(1)}, u32[]{:S(2)}, u32[]{:S(2)}) collective-permute-start(bf16[512,256]{1,0:T(8,128)(2,1)S(1)} %bitcast.16), channel_id=1, source_target_pairs={{0,64},{64,0},{1,65},{65,1},{2,66},{66,2},{3,67},{67,3},{4,68},{68... | collective-permute-start | bytes 786440 | tf_op jit(solution)/shard_map/ppermute | solution.py:307
  68.5 30.2 %all-to-all-start.2 = ((bf16[64,8,256]{2,1,0:T(8,128)(2,1)}), bf16[64,8,256]{2,1,0:T(8,128)(2,1)S(1)}, u32[]{:S(2)}, u32[]{:S(2)}) async-start(bf16[64,8,256]{2,1,0:T(8,128)(2,1)} %bitcast.8), calls=%async_computation.2 | async-start | bytes 524288 | tf_op jit(solution)/shard_map/all_to_all | solution.py:294
  81.0 19.2 %collective-permute-start.5 = (bf16[2,2,64,512]{3,2,1,0:T(8,128)(2,1)S(1)}, bf16[2,2,64,512]{3,2,1,0:T(8,128)(2,1)S(1)}, u32[]{:S(2)}, u32[]{:S(2)}) collective-permute-start(bf16[2,2,64,512]{3,2,1,0:T(8,128)(2,1)S(1)} %get-tuple-element.46), channel_id=1, source_target_pairs={{0,128},{128,256},{256,384},{384,0},{64,448},{192,64},{320,192},{4... | collective-permute-start | bytes 786440 | tf_op jit(solution)/shard_map/ppermute | solution.py:408
  83.8 16.3 %collective-permute-start.6 = (bf16[2,64,512]{2,1,0:T(8,128)(2,1)S(1)}, bf16[2,64,512]{2,1,0:T(8,128)(2,1)S(1)}, u32[]{:S(2)}, u32[]{:S(2)}) collective-permute-start(bf16[2,64,512]{2,1,0:T(8,128)(2,1)S(1)} %get-tuple-element.47), channel_id=1, source_target_pairs={{0,256},{128,384},{256,0},{384,128},{1,257},{129,385},{257,1},{385... | collective-permute-start | bytes 393224 | tf_op jit(solution)/shard_map/ppermute | solution.py:303
  100.1 9.2 %copy-start = (f32[4,64,512]{2,1,0:T(8,128)S(1)}, f32[4,64,512]{2,1,0:T(8,128)}, u32[]{:S(2)}) copy-start(f32[4,64,512]{2,1,0:T(8,128)} %left.1) | copy-start | bytes 1572868
  100.1 9.2 %copy-start.1 = (f32[4,64,512]{2,1,0:T(8,128)S(1)}, f32[4,64,512]{2,1,0:T(8,128)}, u32[]{:S(2)}) copy-start(f32[4,64,512]{2,1,0:T(8,128)} %right.1) | copy-start | bytes 1572868
  100.1 10.9 %all-to-all-start.3 = ((bf16[4,32,8,256]{3,2,1,0:T(8,128)(2,1)}), bf16[4,32,8,256]{3,2,1,0:T(8,128)(2,1)S(1)}, u32[]{:S(2)}, u32[]{:S(2)}) async-start(bf16[4,32,8,256]{3,2,1,0:T(8,128)(2,1)} %shard_map.94), calls=%async_computation.3 | async-start | bytes 1048576 | tf_op jit(solution)/shard_map/all_to_all | solution.py:294
  103.8 5.6 %collective-permute-start.7 = (bf16[2,64,512]{2,1,0:T(8,128)(2,1)S(1)}, bf16[2,64,512]{2,1,0:T(8,128)(2,1)S(1)}, u32[]{:S(2)}, u32[]{:S(2)}) collective-permute-start(bf16[2,64,512]{2,1,0:T(8,128)(2,1)S(1)} %dynamic-slice_bitcast_fusion), channel_id=1, source_target_pairs={{0,64},{64,0},{1,65},{65,1},{2,66},{66,2},{3,67},{67,3},{4,68},{68... | collective-permute-start | bytes 393224 | tf_op jit(solution)/shard_map/ppermute | solution.py:307
  111.1 7.0 %collective-permute-start.8 = (bf16[128,8,256]{2,1,0:T(8,128)(2,1)S(1)}, bf16[128,8,256]{2,1,0:T(8,128)(2,1)S(1)}, u32[]{:S(2)}, u32[]{:S(2)}) collective-permute-start(bf16[128,8,256]{2,1,0:T(8,128)(2,1)S(1)} %bitcast.13), channel_id=1, source_target_pairs={{0,64},{64,0},{1,65},{65,1},{2,66},{66,2},{3,67},{67,3},{4,68},{68... | collective-permute-start | bytes 1572872 | tf_op jit(solution)/shard_map/ppermute | solution.py:307

commit v6 on v5

--- a/solution.py
+++ b/solution.py
@@ -24,7 +24,7 @@
 ORDER, SOURCE, PLACE, OWNER, SLOT, FULL, CHIP, WHERE = range(8)
 
 
-def fill_table(slots, core, x, me, capacity, chips, table):
+def fill_table(slots, core, x, me, capacity, chips, first, first_done, table):
     blocks = slots.shape[1]
     square = (blocks, blocks)
     cap_bits, chip_bits = capacity.bit_length() - 1, chips.bit_length() - 1
@@ -42,12 +42,14 @@
     chip = rank & (chips - 1)
     spot = rank >> chip_bits
     owner = slot >> cap_bits
+    first[...] = total((owner == me) & (chip == lane), slot & (capacity - 1))
+    first_done()
     local_slot = slot == me * capacity + lane
     table[pl.ds(ORDER, 1)] = total(rank == lane, sublane)
     table[pl.ds(SOURCE, 1)] = (rank_row & (chips - 1)) * depth + (rank_row >> chip_bits)
     table[pl.ds(PLACE, 1)] = total((chip == x) & (owner == lane), spot - depth) + depth
     table[pl.ds(OWNER, 1)] = total((chip == x) & (spot == lane), owner)
-    table[pl.ds(SLOT, 1)] = total((owner == me) & (chip == lane), slot & (capacity - 1))
+    table[pl.ds(SLOT, 1)] = first[...]
     table[pl.ds(FULL, 1)] = total(local_slot, 1)
     table[pl.ds(CHIP, 1)] = total(local_slot, chip)
     row = lax.broadcasted_iota(jnp.int32, (1, blocks), 1)
@@ -69,36 +71,42 @@
         load.wait()
 
 
-def keep_kernel(chips, capacity, core_ref, x_ref, me_ref, slots_hbm, grads, kept, table, slots, sems):
-    core = core_ref[0]
+def keep_kernel(
+    core_ref, x_ref, me_ref, slots_hbm, grads, left_root, right_root, kept, table, beside, mine, across, slots, first, scalars, sems, root_sems
+):
+    core, x = core_ref[0], x_ref[0]
     width = kept.shape[2]
     near = pl.ds(pl.multiple_of(core * width, 128), width)
     slots_load = pltpu.make_async_copy(slots_hbm, slots, sems.at[0])
     load = pltpu.make_async_copy(grads.at[:, :, near], kept, sems.at[1])
+    first_load = pltpu.make_async_copy(first, scalars, sems.at[2])
     slots_load.start()
     load.start()
     slots_load.wait()
-    fill_table(slots, core, x_ref[0], me_ref[0], capacity, chips, table)
-    load.wait()
-
-
-def select_roots_kernel(groups, table, other, left_root, right_root, beside, across, mine, sems):
-    core, x = table[WHERE, 0], table[WHERE, 1]
-    capacity = left_root.shape[0]
-    width = other.shape[2]
-    loads = []
-    for i, (chip, out) in enumerate(((lax.rem(x + 1 + 2 * core, 4), beside), (x, mine), (lax.rem(x + 2, 4), across))):
-        slot = table[SLOT, chip]
-        target = across if i == 2 else out.at[core]
+    fill_table(slots, core, x, me_ref[0], left_root.shape[0], 4, first, first_load.start, table)
+    first_load.wait()
+    loads = [load]
+    for i, (chip, out) in enumerate(((x + 1 + 2 * core, beside), (x, mine), (x + 2, across))):
+        slot = scalars[0, lax.rem(chip, 4)]
         for side, root in enumerate((left_root, right_root)):
-            loads.append(pltpu.make_async_copy(root.at[slot], target.at[side], sems.at[i, side]))
+            loads.append(pltpu.make_async_copy(root.at[slot], out.at[side], root_sems.at[i, side]))
             loads[-1].start()
-    for chip, out in ((lax.rem(x + 1 + 2 * core, 4), beside), (x, mine)):
-        slot = table[SLOT, chip]
-        for i in range(4):
-            out[1 - core, i // 2, :, i % 2 * width : (i % 2 + 1) * width] = other[groups + i * capacity + slot]
     for load in loads:
         load.wait()
+
+
+def from_other(groups, capacity, other, slot, side, out):
+    width = other.shape[2]
+    for h in range(2):
+        out[:, h * width : (h + 1) * width] = other[groups + (2 * side + h) * capacity + slot]
+
+
+def pair_roots_kernel(groups, capacity, table, other, beside, out):
+    core, x = table[WHERE, 0], table[WHERE, 1]
+    slot = table[SLOT, lax.rem(x + 1 + 2 * core, 4)]
+    out[core] = beside[...]
+    for side in range(2):
+        from_other(groups, capacity, other, slot, side, out.at[1 - core, side])
 
 
 def stack_kernel(beside, across, out):
@@ -106,12 +114,13 @@
     out[2] = across[...]
 
 
-def merge_roots_kernel(table, mine, beside, across, others, left, right):
+def merge_roots_kernel(groups, capacity, table, other, mine, beside, across, others, left, right):
     core, x = table[WHERE, 0], table[WHERE, 1]
     near, far, opposite = lax.rem(x + 3 - 2 * core, 4), lax.rem(x + 1 + 2 * core, 4), lax.rem(x + 2, 4)
     for side, out in enumerate((left, right)):
+        out[2 * x + core] = mine[side]
+        from_other(groups, capacity, other, table[SLOT, x], side, out.at[2 * x + 1 - core])
         for parity in range(2):
-            out[2 * x + parity] = mine[parity, side]
             out[2 * near + parity] = beside[parity, side]
             out[2 * far + parity] = others[parity, side]
         out[2 * opposite + core] = across[side]
@@ -143,16 +152,19 @@
         store.wait()
 
 
-def chip_sum_kernel(table, parts, out, total):
+def chip_sum_kernel(table, parts, out, total, place, sem):
     depth = parts.shape[1]
+    load = pltpu.make_async_copy(table, place, sem)
+    load.start()
     acc = parts[0].astype(F32)
     for x in range(1, parts.shape[0]):
         acc = acc + parts[x].astype(F32)
     total[0:depth] = acc.astype(BF16)
     total[depth] = jnp.zeros(total.shape[1:], BF16)
+    load.wait()
 
     def body(o, carry):
-        out[o] = total[table[PLACE, o]]
+        out[o] = total[place[PLACE, o]]
         return carry
 
     lax.fori_loop(0, out.shape[0], body, 0, unroll=8)
@@ -333,13 +345,28 @@
     )(core.reshape(1), grads, left_root, right_root)
     sent, late_grads = lax.optimization_barrier((sent, grads))
     other = swap_cores(sent)
-    kept, table = call(
-        functools.partial(keep_kernel, chips, capacity),
-        [jax.ShapeDtypeStruct((grad_groups, stat_rows, half), BF16), jax.ShapeDtypeStruct((8, blocks), jnp.int32)],
-        [SMEM_SPEC] * 3 + [HBM_SPEC] * 2,
-        [pltpu.VMEM((1, blocks), jnp.int32), pltpu.SemaphoreType.DMA((2,))],
+    kept, table, beside, mine, across = call(
+        keep_kernel,
+        [jax.ShapeDtypeStruct((grad_groups, stat_rows, half), BF16), jax.ShapeDtypeStruct((8, blocks), jnp.int32)]
+        + [piece] * 3,
+        [SMEM_SPEC] * 3 + [HBM_SPEC] * 4,
+        [
+            pltpu.VMEM((1, blocks), jnp.int32),
+            pltpu.VMEM((1, blocks), jnp.int32),
+            pltpu.SMEM((1, blocks), jnp.int32),
+            pltpu.SemaphoreType.DMA((3,)),
+            pltpu.SemaphoreType.DMA((3, 2)),
+        ],
         cost=(0, 4_000_000),
-    )(core.reshape(1), x.reshape(1), me.reshape(1), in_hbm(block_slot.reshape(1, blocks)), in_hbm(late_grads))
+    )(
+        core.reshape(1),
+        x.reshape(1),
+        me.reshape(1),
+        in_hbm(block_slot.reshape(1, blocks)),
+        in_hbm(late_grads),
+        left_root,
+        right_root,
+    )
 
     parts = call(
         pair_sum_kernel,
@@ -350,20 +377,23 @@
     outgoing = call(
         chip_sum_kernel,
         jax.ShapeDtypeStruct((owners, shard_rows, half), BF16),
-        [SMEM_SPEC, VMEM_SPEC],
-        [pltpu.VMEM((depth + 1, shard_rows, half), BF16)],
+        [VMEM_SPEC, VMEM_SPEC],
+        [
+            pltpu.VMEM((depth + 1, shard_rows, half), BF16),
+            pltpu.SMEM((8, blocks), jnp.int32),
+            pltpu.SemaphoreType.DMA,
+        ],
     )(table, parts)
 
-    outgoing, late_other = lax.optimization_barrier((outgoing, other))
+    outgoing, late_other, beside, across = lax.optimization_barrier((outgoing, other, beside, across))
     own = exchange(outgoing, ("y", "z"))
     both = jax.ShapeDtypeStruct((2, 2, stat_rows, width), BF16)
-    beside, across, mine = call(
-        functools.partial(select_roots_kernel, grad_groups),
-        [both, piece, both],
-        [SMEM_SPEC, VMEM_SPEC, HBM_SPEC, HBM_SPEC],
-        [pltpu.SemaphoreType.DMA((3, 2))],
-        cost=(0, 2_000_000),
-    )(table, late_other, left_root, right_root)
+    beside = call(
+        functools.partial(pair_roots_kernel, grad_groups, capacity),
+        both,
+        [SMEM_SPEC, VMEM_SPEC, VMEM_SPEC],
+        cost=(0, 1_000_000),
+    )(table, late_other, beside)
     ways = [(2 * i, 2 * ((i + 1) % chips)) for i in range(chips)]
     ways += [(2 * i + 1, 2 * ((i - 1) % chips) + 1) for i in range(chips)]
     beside, across = lax.ppermute(beside, ("x", "core"), ways), turn(across, 2)
@@ -375,11 +405,11 @@
     )(beside, across)
     others = swap_cores(stacked)
     left, right = call(
-        merge_roots_kernel,
+        functools.partial(merge_roots_kernel, grad_groups, capacity),
         [jax.ShapeDtypeStruct((groups, stat_rows, width), BF16)] * 2,
-        [SMEM_SPEC] + [VMEM_SPEC] * 4,
+        [SMEM_SPEC] + [VMEM_SPEC] * 5,
         cost=(0, 2_000_000),
-    )(table, mine, beside, across, others)
+    )(table, late_other, mine, beside, across, others)
 
     own = own.reshape(width, half)
     far = swap_cores(own)

time: 121 us -> 120 us (level)
  starting transfers between devices: 68.2 us -> 66.2 us
    all_to_all x3, waiting for transfers between devices: 12.9 us -> 14.8 us  [exchange(): return lax.all_to_all(value, axis, 0, 0, tiled=True)]
where the time goes in v6:
time: 120 us; the launch traced here: 119 us
  starting transfers between devices  66.2 us (55%)
  waiting for transfers between devices  21.6 us (18%)
  Pallas kernels  18.6 us (16%)
  blocking collectives  11.7 us (10%)
    ppermute x5, starting transfers between devices, swap_cores(): return lax.ppermute(value, 'core', [(0, 1), (1, 0)])  28.2 us
    all_to_all x3, starting transfers between devices, exchange(): return lax.all_to_all(value, axis, 0, 0, tiled=True)  27.4 us
    all_to_all x3, waiting for transfers between devices, exchange(): return lax.all_to_all(value, axis, 0, 0, tiled=True)  14.8 us
    all_to_all x1, blocking collectives, exchange(): return lax.all_to_all(value, axis, 0, 0, tiled=True)  11.7 us
    ppermute x2, waiting for transfers between devices, turn(): lax.ppermute(value, 'x', [(i, (i + k) % chips) for i in range(chips)])  5.88 us
    ppermute x2, starting transfers between devices, turn(): lax.ppermute(value, 'x', [(i, (i + k) % chips) for i in range(chips)])  5.01 us
    ppermute x1, starting transfers between devices, local(): beside = lax.ppermute(beside, ('x', 'core'), ways)  2.85 us
    ppermute x1, starting transfers between devices, local(): lax.ppermute(beside, ('x', 'core'), ways)  2.8 us
  transfers between devices with their start and end apart: 12, of which 4 were waited for; matrix products, arithmetic and copies ran while one was open for 0% of the time, Pallas kernels for 9%

profile of v6, /device:TPU:1, one launch (start us, length us, event | category | flops | bytes accessed | tf_op | source)
XLA Modules:
  0.0 119.0 jit_solution(7643153325523176051)
XLA Ops:
  0.6 1.2 %shard_map.85 = bf16[32,64,256]{2,1,0:T(8,128)(2,1)S(1)} custom-call(s32[1]{0:T(128)} %bitcast.core_ref, bf16[16,64,512]{2,1,0:T(8,128)(2,1)} %bitcast.19, bf16[4,64,512]{2,1,0:T(8,128)(2,1)} %left_root.3, bf16[4,64,512]{2,1,0:T(8,128)(2,1)} %right_root.3), custom_call_target="tpu_custom_call" | custom-call | tf_op jit(solution)/shard_map/pallas_call | solution.py:340
  1.9 8.8 %collective-permute-start = (bf16[32,64,256]{2,1,0:T(8,128)(2,1)S(1)}, bf16[32,64,256]{2,1,0:T(8,128)(2,1)S(1)}, u32[]{:S(2)}, u32[]{:S(2)}) collective-permute-start(bf16[32,64,256]{2,1,0:T(8,128)(2,1)S(1)} %shard_map.85), channel_id=1, source_target_pairs={{0,64},{64,0},{1,65},{65,1},{2,66},{66,2},{3,67},{67,3},{4,68},{68... | collective-permute-start | bytes 3145736 | tf_op jit(solution)/shard_map/ppermute | solution.py:319
  10.7 2.5 %shard_map.86 = (bf16[16,64,256]{2,1,0:T(8,128)(2,1)S(1)}, s32[8,128]{1,0:T(8,128)S(1)}, bf16[2,64,512]{2,1,0:T(8,128)(2,1)S(1)}, bf16[2,64,512]{2,1,0:T(8,128)(2,1)S(1)}, bf16[2,64,512]{2,1,0:T(8,128)(2,1)S(1)}) custom-call(s32[1]{0:T(128)} %bitcast.core_ref, s32[1]{0:T(128)} %bitcast.1.x_ref, s32[1]{0:T(128)} %bitcast.2.me_ref, s32[1,128]{1,0:T(1,128)} %bitcast.21, ...), custom_call_target="tpu_custom_call" | custom-call | bytes 4000000 | tf_op jit(solution)/shard_map/pallas_call | solution.py:348
  13.2 0.0 collective-permute-done.other
  13.2 0.8 shard_map.87
  14.0 11.7 %all_to_all.20.parts = bf16[4,32,8,256]{3,2,1,0:T(8,128)(2,1)S(1)} all-to-all(bf16[4,32,8,256]{3,2,1,0:T(8,128)(2,1)S(1)} %shard_map.87), channel_id=1, replica_groups=mesh['x'=4,'core'=2,'y'=4,'z'=16] {'x'}, dimensions={0} | all-to-all | bytes 1048576 | tf_op jit(solution)/shard_map/all_to_all | solution.py:306
  25.7 1.5 %shard_map.88 = bf16[64,8,256]{2,1,0:T(8,128)(2,1)} custom-call(s32[8,128]{1,0:T(8,128)S(1)} %get-tuple-element.33.table, bf16[4,32,8,256]{3,2,1,0:T(8,128)(2,1)S(1)} %all_to_all.20.parts), custom_call_target="tpu_custom_call" | custom-call | tf_op jit(solution)/shard_map/pallas_call | solution.py:377
  27.2 14.5 %all-to-all-start.1 = ((bf16[64,8,256]{2,1,0:T(8,128)(2,1)}), bf16[64,8,256]{2,1,0:T(8,128)(2,1)S(1)}, u32[]{:S(2)}, u32[]{:S(2)}) async-start(bf16[64,8,256]{2,1,0:T(8,128)(2,1)} %shard_map.88), calls=%async_computation.1 | async-start | bytes 524288 | tf_op jit(solution)/shard_map/all_to_all | solution.py:306
  41.7 0.6 shard_map.89
  42.3 2.8 %collective-permute-start.2 = (bf16[2,2,64,512]{3,2,1,0:T(8,128)(2,1)S(1)}, bf16[2,2,64,512]{3,2,1,0:T(8,128)(2,1)S(1)}, u32[]{:S(2)}, u32[]{:S(2)}) collective-permute-start(bf16[2,2,64,512]{3,2,1,0:T(8,128)(2,1)S(1)} %shard_map.89), channel_id=1, source_target_pairs={{0,128},{128,256},{256,384},{384,0},{64,448},{192,64},{320,192},{4... | collective-permute-start | bytes 786440 | tf_op jit(solution)/shard_map/ppermute | solution.py:399
  45.1 3.1 %collective-permute-start.3 = (bf16[2,64,512]{2,1,0:T(8,128)(2,1)S(1)}, bf16[2,64,512]{2,1,0:T(8,128)(2,1)S(1)}, u32[]{:S(2)}, u32[]{:S(2)}) collective-permute-start(bf16[2,64,512]{2,1,0:T(8,128)(2,1)S(1)} %get-tuple-element.42), channel_id=1, source_target_pairs={{0,256},{128,384},{256,0},{384,128},{1,257},{129,385},{257,1},{385... | collective-permute-start | bytes 393224 | tf_op jit(solution)/shard_map/ppermute | solution.py:315
  48.2 5.9 %collective-permute-done.3.across = bf16[2,64,512]{2,1,0:T(8,128)(2,1)S(1)} collective-permute-done((bf16[2,64,512]{2,1,0:T(8,128)(2,1)S(1)}, bf16[2,64,512]{2,1,0:T(8,128)(2,1)S(1)}, u32[]{:S(2)}, u32[]{:S(2)}) %collective-permute-start.3) | collective-permute-done | bytes 131104 | tf_op jit(solution)/shard_map/ppermute | solution.py:315
  54.1 0.0 collective-permute-done.2.beside
  54.1 3.9 %collective-permute-start.4 = (bf16[3,2,64,512]{3,2,1,0:T(8,128)(2,1)S(1)}, bf16[3,2,64,512]{3,2,1,0:T(8,128)(2,1)S(1)}, u32[]{:S(2)}, u32[]{:S(2)}) collective-permute-start(bf16[3,2,64,512]{3,2,1,0:T(8,128)(2,1)S(1)} %shard_map.90), channel_id=1, source_target_pairs={{0,64},{64,0},{1,65},{65,1},{2,66},{66,2},{3,67},{67,3},{4,68},{68... | collective-permute-start | bytes 1179656 | tf_op jit(solution)/shard_map/ppermute | solution.py:319
  58.0 1.8 %all-to-all-done.1 = bf16[64,8,256]{2,1,0:T(8,128)(2,1)S(1)} async-done(((bf16[64,8,256]{2,1,0:T(8,128)(2,1)}), bf16[64,8,256]{2,1,0:T(8,128)(2,1)S(1)}, u32[]{:S(2)}, u32[]{:S(2)}) %all-to-all-start.1) | async-done | bytes 262176 | tf_op jit(solution)/shard_map/all_to_all | solution.py:306
  59.9 5.7 %collective-permute-start.1 = (bf16[512,256]{1,0:T(8,128)(2,1)S(1)}, bf16[512,256]{1,0:T(8,128)(2,1)S(1)}, u32[]{:S(2)}, u32[]{:S(2)}) collective-permute-start(bf16[512,256]{1,0:T(8,128)(2,1)S(1)} %bitcast.16), channel_id=1, source_target_pairs={{0,64},{64,0},{1,65},{65,1},{2,66},{66,2},{3,67},{67,3},{4,68},{68... | collective-permute-start | bytes 786440 | tf_op jit(solution)/shard_map/ppermute | solution.py:319
  65.6 0.0 collective-permute-done.4.others
  65.6 0.7 shard_map.91
  66.3 0.9 shard_map.92
  67.2 0.0 collective-permute-done.1.other
  67.2 2.2 %shard_map.93 = bf16[512,256]{1,0:T(8,128)(2,1)} custom-call(s32[8,128]{1,0:T(8,128)S(1)} %get-tuple-element.33.table, bf16[512,256]{1,0:T(8,128)(2,1)S(1)} %collective-permute-done.1.other, f32[512,512]{1,0:T(8,128)S(1)} %get-tuple-element.44.partial, bf16[8,64,512]{2,1,0:T(8,128)(2,1)S(1)} %get-tuple-element.45.left, ...), custom_call_target="tpu_custom_call" | custom-call | tf_op jit(solution)/shard_map/pallas_call | solution.py:422
  69.4 9.3 %all-to-all-start.2 = ((bf16[64,8,256]{2,1,0:T(8,128)(2,1)}), bf16[64,8,256]{2,1,0:T(8,128)(2,1)S(1)}, u32[]{:S(2)}, u32[]{:S(2)}) async-start(bf16[64,8,256]{2,1,0:T(8,128)(2,1)} %bitcast.8), calls=%async_computation.2 | async-start | bytes 524288 | tf_op jit(solution)/shard_map/all_to_all | solution.py:306
  78.6 1.5 %shard_map.95 = (bf16[2,2,64,512]{3,2,1,0:T(8,128)(2,1)S(1)}, bf16[2,64,512]{2,1,0:T(8,128)(2,1)S(1)}, bf16[2,64,512]{2,1,0:T(8,128)(2,1)S(1)}) custom-call(s32[8,128]{1,0:T(8,128)S(1)} %get-tuple-element.33.table, bf16[512,256]{1,0:T(8,128)(2,1)S(1)} %bitcast.18, bf16[512,256]{1,0:T(8,128)(2,1)S(1)} %collective-permute-done.1.other), custom_call_target="tpu_custom_call" | custom-call | flops 800000000 | bytes 2000000 | tf_op jit(solution)/shard_map/pallas_call | solution.py:430
  80.2 2.9 %collective-permute-start.5 = (bf16[2,2,64,512]{3,2,1,0:T(8,128)(2,1)S(1)}, bf16[2,2,64,512]{3,2,1,0:T(8,128)(2,1)S(1)}, u32[]{:S(2)}, u32[]{:S(2)}) collective-permute-start(bf16[2,2,64,512]{3,2,1,0:T(8,128)(2,1)S(1)} %get-tuple-element.50), channel_id=1, source_target_pairs={{0,128},{128,256},{256,384},{384,0},{64,448},{192,64},{320,192},{4... | collective-permute-start | bytes 786440 | tf_op jit(solution)/shard_map/ppermute | solution.py:438
  83.1 1.9 %collective-permute-start.6 = (bf16[2,64,512]{2,1,0:T(8,128)(2,1)S(1)}, bf16[2,64,512]{2,1,0:T(8,128)(2,1)S(1)}, u32[]{:S(2)}, u32[]{:S(2)}) collective-permute-start(bf16[2,64,512]{2,1,0:T(8,128)(2,1)S(1)} %get-tuple-element.51), channel_id=1, source_target_pairs={{0,256},{128,384},{256,0},{384,128},{1,257},{129,385},{257,1},{385... | collective-permute-start | bytes 393224 | tf_op jit(solution)/shard_map/ppermute | solution.py:315
  85.0 12.9 %all-to-all-done.2.rows = bf16[64,8,256]{2,1,0:T(8,128)(2,1)S(1)} async-done(((bf16[64,8,256]{2,1,0:T(8,128)(2,1)}), bf16[64,8,256]{2,1,0:T(8,128)(2,1)S(1)}, u32[]{:S(2)}, u32[]{:S(2)}) %all-to-all-start.2) | async-done | bytes 262176 | tf_op jit(solution)/shard_map/all_to_all | solution.py:306
  97.9 1.5 %shard_map.94 = bf16[4,32,8,256]{3,2,1,0:T(8,128)(2,1)} custom-call(s32[8,128]{1,0:T(8,128)S(1)} %get-tuple-element.33.table, bf16[64,8,256]{2,1,0:T(8,128)(2,1)S(1)} %all-to-all-done.2.rows), custom_call_target="tpu_custom_call" | custom-call | tf_op jit(solution)/shard_map/pallas_call | solution.py:439
  99.4 0.0 copy-start
  99.4 0.0 copy-start.1
  99.4 0.0 collective-permute-done.6.across
  99.4 0.0 collective-permute-done.5.beside
  99.4 3.6 %all-to-all-start.3 = ((bf16[4,32,8,256]{3,2,1,0:T(8,128)(2,1)}), bf16[4,32,8,256]{3,2,1,0:T(8,128)(2,1)S(1)}, u32[]{:S(2)}, u32[]{:S(2)}) async-start(bf16[4,32,8,256]{3,2,1,0:T(8,128)(2,1)} %shard_map.94), calls=%async_computation.3 | async-start | bytes 1048576 | tf_op jit(solution)/shard_map/all_to_all | solution.py:306
  103.1 4.5 %collective-permute-start.7 = (bf16[2,64,512]{2,1,0:T(8,128)(2,1)S(1)}, bf16[2,64,512]{2,1,0:T(8,128)(2,1)S(1)}, u32[]{:S(2)}, u32[]{:S(2)}) collective-permute-start(bf16[2,64,512]{2,1,0:T(8,128)(2,1)S(1)} %dynamic-slice_bitcast_fusion), channel_id=1, source_target_pairs={{0,64},{64,0},{1,65},{65,1},{2,66},{66,2},{3,67},{67,3},{4,68},{68... | collective-permute-start | bytes 393224 | tf_op jit(solution)/shard_map/ppermute | solution.py:319
  107.6 1.0 collective-permute-done.7.passed
  108.6 0.0 copy-done
  108.6 0.0 copy-done.1
  108.6 1.7 %shard_map.96 = (f32[4,64,512]{2,1,0:T(8,128)}, f32[4,64,512]{2,1,0:T(8,128)}) custom-call(s32[8,128]{1,0:T(8,128)S(1)} %get-tuple-element.33.table, bf16[2,64,512]{2,1,0:T(8,128)(2,1)S(1)} %get-tuple-element.53.mine, bf16[2,64,512]{2,1,0:T(8,128)(2,1)S(1)} %collective-permute-done.6.across, bf16[2,2,64,512]{3,2,1,0:T(8,128)(2,1)S(1)} %collective-permute-done.5.beside, ...), custom_call_target="tpu_custom_call" | custom-call | flops 10000000 | bytes 5000000 | tf_op jit(solution)/shard_map/pallas_call | solution.py:448
  110.3 0.0 all-to-all-done.3
  110.3 5.3 %collective-permute-start.8 = (bf16[128,8,256]{2,1,0:T(8,128)(2,1)S(1)}, bf16[128,8,256]{2,1,0:T(8,128)(2,1)S(1)}, u32[]{:S(2)}, u32[]{:S(2)}) collective-permute-start(bf16[128,8,256]{2,1,0:T(8,128)(2,1)S(1)} %bitcast.13), channel_id=1, source_target_pairs={{0,64},{64,0},{1,65},{65,1},{2,66},{66,2},{3,67},{67,3},{4,68},{68... | collective-permute-start | bytes 1572872 | tf_op jit(solution)/shard_map/ppermute | solution.py:319
  115.6 1.7 %shard_map.97.begun = bf16[128,8,512]{2,1,0:T(8,128)(2,1)} custom-call(s32[8,128]{1,0:T(8,128)S(1)} %get-tuple-element.33.table, bf16[128,8,256]{2,1,0:T(8,128)(2,1)S(1)} %bitcast.14), custom_call_target="tpu_custom_call" | custom-call | bytes 4000000 | tf_op jit(solution)/shard_map/pallas_call | solution.py:464
  117.3 0.0 collective-permute-done.8.rows
  117.3 1.7 %shard_map.98 = bf16[128,8,512]{2,1,0:T(8,128)(2,1)} custom-call(s32[8,128]{1,0:T(8,128)S(1)} %get-tuple-element.33.table, bf16[128,8,256]{2,1,0:T(8,128)(2,1)S(1)} %collective-permute-done.8.rows, bf16[128,8,512]{2,1,0:T(8,128)(2,1)} %shard_map.97.begun), custom_call_target="tpu_custom_call", output_to_operand_aliasing={{}: (2, {})} | custom-call | tf_op jit(solution)/shard_map/pallas_call | solution.py:467
  (2 shorter events, 0.0 us)
Async XLA Ops:
  1.9 11.3 %collective-permute-start = (bf16[32,64,256]{2,1,0:T(8,128)(2,1)S(1)}, bf16[32,64,256]{2,1,0:T(8,128)(2,1)S(1)}, u32[]{:S(2)}, u32[]{:S(2)}) collective-permute-start(bf16[32,64,256]{2,1,0:T(8,128)(2,1)S(1)} %shard_map.85), channel_id=1, source_target_pairs={{0,64},{64,0},{1,65},{65,1},{2,66},{66,2},{3,67},{67,3},{4,68},{68... | collective-permute-start | bytes 3145736 | tf_op jit(solution)/shard_map/ppermute | solution.py:319
  27.2 32.7 %all-to-all-start.1 = ((bf16[64,8,256]{2,1,0:T(8,128)(2,1)}), bf16[64,8,256]{2,1,0:T(8,128)(2,1)S(1)}, u32[]{:S(2)}, u32[]{:S(2)}) async-start(bf16[64,8,256]{2,1,0:T(8,128)(2,1)} %shard_map.88), calls=%async_computation.1 | async-start | bytes 524288 | tf_op jit(solution)/shard_map/all_to_all | solution.py:306
  42.3 11.8 %collective-permute-start.2 = (bf16[2,2,64,512]{3,2,1,0:T(8,128)(2,1)S(1)}, bf16[2,2,64,512]{3,2,1,0:T(8,128)(2,1)S(1)}, u32[]{:S(2)}, u32[]{:S(2)}) collective-permute-start(bf16[2,2,64,512]{3,2,1,0:T(8,128)(2,1)S(1)} %shard_map.89), channel_id=1, source_target_pairs={{0,128},{128,256},{256,384},{384,0},{64,448},{192,64},{320,192},{4... | collective-permute-start | bytes 786440 | tf_op jit(solution)/shard_map/ppermute | solution.py:399
  45.1 9.0 %collective-permute-start.3 = (bf16[2,64,512]{2,1,0:T(8,128)(2,1)S(1)}, bf16[2,64,512]{2,1,0:T(8,128)(2,1)S(1)}, u32[]{:S(2)}, u32[]{:S(2)}) collective-permute-start(bf16[2,64,512]{2,1,0:T(8,128)(2,1)S(1)} %get-tuple-element.42), channel_id=1, source_target_pairs={{0,256},{128,384},{256,0},{384,128},{1,257},{129,385},{257,1},{385... | collective-permute-start | bytes 393224 | tf_op jit(solution)/shard_map/ppermute | solution.py:315
  54.1 11.4 %collective-permute-start.4 = (bf16[3,2,64,512]{3,2,1,0:T(8,128)(2,1)S(1)}, bf16[3,2,64,512]{3,2,1,0:T(8,128)(2,1)S(1)}, u32[]{:S(2)}, u32[]{:S(2)}) collective-permute-start(bf16[3,2,64,512]{3,2,1,0:T(8,128)(2,1)S(1)} %shard_map.90), channel_id=1, source_target_pairs={{0,64},{64,0},{1,65},{65,1},{2,66},{66,2},{3,67},{67,3},{4,68},{68... | collective-permute-start | bytes 1179656 | tf_op jit(solution)/shard_map/ppermute | solution.py:319
  59.9 7.3 %collective-permute-start.1 = (bf16[512,256]{1,0:T(8,128)(2,1)S(1)}, bf16[512,256]{1,0:T(8,128)(2,1)S(1)}, u32[]{:S(2)}, u32[]{:S(2)}) collective-permute-start(bf16[512,256]{1,0:T(8,128)(2,1)S(1)} %bitcast.16), channel_id=1, source_target_pairs={{0,64},{64,0},{1,65},{65,1},{2,66},{66,2},{3,67},{67,3},{4,68},{68... | collective-permute-start | bytes 786440 | tf_op jit(solution)/shard_map/ppermute | solution.py:319
  69.4 28.6 %all-to-all-start.2 = ((bf16[64,8,256]{2,1,0:T(8,128)(2,1)}), bf16[64,8,256]{2,1,0:T(8,128)(2,1)S(1)}, u32[]{:S(2)}, u32[]{:S(2)}) async-start(bf16[64,8,256]{2,1,0:T(8,128)(2,1)} %bitcast.8), calls=%async_computation.2 | async-start | bytes 524288 | tf_op jit(solution)/shard_map/all_to_all | solution.py:306
  80.2 19.2 %collective-permute-start.5 = (bf16[2,2,64,512]{3,2,1,0:T(8,128)(2,1)S(1)}, bf16[2,2,64,512]{3,2,1,0:T(8,128)(2,1)S(1)}, u32[]{:S(2)}, u32[]{:S(2)}) collective-permute-start(bf16[2,2,64,512]{3,2,1,0:T(8,128)(2,1)S(1)} %get-tuple-element.50), channel_id=1, source_target_pairs={{0,128},{128,256},{256,384},{384,0},{64,448},{192,64},{320,192},{4... | collective-permute-start | bytes 786440 | tf_op jit(solution)/shard_map/ppermute | solution.py:438
  83.1 16.4 %collective-permute-start.6 = (bf16[2,64,512]{2,1,0:T(8,128)(2,1)S(1)}, bf16[2,64,512]{2,1,0:T(8,128)(2,1)S(1)}, u32[]{:S(2)}, u32[]{:S(2)}) collective-permute-start(bf16[2,64,512]{2,1,0:T(8,128)(2,1)S(1)} %get-tuple-element.51), channel_id=1, source_target_pairs={{0,256},{128,384},{256,0},{384,128},{1,257},{129,385},{257,1},{385... | collective-permute-start | bytes 393224 | tf_op jit(solution)/shard_map/ppermute | solution.py:315
  99.4 9.1 %copy-start = (f32[4,64,512]{2,1,0:T(8,128)S(1)}, f32[4,64,512]{2,1,0:T(8,128)}, u32[]{:S(2)}) copy-start(f32[4,64,512]{2,1,0:T(8,128)} %left.1) | copy-start | bytes 1572868
  99.4 9.1 %copy-start.1 = (f32[4,64,512]{2,1,0:T(8,128)S(1)}, f32[4,64,512]{2,1,0:T(8,128)}, u32[]{:S(2)}) copy-start(f32[4,64,512]{2,1,0:T(8,128)} %right.1) | copy-start | bytes 1572868
  99.4 10.8 %all-to-all-start.3 = ((bf16[4,32,8,256]{3,2,1,0:T(8,128)(2,1)}), bf16[4,32,8,256]{3,2,1,0:T(8,128)(2,1)S(1)}, u32[]{:S(2)}, u32[]{:S(2)}) async-start(bf16[4,32,8,256]{3,2,1,0:T(8,128)(2,1)} %shard_map.94), calls=%async_computation.3 | async-start | bytes 1048576 | tf_op jit(solution)/shard_map/all_to_all | solution.py:306
  103.1 5.5 %collective-permute-start.7 = (bf16[2,64,512]{2,1,0:T(8,128)(2,1)S(1)}, bf16[2,64,512]{2,1,0:T(8,128)(2,1)S(1)}, u32[]{:S(2)}, u32[]{:S(2)}) collective-permute-start(bf16[2,64,512]{2,1,0:T(8,128)(2,1)S(1)} %dynamic-slice_bitcast_fusion), channel_id=1, source_target_pairs={{0,64},{64,0},{1,65},{65,1},{2,66},{66,2},{3,67},{67,3},{4,68},{68... | collective-permute-start | bytes 393224 | tf_op jit(solution)/shard_map/ppermute | solution.py:319
  110.3 7.0 %collective-permute-start.8 = (bf16[128,8,256]{2,1,0:T(8,128)(2,1)S(1)}, bf16[128,8,256]{2,1,0:T(8,128)(2,1)S(1)}, u32[]{:S(2)}, u32[]{:S(2)}) collective-permute-start(bf16[128,8,256]{2,1,0:T(8,128)(2,1)S(1)} %bitcast.13), channel_id=1, source_target_pairs={{0,64},{64,0},{1,65},{65,1},{2,66},{66,2},{3,67},{67,3},{4,68},{68... | collective-permute-start | bytes 1572872 | tf_op jit(solution)/shard_map/ppermute | solution.py:319

commit v7 on v6

--- a/solution.py
+++ b/solution.py
@@ -373,7 +373,16 @@
         jax.ShapeDtypeStruct((chips, depth, shard_rows, half), BF16),
         [SMEM_SPEC, VMEM_SPEC, VMEM_SPEC],
     )(table, kept.reshape(-1, shard_rows, half), other.reshape(-1, shard_rows, half))
+    both = jax.ShapeDtypeStruct((2, 2, stat_rows, width), BF16)
+    parts, late_table = lax.optimization_barrier((parts, table))
     parts = exchange(parts, "x")
+    beside = call(
+        functools.partial(pair_roots_kernel, grad_groups, capacity),
+        both,
+        [SMEM_SPEC, VMEM_SPEC, VMEM_SPEC],
+        cost=(0, 1000),
+    )(late_table, other, beside)
+    parts, beside = lax.optimization_barrier((parts, beside))
     outgoing = call(
         chip_sum_kernel,
         jax.ShapeDtypeStruct((owners, shard_rows, half), BF16),
@@ -385,18 +394,12 @@
         ],
     )(table, parts)
 
+    across = turn(across, 2)
     outgoing, late_other, beside, across = lax.optimization_barrier((outgoing, other, beside, across))
     own = exchange(outgoing, ("y", "z"))
-    both = jax.ShapeDtypeStruct((2, 2, stat_rows, width), BF16)
-    beside = call(
-        functools.partial(pair_roots_kernel, grad_groups, capacity),
-        both,
-        [SMEM_SPEC, VMEM_SPEC, VMEM_SPEC],
-        cost=(0, 1_000_000),
-    )(table, late_other, beside)
     ways = [(2 * i, 2 * ((i + 1) % chips)) for i in range(chips)]
     ways += [(2 * i + 1, 2 * ((i - 1) % chips) + 1) for i in range(chips)]
-    beside, across = lax.ppermute(beside, ("x", "core"), ways), turn(across, 2)
+    beside = lax.ppermute(beside, ("x", "core"), ways)
     stacked = call(
         stack_kernel,
         jax.ShapeDtypeStruct((3, 2, stat_rows, width), BF16),

time: 120 us -> 120 us (level)
  blocking collectives: 11.7 us -> 0 us
  waiting for transfers between devices: 21.6 us -> 30 us
  starting transfers between devices: 66.2 us -> 68.5 us
    all_to_all x1 -> x0, blocking collectives: 11.7 us -> none  [exchange(): return lax.all_to_all(value, axis, 0, 0, tiled=True)]
    all_to_all x3 -> x4, waiting for transfers between devices: 14.8 us -> 23.1 us  [exchange(): return lax.all_to_all(value, axis, 0, 0, tiled=True)]
    ppermute x1 -> x2, waiting for transfers between devices: 0.01 us -> 4.61 us  [local(): beside = lax.ppermute(beside, ('x', 'core'), ways)]
    ppermute x2, waiting for transfers between devices: 5.88 us -> 1.3 us  [turn(): lax.ppermute(value, 'x', [(i, (i + k) % chips) for i in range(chips)])]
    ppermute x2, starting transfers between devices: 5.01 us -> 7.94 us  [turn(): lax.ppermute(value, 'x', [(i, (i + k) % chips) for i in range(chips)])]
    ppermute x1 -> x0, starting transfers between devices: 2.8 us -> none  [local(): lax.ppermute(beside, ('x', 'core'), ways)]
    ppermute x1 -> x2, starting transfers between devices: 2.85 us -> 5.58 us  [local(): beside = lax.ppermute(beside, ('x', 'core'), ways)]
    all_to_all x3 -> x4, starting transfers between devices: 27.4 us -> 26.6 us  [exchange(): return lax.all_to_all(value, axis, 0, 0, tiled=True)]
  transfers between devices with their start and end apart: 12 -> 13, of which waited for: 4 -> 7; matrix products, arithmetic and copies ran while one was open for 0% -> 0% of each run, Pallas kernels for 9% -> 11%
where the time goes in v7:
time: 120 us; the launch traced here: 119 us
  starting transfers between devices  68.5 us (57%)
  waiting for transfers between devices  30 us (25%)
  Pallas kernels  19.4 us (16%)
    ppermute x5, starting transfers between devices, swap_cores(): return lax.ppermute(value, 'core', [(0, 1), (1, 0)])  28.4 us
    all_to_all x4, starting transfers between devices, exchange(): return lax.all_to_all(value, axis, 0, 0, tiled=True)  26.6 us
    all_to_all x4, waiting for transfers between devices, exchange(): return lax.all_to_all(value, axis, 0, 0, tiled=True)  23.1 us
    ppermute x2, starting transfers between devices, turn(): lax.ppermute(value, 'x', [(i, (i + k) % chips) for i in range(chips)])  7.94 us
    ppermute x2, starting transfers between devices, local(): beside = lax.ppermute(beside, ('x', 'core'), ways)  5.58 us
    ppermute x2, waiting for transfers between devices, local(): beside = lax.ppermute(beside, ('x', 'core'), ways)  4.61 us
    pallas_call x1, Pallas kernels, local(): call(keep_kernel, [jax.ShapeDtypeStruct((grad_groups, stat_rows, half), B...  2.52 us
  transfers between devices with their start and end apart: 13, of which 7 were waited for; matrix products, arithmetic and copies ran while one was open for 0% of the time, Pallas kernels for 11%

profile of v7, /device:TPU:1, one launch (start us, length us, event | category | flops | bytes accessed | tf_op | source)
XLA Modules:
  0.0 118.9 jit_solution(14753646948828636046)
XLA Ops:
  0.6 1.2 %shard_map.85 = bf16[32,64,256]{2,1,0:T(8,128)(2,1)S(1)} custom-call(s32[1]{0:T(128)} %bitcast.core_ref, bf16[16,64,512]{2,1,0:T(8,128)(2,1)} %bitcast.19, bf16[4,64,512]{2,1,0:T(8,128)(2,1)} %left_root.3, bf16[4,64,512]{2,1,0:T(8,128)(2,1)} %right_root.3), custom_call_target="tpu_custom_call" | custom-call | tf_op jit(solution)/shard_map/pallas_call | solution.py:340
  1.9 8.8 %collective-permute-start = (bf16[32,64,256]{2,1,0:T(8,128)(2,1)S(1)}, bf16[32,64,256]{2,1,0:T(8,128)(2,1)S(1)}, u32[]{:S(2)}, u32[]{:S(2)}) collective-permute-start(bf16[32,64,256]{2,1,0:T(8,128)(2,1)S(1)} %shard_map.85), channel_id=1, source_target_pairs={{0,64},{64,0},{1,65},{65,1},{2,66},{66,2},{3,67},{67,3},{4,68},{68... | collective-permute-start | bytes 3145736 | tf_op jit(solution)/shard_map/ppermute | solution.py:319
  10.7 2.5 %shard_map.86 = (bf16[16,64,256]{2,1,0:T(8,128)(2,1)S(1)}, s32[8,128]{1,0:T(8,128)S(1)}, bf16[2,64,512]{2,1,0:T(8,128)(2,1)S(1)}, bf16[2,64,512]{2,1,0:T(8,128)(2,1)S(1)}, bf16[2,64,512]{2,1,0:T(8,128)(2,1)S(1)}) custom-call(s32[1]{0:T(128)} %bitcast.core_ref, s32[1]{0:T(128)} %bitcast.1.x_ref, s32[1]{0:T(128)} %bitcast.2.me_ref, s32[1,128]{1,0:T(1,128)} %bitcast.21, ...), custom_call_target="tpu_custom_call" | custom-call | bytes 4000000 | tf_op jit(solution)/shard_map/pallas_call | solution.py:348
  13.2 0.0 collective-permute-done.other
  13.2 1.6 %shard_map.87 = bf16[4,32,8,256]{3,2,1,0:T(8,128)(2,1)} custom-call(s32[8,128]{1,0:T(8,128)S(1)} %get-tuple-element.41.table, bf16[128,8,256]{2,1,0:T(8,128)(2,1)S(1)} %bitcast.15, bf16[256,8,256]{2,1,0:T(8,128)(2,1)S(1)} %bitcast.12), custom_call_target="tpu_custom_call" | custom-call | tf_op jit(solution)/shard_map/pallas_call | solution.py:371
  14.8 3.5 %all-to-all-start = ((bf16[4,32,8,256]{3,2,1,0:T(8,128)(2,1)}), bf16[4,32,8,256]{3,2,1,0:T(8,128)(2,1)S(1)}, u32[]{:S(2)}, u32[]{:S(2)}) async-start(bf16[4,32,8,256]{3,2,1,0:T(8,128)(2,1)} %shard_map.87), calls=%async_computation | async-start | bytes 1048576 | tf_op jit(solution)/shard_map/all_to_all | solution.py:306
  18.3 4.8 %collective-permute-start.1 = (bf16[2,64,512]{2,1,0:T(8,128)(2,1)S(1)}, bf16[2,64,512]{2,1,0:T(8,128)(2,1)S(1)}, u32[]{:S(2)}, u32[]{:S(2)}) collective-permute-start(bf16[2,64,512]{2,1,0:T(8,128)(2,1)S(1)} %get-tuple-element.45), channel_id=1, source_target_pairs={{0,256},{128,384},{256,0},{384,128},{1,257},{129,385},{257,1},{385... | collective-permute-start | bytes 393224 | tf_op jit(solution)/shard_map/ppermute | solution.py:315
  23.1 0.6 shard_map.88
  23.8 4.1 %all-to-all-done.parts = bf16[4,32,8,256]{3,2,1,0:T(8,128)(2,1)S(1)} async-done(((bf16[4,32,8,256]{3,2,1,0:T(8,128)(2,1)}), bf16[4,32,8,256]{3,2,1,0:T(8,128)(2,1)S(1)}, u32[]{:S(2)}, u32[]{:S(2)}) %all-to-all-start) | async-done | bytes 524320 | tf_op jit(solution)/shard_map/all_to_all | solution.py:306
  27.8 1.5 %shard_map.89 = bf16[64,8,256]{2,1,0:T(8,128)(2,1)} custom-call(s32[8,128]{1,0:T(8,128)S(1)} %get-tuple-element.41.table, bf16[4,32,8,256]{3,2,1,0:T(8,128)(2,1)S(1)} %all-to-all-done.parts), custom_call_target="tpu_custom_call" | custom-call | tf_op jit(solution)/shard_map/pallas_call | solution.py:386
  29.3 1.3 %collective-permute-done.1.across = bf16[2,64,512]{2,1,0:T(8,128)(2,1)S(1)} collective-permute-done((bf16[2,64,512]{2,1,0:T(8,128)(2,1)S(1)}, bf16[2,64,512]{2,1,0:T(8,128)(2,1)S(1)}, u32[]{:S(2)}, u32[]{:S(2)}) %collective-permute-start.1) | collective-permute-done | bytes 131104 | tf_op jit(solution)/shard_map/ppermute | solution.py:315
  30.6 13.3 %all-to-all-start.1 = ((bf16[64,8,256]{2,1,0:T(8,128)(2,1)}), bf16[64,8,256]{2,1,0:T(8,128)(2,1)S(1)}, u32[]{:S(2)}, u32[]{:S(2)}) async-start(bf16[64,8,256]{2,1,0:T(8,128)(2,1)} %shard_map.89), calls=%async_computation.1 | async-start | bytes 524288 | tf_op jit(solution)/shard_map/all_to_all | solution.py:306
  44.0 2.8 %collective-permute-start.3 = (bf16[2,2,64,512]{3,2,1,0:T(8,128)(2,1)S(1)}, bf16[2,2,64,512]{3,2,1,0:T(8,128)(2,1)S(1)}, u32[]{:S(2)}, u32[]{:S(2)}) collective-permute-start(bf16[2,2,64,512]{3,2,1,0:T(8,128)(2,1)S(1)} %shard_map.88), channel_id=1, source_target_pairs={{0,128},{128,256},{256,384},{384,0},{64,448},{192,64},{320,192},{4... | collective-permute-start | bytes 786440 | tf_op jit(solution)/shard_map/ppermute | solution.py:402
  46.8 4.6 %collective-permute-done.3.beside = bf16[2,2,64,512]{3,2,1,0:T(8,128)(2,1)S(1)} collective-permute-done((bf16[2,2,64,512]{3,2,1,0:T(8,128)(2,1)S(1)}, bf16[2,2,64,512]{3,2,1,0:T(8,128)(2,1)S(1)}, u32[]{:S(2)}, u32[]{:S(2)}) %collective-permute-start.3) | collective-permute-done | bytes 262176 | tf_op jit(solution)/shard_map/ppermute | solution.py:402
  51.4 5.4 %collective-permute-start.4 = (bf16[3,2,64,512]{3,2,1,0:T(8,128)(2,1)S(1)}, bf16[3,2,64,512]{3,2,1,0:T(8,128)(2,1)S(1)}, u32[]{:S(2)}, u32[]{:S(2)}) collective-permute-start(bf16[3,2,64,512]{3,2,1,0:T(8,128)(2,1)S(1)} %shard_map.90), channel_id=1, source_target_pairs={{0,64},{64,0},{1,65},{65,1},{2,66},{66,2},{3,67},{67,3},{4,68},{68... | collective-permute-start | bytes 1179656 | tf_op jit(solution)/shard_map/ppermute | solution.py:319
  56.9 5.3 %all-to-all-done.1 = bf16[64,8,256]{2,1,0:T(8,128)(2,1)S(1)} async-done(((bf16[64,8,256]{2,1,0:T(8,128)(2,1)}), bf16[64,8,256]{2,1,0:T(8,128)(2,1)S(1)}, u32[]{:S(2)}, u32[]{:S(2)}) %all-to-all-start.1) | async-done | bytes 262176 | tf_op jit(solution)/shard_map/all_to_all | solution.py:306
  62.1 5.7 %collective-permute-start.2 = (bf16[512,256]{1,0:T(8,128)(2,1)S(1)}, bf16[512,256]{1,0:T(8,128)(2,1)S(1)}, u32[]{:S(2)}, u32[]{:S(2)}) collective-permute-start(bf16[512,256]{1,0:T(8,128)(2,1)S(1)} %bitcast.16), channel_id=1, source_target_pairs={{0,64},{64,0},{1,65},{65,1},{2,66},{66,2},{3,67},{67,3},{4,68},{68... | collective-permute-start | bytes 786440 | tf_op jit(solution)/shard_map/ppermute | solution.py:319
  67.8 0.0 collective-permute-done.4.others
  67.8 0.7 shard_map.91
  68.5 0.9 shard_map.92
  69.4 0.0 collective-permute-done.2.other
  69.5 2.2 %shard_map.93 = bf16[512,256]{1,0:T(8,128)(2,1)} custom-call(s32[8,128]{1,0:T(8,128)S(1)} %get-tuple-element.41.table, bf16[512,256]{1,0:T(8,128)(2,1)S(1)} %collective-permute-done.2.other, f32[512,512]{1,0:T(8,128)S(1)} %get-tuple-element.52.partial, bf16[8,64,512]{2,1,0:T(8,128)(2,1)S(1)} %get-tuple-element.53.left, ...), custom_call_target="tpu_custom_call" | custom-call | tf_op jit(solution)/shard_map/pallas_call | solution.py:425
  71.7 6.2 %all-to-all-start.2 = ((bf16[64,8,256]{2,1,0:T(8,128)(2,1)}), bf16[64,8,256]{2,1,0:T(8,128)(2,1)S(1)}, u32[]{:S(2)}, u32[]{:S(2)}) async-start(bf16[64,8,256]{2,1,0:T(8,128)(2,1)} %bitcast.8), calls=%async_computation.2 | async-start | bytes 524288 | tf_op jit(solution)/shard_map/all_to_all | solution.py:306
  77.8 1.5 %shard_map.95 = (bf16[2,2,64,512]{3,2,1,0:T(8,128)(2,1)S(1)}, bf16[2,64,512]{2,1,0:T(8,128)(2,1)S(1)}, bf16[2,64,512]{2,1,0:T(8,128)(2,1)S(1)}) custom-call(s32[8,128]{1,0:T(8,128)S(1)} %get-tuple-element.41.table, bf16[512,256]{1,0:T(8,128)(2,1)S(1)} %bitcast.18, bf16[512,256]{1,0:T(8,128)(2,1)S(1)} %collective-permute-done.2.other), custom_call_target="tpu_custom_call" | custom-call | flops 800000000 | bytes 2000000 | tf_op jit(solution)/shard_map/pallas_call | solution.py:433
  79.4 2.8 %collective-permute-start.5 = (bf16[2,2,64,512]{3,2,1,0:T(8,128)(2,1)S(1)}, bf16[2,2,64,512]{3,2,1,0:T(8,128)(2,1)S(1)}, u32[]{:S(2)}, u32[]{:S(2)}) collective-permute-start(bf16[2,2,64,512]{3,2,1,0:T(8,128)(2,1)S(1)} %get-tuple-element.58), channel_id=1, source_target_pairs={{0,128},{128,256},{256,384},{384,0},{64,448},{192,64},{320,192},{4... | collective-permute-start | bytes 786440 | tf_op jit(solution)/shard_map/ppermute | solution.py:441
  82.2 3.1 %collective-permute-start.6 = (bf16[2,64,512]{2,1,0:T(8,128)(2,1)S(1)}, bf16[2,64,512]{2,1,0:T(8,128)(2,1)S(1)}, u32[]{:S(2)}, u32[]{:S(2)}) collective-permute-start(bf16[2,64,512]{2,1,0:T(8,128)(2,1)S(1)} %get-tuple-element.59), channel_id=1, source_target_pairs={{0,256},{128,384},{256,0},{384,128},{1,257},{129,385},{257,1},{385... | collective-permute-start | bytes 393224 | tf_op jit(solution)/shard_map/ppermute | solution.py:315
  85.3 12.7 %all-to-all-done.2.rows = bf16[64,8,256]{2,1,0:T(8,128)(2,1)S(1)} async-done(((bf16[64,8,256]{2,1,0:T(8,128)(2,1)}), bf16[64,8,256]{2,1,0:T(8,128)(2,1)S(1)}, u32[]{:S(2)}, u32[]{:S(2)}) %all-to-all-start.2) | async-done | bytes 262176 | tf_op jit(solution)/shard_map/all_to_all | solution.py:306
  98.0 1.5 %shard_map.94 = bf16[4,32,8,256]{3,2,1,0:T(8,128)(2,1)} custom-call(s32[8,128]{1,0:T(8,128)S(1)} %get-tuple-element.41.table, bf16[64,8,256]{2,1,0:T(8,128)(2,1)S(1)} %all-to-all-done.2.rows), custom_call_target="tpu_custom_call" | custom-call | tf_op jit(solution)/shard_map/pallas_call | solution.py:442
  99.5 0.0 copy-start
  99.5 0.0 copy-start.1
  99.5 0.0 collective-permute-done.6.across
  99.5 0.0 collective-permute-done.5.beside
  99.5 3.6 %all-to-all-start.3 = ((bf16[4,32,8,256]{3,2,1,0:T(8,128)(2,1)}), bf16[4,32,8,256]{3,2,1,0:T(8,128)(2,1)S(1)}, u32[]{:S(2)}, u32[]{:S(2)}) async-start(bf16[4,32,8,256]{3,2,1,0:T(8,128)(2,1)} %shard_map.94), calls=%async_computation.3 | async-start | bytes 1048576 | tf_op jit(solution)/shard_map/all_to_all | solution.py:306
  103.2 3.6 %collective-permute-start.7 = (bf16[2,64,512]{2,1,0:T(8,128)(2,1)S(1)}, bf16[2,64,512]{2,1,0:T(8,128)(2,1)S(1)}, u32[]{:S(2)}, u32[]{:S(2)}) collective-permute-start(bf16[2,64,512]{2,1,0:T(8,128)(2,1)S(1)} %dynamic-slice_bitcast_fusion), channel_id=1, source_target_pairs={{0,64},{64,0},{1,65},{65,1},{2,66},{66,2},{3,67},{67,3},{4,68},{68... | collective-permute-start | bytes 393224 | tf_op jit(solution)/shard_map/ppermute | solution.py:319
  106.8 1.0 collective-permute-done.7.passed
  107.8 0.0 copy-done
  107.8 0.0 copy-done.1
  107.8 1.7 %shard_map.96 = (f32[4,64,512]{2,1,0:T(8,128)}, f32[4,64,512]{2,1,0:T(8,128)}) custom-call(s32[8,128]{1,0:T(8,128)S(1)} %get-tuple-element.41.table, bf16[2,64,512]{2,1,0:T(8,128)(2,1)S(1)} %get-tuple-element.61.mine, bf16[2,64,512]{2,1,0:T(8,128)(2,1)S(1)} %collective-permute-done.6.across, bf16[2,2,64,512]{3,2,1,0:T(8,128)(2,1)S(1)} %collective-permute-done.5.beside, ...), custom_call_target="tpu_custom_call" | custom-call | flops 10000000 | bytes 5000000 | tf_op jit(solution)/shard_map/pallas_call | solution.py:451
  109.5 1.1 all-to-all-done.3
  110.6 4.9 %collective-permute-start.8 = (bf16[128,8,256]{2,1,0:T(8,128)(2,1)S(1)}, bf16[128,8,256]{2,1,0:T(8,128)(2,1)S(1)}, u32[]{:S(2)}, u32[]{:S(2)}) collective-permute-start(bf16[128,8,256]{2,1,0:T(8,128)(2,1)S(1)} %bitcast.13), channel_id=1, source_target_pairs={{0,64},{64,0},{1,65},{65,1},{2,66},{66,2},{3,67},{67,3},{4,68},{68... | collective-permute-start | bytes 1572872 | tf_op jit(solution)/shard_map/ppermute | solution.py:319
  115.5 1.7 %shard_map.97.begun = bf16[128,8,512]{2,1,0:T(8,128)(2,1)} custom-call(s32[8,128]{1,0:T(8,128)S(1)} %get-tuple-element.41.table, bf16[128,8,256]{2,1,0:T(8,128)(2,1)S(1)} %bitcast.14), custom_call_target="tpu_custom_call" | custom-call | bytes 4000000 | tf_op jit(solution)/shard_map/pallas_call | solution.py:467
  117.2 0.0 collective-permute-done.8.rows
  117.2 1.7 %shard_map.98 = bf16[128,8,512]{2,1,0:T(8,128)(2,1)} custom-call(s32[8,128]{1,0:T(8,128)S(1)} %get-tuple-element.41.table, bf16[128,8,256]{2,1,0:T(8,128)(2,1)S(1)} %collective-permute-done.8.rows, bf16[128,8,512]{2,1,0:T(8,128)(2,1)} %shard_map.97.begun), custom_call_target="tpu_custom_call", output_to_operand_aliasing={{}: (2, {})} | custom-call | tf_op jit(solution)/shard_map/pallas_call | solution.py:470
  (2 shorter events, 0.0 us)
Async XLA Ops:
  1.9 11.3 %collective-permute-start = (bf16[32,64,256]{2,1,0:T(8,128)(2,1)S(1)}, bf16[32,64,256]{2,1,0:T(8,128)(2,1)S(1)}, u32[]{:S(2)}, u32[]{:S(2)}) collective-permute-start(bf16[32,64,256]{2,1,0:T(8,128)(2,1)S(1)} %shard_map.85), channel_id=1, source_target_pairs={{0,64},{64,0},{1,65},{65,1},{2,66},{66,2},{3,67},{67,3},{4,68},{68... | collective-permute-start | bytes 3145736 | tf_op jit(solution)/shard_map/ppermute | solution.py:319
  14.8 13.0 %all-to-all-start = ((bf16[4,32,8,256]{3,2,1,0:T(8,128)(2,1)}), bf16[4,32,8,256]{3,2,1,0:T(8,128)(2,1)S(1)}, u32[]{:S(2)}, u32[]{:S(2)}) async-start(bf16[4,32,8,256]{3,2,1,0:T(8,128)(2,1)} %shard_map.87), calls=%async_computation | async-start | bytes 1048576 | tf_op jit(solution)/shard_map/all_to_all | solution.py:306
  18.3 12.3 %collective-permute-start.1 = (bf16[2,64,512]{2,1,0:T(8,128)(2,1)S(1)}, bf16[2,64,512]{2,1,0:T(8,128)(2,1)S(1)}, u32[]{:S(2)}, u32[]{:S(2)}) collective-permute-start(bf16[2,64,512]{2,1,0:T(8,128)(2,1)S(1)} %get-tuple-element.45), channel_id=1, source_target_pairs={{0,256},{128,384},{256,0},{384,128},{1,257},{129,385},{257,1},{385... | collective-permute-start | bytes 393224 | tf_op jit(solution)/shard_map/ppermute | solution.py:315
  30.6 31.5 %all-to-all-start.1 = ((bf16[64,8,256]{2,1,0:T(8,128)(2,1)}), bf16[64,8,256]{2,1,0:T(8,128)(2,1)S(1)}, u32[]{:S(2)}, u32[]{:S(2)}) async-start(bf16[64,8,256]{2,1,0:T(8,128)(2,1)} %shard_map.89), calls=%async_computation.1 | async-start | bytes 524288 | tf_op jit(solution)/shard_map/all_to_all | solution.py:306
  44.0 7.4 %collective-permute-start.3 = (bf16[2,2,64,512]{3,2,1,0:T(8,128)(2,1)S(1)}, bf16[2,2,64,512]{3,2,1,0:T(8,128)(2,1)S(1)}, u32[]{:S(2)}, u32[]{:S(2)}) collective-permute-start(bf16[2,2,64,512]{3,2,1,0:T(8,128)(2,1)S(1)} %shard_map.88), channel_id=1, source_target_pairs={{0,128},{128,256},{256,384},{384,0},{64,448},{192,64},{320,192},{4... | collective-permute-start | bytes 786440 | tf_op jit(solution)/shard_map/ppermute | solution.py:402
  51.4 16.4 %collective-permute-start.4 = (bf16[3,2,64,512]{3,2,1,0:T(8,128)(2,1)S(1)}, bf16[3,2,64,512]{3,2,1,0:T(8,128)(2,1)S(1)}, u32[]{:S(2)}, u32[]{:S(2)}) collective-permute-start(bf16[3,2,64,512]{3,2,1,0:T(8,128)(2,1)S(1)} %shard_map.90), channel_id=1, source_target_pairs={{0,64},{64,0},{1,65},{65,1},{2,66},{66,2},{3,67},{67,3},{4,68},{68... | collective-permute-start | bytes 1179656 | tf_op jit(solution)/shard_map/ppermute | solution.py:319
  62.1 7.3 %collective-permute-start.2 = (bf16[512,256]{1,0:T(8,128)(2,1)S(1)}, bf16[512,256]{1,0:T(8,128)(2,1)S(1)}, u32[]{:S(2)}, u32[]{:S(2)}) collective-permute-start(bf16[512,256]{1,0:T(8,128)(2,1)S(1)} %bitcast.16), channel_id=1, source_target_pairs={{0,64},{64,0},{1,65},{65,1},{2,66},{66,2},{3,67},{67,3},{4,68},{68... | collective-permute-start | bytes 786440 | tf_op jit(solution)/shard_map/ppermute | solution.py:319
  71.7 26.4 %all-to-all-start.2 = ((bf16[64,8,256]{2,1,0:T(8,128)(2,1)}), bf16[64,8,256]{2,1,0:T(8,128)(2,1)S(1)}, u32[]{:S(2)}, u32[]{:S(2)}) async-start(bf16[64,8,256]{2,1,0:T(8,128)(2,1)} %bitcast.8), calls=%async_computation.2 | async-start | bytes 524288 | tf_op jit(solution)/shard_map/all_to_all | solution.py:306
  79.4 20.1 %collective-permute-start.5 = (bf16[2,2,64,512]{3,2,1,0:T(8,128)(2,1)S(1)}, bf16[2,2,64,512]{3,2,1,0:T(8,128)(2,1)S(1)}, u32[]{:S(2)}, u32[]{:S(2)}) collective-permute-start(bf16[2,2,64,512]{3,2,1,0:T(8,128)(2,1)S(1)} %get-tuple-element.58), channel_id=1, source_target_pairs={{0,128},{128,256},{256,384},{384,0},{64,448},{192,64},{320,192},{4... | collective-permute-start | bytes 786440 | tf_op jit(solution)/shard_map/ppermute | solution.py:441
  82.2 17.3 %collective-permute-start.6 = (bf16[2,64,512]{2,1,0:T(8,128)(2,1)S(1)}, bf16[2,64,512]{2,1,0:T(8,128)(2,1)S(1)}, u32[]{:S(2)}, u32[]{:S(2)}) collective-permute-start(bf16[2,64,512]{2,1,0:T(8,128)(2,1)S(1)} %get-tuple-element.59), channel_id=1, source_target_pairs={{0,256},{128,384},{256,0},{384,128},{1,257},{129,385},{257,1},{385... | collective-permute-start | bytes 393224 | tf_op jit(solution)/shard_map/ppermute | solution.py:315
  99.5 8.3 %copy-start = (f32[4,64,512]{2,1,0:T(8,128)S(1)}, f32[4,64,512]{2,1,0:T(8,128)}, u32[]{:S(2)}) copy-start(f32[4,64,512]{2,1,0:T(8,128)} %left.1) | copy-start | bytes 1572868
  99.5 8.3 %copy-start.1 = (f32[4,64,512]{2,1,0:T(8,128)S(1)}, f32[4,64,512]{2,1,0:T(8,128)}, u32[]{:S(2)}) copy-start(f32[4,64,512]{2,1,0:T(8,128)} %right.1) | copy-start | bytes 1572868
  99.5 11.1 %all-to-all-start.3 = ((bf16[4,32,8,256]{3,2,1,0:T(8,128)(2,1)}), bf16[4,32,8,256]{3,2,1,0:T(8,128)(2,1)S(1)}, u32[]{:S(2)}, u32[]{:S(2)}) async-start(bf16[4,32,8,256]{3,2,1,0:T(8,128)(2,1)} %shard_map.94), calls=%async_computation.3 | async-start | bytes 1048576 | tf_op jit(solution)/shard_map/all_to_all | solution.py:306
  103.2 4.6 %collective-permute-start.7 = (bf16[2,64,512]{2,1,0:T(8,128)(2,1)S(1)}, bf16[2,64,512]{2,1,0:T(8,128)(2,1)S(1)}, u32[]{:S(2)}, u32[]{:S(2)}) collective-permute-start(bf16[2,64,512]{2,1,0:T(8,128)(2,1)S(1)} %dynamic-slice_bitcast_fusion), channel_id=1, source_target_pairs={{0,64},{64,0},{1,65},{65,1},{2,66},{66,2},{3,67},{67,3},{4,68},{68... | collective-permute-start | bytes 393224 | tf_op jit(solution)/shard_map/ppermute | solution.py:319
  110.6 6.6 %collective-permute-start.8 = (bf16[128,8,256]{2,1,0:T(8,128)(2,1)S(1)}, bf16[128,8,256]{2,1,0:T(8,128)(2,1)S(1)}, u32[]{:S(2)}, u32[]{:S(2)}) collective-permute-start(bf16[128,8,256]{2,1,0:T(8,128)(2,1)S(1)} %bitcast.13), channel_id=1, source_target_pairs={{0,64},{64,0},{1,65},{65,1},{2,66},{66,2},{3,67},{67,3},{4,68},{68... | collective-permute-start | bytes 1572872 | tf_op jit(solution)/shard_map/ppermute | solution.py:319

commit v8 on v7

--- a/solution.py
+++ b/solution.py
@@ -262,27 +262,28 @@
     lax.fori_loop(0, out.shape[1], body, 0, unroll=8)
 
 
-def place_half(core, table, rows, out_hbm, ordered, sems):
+def order_kernel(table, rows, out):
+    def body(b, carry):
+        out[b] = rows[table[SOURCE, b]]
+        return carry
+
+    lax.fori_loop(0, out.shape[0], body, 0, unroll=8)
+
+
+def place_half(half, rows, out_hbm, sem):
     width = rows.shape[2]
-    cols = pl.ds(pl.multiple_of(core * width, 128), width)
-
-    def fill(first, count):
-        def body(b, carry):
-            ordered[first + b] = rows[table[SOURCE, first + b]]
-            return carry
-
-        lax.fori_loop(0, count, body, 0, unroll=8)
-
-    store_in_steps(ordered, out_hbm.at[:, :, cols], sems, 0, fill)
-
-
-def place_near_kernel(table, rows, out_hbm, ordered, sems):
-    place_half(table[WHERE, 0], table, rows, out_hbm, ordered, sems)
-
-
-def place_far_kernel(table, rows, begun, out_hbm, ordered, sems):
+    store = pltpu.make_async_copy(rows, out_hbm.at[:, :, pl.ds(pl.multiple_of(half * width, 128), width)], sem)
+    store.start()
+    store.wait()
+
+
+def place_near_kernel(core_ref, rows, out_hbm, sem):
+    place_half(core_ref[0], rows, out_hbm, sem)
+
+
+def place_far_kernel(core_ref, rows, begun, out_hbm, sem):
     del begun
-    place_half(1 - table[WHERE, 0], table, rows, out_hbm, ordered, sems)
+    place_half(1 - core_ref[0], rows, out_hbm, sem)
 
 
 def call(kernel, out_shape, in_specs, scratch=(), out_specs=None, cost=None, aliases=None):
@@ -333,6 +334,7 @@
 
     piece = jax.ShapeDtypeStruct((2, stat_rows, width), BF16)
     groups = width // stat_rows
+    half_rows = jax.ShapeDtypeStruct((blocks, shard_rows, half), BF16)
     grads = in_hbm(grads.reshape(-1, stat_rows, width))
     left_root, right_root = in_hbm(left_root), in_hbm(right_root)
     grad_groups = grads.shape[0]
@@ -382,7 +384,9 @@
         [SMEM_SPEC, VMEM_SPEC, VMEM_SPEC],
         cost=(0, 1000),
     )(late_table, other, beside)
-    parts, beside = lax.optimization_barrier((parts, beside))
+    ways = [(2 * i, 2 * ((i + 1) % chips)) for i in range(chips)]
+    ways += [(2 * i + 1, 2 * ((i - 1) % chips) + 1) for i in range(chips)]
+    beside = lax.ppermute(beside, ("x", "core"), ways)
     outgoing = call(
         chip_sum_kernel,
         jax.ShapeDtypeStruct((owners, shard_rows, half), BF16),
@@ -394,12 +398,9 @@
         ],
     )(table, parts)
 
-    across = turn(across, 2)
     outgoing, late_other, beside, across = lax.optimization_barrier((outgoing, other, beside, across))
     own = exchange(outgoing, ("y", "z"))
-    ways = [(2 * i, 2 * ((i + 1) % chips)) for i in range(chips)]
-    ways += [(2 * i + 1, 2 * ((i - 1) % chips) + 1) for i in range(chips)]
-    beside = lax.ppermute(beside, ("x", "core"), ways)
+    across = turn(across, 2)
     stacked = call(
         stack_kernel,
         jax.ShapeDtypeStruct((3, 2, stat_rows, width), BF16),
@@ -461,15 +462,25 @@
         cost=(10_000_000, 5_000_000),
     )(table, mine, across, beside, passed, left_stat, right_stat)
     near, left_new, right_new = lax.optimization_barrier((near, left_new, right_new))
+    near = call(order_kernel, half_rows, [SMEM_SPEC, VMEM_SPEC])(table, near)
     beyond = swap_cores(near)
     whole_rows = jax.ShapeDtypeStruct((blocks, shard_rows, width), BF16)
-    scratch = [pltpu.VMEM((blocks, shard_rows, half), BF16), pltpu.SemaphoreType.DMA((4,))]
     begun = call(
-        place_near_kernel, whole_rows, [SMEM_SPEC, VMEM_SPEC], scratch, HBM_SPEC, cost=(0, 4_000_000)
-    )(table, near)
+        place_near_kernel,
+        whole_rows,
+        [SMEM_SPEC, VMEM_SPEC],
+        [pltpu.SemaphoreType.DMA],
+        HBM_SPEC,
+        cost=(0, 4_000_000),
+    )(core.reshape(1), near)
     result = call(
-        place_far_kernel, whole_rows, [SMEM_SPEC, VMEM_SPEC, HBM_SPEC], scratch, HBM_SPEC, aliases={2: 0}
-    )(table, beyond, begun)
+        place_far_kernel,
+        whole_rows,
+        [SMEM_SPEC, VMEM_SPEC, HBM_SPEC],
+        [pltpu.SemaphoreType.DMA],
+        HBM_SPEC,
+        aliases={2: 0},
+    )(core.reshape(1), beyond, begun)
     return (result, left_new, right_new)
 
 

time: 120 us -> 119 us (level)
  starting transfers between devices: 68.5 us -> 70.5 us
  waiting for transfers between devices: 30 us -> 28 us
    ppermute x2, waiting for transfers between devices: 4.61 us -> 0.22 us  [local(): beside = lax.ppermute(beside, ('x', 'core'), ways)]
    ppermute x2, starting transfers between devices: 5.58 us -> 8.56 us  [local(): beside = lax.ppermute(beside, ('x', 'core'), ways)]
    ppermute x2, waiting for transfers between devices: 1.3 us -> 3.16 us  [turn(): lax.ppermute(value, 'x', [(i, (i + k) % chips) for i in range(chips)])]
    ppermute x2, starting transfers between devices: 7.94 us -> 6.55 us  [turn(): lax.ppermute(value, 'x', [(i, (i + k) % chips) for i in range(chips)])]
    pallas_call x2 -> x3, Pallas kernels: 3.42 us -> 2.58 us  [the longest x1 0.98 us: local(): near = call(order_kernel, half_rows, [SMEM_SPEC, VMEM_SPEC])(table, near)]
  transfers between devices with their start and end apart: 13 -> 13, of which waited for: 7 -> 8; matrix products, arithmetic and copies ran while one was open for 0% -> 0% of each run, Pallas kernels for 11% -> 10%
where the time goes in v8:
time: 119 us; the launch traced here: 118 us
  starting transfers between devices  70.5 us (59%)
  waiting for transfers between devices  28 us (24%)
  Pallas kernels  18.6 us (16%)
    ppermute x5, starting transfers between devices, swap_cores(): return lax.ppermute(value, 'core', [(0, 1), (1, 0)])  28.5 us
    all_to_all x4, starting transfers between devices, exchange(): return lax.all_to_all(value, axis, 0, 0, tiled=True)  26.9 us
    all_to_all x4, waiting for transfers between devices, exchange(): return lax.all_to_all(value, axis, 0, 0, tiled=True)  22.9 us
    ppermute x2, starting transfers between devices, local(): beside = lax.ppermute(beside, ('x', 'core'), ways)  8.56 us
    ppermute x2, starting transfers between devices, turn(): lax.ppermute(value, 'x', [(i, (i + k) % chips) for i in range(chips)])  6.55 us
    ppermute x2, waiting for transfers between devices, turn(): lax.ppermute(value, 'x', [(i, (i + k) % chips) for i in range(chips)])  3.16 us
    pallas_call x1, Pallas kernels, local(): call(keep_kernel, [jax.ShapeDtypeStruct((grad_groups, stat_rows, half), B...  2.52 us
  transfers between devices with their start and end apart: 13, of which 8 were waited for; matrix products, arithmetic and copies ran while one was open for 0% of the time, Pallas kernels for 10%

profile of v8, /device:TPU:1, one launch (start us, length us, event | category | flops | bytes accessed | tf_op | source)
XLA Modules:
  0.0 118.0 jit_solution(12957437154627901841)
XLA Ops:
  0.6 1.2 %shard_map.85 = bf16[32,64,256]{2,1,0:T(8,128)(2,1)S(1)} custom-call(s32[1]{0:T(128)} %bitcast.core_ref, bf16[16,64,512]{2,1,0:T(8,128)(2,1)} %bitcast.18, bf16[4,64,512]{2,1,0:T(8,128)(2,1)} %left_root.3, bf16[4,64,512]{2,1,0:T(8,128)(2,1)} %right_root.3), custom_call_target="tpu_custom_call" | custom-call | tf_op jit(solution)/shard_map/pallas_call | solution.py:342
  1.9 8.8 %collective-permute-start = (bf16[32,64,256]{2,1,0:T(8,128)(2,1)S(1)}, bf16[32,64,256]{2,1,0:T(8,128)(2,1)S(1)}, u32[]{:S(2)}, u32[]{:S(2)}) collective-permute-start(bf16[32,64,256]{2,1,0:T(8,128)(2,1)S(1)} %shard_map.85), channel_id=1, source_target_pairs={{0,64},{64,0},{1,65},{65,1},{2,66},{66,2},{3,67},{67,3},{4,68},{68... | collective-permute-start | bytes 3145736 | tf_op jit(solution)/shard_map/ppermute | solution.py:320
  10.7 2.5 %shard_map.86 = (bf16[16,64,256]{2,1,0:T(8,128)(2,1)S(1)}, s32[8,128]{1,0:T(8,128)S(1)}, bf16[2,64,512]{2,1,0:T(8,128)(2,1)S(1)}, bf16[2,64,512]{2,1,0:T(8,128)(2,1)S(1)}, bf16[2,64,512]{2,1,0:T(8,128)(2,1)S(1)}) custom-call(s32[1]{0:T(128)} %bitcast.core_ref, s32[1]{0:T(128)} %bitcast.1.x_ref, s32[1]{0:T(128)} %bitcast.2.me_ref, s32[1,128]{1,0:T(1,128)} %bitcast.20, ...), custom_call_target="tpu_custom_call" | custom-call | bytes 4000000 | tf_op jit(solution)/shard_map/pallas_call | solution.py:350
  13.2 0.0 collective-permute-done.other
  13.2 1.6 %shard_map.87 = bf16[4,32,8,256]{3,2,1,0:T(8,128)(2,1)} custom-call(s32[8,128]{1,0:T(8,128)S(1)} %get-tuple-element.39.table, bf16[128,8,256]{2,1,0:T(8,128)(2,1)S(1)} %bitcast.14, bf16[256,8,256]{2,1,0:T(8,128)(2,1)S(1)} %bitcast.12), custom_call_target="tpu_custom_call" | custom-call | tf_op jit(solution)/shard_map/pallas_call | solution.py:373
  14.8 3.5 %all-to-all-start = ((bf16[4,32,8,256]{3,2,1,0:T(8,128)(2,1)}), bf16[4,32,8,256]{3,2,1,0:T(8,128)(2,1)S(1)}, u32[]{:S(2)}, u32[]{:S(2)}) async-start(bf16[4,32,8,256]{3,2,1,0:T(8,128)(2,1)} %shard_map.87), calls=%async_computation | async-start | bytes 1048576 | tf_op jit(solution)/shard_map/all_to_all | solution.py:307
  18.3 0.6 shard_map.89
  18.9 4.6 %collective-permute-start.1 = (bf16[2,2,64,512]{3,2,1,0:T(8,128)(2,1)S(1)}, bf16[2,2,64,512]{3,2,1,0:T(8,128)(2,1)S(1)}, u32[]{:S(2)}, u32[]{:S(2)}) collective-permute-start(bf16[2,2,64,512]{3,2,1,0:T(8,128)(2,1)S(1)} %shard_map.89), channel_id=1, source_target_pairs={{0,128},{128,256},{256,384},{384,0},{64,448},{192,64},{320,192},{4... | collective-permute-start | bytes 786440 | tf_op jit(solution)/shard_map/ppermute | solution.py:389
  23.5 4.4 %all-to-all-done.parts = bf16[4,32,8,256]{3,2,1,0:T(8,128)(2,1)S(1)} async-done(((bf16[4,32,8,256]{3,2,1,0:T(8,128)(2,1)}), bf16[4,32,8,256]{3,2,1,0:T(8,128)(2,1)S(1)}, u32[]{:S(2)}, u32[]{:S(2)}) %all-to-all-start) | async-done | bytes 524320 | tf_op jit(solution)/shard_map/all_to_all | solution.py:307
  27.9 1.5 %shard_map.88 = bf16[64,8,256]{2,1,0:T(8,128)(2,1)} custom-call(s32[8,128]{1,0:T(8,128)S(1)} %get-tuple-element.39.table, bf16[4,32,8,256]{3,2,1,0:T(8,128)(2,1)S(1)} %all-to-all-done.parts), custom_call_target="tpu_custom_call" | custom-call | tf_op jit(solution)/shard_map/pallas_call | solution.py:390
  29.4 0.2 collective-permute-done.1.beside
  29.6 13.7 %all-to-all-start.1 = ((bf16[64,8,256]{2,1,0:T(8,128)(2,1)}), bf16[64,8,256]{2,1,0:T(8,128)(2,1)S(1)}, u32[]{:S(2)}, u32[]{:S(2)}) async-start(bf16[64,8,256]{2,1,0:T(8,128)(2,1)} %shard_map.88), calls=%async_computation.1 | async-start | bytes 524288 | tf_op jit(solution)/shard_map/all_to_all | solution.py:307
  43.2 4.1 %collective-permute-start.3 = (bf16[2,64,512]{2,1,0:T(8,128)(2,1)S(1)}, bf16[2,64,512]{2,1,0:T(8,128)(2,1)S(1)}, u32[]{:S(2)}, u32[]{:S(2)}) collective-permute-start(bf16[2,64,512]{2,1,0:T(8,128)(2,1)S(1)} %get-tuple-element.46), channel_id=1, source_target_pairs={{0,256},{128,384},{256,0},{384,128},{1,257},{129,385},{257,1},{385... | collective-permute-start | bytes 393224 | tf_op jit(solution)/shard_map/ppermute | solution.py:316
  47.3 3.2 %collective-permute-done.3.across = bf16[2,64,512]{2,1,0:T(8,128)(2,1)S(1)} collective-permute-done((bf16[2,64,512]{2,1,0:T(8,128)(2,1)S(1)}, bf16[2,64,512]{2,1,0:T(8,128)(2,1)S(1)}, u32[]{:S(2)}, u32[]{:S(2)}) %collective-permute-start.3) | collective-permute-done | bytes 131104 | tf_op jit(solution)/shard_map/ppermute | solution.py:316
  50.5 4.9 %collective-permute-start.4 = (bf16[3,2,64,512]{3,2,1,0:T(8,128)(2,1)S(1)}, bf16[3,2,64,512]{3,2,1,0:T(8,128)(2,1)S(1)}, u32[]{:S(2)}, u32[]{:S(2)}) collective-permute-start(bf16[3,2,64,512]{3,2,1,0:T(8,128)(2,1)S(1)} %shard_map.90), channel_id=1, source_target_pairs={{0,64},{64,0},{1,65},{65,1},{2,66},{66,2},{3,67},{67,3},{4,68},{68... | collective-permute-start | bytes 1179656 | tf_op jit(solution)/shard_map/ppermute | solution.py:320
  55.4 5.9 %all-to-all-done.1 = bf16[64,8,256]{2,1,0:T(8,128)(2,1)S(1)} async-done(((bf16[64,8,256]{2,1,0:T(8,128)(2,1)}), bf16[64,8,256]{2,1,0:T(8,128)(2,1)S(1)}, u32[]{:S(2)}, u32[]{:S(2)}) %all-to-all-start.1) | async-done | bytes 262176 | tf_op jit(solution)/shard_map/all_to_all | solution.py:307
  61.3 5.8 %collective-permute-start.2 = (bf16[512,256]{1,0:T(8,128)(2,1)S(1)}, bf16[512,256]{1,0:T(8,128)(2,1)S(1)}, u32[]{:S(2)}, u32[]{:S(2)}) collective-permute-start(bf16[512,256]{1,0:T(8,128)(2,1)S(1)} %bitcast.15), channel_id=1, source_target_pairs={{0,64},{64,0},{1,65},{65,1},{2,66},{66,2},{3,67},{67,3},{4,68},{68... | collective-permute-start | bytes 786440 | tf_op jit(solution)/shard_map/ppermute | solution.py:320
  67.1 0.0 collective-permute-done.4.others
  67.1 0.7 shard_map.91
  67.8 0.9 shard_map.92
  68.7 0.0 collective-permute-done.2.other
  68.7 2.2 %shard_map.93 = bf16[512,256]{1,0:T(8,128)(2,1)} custom-call(s32[8,128]{1,0:T(8,128)S(1)} %get-tuple-element.39.table, bf16[512,256]{1,0:T(8,128)(2,1)S(1)} %collective-permute-done.2.other, f32[512,512]{1,0:T(8,128)S(1)} %get-tuple-element.48.partial, bf16[8,64,512]{2,1,0:T(8,128)(2,1)S(1)} %get-tuple-element.49.left, ...), custom_call_target="tpu_custom_call" | custom-call | tf_op jit(solution)/shard_map/pallas_call | solution.py:426
  70.9 6.2 %all-to-all-start.2 = ((bf16[64,8,256]{2,1,0:T(8,128)(2,1)}), bf16[64,8,256]{2,1,0:T(8,128)(2,1)S(1)}, u32[]{:S(2)}, u32[]{:S(2)}) async-start(bf16[64,8,256]{2,1,0:T(8,128)(2,1)} %bitcast.8), calls=%async_computation.2 | async-start | bytes 524288 | tf_op jit(solution)/shard_map/all_to_all | solution.py:307
  77.1 1.5 %shard_map.95 = (bf16[2,2,64,512]{3,2,1,0:T(8,128)(2,1)S(1)}, bf16[2,64,512]{2,1,0:T(8,128)(2,1)S(1)}, bf16[2,64,512]{2,1,0:T(8,128)(2,1)S(1)}) custom-call(s32[8,128]{1,0:T(8,128)S(1)} %get-tuple-element.39.table, bf16[512,256]{1,0:T(8,128)(2,1)S(1)} %bitcast.17, bf16[512,256]{1,0:T(8,128)(2,1)S(1)} %collective-permute-done.2.other), custom_call_target="tpu_custom_call" | custom-call | flops 800000000 | bytes 2000000 | tf_op jit(solution)/shard_map/pallas_call | solution.py:434
  78.6 4.0 %collective-permute-start.5 = (bf16[2,2,64,512]{3,2,1,0:T(8,128)(2,1)S(1)}, bf16[2,2,64,512]{3,2,1,0:T(8,128)(2,1)S(1)}, u32[]{:S(2)}, u32[]{:S(2)}) collective-permute-start(bf16[2,2,64,512]{3,2,1,0:T(8,128)(2,1)S(1)} %get-tuple-element.54), channel_id=1, source_target_pairs={{0,128},{128,256},{256,384},{384,0},{64,448},{192,64},{320,192},{4... | collective-permute-start | bytes 786440 | tf_op jit(solution)/shard_map/ppermute | solution.py:442
  82.7 2.5 %collective-permute-start.6 = (bf16[2,64,512]{2,1,0:T(8,128)(2,1)S(1)}, bf16[2,64,512]{2,1,0:T(8,128)(2,1)S(1)}, u32[]{:S(2)}, u32[]{:S(2)}) collective-permute-start(bf16[2,64,512]{2,1,0:T(8,128)(2,1)S(1)} %get-tuple-element.55), channel_id=1, source_target_pairs={{0,256},{128,384},{256,0},{384,128},{1,257},{129,385},{257,1},{385... | collective-permute-start | bytes 393224 | tf_op jit(solution)/shard_map/ppermute | solution.py:316
  85.2 12.1 %all-to-all-done.2.rows = bf16[64,8,256]{2,1,0:T(8,128)(2,1)S(1)} async-done(((bf16[64,8,256]{2,1,0:T(8,128)(2,1)}), bf16[64,8,256]{2,1,0:T(8,128)(2,1)S(1)}, u32[]{:S(2)}, u32[]{:S(2)}) %all-to-all-start.2) | async-done | bytes 262176 | tf_op jit(solution)/shard_map/all_to_all | solution.py:307
  97.2 1.5 %shard_map.94 = bf16[4,32,8,256]{3,2,1,0:T(8,128)(2,1)} custom-call(s32[8,128]{1,0:T(8,128)S(1)} %get-tuple-element.39.table, bf16[64,8,256]{2,1,0:T(8,128)(2,1)S(1)} %all-to-all-done.2.rows), custom_call_target="tpu_custom_call" | custom-call | tf_op jit(solution)/shard_map/pallas_call | solution.py:443
  98.7 0.0 copy-start
  98.7 0.0 copy-start.1
  98.7 0.0 collective-permute-done.6.across
  98.7 0.0 collective-permute-done.5.beside
  98.7 3.6 %all-to-all-start.3 = ((bf16[4,32,8,256]{3,2,1,0:T(8,128)(2,1)}), bf16[4,32,8,256]{3,2,1,0:T(8,128)(2,1)S(1)}, u32[]{:S(2)}, u32[]{:S(2)}) async-start(bf16[4,32,8,256]{3,2,1,0:T(8,128)(2,1)} %shard_map.94), calls=%async_computation.3 | async-start | bytes 1048576 | tf_op jit(solution)/shard_map/all_to_all | solution.py:307
  102.4 3.9 %collective-permute-start.7 = (bf16[2,64,512]{2,1,0:T(8,128)(2,1)S(1)}, bf16[2,64,512]{2,1,0:T(8,128)(2,1)S(1)}, u32[]{:S(2)}, u32[]{:S(2)}) collective-permute-start(bf16[2,64,512]{2,1,0:T(8,128)(2,1)S(1)} %dynamic-slice_bitcast_fusion), channel_id=1, source_target_pairs={{0,64},{64,0},{1,65},{65,1},{2,66},{66,2},{3,67},{67,3},{4,68},{68... | collective-permute-start | bytes 393224 | tf_op jit(solution)/shard_map/ppermute | solution.py:320
  106.3 1.0 collective-permute-done.7.passed
  107.2 0.0 copy-done
  107.2 0.0 copy-done.1
  107.2 1.7 %shard_map.96 = (f32[4,64,512]{2,1,0:T(8,128)}, f32[4,64,512]{2,1,0:T(8,128)}) custom-call(s32[8,128]{1,0:T(8,128)S(1)} %get-tuple-element.39.table, bf16[2,64,512]{2,1,0:T(8,128)(2,1)S(1)} %get-tuple-element.57.mine, bf16[2,64,512]{2,1,0:T(8,128)(2,1)S(1)} %collective-permute-done.6.across, bf16[2,2,64,512]{3,2,1,0:T(8,128)(2,1)S(1)} %collective-permute-done.5.beside, ...), custom_call_target="tpu_custom_call" | custom-call | flops 10000000 | bytes 5000000 | tf_op jit(solution)/shard_map/pallas_call | solution.py:452
  108.9 0.6 all-to-all-done.3
  109.5 1.0 shard_map.97.rows
  110.5 5.1 %collective-permute-start.8 = (bf16[128,8,256]{2,1,0:T(8,128)(2,1)S(1)}, bf16[128,8,256]{2,1,0:T(8,128)(2,1)S(1)}, u32[]{:S(2)}, u32[]{:S(2)}) collective-permute-start(bf16[128,8,256]{2,1,0:T(8,128)(2,1)S(1)} %shard_map.97.rows), channel_id=1, source_target_pairs={{0,64},{64,0},{1,65},{65,1},{2,66},{66,2},{3,67},{67,3},{4,68},{68... | collective-permute-start | bytes 1572872 | tf_op jit(solution)/shard_map/ppermute | solution.py:320
  115.6 0.8 shard_map.98.begun
  116.5 0.7 collective-permute-done.8.rows
  117.2 0.8 shard_map.99
  (2 shorter events, 0.0 us)
Async XLA Ops:
  1.9 11.3 %collective-permute-start = (bf16[32,64,256]{2,1,0:T(8,128)(2,1)S(1)}, bf16[32,64,256]{2,1,0:T(8,128)(2,1)S(1)}, u32[]{:S(2)}, u32[]{:S(2)}) collective-permute-start(bf16[32,64,256]{2,1,0:T(8,128)(2,1)S(1)} %shard_map.85), channel_id=1, source_target_pairs={{0,64},{64,0},{1,65},{65,1},{2,66},{66,2},{3,67},{67,3},{4,68},{68... | collective-permute-start | bytes 3145736 | tf_op jit(solution)/shard_map/ppermute | solution.py:320
  14.8 13.1 %all-to-all-start = ((bf16[4,32,8,256]{3,2,1,0:T(8,128)(2,1)}), bf16[4,32,8,256]{3,2,1,0:T(8,128)(2,1)S(1)}, u32[]{:S(2)}, u32[]{:S(2)}) async-start(bf16[4,32,8,256]{3,2,1,0:T(8,128)(2,1)} %shard_map.87), calls=%async_computation | async-start | bytes 1048576 | tf_op jit(solution)/shard_map/all_to_all | solution.py:307
  18.9 10.7 %collective-permute-start.1 = (bf16[2,2,64,512]{3,2,1,0:T(8,128)(2,1)S(1)}, bf16[2,2,64,512]{3,2,1,0:T(8,128)(2,1)S(1)}, u32[]{:S(2)}, u32[]{:S(2)}) collective-permute-start(bf16[2,2,64,512]{3,2,1,0:T(8,128)(2,1)S(1)} %shard_map.89), channel_id=1, source_target_pairs={{0,128},{128,256},{256,384},{384,0},{64,448},{192,64},{320,192},{4... | collective-permute-start | bytes 786440 | tf_op jit(solution)/shard_map/ppermute | solution.py:389
  29.6 31.7 %all-to-all-start.1 = ((bf16[64,8,256]{2,1,0:T(8,128)(2,1)}), bf16[64,8,256]{2,1,0:T(8,128)(2,1)S(1)}, u32[]{:S(2)}, u32[]{:S(2)}) async-start(bf16[64,8,256]{2,1,0:T(8,128)(2,1)} %shard_map.88), calls=%async_computation.1 | async-start | bytes 524288 | tf_op jit(solution)/shard_map/all_to_all | solution.py:307
  43.2 7.2 %collective-permute-start.3 = (bf16[2,64,512]{2,1,0:T(8,128)(2,1)S(1)}, bf16[2,64,512]{2,1,0:T(8,128)(2,1)S(1)}, u32[]{:S(2)}, u32[]{:S(2)}) collective-permute-start(bf16[2,64,512]{2,1,0:T(8,128)(2,1)S(1)} %get-tuple-element.46), channel_id=1, source_target_pairs={{0,256},{128,384},{256,0},{384,128},{1,257},{129,385},{257,1},{385... | collective-permute-start | bytes 393224 | tf_op jit(solution)/shard_map/ppermute | solution.py:316
  50.5 16.6 %collective-permute-start.4 = (bf16[3,2,64,512]{3,2,1,0:T(8,128)(2,1)S(1)}, bf16[3,2,64,512]{3,2,1,0:T(8,128)(2,1)S(1)}, u32[]{:S(2)}, u32[]{:S(2)}) collective-permute-start(bf16[3,2,64,512]{3,2,1,0:T(8,128)(2,1)S(1)} %shard_map.90), channel_id=1, source_target_pairs={{0,64},{64,0},{1,65},{65,1},{2,66},{66,2},{3,67},{67,3},{4,68},{68... | collective-permute-start | bytes 1179656 | tf_op jit(solution)/shard_map/ppermute | solution.py:320
  61.3 7.4 %collective-permute-start.2 = (bf16[512,256]{1,0:T(8,128)(2,1)S(1)}, bf16[512,256]{1,0:T(8,128)(2,1)S(1)}, u32[]{:S(2)}, u32[]{:S(2)}) collective-permute-start(bf16[512,256]{1,0:T(8,128)(2,1)S(1)} %bitcast.15), channel_id=1, source_target_pairs={{0,64},{64,0},{1,65},{65,1},{2,66},{66,2},{3,67},{67,3},{4,68},{68... | collective-permute-start | bytes 786440 | tf_op jit(solution)/shard_map/ppermute | solution.py:320
  70.9 26.3 %all-to-all-start.2 = ((bf16[64,8,256]{2,1,0:T(8,128)(2,1)}), bf16[64,8,256]{2,1,0:T(8,128)(2,1)S(1)}, u32[]{:S(2)}, u32[]{:S(2)}) async-start(bf16[64,8,256]{2,1,0:T(8,128)(2,1)} %bitcast.8), calls=%async_computation.2 | async-start | bytes 524288 | tf_op jit(solution)/shard_map/all_to_all | solution.py:307
  78.6 20.1 %collective-permute-start.5 = (bf16[2,2,64,512]{3,2,1,0:T(8,128)(2,1)S(1)}, bf16[2,2,64,512]{3,2,1,0:T(8,128)(2,1)S(1)}, u32[]{:S(2)}, u32[]{:S(2)}) collective-permute-start(bf16[2,2,64,512]{3,2,1,0:T(8,128)(2,1)S(1)} %get-tuple-element.54), channel_id=1, source_target_pairs={{0,128},{128,256},{256,384},{384,0},{64,448},{192,64},{320,192},{4... | collective-permute-start | bytes 786440 | tf_op jit(solution)/shard_map/ppermute | solution.py:442
  82.7 16.1 %collective-permute-start.6 = (bf16[2,64,512]{2,1,0:T(8,128)(2,1)S(1)}, bf16[2,64,512]{2,1,0:T(8,128)(2,1)S(1)}, u32[]{:S(2)}, u32[]{:S(2)}) collective-permute-start(bf16[2,64,512]{2,1,0:T(8,128)(2,1)S(1)} %get-tuple-element.55), channel_id=1, source_target_pairs={{0,256},{128,384},{256,0},{384,128},{1,257},{129,385},{257,1},{385... | collective-permute-start | bytes 393224 | tf_op jit(solution)/shard_map/ppermute | solution.py:316
  98.7 8.5 %copy-start = (f32[4,64,512]{2,1,0:T(8,128)S(1)}, f32[4,64,512]{2,1,0:T(8,128)}, u32[]{:S(2)}) copy-start(f32[4,64,512]{2,1,0:T(8,128)} %left.1) | copy-start | bytes 1572868
  98.7 8.5 %copy-start.1 = (f32[4,64,512]{2,1,0:T(8,128)S(1)}, f32[4,64,512]{2,1,0:T(8,128)}, u32[]{:S(2)}) copy-start(f32[4,64,512]{2,1,0:T(8,128)} %right.1) | copy-start | bytes 1572868
  98.7 10.8 %all-to-all-start.3 = ((bf16[4,32,8,256]{3,2,1,0:T(8,128)(2,1)}), bf16[4,32,8,256]{3,2,1,0:T(8,128)(2,1)S(1)}, u32[]{:S(2)}, u32[]{:S(2)}) async-start(bf16[4,32,8,256]{3,2,1,0:T(8,128)(2,1)} %shard_map.94), calls=%async_computation.3 | async-start | bytes 1048576 | tf_op jit(solution)/shard_map/all_to_all | solution.py:307
  102.4 4.8 %collective-permute-start.7 = (bf16[2,64,512]{2,1,0:T(8,128)(2,1)S(1)}, bf16[2,64,512]{2,1,0:T(8,128)(2,1)S(1)}, u32[]{:S(2)}, u32[]{:S(2)}) collective-permute-start(bf16[2,64,512]{2,1,0:T(8,128)(2,1)S(1)} %dynamic-slice_bitcast_fusion), channel_id=1, source_target_pairs={{0,64},{64,0},{1,65},{65,1},{2,66},{66,2},{3,67},{67,3},{4,68},{68... | collective-permute-start | bytes 393224 | tf_op jit(solution)/shard_map/ppermute | solution.py:320
  110.5 6.7 %collective-permute-start.8 = (bf16[128,8,256]{2,1,0:T(8,128)(2,1)S(1)}, bf16[128,8,256]{2,1,0:T(8,128)(2,1)S(1)}, u32[]{:S(2)}, u32[]{:S(2)}) collective-permute-start(bf16[128,8,256]{2,1,0:T(8,128)(2,1)S(1)} %shard_map.97.rows), channel_id=1, source_target_pairs={{0,64},{64,0},{1,65},{65,1},{2,66},{66,2},{3,67},{67,3},{4,68},{68... | collective-permute-start | bytes 1572872 | tf_op jit(solution)/shard_map/ppermute | solution.py:320

commit v9 on v8

--- a/solution.py
+++ b/solution.py
@@ -445,9 +445,10 @@
         jax.ShapeDtypeStruct((chips, depth, shard_rows, half), BF16),
         [SMEM_SPEC, VMEM_SPEC],
     )(table, rows)
-    packed, beside, across = lax.optimization_barrier((packed, beside, across))
+    passed = swap_cores(lax.dynamic_index_in_dim(beside, 1 - core, keepdims=False))
+    packed, beside, across, passed = lax.optimization_barrier((packed, beside, across, passed))
     near = exchange(packed, "x").reshape(blocks, shard_rows, half)
-    passed = swap_cores(lax.dynamic_index_in_dim(beside, 1 - core, keepdims=False))
+    near, beside, across, passed = lax.optimization_barrier((near, beside, across, passed))
     stat = jax.ShapeDtypeStruct(left_stat.shape, F32)
     left_new, right_new = call(
         stats_kernel,
@@ -461,7 +462,6 @@
         [HBM_SPEC, HBM_SPEC],
         cost=(10_000_000, 5_000_000),
     )(table, mine, across, beside, passed, left_stat, right_stat)
-    near, left_new, right_new = lax.optimization_barrier((near, left_new, right_new))
     near = call(order_kernel, half_rows, [SMEM_SPEC, VMEM_SPEC])(table, near)
     beyond = swap_cores(near)
     whole_rows = jax.ShapeDtypeStruct((blocks, shard_rows, width), BF16)

time: 119 us -> 119 us (level)
  blocking collectives: 0 us -> 10.4 us
  waiting for transfers between devices: 28 us -> 21.4 us
  starting transfers between devices: 70.5 us -> 67.4 us
    all_to_all x0 -> x1, blocking collectives: none -> 10.4 us  [exchange(): return lax.all_to_all(value, axis, 0, 0, tiled=True)]
    all_to_all x4 -> x3, waiting for transfers between devices: 22.9 us -> 17.2 us  [exchange(): return lax.all_to_all(value, axis, 0, 0, tiled=True)]
    all_to_all x4 -> x3, starting transfers between devices: 26.9 us -> 23.3 us  [exchange(): return lax.all_to_all(value, axis, 0, 0, tiled=True)]
    ppermute x5, waiting for transfers between devices: 1.67 us -> 0.01 us  [swap_cores(): return lax.ppermute(value, 'core', [(0, 1), (1, 0)])]
  transfers between devices with their start and end apart: 13 -> 12, of which waited for: 8 -> 6; matrix products, arithmetic and copies ran while one was open for 0% -> 0% of each run, Pallas kernels for 10% -> 9%
where the time goes in v9:
time: 119 us; the launch traced here: 118 us
  starting transfers between devices  67.4 us (57%)
  waiting for transfers between devices  21.4 us (18%)
  Pallas kernels  17.8 us (15%)
  blocking collectives  10.4 us (9%)
    ppermute x5, starting transfers between devices, swap_cores(): return lax.ppermute(value, 'core', [(0, 1), (1, 0)])  29.1 us
    all_to_all x3, starting transfers between devices, exchange(): return lax.all_to_all(value, axis, 0, 0, tiled=True)  23.3 us
    all_to_all x3, waiting for transfers between devices, exchange(): return lax.all_to_all(value, axis, 0, 0, tiled=True)  17.2 us
    all_to_all x1, blocking collectives, exchange(): return lax.all_to_all(value, axis, 0, 0, tiled=True)  10.4 us
    ppermute x2, starting transfers between devices, local(): beside = lax.ppermute(beside, ('x', 'core'), ways)  8.56 us
    ppermute x2, starting transfers between devices, turn(): lax.ppermute(value, 'x', [(i, (i + k) % chips) for i in range(chips)])  6.55 us
    ppermute x2, waiting for transfers between devices, turn(): lax.ppermute(value, 'x', [(i, (i + k) % chips) for i in range(chips)])  3.16 us
    pallas_call x1, Pallas kernels, local(): call(keep_kernel, [jax.ShapeDtypeStruct((grad_groups, stat_rows, half), B...  2.52 us
  transfers between devices with their start and end apart: 12, of which 6 were waited for; matrix products, arithmetic and copies ran while one was open for 0% of the time, Pallas kernels for 9%

profile of v9, /device:TPU:1, one launch (start us, length us, event | category | flops | bytes accessed | tf_op | source)
XLA Modules:
  0.0 118.0 jit_solution(3879221486621613063)
XLA Ops:
  0.6 1.2 %shard_map.85 = bf16[32,64,256]{2,1,0:T(8,128)(2,1)S(1)} custom-call(s32[1]{0:T(128)} %bitcast.core_ref, bf16[16,64,512]{2,1,0:T(8,128)(2,1)} %bitcast.18, bf16[4,64,512]{2,1,0:T(8,128)(2,1)} %left_root.3, bf16[4,64,512]{2,1,0:T(8,128)(2,1)} %right_root.3), custom_call_target="tpu_custom_call" | custom-call | tf_op jit(solution)/shard_map/pallas_call | solution.py:342
  1.9 8.8 %collective-permute-start = (bf16[32,64,256]{2,1,0:T(8,128)(2,1)S(1)}, bf16[32,64,256]{2,1,0:T(8,128)(2,1)S(1)}, u32[]{:S(2)}, u32[]{:S(2)}) collective-permute-start(bf16[32,64,256]{2,1,0:T(8,128)(2,1)S(1)} %shard_map.85), channel_id=1, source_target_pairs={{0,64},{64,0},{1,65},{65,1},{2,66},{66,2},{3,67},{67,3},{4,68},{68... | collective-permute-start | bytes 3145736 | tf_op jit(solution)/shard_map/ppermute | solution.py:320
  10.7 2.5 %shard_map.86 = (bf16[16,64,256]{2,1,0:T(8,128)(2,1)S(1)}, s32[8,128]{1,0:T(8,128)S(1)}, bf16[2,64,512]{2,1,0:T(8,128)(2,1)S(1)}, bf16[2,64,512]{2,1,0:T(8,128)(2,1)S(1)}, bf16[2,64,512]{2,1,0:T(8,128)(2,1)S(1)}) custom-call(s32[1]{0:T(128)} %bitcast.core_ref, s32[1]{0:T(128)} %bitcast.1.x_ref, s32[1]{0:T(128)} %bitcast.2.me_ref, s32[1,128]{1,0:T(1,128)} %bitcast.20, ...), custom_call_target="tpu_custom_call" | custom-call | bytes 4000000 | tf_op jit(solution)/shard_map/pallas_call | solution.py:350
  13.2 0.0 collective-permute-done.other
  13.2 1.6 %shard_map.87 = bf16[4,32,8,256]{3,2,1,0:T(8,128)(2,1)} custom-call(s32[8,128]{1,0:T(8,128)S(1)} %get-tuple-element.41.table, bf16[128,8,256]{2,1,0:T(8,128)(2,1)S(1)} %bitcast.14, bf16[256,8,256]{2,1,0:T(8,128)(2,1)S(1)} %bitcast.12), custom_call_target="tpu_custom_call" | custom-call | tf_op jit(solution)/shard_map/pallas_call | solution.py:373
  14.8 3.5 %all-to-all-start = ((bf16[4,32,8,256]{3,2,1,0:T(8,128)(2,1)}), bf16[4,32,8,256]{3,2,1,0:T(8,128)(2,1)S(1)}, u32[]{:S(2)}, u32[]{:S(2)}) async-start(bf16[4,32,8,256]{3,2,1,0:T(8,128)(2,1)} %shard_map.87), calls=%async_computation | async-start | bytes 1048576 | tf_op jit(solution)/shard_map/all_to_all | solution.py:307
  18.3 0.6 shard_map.89
  18.9 4.6 %collective-permute-start.1 = (bf16[2,2,64,512]{3,2,1,0:T(8,128)(2,1)S(1)}, bf16[2,2,64,512]{3,2,1,0:T(8,128)(2,1)S(1)}, u32[]{:S(2)}, u32[]{:S(2)}) collective-permute-start(bf16[2,2,64,512]{3,2,1,0:T(8,128)(2,1)S(1)} %shard_map.89), channel_id=1, source_target_pairs={{0,128},{128,256},{256,384},{384,0},{64,448},{192,64},{320,192},{4... | collective-permute-start | bytes 786440 | tf_op jit(solution)/shard_map/ppermute | solution.py:389
  23.5 4.4 %all-to-all-done.parts = bf16[4,32,8,256]{3,2,1,0:T(8,128)(2,1)S(1)} async-done(((bf16[4,32,8,256]{3,2,1,0:T(8,128)(2,1)}), bf16[4,32,8,256]{3,2,1,0:T(8,128)(2,1)S(1)}, u32[]{:S(2)}, u32[]{:S(2)}) %all-to-all-start) | async-done | bytes 524320 | tf_op jit(solution)/shard_map/all_to_all | solution.py:307
  27.9 1.5 %shard_map.88 = bf16[64,8,256]{2,1,0:T(8,128)(2,1)} custom-call(s32[8,128]{1,0:T(8,128)S(1)} %get-tuple-element.41.table, bf16[4,32,8,256]{3,2,1,0:T(8,128)(2,1)S(1)} %all-to-all-done.parts), custom_call_target="tpu_custom_call" | custom-call | tf_op jit(solution)/shard_map/pallas_call | solution.py:390
  29.4 0.2 collective-permute-done.1.beside
  29.6 13.7 %all-to-all-start.1 = ((bf16[64,8,256]{2,1,0:T(8,128)(2,1)}), bf16[64,8,256]{2,1,0:T(8,128)(2,1)S(1)}, u32[]{:S(2)}, u32[]{:S(2)}) async-start(bf16[64,8,256]{2,1,0:T(8,128)(2,1)} %shard_map.88), calls=%async_computation.1 | async-start | bytes 524288 | tf_op jit(solution)/shard_map/all_to_all | solution.py:307
  43.2 4.1 %collective-permute-start.3 = (bf16[2,64,512]{2,1,0:T(8,128)(2,1)S(1)}, bf16[2,64,512]{2,1,0:T(8,128)(2,1)S(1)}, u32[]{:S(2)}, u32[]{:S(2)}) collective-permute-start(bf16[2,64,512]{2,1,0:T(8,128)(2,1)S(1)} %get-tuple-element.48), channel_id=1, source_target_pairs={{0,256},{128,384},{256,0},{384,128},{1,257},{129,385},{257,1},{385... | collective-permute-start | bytes 393224 | tf_op jit(solution)/shard_map/ppermute | solution.py:316
  47.3 3.2 %collective-permute-done.3.across = bf16[2,64,512]{2,1,0:T(8,128)(2,1)S(1)} collective-permute-done((bf16[2,64,512]{2,1,0:T(8,128)(2,1)S(1)}, bf16[2,64,512]{2,1,0:T(8,128)(2,1)S(1)}, u32[]{:S(2)}, u32[]{:S(2)}) %collective-permute-start.3) | collective-permute-done | bytes 131104 | tf_op jit(solution)/shard_map/ppermute | solution.py:316
  50.5 4.9 %collective-permute-start.4 = (bf16[3,2,64,512]{3,2,1,0:T(8,128)(2,1)S(1)}, bf16[3,2,64,512]{3,2,1,0:T(8,128)(2,1)S(1)}, u32[]{:S(2)}, u32[]{:S(2)}) collective-permute-start(bf16[3,2,64,512]{3,2,1,0:T(8,128)(2,1)S(1)} %shard_map.90), channel_id=1, source_target_pairs={{0,64},{64,0},{1,65},{65,1},{2,66},{66,2},{3,67},{67,3},{4,68},{68... | collective-permute-start | bytes 1179656 | tf_op jit(solution)/shard_map/ppermute | solution.py:320
  55.4 5.9 %all-to-all-done.1 = bf16[64,8,256]{2,1,0:T(8,128)(2,1)S(1)} async-done(((bf16[64,8,256]{2,1,0:T(8,128)(2,1)}), bf16[64,8,256]{2,1,0:T(8,128)(2,1)S(1)}, u32[]{:S(2)}, u32[]{:S(2)}) %all-to-all-start.1) | async-done | bytes 262176 | tf_op jit(solution)/shard_map/all_to_all | solution.py:307
  61.3 5.8 %collective-permute-start.2 = (bf16[512,256]{1,0:T(8,128)(2,1)S(1)}, bf16[512,256]{1,0:T(8,128)(2,1)S(1)}, u32[]{:S(2)}, u32[]{:S(2)}) collective-permute-start(bf16[512,256]{1,0:T(8,128)(2,1)S(1)} %bitcast.15), channel_id=1, source_target_pairs={{0,64},{64,0},{1,65},{65,1},{2,66},{66,2},{3,67},{67,3},{4,68},{68... | collective-permute-start | bytes 786440 | tf_op jit(solution)/shard_map/ppermute | solution.py:320
  67.1 0.0 collective-permute-done.4.others
  67.1 0.7 shard_map.91
  67.8 0.9 shard_map.92
  68.7 0.0 collective-permute-done.2.other
  68.7 2.2 %shard_map.93 = bf16[512,256]{1,0:T(8,128)(2,1)} custom-call(s32[8,128]{1,0:T(8,128)S(1)} %get-tuple-element.41.table, bf16[512,256]{1,0:T(8,128)(2,1)S(1)} %collective-permute-done.2.other, f32[512,512]{1,0:T(8,128)S(1)} %get-tuple-element.50.partial, bf16[8,64,512]{2,1,0:T(8,128)(2,1)S(1)} %get-tuple-element.51.left, ...), custom_call_target="tpu_custom_call" | custom-call | tf_op jit(solution)/shard_map/pallas_call | solution.py:426
  70.9 6.2 %all-to-all-start.2 = ((bf16[64,8,256]{2,1,0:T(8,128)(2,1)}), bf16[64,8,256]{2,1,0:T(8,128)(2,1)S(1)}, u32[]{:S(2)}, u32[]{:S(2)}) async-start(bf16[64,8,256]{2,1,0:T(8,128)(2,1)} %bitcast.8), calls=%async_computation.2 | async-start | bytes 524288 | tf_op jit(solution)/shard_map/all_to_all | solution.py:307
  77.1 1.5 %shard_map.95 = (bf16[2,2,64,512]{3,2,1,0:T(8,128)(2,1)S(1)}, bf16[2,64,512]{2,1,0:T(8,128)(2,1)S(1)}, bf16[2,64,512]{2,1,0:T(8,128)(2,1)S(1)}) custom-call(s32[8,128]{1,0:T(8,128)S(1)} %get-tuple-element.41.table, bf16[512,256]{1,0:T(8,128)(2,1)S(1)} %bitcast.17, bf16[512,256]{1,0:T(8,128)(2,1)S(1)} %collective-permute-done.2.other), custom_call_target="tpu_custom_call" | custom-call | flops 800000000 | bytes 2000000 | tf_op jit(solution)/shard_map/pallas_call | solution.py:434
  78.6 4.0 %collective-permute-start.5 = (bf16[2,2,64,512]{3,2,1,0:T(8,128)(2,1)S(1)}, bf16[2,2,64,512]{3,2,1,0:T(8,128)(2,1)S(1)}, u32[]{:S(2)}, u32[]{:S(2)}) collective-permute-start(bf16[2,2,64,512]{3,2,1,0:T(8,128)(2,1)S(1)} %get-tuple-element.56), channel_id=1, source_target_pairs={{0,128},{128,256},{256,384},{384,0},{64,448},{192,64},{320,192},{4... | collective-permute-start | bytes 786440 | tf_op jit(solution)/shard_map/ppermute | solution.py:442
  82.7 2.5 %collective-permute-start.6 = (bf16[2,64,512]{2,1,0:T(8,128)(2,1)S(1)}, bf16[2,64,512]{2,1,0:T(8,128)(2,1)S(1)}, u32[]{:S(2)}, u32[]{:S(2)}) collective-permute-start(bf16[2,64,512]{2,1,0:T(8,128)(2,1)S(1)} %get-tuple-element.57), channel_id=1, source_target_pairs={{0,256},{128,384},{256,0},{384,128},{1,257},{129,385},{257,1},{385... | collective-permute-start | bytes 393224 | tf_op jit(solution)/shard_map/ppermute | solution.py:316
  85.2 0.9 collective-permute-done.5.beside
  86.1 4.3 %collective-permute-start.7 = (bf16[2,64,512]{2,1,0:T(8,128)(2,1)S(1)}, bf16[2,64,512]{2,1,0:T(8,128)(2,1)S(1)}, u32[]{:S(2)}, u32[]{:S(2)}) collective-permute-start(bf16[2,64,512]{2,1,0:T(8,128)(2,1)S(1)} %dynamic-slice_bitcast_fusion), channel_id=1, source_target_pairs={{0,64},{64,0},{1,65},{65,1},{2,66},{66,2},{3,67},{67,3},{4,68},{68... | collective-permute-start | bytes 393224 | tf_op jit(solution)/shard_map/ppermute | solution.py:320
  90.3 6.9 %all-to-all-done.2.rows = bf16[64,8,256]{2,1,0:T(8,128)(2,1)S(1)} async-done(((bf16[64,8,256]{2,1,0:T(8,128)(2,1)}), bf16[64,8,256]{2,1,0:T(8,128)(2,1)S(1)}, u32[]{:S(2)}, u32[]{:S(2)}) %all-to-all-start.2) | async-done | bytes 262176 | tf_op jit(solution)/shard_map/all_to_all | solution.py:307
  97.2 0.7 shard_map.94
  97.9 0.0 collective-permute-done.6.across
  97.9 0.0 collective-permute-done.7.passed
  97.9 10.4 %all_to_all.20 = bf16[4,32,8,256]{3,2,1,0:T(8,128)(2,1)S(1)} all-to-all(bf16[4,32,8,256]{3,2,1,0:T(8,128)(2,1)S(1)} %shard_map.94), channel_id=1, replica_groups=mesh['x'=4,'core'=2,'y'=4,'z'=16] {'x'}, dimensions={0} | all-to-all | bytes 1048576 | tf_op jit(solution)/shard_map/all_to_all | solution.py:307
  108.3 1.0 shard_map.96.rows
  109.3 0.0 copy-start
  109.3 0.0 copy-start.1
  109.3 5.3 %collective-permute-start.8 = (bf16[128,8,256]{2,1,0:T(8,128)(2,1)S(1)}, bf16[128,8,256]{2,1,0:T(8,128)(2,1)S(1)}, u32[]{:S(2)}, u32[]{:S(2)}) collective-permute-start(bf16[128,8,256]{2,1,0:T(8,128)(2,1)S(1)} %shard_map.96.rows), channel_id=1, source_target_pairs={{0,64},{64,0},{1,65},{65,1},{2,66},{66,2},{3,67},{67,3},{4,68},{68... | collective-permute-start | bytes 1572872 | tf_op jit(solution)/shard_map/ppermute | solution.py:320
  114.6 0.8 shard_map.97.begun
  115.5 0.0 copy-done
  115.5 0.0 copy-done.1
  115.5 1.7 %shard_map.99 = (f32[4,64,512]{2,1,0:T(8,128)}, f32[4,64,512]{2,1,0:T(8,128)}) custom-call(s32[8,128]{1,0:T(8,128)S(1)} %get-tuple-element.41.table, bf16[2,64,512]{2,1,0:T(8,128)(2,1)S(1)} %get-tuple-element.63.mine, bf16[2,64,512]{2,1,0:T(8,128)(2,1)S(1)} %collective-permute-done.6.across, bf16[2,2,64,512]{3,2,1,0:T(8,128)(2,1)S(1)} %collective-permute-done.5.beside, ...), custom_call_target="tpu_custom_call" | custom-call | flops 10000000 | bytes 5000000 | tf_op jit(solution)/shard_map/pallas_call | solution.py:453
  117.2 0.0 collective-permute-done.8.rows
  117.2 0.8 shard_map.98
  (2 shorter events, 0.0 us)
Async XLA Ops:
  1.9 11.3 %collective-permute-start = (bf16[32,64,256]{2,1,0:T(8,128)(2,1)S(1)}, bf16[32,64,256]{2,1,0:T(8,128)(2,1)S(1)}, u32[]{:S(2)}, u32[]{:S(2)}) collective-permute-start(bf16[32,64,256]{2,1,0:T(8,128)(2,1)S(1)} %shard_map.85), channel_id=1, source_target_pairs={{0,64},{64,0},{1,65},{65,1},{2,66},{66,2},{3,67},{67,3},{4,68},{68... | collective-permute-start | bytes 3145736 | tf_op jit(solution)/shard_map/ppermute | solution.py:320
  14.8 13.1 %all-to-all-start = ((bf16[4,32,8,256]{3,2,1,0:T(8,128)(2,1)}), bf16[4,32,8,256]{3,2,1,0:T(8,128)(2,1)S(1)}, u32[]{:S(2)}, u32[]{:S(2)}) async-start(bf16[4,32,8,256]{3,2,1,0:T(8,128)(2,1)} %shard_map.87), calls=%async_computation | async-start | bytes 1048576 | tf_op jit(solution)/shard_map/all_to_all | solution.py:307
  18.9 10.7 %collective-permute-start.1 = (bf16[2,2,64,512]{3,2,1,0:T(8,128)(2,1)S(1)}, bf16[2,2,64,512]{3,2,1,0:T(8,128)(2,1)S(1)}, u32[]{:S(2)}, u32[]{:S(2)}) collective-permute-start(bf16[2,2,64,512]{3,2,1,0:T(8,128)(2,1)S(1)} %shard_map.89), channel_id=1, source_target_pairs={{0,128},{128,256},{256,384},{384,0},{64,448},{192,64},{320,192},{4... | collective-permute-start | bytes 786440 | tf_op jit(solution)/shard_map/ppermute | solution.py:389
  29.6 31.7 %all-to-all-start.1 = ((bf16[64,8,256]{2,1,0:T(8,128)(2,1)}), bf16[64,8,256]{2,1,0:T(8,128)(2,1)S(1)}, u32[]{:S(2)}, u32[]{:S(2)}) async-start(bf16[64,8,256]{2,1,0:T(8,128)(2,1)} %shard_map.88), calls=%async_computation.1 | async-start | bytes 524288 | tf_op jit(solution)/shard_map/all_to_all | solution.py:307
  43.2 7.2 %collective-permute-start.3 = (bf16[2,64,512]{2,1,0:T(8,128)(2,1)S(1)}, bf16[2,64,512]{2,1,0:T(8,128)(2,1)S(1)}, u32[]{:S(2)}, u32[]{:S(2)}) collective-permute-start(bf16[2,64,512]{2,1,0:T(8,128)(2,1)S(1)} %get-tuple-element.48), channel_id=1, source_target_pairs={{0,256},{128,384},{256,0},{384,128},{1,257},{129,385},{257,1},{385... | collective-permute-start | bytes 393224 | tf_op jit(solution)/shard_map/ppermute | solution.py:316
  50.5 16.6 %collective-permute-start.4 = (bf16[3,2,64,512]{3,2,1,0:T(8,128)(2,1)S(1)}, bf16[3,2,64,512]{3,2,1,0:T(8,128)(2,1)S(1)}, u32[]{:S(2)}, u32[]{:S(2)}) collective-permute-start(bf16[3,2,64,512]{3,2,1,0:T(8,128)(2,1)S(1)} %shard_map.90), channel_id=1, source_target_pairs={{0,64},{64,0},{1,65},{65,1},{2,66},{66,2},{3,67},{67,3},{4,68},{68... | collective-permute-start | bytes 1179656 | tf_op jit(solution)/shard_map/ppermute | solution.py:320
  61.3 7.4 %collective-permute-start.2 = (bf16[512,256]{1,0:T(8,128)(2,1)S(1)}, bf16[512,256]{1,0:T(8,128)(2,1)S(1)}, u32[]{:S(2)}, u32[]{:S(2)}) collective-permute-start(bf16[512,256]{1,0:T(8,128)(2,1)S(1)} %bitcast.15), channel_id=1, source_target_pairs={{0,64},{64,0},{1,65},{65,1},{2,66},{66,2},{3,67},{67,3},{4,68},{68... | collective-permute-start | bytes 786440 | tf_op jit(solution)/shard_map/ppermute | solution.py:320
  70.9 26.3 %all-to-all-start.2 = ((bf16[64,8,256]{2,1,0:T(8,128)(2,1)}), bf16[64,8,256]{2,1,0:T(8,128)(2,1)S(1)}, u32[]{:S(2)}, u32[]{:S(2)}) async-start(bf16[64,8,256]{2,1,0:T(8,128)(2,1)} %bitcast.8), calls=%async_computation.2 | async-start | bytes 524288 | tf_op jit(solution)/shard_map/all_to_all | solution.py:307
  78.6 7.4 %collective-permute-start.5 = (bf16[2,2,64,512]{3,2,1,0:T(8,128)(2,1)S(1)}, bf16[2,2,64,512]{3,2,1,0:T(8,128)(2,1)S(1)}, u32[]{:S(2)}, u32[]{:S(2)}) collective-permute-start(bf16[2,2,64,512]{3,2,1,0:T(8,128)(2,1)S(1)} %get-tuple-element.56), channel_id=1, source_target_pairs={{0,128},{128,256},{256,384},{384,0},{64,448},{192,64},{320,192},{4... | collective-permute-start | bytes 786440 | tf_op jit(solution)/shard_map/ppermute | solution.py:442
  82.7 15.3 %collective-permute-start.6 = (bf16[2,64,512]{2,1,0:T(8,128)(2,1)S(1)}, bf16[2,64,512]{2,1,0:T(8,128)(2,1)S(1)}, u32[]{:S(2)}, u32[]{:S(2)}) collective-permute-start(bf16[2,64,512]{2,1,0:T(8,128)(2,1)S(1)} %get-tuple-element.57), channel_id=1, source_target_pairs={{0,256},{128,384},{256,0},{384,128},{1,257},{129,385},{257,1},{385... | collective-permute-start | bytes 393224 | tf_op jit(solution)/shard_map/ppermute | solution.py:316
  86.1 11.9 %collective-permute-start.7 = (bf16[2,64,512]{2,1,0:T(8,128)(2,1)S(1)}, bf16[2,64,512]{2,1,0:T(8,128)(2,1)S(1)}, u32[]{:S(2)}, u32[]{:S(2)}) collective-permute-start(bf16[2,64,512]{2,1,0:T(8,128)(2,1)S(1)} %dynamic-slice_bitcast_fusion), channel_id=1, source_target_pairs={{0,64},{64,0},{1,65},{65,1},{2,66},{66,2},{3,67},{67,3},{4,68},{68... | collective-permute-start | bytes 393224 | tf_op jit(solution)/shard_map/ppermute | solution.py:320
  109.3 6.1 %copy-start = (f32[4,64,512]{2,1,0:T(8,128)S(1)}, f32[4,64,512]{2,1,0:T(8,128)}, u32[]{:S(2)}) copy-start(f32[4,64,512]{2,1,0:T(8,128)} %left.1) | copy-start | bytes 1572868
  109.3 6.1 %copy-start.1 = (f32[4,64,512]{2,1,0:T(8,128)S(1)}, f32[4,64,512]{2,1,0:T(8,128)}, u32[]{:S(2)}) copy-start(f32[4,64,512]{2,1,0:T(8,128)} %right.1) | copy-start | bytes 1572868
  109.3 7.8 %collective-permute-start.8 = (bf16[128,8,256]{2,1,0:T(8,128)(2,1)S(1)}, bf16[128,8,256]{2,1,0:T(8,128)(2,1)S(1)}, u32[]{:S(2)}, u32[]{:S(2)}) collective-permute-start(bf16[128,8,256]{2,1,0:T(8,128)(2,1)S(1)} %shard_map.96.rows), channel_id=1, source_target_pairs={{0,64},{64,0},{1,65},{65,1},{2,66},{66,2},{3,67},{67,3},{4,68},{68... | collective-permute-start | bytes 1572872 | tf_op jit(solution)/shard_map/ppermute | solution.py:320

commit v10 on v9

--- a/solution.py
+++ b/solution.py
@@ -21,10 +21,7 @@
     return lax.dot_general(a, b, (dims, ((), ())), preferred_element_type=F32)
 
 
-ORDER, SOURCE, PLACE, OWNER, SLOT, FULL, CHIP, WHERE = range(8)
-
-
-def fill_table(slots, core, x, me, capacity, chips, first, first_done, table):
+def fill_tables(slots, x, me, capacity, chips, order, source, place, owned, slot_of, chip_of, slot_done):
     blocks = slots.shape[1]
     square = (blocks, blocks)
     cap_bits, chip_bits = capacity.bit_length() - 1, chips.bit_length() - 1
@@ -42,25 +39,20 @@
     chip = rank & (chips - 1)
     spot = rank >> chip_bits
     owner = slot >> cap_bits
-    first[...] = total((owner == me) & (chip == lane), slot & (capacity - 1))
-    first_done()
-    local_slot = slot == me * capacity + lane
-    table[pl.ds(ORDER, 1)] = total(rank == lane, sublane)
-    table[pl.ds(SOURCE, 1)] = (rank_row & (chips - 1)) * depth + (rank_row >> chip_bits)
-    table[pl.ds(PLACE, 1)] = total((chip == x) & (owner == lane), spot - depth) + depth
-    table[pl.ds(OWNER, 1)] = total((chip == x) & (spot == lane), owner)
-    table[pl.ds(SLOT, 1)] = first[...]
-    table[pl.ds(FULL, 1)] = total(local_slot, 1)
-    table[pl.ds(CHIP, 1)] = total(local_slot, chip)
-    row = lax.broadcasted_iota(jnp.int32, (1, blocks), 1)
-    table[pl.ds(WHERE, 1)] = jnp.where(row == 0, core, x)
-
-
-def send_kernel(core_ref, grads, left_root, right_root, sent, sems):
+    slot_of[...] = total((owner == me) & (chip == lane), slot & (capacity - 1))
+    slot_done()
+    order[...] = total(rank == lane, sublane)
+    source[...] = (rank_row & (chips - 1)) * depth + (rank_row >> chip_bits)
+    place[...] = total((chip == x) & (owner == lane), spot - depth) + depth
+    owned[...] = total((chip == x) & (spot == lane), owner)
+    chip_of[...] = total(slot == me * capacity + lane, chip + 1) - 1
+
+
+def send_kernel(grads, left_root, right_root, sent, sems):
     width = sent.shape[2]
     groups = grads.shape[0]
     capacity = left_root.shape[0]
-    far = pl.ds(pl.multiple_of((1 - core_ref[0]) * width, 128), width)
+    far = pl.ds(pl.multiple_of((1 - lax.axis_index("core")) * width, 128), width)
     loads = [pltpu.make_async_copy(grads.at[:, :, far], sent.at[pl.ds(0, groups)], sems.at[0])]
     for i in range(4):
         root = (left_root, right_root)[i // 2].at[:, :, pl.ds(i % 2 * width, width)]
@@ -71,20 +63,20 @@
         load.wait()
 
 
-def keep_kernel(
-    core_ref, x_ref, me_ref, slots_hbm, grads, left_root, right_root, kept, table, beside, mine, across, slots, first, scalars, sems, root_sems
-):
-    core, x = core_ref[0], x_ref[0]
+def keep_kernel(slots_hbm, grads, left_root, right_root, kept, beside, mine, across, *refs):
+    tables, (slots, scalars, sems, root_sems) = refs[:6], refs[6:]
+    core, x = lax.axis_index("core"), lax.axis_index("x")
+    me = lax.axis_index("y") * lax.axis_size("z") + lax.axis_index("z")
     width = kept.shape[2]
     near = pl.ds(pl.multiple_of(core * width, 128), width)
     slots_load = pltpu.make_async_copy(slots_hbm, slots, sems.at[0])
     load = pltpu.make_async_copy(grads.at[:, :, near], kept, sems.at[1])
-    first_load = pltpu.make_async_copy(first, scalars, sems.at[2])
+    slot_load = pltpu.make_async_copy(tables[4], scalars, sems.at[2])
     slots_load.start()
     load.start()
     slots_load.wait()
-    fill_table(slots, core, x, me_ref[0], left_root.shape[0], 4, first, first_load.start, table)
-    first_load.wait()
+    fill_tables(slots, x, me, left_root.shape[0], 4, *tables, slot_load.start)
+    slot_load.wait()
     loads = [load]
     for i, (chip, out) in enumerate(((x + 1 + 2 * core, beside), (x, mine), (x + 2, across))):
         slot = scalars[0, lax.rem(chip, 4)]
@@ -101,9 +93,9 @@
         out[:, h * width : (h + 1) * width] = other[groups + (2 * side + h) * capacity + slot]
 
 
-def pair_roots_kernel(groups, capacity, table, other, beside, out):
-    core, x = table[WHERE, 0], table[WHERE, 1]
-    slot = table[SLOT, lax.rem(x + 1 + 2 * core, 4)]
+def pair_roots_kernel(groups, capacity, slot_of, other, beside, out):
+    core, x = lax.axis_index("core"), lax.axis_index("x")
+    slot = slot_of[0, lax.rem(x + 1 + 2 * core, 4)]
     out[core] = beside[...]
     for side in range(2):
         from_other(groups, capacity, other, slot, side, out.at[1 - core, side])
@@ -114,12 +106,12 @@
     out[2] = across[...]
 
 
-def merge_roots_kernel(groups, capacity, table, other, mine, beside, across, others, left, right):
-    core, x = table[WHERE, 0], table[WHERE, 1]
+def merge_roots_kernel(groups, capacity, slot_of, other, mine, beside, across, others, left, right):
+    core, x = lax.axis_index("core"), lax.axis_index("x")
     near, far, opposite = lax.rem(x + 3 - 2 * core, 4), lax.rem(x + 1 + 2 * core, 4), lax.rem(x + 2, 4)
     for side, out in enumerate((left, right)):
         out[2 * x + core] = mine[side]
-        from_other(groups, capacity, other, table[SLOT, x], side, out.at[2 * x + 1 - core])
+        from_other(groups, capacity, other, slot_of[0, x], side, out.at[2 * x + 1 - core])
         for parity in range(2):
             out[2 * near + parity] = beside[parity, side]
             out[2 * far + parity] = others[parity, side]
@@ -127,12 +119,12 @@
         out[2 * opposite + 1 - core] = others[2, side]
 
 
-def pair_sum_kernel(table, own, other, out):
+def pair_sum_kernel(order, own, other, out):
     chips, depth = out.shape[:2]
 
     def body(i, carry):
         for x in range(chips):
-            block = table[ORDER, i * chips + x]
+            block = order[0, i * chips + x]
             out[x, i] = own[block] + other[block]
         return carry
 
@@ -152,9 +144,9 @@
         store.wait()
 
 
-def chip_sum_kernel(table, parts, out, total, place, sem):
+def chip_sum_kernel(place_vmem, parts, out, total, place, sem):
     depth = parts.shape[1]
-    load = pltpu.make_async_copy(table, place, sem)
+    load = pltpu.make_async_copy(place_vmem, place, sem)
     load.start()
     acc = parts[0].astype(F32)
     for x in range(1, parts.shape[0]):
@@ -164,14 +156,14 @@
     load.wait()
 
     def body(o, carry):
-        out[o] = total[place[PLACE, o]]
+        out[o] = total[place[0, o]]
         return carry
 
     lax.fori_loop(0, out.shape[0], body, 0, unroll=8)
 
 
-def near_kernel(table, own, right, partial, grad_sq):
-    core = table[WHERE, 0]
+def near_kernel(own, right, partial, grad_sq):
+    core = lax.axis_index("core")
     half = own.shape[1]
     groups = right.shape[0] // 2
     grad = own[...]
@@ -180,8 +172,8 @@
     partial[...] = dot(grad, upper, ((1,), (0,)))
 
 
-def direction_kernel(table, other, partial, left, right, grad_sq_near, out):
-    core = table[WHERE, 0]
+def direction_kernel(other, partial, left, right, grad_sq_near, out):
+    core = lax.axis_index("core")
     half = other.shape[1]
     groups = right.shape[0] // 2
     size = 2 * half
@@ -202,8 +194,8 @@
     out[...] = (-near * ratio).astype(BF16)
 
 
-def terms_kernel(table, own, other, beside, across, mine, grad):
-    core, x = table[WHERE, 0], table[WHERE, 1]
+def terms_kernel(own, other, beside, across, mine, grad):
+    core, x = lax.axis_index("core"), lax.axis_index("x")
     half = own.shape[1]
     rows = mine.shape[1]
     grad[:, pl.ds(pl.multiple_of(core * half, 128), half)] = own[...]
@@ -222,12 +214,12 @@
             out[side] = jnp.where(core == 0, term[:rows], term[rows:]).astype(BF16)
 
 
-def stats_kernel(table, mine, across, beside, passed, left, right, left_hbm, right_hbm, left_out, right_out, sems):
-    core, x = table[WHERE, 0], table[WHERE, 1]
+def stats_kernel(chip_of, mine, across, beside, passed, left, right, left_hbm, right_hbm, left_out, right_out, sems):
+    core, x = lax.axis_index("core"), lax.axis_index("x")
     stores = []
     for j in range(left.shape[0]):
-        full = table[FULL, j] > 0
-        way = lax.rem(table[CHIP, j] + 4 - x, 4)
+        full = chip_of[0, j] >= 0
+        way = lax.rem(chip_of[0, j] + 4 - x, 4)
 
         def add(here, term):
             @pl.when(jnp.logical_and(full, here))
@@ -252,9 +244,9 @@
         store.wait()
 
 
-def compact_kernel(table, rows, out):
+def compact_kernel(owned, rows, out):
     def body(i, carry):
-        block = rows[table[OWNER, i]]
+        block = rows[owned[0, i]]
         for x in range(out.shape[0]):
             out[x, i] = block
         return carry
@@ -262,9 +254,9 @@
     lax.fori_loop(0, out.shape[1], body, 0, unroll=8)
 
 
-def order_kernel(table, rows, out):
+def order_kernel(source, rows, out):
     def body(b, carry):
-        out[b] = rows[table[SOURCE, b]]
+        out[b] = rows[source[0, b]]
         return carry
 
     lax.fori_loop(0, out.shape[0], body, 0, unroll=8)
@@ -277,13 +269,13 @@
     store.wait()
 
 
-def place_near_kernel(core_ref, rows, out_hbm, sem):
-    place_half(core_ref[0], rows, out_hbm, sem)
-
-
-def place_far_kernel(core_ref, rows, begun, out_hbm, sem):
+def place_near_kernel(rows, out_hbm, sem):
+    place_half(lax.axis_index("core"), rows, out_hbm, sem)
+
+
+def place_far_kernel(rows, begun, out_hbm, sem):
     del begun
-    place_half(1 - core_ref[0], rows, out_hbm, sem)
+    place_half(1 - lax.axis_index("core"), rows, out_hbm, sem)
 
 
 def call(kernel, out_shape, in_specs, scratch=(), out_specs=None, cost=None, aliases=None):
@@ -342,48 +334,40 @@
     sent = call(
         send_kernel,
         jax.ShapeDtypeStruct((grad_groups + 4 * capacity, stat_rows, half), BF16),
-        [SMEM_SPEC] + [HBM_SPEC] * 3,
+        [HBM_SPEC] * 3,
         [pltpu.SemaphoreType.DMA((5,))],
-    )(core.reshape(1), grads, left_root, right_root)
+    )(grads, left_root, right_root)
     sent, late_grads = lax.optimization_barrier((sent, grads))
     other = swap_cores(sent)
-    kept, table, beside, mine, across = call(
+    kept, beside, mine, across, order, source, place, owned, slot_of, chip_of = call(
         keep_kernel,
-        [jax.ShapeDtypeStruct((grad_groups, stat_rows, half), BF16), jax.ShapeDtypeStruct((8, blocks), jnp.int32)]
-        + [piece] * 3,
-        [SMEM_SPEC] * 3 + [HBM_SPEC] * 4,
+        [jax.ShapeDtypeStruct((grad_groups, stat_rows, half), BF16)]
+        + [piece] * 3
+        + [jax.ShapeDtypeStruct((1, blocks), jnp.int32)] * 6,
+        [HBM_SPEC] * 4,
         [
-            pltpu.VMEM((1, blocks), jnp.int32),
             pltpu.VMEM((1, blocks), jnp.int32),
             pltpu.SMEM((1, blocks), jnp.int32),
             pltpu.SemaphoreType.DMA((3,)),
             pltpu.SemaphoreType.DMA((3, 2)),
         ],
         cost=(0, 4_000_000),
-    )(
-        core.reshape(1),
-        x.reshape(1),
-        me.reshape(1),
-        in_hbm(block_slot.reshape(1, blocks)),
-        in_hbm(late_grads),
-        left_root,
-        right_root,
-    )
+    )(in_hbm(block_slot.reshape(1, blocks)), in_hbm(late_grads), left_root, right_root)
 
     parts = call(
         pair_sum_kernel,
         jax.ShapeDtypeStruct((chips, depth, shard_rows, half), BF16),
         [SMEM_SPEC, VMEM_SPEC, VMEM_SPEC],
-    )(table, kept.reshape(-1, shard_rows, half), other.reshape(-1, shard_rows, half))
+    )(order, kept.reshape(-1, shard_rows, half), other.reshape(-1, shard_rows, half))
     both = jax.ShapeDtypeStruct((2, 2, stat_rows, width), BF16)
-    parts, late_table = lax.optimization_barrier((parts, table))
+    parts, late_slot_of = lax.optimization_barrier((parts, slot_of))
     parts = exchange(parts, "x")
     beside = call(
         functools.partial(pair_roots_kernel, grad_groups, capacity),
         both,
         [SMEM_SPEC, VMEM_SPEC, VMEM_SPEC],
         cost=(0, 1000),
-    )(late_table, other, beside)
+    )(late_slot_of, other, beside)
     ways = [(2 * i, 2 * ((i + 1) % chips)) for i in range(chips)]
     ways += [(2 * i + 1, 2 * ((i - 1) % chips) + 1) for i in range(chips)]
     beside = lax.ppermute(beside, ("x", "core"), ways)
@@ -393,10 +377,10 @@
         [VMEM_SPEC, VMEM_SPEC],
         [
             pltpu.VMEM((depth + 1, shard_rows, half), BF16),
-            pltpu.SMEM((8, blocks), jnp.int32),
+            pltpu.SMEM((1, blocks), jnp.int32),
             pltpu.SemaphoreType.DMA,
         ],
-    )(table, parts)
+    )(place, parts)
 
     outgoing, late_other, beside, across = lax.optimization_barrier((outgoing, other, beside, across))
     own = exchange(outgoing, ("y", "z"))
@@ -413,38 +397,38 @@
         [jax.ShapeDtypeStruct((groups, stat_rows, width), BF16)] * 2,
         [SMEM_SPEC] + [VMEM_SPEC] * 5,
         cost=(0, 2_000_000),
-    )(table, late_other, mine, beside, across, others)
+    )(slot_of, late_other, mine, beside, across, others)
 
     own = own.reshape(width, half)
     far = swap_cores(own)
     partial, grad_sq = call(
         near_kernel,
         [jax.ShapeDtypeStruct((width, width), F32), jax.ShapeDtypeStruct((8, 128), F32)],
-        [SMEM_SPEC, VMEM_SPEC, VMEM_SPEC],
+        [VMEM_SPEC, VMEM_SPEC],
         cost=(270_000_000, 4_000_000),
-    )(table, own, right)
+    )(own, right)
     update = call(
         direction_kernel,
         jax.ShapeDtypeStruct((width, half), BF16),
-        [SMEM_SPEC] + [VMEM_SPEC] * 5,
-    )(table, far, partial, left, right, grad_sq)
+        [VMEM_SPEC] * 5,
+    )(far, partial, left, right, grad_sq)
 
     update, own, far = lax.optimization_barrier((update, own, far))
     rows = exchange(update.reshape(owners, shard_rows, half), ("y", "z"))
     beside, across, mine = call(
         terms_kernel,
         [both, piece, piece],
-        [SMEM_SPEC, VMEM_SPEC, VMEM_SPEC],
+        [VMEM_SPEC, VMEM_SPEC],
         [pltpu.VMEM((width, width), BF16)],
         cost=(800_000_000, 2_000_000),
-    )(table, own, far)
+    )(own, far)
     across = turn(across, 2)
     beside = lax.ppermute(beside, ("x", "core"), ways)
     packed = call(
         compact_kernel,
         jax.ShapeDtypeStruct((chips, depth, shard_rows, half), BF16),
         [SMEM_SPEC, VMEM_SPEC],
-    )(table, rows)
+    )(owned, rows)
     passed = swap_cores(lax.dynamic_index_in_dim(beside, 1 - core, keepdims=False))
     packed, beside, across, passed = lax.optimization_barrier((packed, beside, across, passed))
     near = exchange(packed, "x").reshape(blocks, shard_rows, half)
@@ -461,26 +445,26 @@
         ],
         [HBM_SPEC, HBM_SPEC],
         cost=(10_000_000, 5_000_000),
-    )(table, mine, across, beside, passed, left_stat, right_stat)
-    near = call(order_kernel, half_rows, [SMEM_SPEC, VMEM_SPEC])(table, near)
+    )(chip_of, mine, across, beside, passed, left_stat, right_stat)
+    near = call(order_kernel, half_rows, [SMEM_SPEC, VMEM_SPEC])(source, near)
     beyond = swap_cores(near)
     whole_rows = jax.ShapeDtypeStruct((blocks, shard_rows, width), BF16)
     begun = call(
         place_near_kernel,
         whole_rows,
-        [SMEM_SPEC, VMEM_SPEC],
+        [VMEM_SPEC],
         [pltpu.SemaphoreType.DMA],
         HBM_SPEC,
         cost=(0, 4_000_000),
-    )(core.reshape(1), near)
+    )(near)
     result = call(
         place_far_kernel,
         whole_rows,
-        [SMEM_SPEC, VMEM_SPEC, HBM_SPEC],
+        [VMEM_SPEC, HBM_SPEC],
         [pltpu.SemaphoreType.DMA],
         HBM_SPEC,
-        aliases={2: 0},
-    )(core.reshape(1), beyond, begun)
+        aliases={1: 0},
+    )(beyond, begun)
     return (result, left_new, right_new)
 
 

time: 119 us -> 117 us (0.983)
  Pallas kernels: 17.8 us -> 15.3 us
    pallas_call x5, Pallas kernels: 6.33 us -> 4.88 us  [the longest x1 1.6 us: local(): call(direction_kernel, jax.ShapeDtypeStruct((width, half), BF16), [VMEM_S...]
  transfers between devices with their start and end apart: 12 -> 12, of which waited for: 6 -> 7; matrix products, arithmetic and copies ran while one was open for 0% -> 0% of each run, Pallas kernels for 9% -> 8%
where the time goes in v10:
time: 117 us; the launch traced here: 116 us
  starting transfers between devices  68.1 us (58%)
  waiting for transfers between devices  21.8 us (19%)
  Pallas kernels  15.3 us (13%)
  blocking collectives  10.1 us (9%)
    ppermute x5, starting transfers between devices, swap_cores(): return lax.ppermute(value, 'core', [(0, 1), (1, 0)])  29.7 us
    all_to_all x3, starting transfers between devices, exchange(): return lax.all_to_all(value, axis, 0, 0, tiled=True)  23.3 us
    all_to_all x3, waiting for transfers between devices, exchange(): return lax.all_to_all(value, axis, 0, 0, tiled=True)  17.2 us
    all_to_all x1, blocking collectives, exchange(): return lax.all_to_all(value, axis, 0, 0, tiled=True)  10.1 us
    ppermute x2, starting transfers between devices, local(): beside = lax.ppermute(beside, ('x', 'core'), ways)  8.55 us
    ppermute x2, starting transfers between devices, turn(): lax.ppermute(value, 'x', [(i, (i + k) % chips) for i in range(chips)])  6.56 us
    ppermute x2, waiting for transfers between devices, turn(): lax.ppermute(value, 'x', [(i, (i + k) % chips) for i in range(chips)])  3.16 us
    pallas_call x1, Pallas kernels, local(): call(keep_kernel, [jax.ShapeDtypeStruct((grad_groups, stat_rows, half), B...  2.52 us
  transfers between devices with their start and end apart: 12, of which 7 were waited for; matrix products, arithmetic and copies ran while one was open for 0% of the time, Pallas kernels for 8%

profile of v10, /device:TPU:1, one launch (start us, length us, event | category | flops | bytes accessed | tf_op | source)
XLA Modules:
  0.0 116.2 jit_solution(14116760719480613449)
XLA Ops:
  0.6 1.2 %shard_map.85 = bf16[32,64,256]{2,1,0:T(8,128)(2,1)S(1)} custom-call(bf16[16,64,512]{2,1,0:T(8,128)(2,1)} %bitcast.15, bf16[4,64,512]{2,1,0:T(8,128)(2,1)} %left_root.3, bf16[4,64,512]{2,1,0:T(8,128)(2,1)} %right_root.3), custom_call_target="tpu_custom_call" | custom-call | tf_op jit(solution)/shard_map/pallas_call | solution.py:334
  1.9 8.8 %collective-permute-start = (bf16[32,64,256]{2,1,0:T(8,128)(2,1)S(1)}, bf16[32,64,256]{2,1,0:T(8,128)(2,1)S(1)}, u32[]{:S(2)}, u32[]{:S(2)}) collective-permute-start(bf16[32,64,256]{2,1,0:T(8,128)(2,1)S(1)} %shard_map.85), channel_id=1, source_target_pairs={{0,64},{64,0},{1,65},{65,1},{2,66},{66,2},{3,67},{67,3},{4,68},{68... | collective-permute-start | bytes 3145736 | tf_op jit(solution)/shard_map/ppermute | solution.py:312
  10.7 2.5 %shard_map.86 = (bf16[16,64,256]{2,1,0:T(8,128)(2,1)S(1)}, bf16[2,64,512]{2,1,0:T(8,128)(2,1)S(1)}, bf16[2,64,512]{2,1,0:T(8,128)(2,1)S(1)}, bf16[2,64,512]{2,1,...) custom-call(s32[1,128]{1,0:T(1,128)} %bitcast.17, ...), custom_call_target="tpu_custom_call" | custom-call | bytes 4000000 | tf_op jit(solution)/shard_map/pallas_call | solution.py:342
  13.2 0.0 collective-permute-done.other
  13.2 1.5 %shard_map.87 = bf16[4,32,8,256]{3,2,1,0:T(8,128)(2,1)} custom-call(s32[1,128]{1,0:T(1,128)S(1)} %get-tuple-element.45.order, bf16[128,8,256]{2,1,0:T(8,128)(2,1)S(1)} %bitcast.11, bf16[256,8,256]{2,1,0:T(8,128)(2,1)S(1)} %bitcast.9), custom_call_target="tpu_custom_call" | custom-call | tf_op jit(solution)/shard_map/pallas_call | solution.py:357
  14.7 3.5 %all-to-all-start = ((bf16[4,32,8,256]{3,2,1,0:T(8,128)(2,1)}), bf16[4,32,8,256]{3,2,1,0:T(8,128)(2,1)S(1)}, u32[]{:S(2)}, u32[]{:S(2)}) async-start(bf16[4,32,8,256]{3,2,1,0:T(8,128)(2,1)} %shard_map.87), calls=%async_computation | async-start | bytes 1048576 | tf_op jit(solution)/shard_map/all_to_all | solution.py:299
  18.2 0.6 shard_map.89
  18.8 4.6 %collective-permute-start.1 = (bf16[2,2,64,512]{3,2,1,0:T(8,128)(2,1)S(1)}, bf16[2,2,64,512]{3,2,1,0:T(8,128)(2,1)S(1)}, u32[]{:S(2)}, u32[]{:S(2)}) collective-permute-start(bf16[2,2,64,512]{3,2,1,0:T(8,128)(2,1)S(1)} %shard_map.89), channel_id=1, source_target_pairs={{0,128},{128,256},{256,384},{384,0},{64,448},{192,64},{320,192},{4... | collective-permute-start | bytes 786440 | tf_op jit(solution)/shard_map/ppermute | solution.py:373
  23.4 4.4 %all-to-all-done.parts = bf16[4,32,8,256]{3,2,1,0:T(8,128)(2,1)S(1)} async-done(((bf16[4,32,8,256]{3,2,1,0:T(8,128)(2,1)}), bf16[4,32,8,256]{3,2,1,0:T(8,128)(2,1)S(1)}, u32[]{:S(2)}, u32[]{:S(2)}) %all-to-all-start) | async-done | bytes 524320 | tf_op jit(solution)/shard_map/all_to_all | solution.py:299
  27.8 1.4 %shard_map.88 = bf16[64,8,256]{2,1,0:T(8,128)(2,1)} custom-call(s32[1,128]{1,0:T(1,128)S(1)} %get-tuple-element.44.place_vmem, bf16[4,32,8,256]{3,2,1,0:T(8,128)(2,1)S(1)} %all-to-all-done.parts), custom_call_target="tpu_custom_call" | custom-call | tf_op jit(solution)/shard_map/pallas_call | solution.py:374
  29.2 0.4 collective-permute-done.1.beside
  29.5 13.6 %all-to-all-start.1 = ((bf16[64,8,256]{2,1,0:T(8,128)(2,1)}), bf16[64,8,256]{2,1,0:T(8,128)(2,1)S(1)}, u32[]{:S(2)}, u32[]{:S(2)}) async-start(bf16[64,8,256]{2,1,0:T(8,128)(2,1)} %shard_map.88), calls=%async_computation.1 | async-start | bytes 524288 | tf_op jit(solution)/shard_map/all_to_all | solution.py:299
  43.2 4.1 %collective-permute-start.3 = (bf16[2,64,512]{2,1,0:T(8,128)(2,1)S(1)}, bf16[2,64,512]{2,1,0:T(8,128)(2,1)S(1)}, u32[]{:S(2)}, u32[]{:S(2)}) collective-permute-start(bf16[2,64,512]{2,1,0:T(8,128)(2,1)S(1)} %get-tuple-element.57), channel_id=1, source_target_pairs={{0,256},{128,384},{256,0},{384,128},{1,257},{129,385},{257,1},{385... | collective-permute-start | bytes 393224 | tf_op jit(solution)/shard_map/ppermute | solution.py:308
  47.3 3.2 %collective-permute-done.3.across = bf16[2,64,512]{2,1,0:T(8,128)(2,1)S(1)} collective-permute-done((bf16[2,64,512]{2,1,0:T(8,128)(2,1)S(1)}, bf16[2,64,512]{2,1,0:T(8,128)(2,1)S(1)}, u32[]{:S(2)}, u32[]{:S(2)}) %collective-permute-start.3) | collective-permute-done | bytes 131104 | tf_op jit(solution)/shard_map/ppermute | solution.py:308
  50.4 4.9 %collective-permute-start.4 = (bf16[3,2,64,512]{3,2,1,0:T(8,128)(2,1)S(1)}, bf16[3,2,64,512]{3,2,1,0:T(8,128)(2,1)S(1)}, u32[]{:S(2)}, u32[]{:S(2)}) collective-permute-start(bf16[3,2,64,512]{3,2,1,0:T(8,128)(2,1)S(1)} %shard_map.90), channel_id=1, source_target_pairs={{0,64},{64,0},{1,65},{65,1},{2,66},{66,2},{3,67},{67,3},{4,68},{68... | collective-permute-start | bytes 1179656 | tf_op jit(solution)/shard_map/ppermute | solution.py:312
  55.4 5.9 %all-to-all-done.1 = bf16[64,8,256]{2,1,0:T(8,128)(2,1)S(1)} async-done(((bf16[64,8,256]{2,1,0:T(8,128)(2,1)}), bf16[64,8,256]{2,1,0:T(8,128)(2,1)S(1)}, u32[]{:S(2)}, u32[]{:S(2)}) %all-to-all-start.1) | async-done | bytes 262176 | tf_op jit(solution)/shard_map/all_to_all | solution.py:299
  61.3 5.8 %collective-permute-start.2 = (bf16[512,256]{1,0:T(8,128)(2,1)S(1)}, bf16[512,256]{1,0:T(8,128)(2,1)S(1)}, u32[]{:S(2)}, u32[]{:S(2)}) collective-permute-start(bf16[512,256]{1,0:T(8,128)(2,1)S(1)} %bitcast.12), channel_id=1, source_target_pairs={{0,64},{64,0},{1,65},{65,1},{2,66},{66,2},{3,67},{67,3},{4,68},{68... | collective-permute-start | bytes 786440 | tf_op jit(solution)/shard_map/ppermute | solution.py:312
  67.1 0.0 collective-permute-done.4.others
  67.1 0.6 shard_map.91
  67.7 0.3 shard_map.92
  68.0 0.2 collective-permute-done.2.other
  68.2 1.6 %shard_map.93 = bf16[512,256]{1,0:T(8,128)(2,1)} custom-call(bf16[512,256]{1,0:T(8,128)(2,1)S(1)} %collective-permute-done.2.other, f32[512,512]{1,0:T(8,128)S(1)} %get-tuple-element.59.partial, bf16[8,64,512]{2,1,0:T(8,128)(2,1)S(1)} %get-tuple-element.60.left, bf16[8,64,512]{2,1,0:T(8,128)(2,1)S(1)} %get-tuple-element.58.right, ...), custom_call_target="tpu_custom_call" | custom-call | tf_op jit(solution)/shard_map/pallas_call | solution.py:410
  69.8 6.1 %all-to-all-start.2 = ((bf16[64,8,256]{2,1,0:T(8,128)(2,1)}), bf16[64,8,256]{2,1,0:T(8,128)(2,1)S(1)}, u32[]{:S(2)}, u32[]{:S(2)}) async-start(bf16[64,8,256]{2,1,0:T(8,128)(2,1)} %bitcast.5), calls=%async_computation.2 | async-start | bytes 524288 | tf_op jit(solution)/shard_map/all_to_all | solution.py:299
  76.0 0.9 shard_map.95
  76.9 4.0 %collective-permute-start.5 = (bf16[2,2,64,512]{3,2,1,0:T(8,128)(2,1)S(1)}, bf16[2,2,64,512]{3,2,1,0:T(8,128)(2,1)S(1)}, u32[]{:S(2)}, u32[]{:S(2)}) collective-permute-start(bf16[2,2,64,512]{3,2,1,0:T(8,128)(2,1)S(1)} %get-tuple-element.65), channel_id=1, source_target_pairs={{0,128},{128,256},{256,384},{384,0},{64,448},{192,64},{320,192},{4... | collective-permute-start | bytes 786440 | tf_op jit(solution)/shard_map/ppermute | solution.py:426
  80.9 2.5 %collective-permute-start.6 = (bf16[2,64,512]{2,1,0:T(8,128)(2,1)S(1)}, bf16[2,64,512]{2,1,0:T(8,128)(2,1)S(1)}, u32[]{:S(2)}, u32[]{:S(2)}) collective-permute-start(bf16[2,64,512]{2,1,0:T(8,128)(2,1)S(1)} %get-tuple-element.66), channel_id=1, source_target_pairs={{0,256},{128,384},{256,0},{384,128},{1,257},{129,385},{257,1},{385... | collective-permute-start | bytes 393224 | tf_op jit(solution)/shard_map/ppermute | solution.py:308
  83.4 0.9 collective-permute-done.5.beside
  84.3 4.6 %collective-permute-start.7 = (bf16[2,64,512]{2,1,0:T(8,128)(2,1)S(1)}, bf16[2,64,512]{2,1,0:T(8,128)(2,1)S(1)}, u32[]{:S(2)}, u32[]{:S(2)}) collective-permute-start(bf16[2,64,512]{2,1,0:T(8,128)(2,1)S(1)} %dynamic-slice_bitcast_fusion), channel_id=1, source_target_pairs={{0,64},{64,0},{1,65},{65,1},{2,66},{66,2},{3,67},{67,3},{4,68},{68... | collective-permute-start | bytes 393224 | tf_op jit(solution)/shard_map/ppermute | solution.py:312
  88.9 6.9 %all-to-all-done.2.rows = bf16[64,8,256]{2,1,0:T(8,128)(2,1)S(1)} async-done(((bf16[64,8,256]{2,1,0:T(8,128)(2,1)}), bf16[64,8,256]{2,1,0:T(8,128)(2,1)S(1)}, u32[]{:S(2)}, u32[]{:S(2)}) %all-to-all-start.2) | async-done | bytes 262176 | tf_op jit(solution)/shard_map/all_to_all | solution.py:299
  95.8 0.6 shard_map.94
  96.4 0.0 collective-permute-done.6.across
  96.4 0.0 collective-permute-done.7.passed
  96.4 10.1 %all_to_all.20 = bf16[4,32,8,256]{3,2,1,0:T(8,128)(2,1)S(1)} all-to-all(bf16[4,32,8,256]{3,2,1,0:T(8,128)(2,1)S(1)} %shard_map.94), channel_id=1, replica_groups=mesh['x'=4,'core'=2,'y'=4,'z'=16] {'x'}, dimensions={0} | all-to-all | bytes 1048576 | tf_op jit(solution)/shard_map/all_to_all | solution.py:299
  106.5 0.8 shard_map.96.rows
  107.3 0.0 copy-start
  107.3 0.0 copy-start.1
  107.3 5.6 %collective-permute-start.8 = (bf16[128,8,256]{2,1,0:T(8,128)(2,1)S(1)}, bf16[128,8,256]{2,1,0:T(8,128)(2,1)S(1)}, u32[]{:S(2)}, u32[]{:S(2)}) collective-permute-start(bf16[128,8,256]{2,1,0:T(8,128)(2,1)S(1)} %shard_map.96.rows), channel_id=1, source_target_pairs={{0,64},{64,0},{1,65},{65,1},{2,66},{66,2},{3,67},{67,3},{4,68},{68... | collective-permute-start | bytes 1572872 | tf_op jit(solution)/shard_map/ppermute | solution.py:312
  112.9 0.8 shard_map.97.begun
  113.7 0.0 copy-done
  113.7 0.0 copy-done.1
  113.7 1.6 %shard_map.99 = (f32[4,64,512]{2,1,0:T(8,128)}, f32[4,64,512]{2,1,0:T(8,128)}) custom-call(s32[1,128]{1,0:T(1,128)S(1)} %get-tuple-element.72.chip_of, bf16[2,64,512]{2,1,0:T(8,128)(2,1)S(1)} %get-tuple-element.73.mine, bf16[2,64,512]{2,1,0:T(8,128)(2,1)S(1)} %collective-permute-done.6.across, bf16[2,2,64,512]{3,2,1,0:T(8,128)(2,1)S(1)} %collective-permute-done.5.beside, ...), custom_call_target="tpu_custom_call" | custom-call | flops 10000000 | bytes 5000000 | tf_op jit(solution)/shard_map/pallas_call | solution.py:437
  115.4 0.0 collective-permute-done.8.rows
  115.4 0.8 shard_map.98
  (2 shorter events, 0.0 us)
Async XLA Ops:
  1.9 11.3 %collective-permute-start = (bf16[32,64,256]{2,1,0:T(8,128)(2,1)S(1)}, bf16[32,64,256]{2,1,0:T(8,128)(2,1)S(1)}, u32[]{:S(2)}, u32[]{:S(2)}) collective-permute-start(bf16[32,64,256]{2,1,0:T(8,128)(2,1)S(1)} %shard_map.85), channel_id=1, source_target_pairs={{0,64},{64,0},{1,65},{65,1},{2,66},{66,2},{3,67},{67,3},{4,68},{68... | collective-permute-start | bytes 3145736 | tf_op jit(solution)/shard_map/ppermute | solution.py:312
  14.7 13.1 %all-to-all-start = ((bf16[4,32,8,256]{3,2,1,0:T(8,128)(2,1)}), bf16[4,32,8,256]{3,2,1,0:T(8,128)(2,1)S(1)}, u32[]{:S(2)}, u32[]{:S(2)}) async-start(bf16[4,32,8,256]{3,2,1,0:T(8,128)(2,1)} %shard_map.87), calls=%async_computation | async-start | bytes 1048576 | tf_op jit(solution)/shard_map/all_to_all | solution.py:299
  18.8 10.7 %collective-permute-start.1 = (bf16[2,2,64,512]{3,2,1,0:T(8,128)(2,1)S(1)}, bf16[2,2,64,512]{3,2,1,0:T(8,128)(2,1)S(1)}, u32[]{:S(2)}, u32[]{:S(2)}) collective-permute-start(bf16[2,2,64,512]{3,2,1,0:T(8,128)(2,1)S(1)} %shard_map.89), channel_id=1, source_target_pairs={{0,128},{128,256},{256,384},{384,0},{64,448},{192,64},{320,192},{4... | collective-permute-start | bytes 786440 | tf_op jit(solution)/shard_map/ppermute | solution.py:373
  29.5 31.7 %all-to-all-start.1 = ((bf16[64,8,256]{2,1,0:T(8,128)(2,1)}), bf16[64,8,256]{2,1,0:T(8,128)(2,1)S(1)}, u32[]{:S(2)}, u32[]{:S(2)}) async-start(bf16[64,8,256]{2,1,0:T(8,128)(2,1)} %shard_map.88), calls=%async_computation.1 | async-start | bytes 524288 | tf_op jit(solution)/shard_map/all_to_all | solution.py:299
  43.2 7.2 %collective-permute-start.3 = (bf16[2,64,512]{2,1,0:T(8,128)(2,1)S(1)}, bf16[2,64,512]{2,1,0:T(8,128)(2,1)S(1)}, u32[]{:S(2)}, u32[]{:S(2)}) collective-permute-start(bf16[2,64,512]{2,1,0:T(8,128)(2,1)S(1)} %get-tuple-element.57), channel_id=1, source_target_pairs={{0,256},{128,384},{256,0},{384,128},{1,257},{129,385},{257,1},{385... | collective-permute-start | bytes 393224 | tf_op jit(solution)/shard_map/ppermute | solution.py:308
  50.4 16.6 %collective-permute-start.4 = (bf16[3,2,64,512]{3,2,1,0:T(8,128)(2,1)S(1)}, bf16[3,2,64,512]{3,2,1,0:T(8,128)(2,1)S(1)}, u32[]{:S(2)}, u32[]{:S(2)}) collective-permute-start(bf16[3,2,64,512]{3,2,1,0:T(8,128)(2,1)S(1)} %shard_map.90), channel_id=1, source_target_pairs={{0,64},{64,0},{1,65},{65,1},{2,66},{66,2},{3,67},{67,3},{4,68},{68... | collective-permute-start | bytes 1179656 | tf_op jit(solution)/shard_map/ppermute | solution.py:312
  61.3 6.9 %collective-permute-start.2 = (bf16[512,256]{1,0:T(8,128)(2,1)S(1)}, bf16[512,256]{1,0:T(8,128)(2,1)S(1)}, u32[]{:S(2)}, u32[]{:S(2)}) collective-permute-start(bf16[512,256]{1,0:T(8,128)(2,1)S(1)} %bitcast.12), channel_id=1, source_target_pairs={{0,64},{64,0},{1,65},{65,1},{2,66},{66,2},{3,67},{67,3},{4,68},{68... | collective-permute-start | bytes 786440 | tf_op jit(solution)/shard_map/ppermute | solution.py:312
  69.8 26.0 %all-to-all-start.2 = ((bf16[64,8,256]{2,1,0:T(8,128)(2,1)}), bf16[64,8,256]{2,1,0:T(8,128)(2,1)S(1)}, u32[]{:S(2)}, u32[]{:S(2)}) async-start(bf16[64,8,256]{2,1,0:T(8,128)(2,1)} %bitcast.5), calls=%async_computation.2 | async-start | bytes 524288 | tf_op jit(solution)/shard_map/all_to_all | solution.py:299
  76.9 7.4 %collective-permute-start.5 = (bf16[2,2,64,512]{3,2,1,0:T(8,128)(2,1)S(1)}, bf16[2,2,64,512]{3,2,1,0:T(8,128)(2,1)S(1)}, u32[]{:S(2)}, u32[]{:S(2)}) collective-permute-start(bf16[2,2,64,512]{3,2,1,0:T(8,128)(2,1)S(1)} %get-tuple-element.65), channel_id=1, source_target_pairs={{0,128},{128,256},{256,384},{384,0},{64,448},{192,64},{320,192},{4... | collective-permute-start | bytes 786440 | tf_op jit(solution)/shard_map/ppermute | solution.py:426
  80.9 15.5 %collective-permute-start.6 = (bf16[2,64,512]{2,1,0:T(8,128)(2,1)S(1)}, bf16[2,64,512]{2,1,0:T(8,128)(2,1)S(1)}, u32[]{:S(2)}, u32[]{:S(2)}) collective-permute-start(bf16[2,64,512]{2,1,0:T(8,128)(2,1)S(1)} %get-tuple-element.66), channel_id=1, source_target_pairs={{0,256},{128,384},{256,0},{384,128},{1,257},{129,385},{257,1},{385... | collective-permute-start | bytes 393224 | tf_op jit(solution)/shard_map/ppermute | solution.py:308
  84.3 12.1 %collective-permute-start.7 = (bf16[2,64,512]{2,1,0:T(8,128)(2,1)S(1)}, bf16[2,64,512]{2,1,0:T(8,128)(2,1)S(1)}, u32[]{:S(2)}, u32[]{:S(2)}) collective-permute-start(bf16[2,64,512]{2,1,0:T(8,128)(2,1)S(1)} %dynamic-slice_bitcast_fusion), channel_id=1, source_target_pairs={{0,64},{64,0},{1,65},{65,1},{2,66},{66,2},{3,67},{67,3},{4,68},{68... | collective-permute-start | bytes 393224 | tf_op jit(solution)/shard_map/ppermute | solution.py:312
  107.3 6.4 %copy-start = (f32[4,64,512]{2,1,0:T(8,128)S(1)}, f32[4,64,512]{2,1,0:T(8,128)}, u32[]{:S(2)}) copy-start(f32[4,64,512]{2,1,0:T(8,128)} %left.1) | copy-start | bytes 1572868
  107.3 6.4 %copy-start.1 = (f32[4,64,512]{2,1,0:T(8,128)S(1)}, f32[4,64,512]{2,1,0:T(8,128)}, u32[]{:S(2)}) copy-start(f32[4,64,512]{2,1,0:T(8,128)} %right.1) | copy-start | bytes 1572868
  107.3 8.1 %collective-permute-start.8 = (bf16[128,8,256]{2,1,0:T(8,128)(2,1)S(1)}, bf16[128,8,256]{2,1,0:T(8,128)(2,1)S(1)}, u32[]{:S(2)}, u32[]{:S(2)}) collective-permute-start(bf16[128,8,256]{2,1,0:T(8,128)(2,1)S(1)} %shard_map.96.rows), channel_id=1, source_target_pairs={{0,64},{64,0},{1,65},{65,1},{2,66},{66,2},{3,67},{67,3},{4,68},{68... | collective-permute-start | bytes 1572872 | tf_op jit(solution)/shard_map/ppermute | solution.py:312

commit v11 on v10

--- a/solution.py
+++ b/solution.py
@@ -64,25 +64,28 @@
 
 
 def keep_kernel(slots_hbm, grads, left_root, right_root, kept, beside, mine, across, *refs):
-    tables, (slots, scalars, sems, root_sems) = refs[:6], refs[6:]
+    tables, (slots, rows, sems, root_sems, table_sems) = refs[:6], refs[6:]
     core, x = lax.axis_index("core"), lax.axis_index("x")
     me = lax.axis_index("y") * lax.axis_size("z") + lax.axis_index("z")
     width = kept.shape[2]
     near = pl.ds(pl.multiple_of(core * width, 128), width)
     slots_load = pltpu.make_async_copy(slots_hbm, slots, sems.at[0])
     load = pltpu.make_async_copy(grads.at[:, :, near], kept, sems.at[1])
-    slot_load = pltpu.make_async_copy(tables[4], scalars, sems.at[2])
+    to_scalars = [pltpu.make_async_copy(rows.at[i], table, table_sems.at[i]) for i, table in enumerate(tables)]
     slots_load.start()
     load.start()
     slots_load.wait()
-    fill_tables(slots, x, me, left_root.shape[0], 4, *tables, slot_load.start)
-    slot_load.wait()
+    fill_tables(slots, x, me, left_root.shape[0], 4, *(rows.at[i] for i in range(6)), to_scalars[4].start)
+    to_scalars[4].wait()
     loads = [load]
     for i, (chip, out) in enumerate(((x + 1 + 2 * core, beside), (x, mine), (x + 2, across))):
-        slot = scalars[0, lax.rem(chip, 4)]
+        slot = tables[4][0, lax.rem(chip, 4)]
         for side, root in enumerate((left_root, right_root)):
             loads.append(pltpu.make_async_copy(root.at[slot], out.at[side], root_sems.at[i, side]))
             loads[-1].start()
+    for i in (0, 1, 2, 3, 5):
+        to_scalars[i].start()
+        loads.append(to_scalars[i])
     for load in loads:
         load.wait()
 
@@ -144,16 +147,13 @@
         store.wait()
 
 
-def chip_sum_kernel(place_vmem, parts, out, total, place, sem):
+def chip_sum_kernel(place, parts, out, total):
     depth = parts.shape[1]
-    load = pltpu.make_async_copy(place_vmem, place, sem)
-    load.start()
     acc = parts[0].astype(F32)
     for x in range(1, parts.shape[0]):
         acc = acc + parts[x].astype(F32)
     total[0:depth] = acc.astype(BF16)
     total[depth] = jnp.zeros(total.shape[1:], BF16)
-    load.wait()
 
     def body(o, carry):
         out[o] = total[place[0, o]]
@@ -214,9 +214,12 @@
             out[side] = jnp.where(core == 0, term[:rows], term[rows:]).astype(BF16)
 
 
-def stats_kernel(chip_of, mine, across, beside, passed, left, right, left_hbm, right_hbm, left_out, right_out, sems):
+def finish_kernel(
+    chip_of, near, mine, across, beside, passed, left, right, out_hbm, left_hbm, right_hbm, left_out, right_out, near_sem, sems
+):
     core, x = lax.axis_index("core"), lax.axis_index("x")
-    stores = []
+    stores = [place_half(core, near, out_hbm, near_sem)]
+    stores[0].start()
     for j in range(left.shape[0]):
         full = chip_of[0, j] >= 0
         way = lax.rem(chip_of[0, j] + 4 - x, 4)
@@ -264,18 +267,14 @@
 
 def place_half(half, rows, out_hbm, sem):
     width = rows.shape[2]
-    store = pltpu.make_async_copy(rows, out_hbm.at[:, :, pl.ds(pl.multiple_of(half * width, 128), width)], sem)
+    return pltpu.make_async_copy(rows, out_hbm.at[:, :, pl.ds(pl.multiple_of(half * width, 128), width)], sem)
+
+
+def place_far_kernel(rows, begun, out_hbm, sem):
+    del begun
+    store = place_half(1 - lax.axis_index("core"), rows, out_hbm, sem)
     store.start()
     store.wait()
-
-
-def place_near_kernel(rows, out_hbm, sem):
-    place_half(lax.axis_index("core"), rows, out_hbm, sem)
-
-
-def place_far_kernel(rows, begun, out_hbm, sem):
-    del begun
-    place_half(1 - lax.axis_index("core"), rows, out_hbm, sem)
 
 
 def call(kernel, out_shape, in_specs, scratch=(), out_specs=None, cost=None, aliases=None):
@@ -343,14 +342,16 @@
         keep_kernel,
         [jax.ShapeDtypeStruct((grad_groups, stat_rows, half), BF16)]
         + [piece] * 3
-        + [jax.ShapeDtypeStruct((1, blocks), jnp.int32)] * 6,
+        + [pltpu.SMEM((1, blocks), jnp.int32)] * 6,
         [HBM_SPEC] * 4,
         [
             pltpu.VMEM((1, blocks), jnp.int32),
-            pltpu.SMEM((1, blocks), jnp.int32),
-            pltpu.SemaphoreType.DMA((3,)),
+            pltpu.VMEM((6, 1, blocks), jnp.int32),
+            pltpu.SemaphoreType.DMA((2,)),
             pltpu.SemaphoreType.DMA((3, 2)),
+            pltpu.SemaphoreType.DMA((6,)),
         ],
+        [VMEM_SPEC] * 4 + [SMEM_SPEC] * 6,
         cost=(0, 4_000_000),
     )(in_hbm(block_slot.reshape(1, blocks)), in_hbm(late_grads), left_root, right_root)
 
@@ -374,12 +375,8 @@
     outgoing = call(
         chip_sum_kernel,
         jax.ShapeDtypeStruct((owners, shard_rows, half), BF16),
-        [VMEM_SPEC, VMEM_SPEC],
-        [
-            pltpu.VMEM((depth + 1, shard_rows, half), BF16),
-            pltpu.SMEM((1, blocks), jnp.int32),
-            pltpu.SemaphoreType.DMA,
-        ],
+        [SMEM_SPEC, VMEM_SPEC],
+        [pltpu.VMEM((depth + 1, shard_rows, half), BF16)],
     )(place, parts)
 
     outgoing, late_other, beside, across = lax.optimization_barrier((outgoing, other, beside, across))
@@ -433,30 +430,23 @@
     packed, beside, across, passed = lax.optimization_barrier((packed, beside, across, passed))
     near = exchange(packed, "x").reshape(blocks, shard_rows, half)
     near, beside, across, passed = lax.optimization_barrier((near, beside, across, passed))
+    near = call(order_kernel, half_rows, [SMEM_SPEC, VMEM_SPEC])(source, near)
+    beyond = swap_cores(near)
     stat = jax.ShapeDtypeStruct(left_stat.shape, F32)
-    left_new, right_new = call(
-        stats_kernel,
-        [stat, stat],
-        [SMEM_SPEC] + [VMEM_SPEC] * 6,
+    whole_rows = jax.ShapeDtypeStruct((blocks, shard_rows, width), BF16)
+    begun, left_new, right_new = call(
+        finish_kernel,
+        [whole_rows, stat, stat],
+        [SMEM_SPEC] + [VMEM_SPEC] * 7,
         [
             pltpu.VMEM(left_stat.shape, F32),
             pltpu.VMEM(right_stat.shape, F32),
+            pltpu.SemaphoreType.DMA,
             pltpu.SemaphoreType.DMA((capacity, 2)),
         ],
-        [HBM_SPEC, HBM_SPEC],
+        [HBM_SPEC] * 3,
         cost=(10_000_000, 5_000_000),
-    )(chip_of, mine, across, beside, passed, left_stat, right_stat)
-    near = call(order_kernel, half_rows, [SMEM_SPEC, VMEM_SPEC])(source, near)
-    beyond = swap_cores(near)
-    whole_rows = jax.ShapeDtypeStruct((blocks, shard_rows, width), BF16)
-    begun = call(
-        place_near_kernel,
-        whole_rows,
-        [VMEM_SPEC],
-        [pltpu.SemaphoreType.DMA],
-        HBM_SPEC,
-        cost=(0, 4_000_000),
-    )(near)
+    )(chip_of, near, mine, across, beside, passed, left_stat, right_stat)
     result = call(
         place_far_kernel,
         whole_rows,

time: 117 us -> 114 us (0.974)
  Pallas kernels: 15.3 us -> 11 us
  waiting for transfers between devices: 21.8 us -> 23.8 us
    pallas_call x2 -> x1, Pallas kernels: 2.46 us -> 1.22 us  [local(): call(finish_kernel, [whole_rows, stat, stat], [SMEM_SPEC] + [VMEM_SPEC] *...]
  transfers between devices with their start and end apart: 12 -> 12, of which waited for: 7 -> 8; matrix products, arithmetic and copies ran while one was open for 0% -> 0% of each run, Pallas kernels for 8% -> 5%
where the time goes in v11:
time: 114 us
  starting transfers between devices  67.9 us (60%)
  waiting for transfers between devices  23.8 us (21%)
  Pallas kernels  11 us (10%)
  blocking collectives  10.1 us (9%)
    ppermute x5, starting transfers between devices, swap_cores(): return lax.ppermute(value, 'core', [(0, 1), (1, 0)])  29.7 us
    all_to_all x3, starting transfers between devices, exchange(): return lax.all_to_all(value, axis, 0, 0, tiled=True)  23.3 us
    all_to_all x3, waiting for transfers between devices, exchange(): return lax.all_to_all(value, axis, 0, 0, tiled=True)  17.8 us
    all_to_all x1, blocking collectives, exchange(): return lax.all_to_all(value, axis, 0, 0, tiled=True)  10.1 us
    ppermute x2, starting transfers between devices, local(): beside = lax.ppermute(beside, ('x', 'core'), ways)  8.31 us
    ppermute x2, starting transfers between devices, turn(): lax.ppermute(value, 'x', [(i, (i + k) % chips) for i in range(chips)])  6.65 us
    ppermute x2, waiting for transfers between devices, turn(): lax.ppermute(value, 'x', [(i, (i + k) % chips) for i in range(chips)])  3.2 us
    pallas_call x1, Pallas kernels, local(): call(keep_kernel, [jax.ShapeDtypeStruct((grad_groups, stat_rows, half), B...  2.61 us
  transfers between devices with their start and end apart: 12, of which 8 were waited for; matrix products, arithmetic and copies ran while one was open for 0% of the time, Pallas kernels for 5%

profile of v11, /device:TPU:1, one launch (start us, length us, event | category | flops | bytes accessed | tf_op | source)
XLA Modules:
  0.0 113.6 jit_solution(991421806291236317)
XLA Ops:
  0.6 1.2 %shard_map.85 = bf16[32,64,256]{2,1,0:T(8,128)(2,1)S(1)} custom-call(bf16[16,64,512]{2,1,0:T(8,128)(2,1)} %bitcast.15, bf16[4,64,512]{2,1,0:T(8,128)(2,1)} %left_root.3, bf16[4,64,512]{2,1,0:T(8,128)(2,1)} %right_root.3), custom_call_target="tpu_custom_call" | custom-call | tf_op jit(solution)/shard_map/pallas_call | solution.py:333
  1.9 8.8 %collective-permute-start = (bf16[32,64,256]{2,1,0:T(8,128)(2,1)S(1)}, bf16[32,64,256]{2,1,0:T(8,128)(2,1)S(1)}, u32[]{:S(2)}, u32[]{:S(2)}) collective-permute-start(bf16[32,64,256]{2,1,0:T(8,128)(2,1)S(1)} %shard_map.85), channel_id=1, source_target_pairs={{0,64},{64,0},{1,65},{65,1},{2,66},{66,2},{3,67},{67,3},{4,68},{68... | collective-permute-start | bytes 3145736 | tf_op jit(solution)/shard_map/ppermute | solution.py:311
  10.7 2.6 %shard_map.86 = (bf16[16,64,256]{2,1,0:T(8,128)(2,1)S(1)}, bf16[2,64,512]{2,1,0:T(8,128)(2,1)S(1)}, bf16[2,64,512]{2,1,0:T(8,128)(2,1)S(1)}, bf16[2,64,512]{2,1,...) custom-call(s32[1,128]{1,0:T(1,128)} %bitcast.17, ...), custom_call_target="tpu_custom_call" | custom-call | bytes 4000000 | tf_op jit(solution)/shard_map/pallas_call | solution.py:341
  13.3 0.0 collective-permute-done.other
  13.3 1.0 shard_map.87
  14.3 3.5 %all-to-all-start = ((bf16[4,32,8,256]{3,2,1,0:T(8,128)(2,1)}), bf16[4,32,8,256]{3,2,1,0:T(8,128)(2,1)S(1)}, u32[]{:S(2)}, u32[]{:S(2)}) async-start(bf16[4,32,8,256]{3,2,1,0:T(8,128)(2,1)} %shard_map.87), calls=%async_computation | async-start | bytes 1048576 | tf_op jit(solution)/shard_map/all_to_all | solution.py:298
  17.8 4.5 %collective-permute-start.1 = (bf16[2,2,64,512]{3,2,1,0:T(8,128)(2,1)S(1)}, bf16[2,2,64,512]{3,2,1,0:T(8,128)(2,1)S(1)}, u32[]{:S(2)}, u32[]{:S(2)}) collective-permute-start(bf16[2,2,64,512]{3,2,1,0:T(8,128)(2,1)S(1)} %shard_map.89), channel_id=1, source_target_pairs={{0,128},{128,256},{256,384},{384,0},{64,448},{192,64},{320,192},{4... | collective-permute-start | bytes 786440 | tf_op jit(solution)/shard_map/ppermute | solution.py:374
  22.3 5.1 %all-to-all-done.parts = bf16[4,32,8,256]{3,2,1,0:T(8,128)(2,1)S(1)} async-done(((bf16[4,32,8,256]{3,2,1,0:T(8,128)(2,1)}), bf16[4,32,8,256]{3,2,1,0:T(8,128)(2,1)S(1)}, u32[]{:S(2)}, u32[]{:S(2)}) %all-to-all-start) | async-done | bytes 524320 | tf_op jit(solution)/shard_map/all_to_all | solution.py:298
  27.4 0.9 shard_map.88
  28.3 0.8 collective-permute-done.1.beside
  29.1 13.6 %all-to-all-start.1 = ((bf16[64,8,256]{2,1,0:T(8,128)(2,1)}), bf16[64,8,256]{2,1,0:T(8,128)(2,1)S(1)}, u32[]{:S(2)}, u32[]{:S(2)}) async-start(bf16[64,8,256]{2,1,0:T(8,128)(2,1)} %shard_map.88), calls=%async_computation.1 | async-start | bytes 524288 | tf_op jit(solution)/shard_map/all_to_all | solution.py:298
  42.8 4.0 %collective-permute-start.3 = (bf16[2,64,512]{2,1,0:T(8,128)(2,1)S(1)}, bf16[2,64,512]{2,1,0:T(8,128)(2,1)S(1)}, u32[]{:S(2)}, u32[]{:S(2)}) collective-permute-start(bf16[2,64,512]{2,1,0:T(8,128)(2,1)S(1)} %get-tuple-element.58), channel_id=1, source_target_pairs={{0,256},{128,384},{256,0},{384,128},{1,257},{129,385},{257,1},{385... | collective-permute-start | bytes 393224 | tf_op jit(solution)/shard_map/ppermute | solution.py:307
  46.8 3.2 %collective-permute-done.3.across = bf16[2,64,512]{2,1,0:T(8,128)(2,1)S(1)} collective-permute-done((bf16[2,64,512]{2,1,0:T(8,128)(2,1)S(1)}, bf16[2,64,512]{2,1,0:T(8,128)(2,1)S(1)}, u32[]{:S(2)}, u32[]{:S(2)}) %collective-permute-start.3) | collective-permute-done | bytes 131104 | tf_op jit(solution)/shard_map/ppermute | solution.py:307
  50.0 4.9 %collective-permute-start.4 = (bf16[3,2,64,512]{3,2,1,0:T(8,128)(2,1)S(1)}, bf16[3,2,64,512]{3,2,1,0:T(8,128)(2,1)S(1)}, u32[]{:S(2)}, u32[]{:S(2)}) collective-permute-start(bf16[3,2,64,512]{3,2,1,0:T(8,128)(2,1)S(1)} %shard_map.90), channel_id=1, source_target_pairs={{0,64},{64,0},{1,65},{65,1},{2,66},{66,2},{3,67},{67,3},{4,68},{68... | collective-permute-start | bytes 1179656 | tf_op jit(solution)/shard_map/ppermute | solution.py:311
  54.9 5.9 %all-to-all-done.1 = bf16[64,8,256]{2,1,0:T(8,128)(2,1)S(1)} async-done(((bf16[64,8,256]{2,1,0:T(8,128)(2,1)}), bf16[64,8,256]{2,1,0:T(8,128)(2,1)S(1)}, u32[]{:S(2)}, u32[]{:S(2)}) %all-to-all-start.1) | async-done | bytes 262176 | tf_op jit(solution)/shard_map/all_to_all | solution.py:298
  60.8 5.8 %collective-permute-start.2 = (bf16[512,256]{1,0:T(8,128)(2,1)S(1)}, bf16[512,256]{1,0:T(8,128)(2,1)S(1)}, u32[]{:S(2)}, u32[]{:S(2)}) collective-permute-start(bf16[512,256]{1,0:T(8,128)(2,1)S(1)} %bitcast.12), channel_id=1, source_target_pairs={{0,64},{64,0},{1,65},{65,1},{2,66},{66,2},{3,67},{67,3},{4,68},{68... | collective-permute-start | bytes 786440 | tf_op jit(solution)/shard_map/ppermute | solution.py:311
  66.6 0.0 collective-permute-done.4.others
  66.6 0.1 shard_map.91
  66.7 0.3 shard_map.92
  67.1 0.7 collective-permute-done.2.other
  67.8 1.6 %shard_map.93 = bf16[512,256]{1,0:T(8,128)(2,1)} custom-call(bf16[512,256]{1,0:T(8,128)(2,1)S(1)} %collective-permute-done.2.other, f32[512,512]{1,0:T(8,128)S(1)} %get-tuple-element.60.partial, bf16[8,64,512]{2,1,0:T(8,128)(2,1)S(1)} %get-tuple-element.61.left, bf16[8,64,512]{2,1,0:T(8,128)(2,1)S(1)} %get-tuple-element.59.right, ...), custom_call_target="tpu_custom_call" | custom-call | tf_op jit(solution)/shard_map/pallas_call | solution.py:407
  69.4 6.1 %all-to-all-start.2 = ((bf16[64,8,256]{2,1,0:T(8,128)(2,1)}), bf16[64,8,256]{2,1,0:T(8,128)(2,1)S(1)}, u32[]{:S(2)}, u32[]{:S(2)}) async-start(bf16[64,8,256]{2,1,0:T(8,128)(2,1)} %bitcast.5), calls=%async_computation.2 | async-start | bytes 524288 | tf_op jit(solution)/shard_map/all_to_all | solution.py:298
  75.5 0.9 shard_map.95
  76.4 3.8 %collective-permute-start.5 = (bf16[2,2,64,512]{3,2,1,0:T(8,128)(2,1)S(1)}, bf16[2,2,64,512]{3,2,1,0:T(8,128)(2,1)S(1)}, u32[]{:S(2)}, u32[]{:S(2)}) collective-permute-start(bf16[2,2,64,512]{3,2,1,0:T(8,128)(2,1)S(1)} %get-tuple-element.66), channel_id=1, source_target_pairs={{0,128},{128,256},{256,384},{384,0},{64,448},{192,64},{320,192},{4... | collective-permute-start | bytes 786440 | tf_op jit(solution)/shard_map/ppermute | solution.py:423
  80.2 2.6 %collective-permute-start.6 = (bf16[2,64,512]{2,1,0:T(8,128)(2,1)S(1)}, bf16[2,64,512]{2,1,0:T(8,128)(2,1)S(1)}, u32[]{:S(2)}, u32[]{:S(2)}) collective-permute-start(bf16[2,64,512]{2,1,0:T(8,128)(2,1)S(1)} %get-tuple-element.67), channel_id=1, source_target_pairs={{0,256},{128,384},{256,0},{384,128},{1,257},{129,385},{257,1},{385... | collective-permute-start | bytes 393224 | tf_op jit(solution)/shard_map/ppermute | solution.py:307
  82.9 1.0 collective-permute-done.5.beside
  83.9 4.6 %collective-permute-start.7 = (bf16[2,64,512]{2,1,0:T(8,128)(2,1)S(1)}, bf16[2,64,512]{2,1,0:T(8,128)(2,1)S(1)}, u32[]{:S(2)}, u32[]{:S(2)}) collective-permute-start(bf16[2,64,512]{2,1,0:T(8,128)(2,1)S(1)} %dynamic-slice_bitcast_fusion), channel_id=1, source_target_pairs={{0,64},{64,0},{1,65},{65,1},{2,66},{66,2},{3,67},{67,3},{4,68},{68... | collective-permute-start | bytes 393224 | tf_op jit(solution)/shard_map/ppermute | solution.py:311
  88.5 6.8 %all-to-all-done.2.rows = bf16[64,8,256]{2,1,0:T(8,128)(2,1)S(1)} async-done(((bf16[64,8,256]{2,1,0:T(8,128)(2,1)}), bf16[64,8,256]{2,1,0:T(8,128)(2,1)S(1)}, u32[]{:S(2)}, u32[]{:S(2)}) %all-to-all-start.2) | async-done | bytes 262176 | tf_op jit(solution)/shard_map/all_to_all | solution.py:298
  95.4 0.0 collective-permute-done.6.across
  95.4 0.0 collective-permute-done.7.passed
  95.4 10.1 %all_to_all.20 = bf16[4,32,8,256]{3,2,1,0:T(8,128)(2,1)S(1)} all-to-all(bf16[4,32,8,256]{3,2,1,0:T(8,128)(2,1)S(1)} %shard_map.94), channel_id=1, replica_groups=mesh['x'=4,'core'=2,'y'=4,'z'=16] {'x'}, dimensions={0} | all-to-all | bytes 1048576 | tf_op jit(solution)/shard_map/all_to_all | solution.py:298
  105.5 0.0 copy-start
  105.5 0.0 copy-start.1
  105.5 0.2 shard_map.96.near
  105.7 5.6 %collective-permute-start.8 = (bf16[128,8,256]{2,1,0:T(8,128)(2,1)S(1)}, bf16[128,8,256]{2,1,0:T(8,128)(2,1)S(1)}, u32[]{:S(2)}, u32[]{:S(2)}) collective-permute-start(bf16[128,8,256]{2,1,0:T(8,128)(2,1)S(1)} %shard_map.96.near), channel_id=1, source_target_pairs={{0,64},{64,0},{1,65},{65,1},{2,66},{66,2},{3,67},{67,3},{4,68},{68... | collective-permute-start | bytes 1572872 | tf_op jit(solution)/shard_map/ppermute | solution.py:311
  111.3 0.0 copy-done
  111.3 0.0 copy-done.1
  111.3 1.2 %shard_map.97 = (bf16[128,8,512]{2,1,0:T(8,128)(2,1)}, f32[4,64,512]{2,1,0:T(8,128)}, f32[4,64,512]{2,1,0:T(8,128)}) custom-call(s32[1,128]{1,0:T(1,128)S(4)} %get-tuple-element.73.chip_of, bf16[128,8,256]{2,1,0:T(8,128)(2,1)S(1)} %shard_map.96.near, bf16[2,64,512]{2,1,0:T(8,128)(2,1)S(1)} %get-tuple-element.74.mine, ...), custom_call_target="tpu_custom_call" | custom-call | flops 10000000 | bytes 5000000 | tf_op jit(solution)/shard_map/pallas_call | solution.py:437
  112.6 0.3 collective-permute-done.8.rows
  112.8 0.8 shard_map.98
  (4 shorter events, 0.1 us)
Async XLA Ops:
  1.9 11.4 %collective-permute-start = (bf16[32,64,256]{2,1,0:T(8,128)(2,1)S(1)}, bf16[32,64,256]{2,1,0:T(8,128)(2,1)S(1)}, u32[]{:S(2)}, u32[]{:S(2)}) collective-permute-start(bf16[32,64,256]{2,1,0:T(8,128)(2,1)S(1)} %shard_map.85), channel_id=1, source_target_pairs={{0,64},{64,0},{1,65},{65,1},{2,66},{66,2},{3,67},{67,3},{4,68},{68... | collective-permute-start | bytes 3145736 | tf_op jit(solution)/shard_map/ppermute | solution.py:311
  14.3 13.1 %all-to-all-start = ((bf16[4,32,8,256]{3,2,1,0:T(8,128)(2,1)}), bf16[4,32,8,256]{3,2,1,0:T(8,128)(2,1)S(1)}, u32[]{:S(2)}, u32[]{:S(2)}) async-start(bf16[4,32,8,256]{3,2,1,0:T(8,128)(2,1)} %shard_map.87), calls=%async_computation | async-start | bytes 1048576 | tf_op jit(solution)/shard_map/all_to_all | solution.py:298
  17.8 11.3 %collective-permute-start.1 = (bf16[2,2,64,512]{3,2,1,0:T(8,128)(2,1)S(1)}, bf16[2,2,64,512]{3,2,1,0:T(8,128)(2,1)S(1)}, u32[]{:S(2)}, u32[]{:S(2)}) collective-permute-start(bf16[2,2,64,512]{3,2,1,0:T(8,128)(2,1)S(1)} %shard_map.89), channel_id=1, source_target_pairs={{0,128},{128,256},{256,384},{384,0},{64,448},{192,64},{320,192},{4... | collective-permute-start | bytes 786440 | tf_op jit(solution)/shard_map/ppermute | solution.py:374
  29.1 31.7 %all-to-all-start.1 = ((bf16[64,8,256]{2,1,0:T(8,128)(2,1)}), bf16[64,8,256]{2,1,0:T(8,128)(2,1)S(1)}, u32[]{:S(2)}, u32[]{:S(2)}) async-start(bf16[64,8,256]{2,1,0:T(8,128)(2,1)} %shard_map.88), calls=%async_computation.1 | async-start | bytes 524288 | tf_op jit(solution)/shard_map/all_to_all | solution.py:298
  42.8 7.2 %collective-permute-start.3 = (bf16[2,64,512]{2,1,0:T(8,128)(2,1)S(1)}, bf16[2,64,512]{2,1,0:T(8,128)(2,1)S(1)}, u32[]{:S(2)}, u32[]{:S(2)}) collective-permute-start(bf16[2,64,512]{2,1,0:T(8,128)(2,1)S(1)} %get-tuple-element.58), channel_id=1, source_target_pairs={{0,256},{128,384},{256,0},{384,128},{1,257},{129,385},{257,1},{385... | collective-permute-start | bytes 393224 | tf_op jit(solution)/shard_map/ppermute | solution.py:307
  50.0 16.6 %collective-permute-start.4 = (bf16[3,2,64,512]{3,2,1,0:T(8,128)(2,1)S(1)}, bf16[3,2,64,512]{3,2,1,0:T(8,128)(2,1)S(1)}, u32[]{:S(2)}, u32[]{:S(2)}) collective-permute-start(bf16[3,2,64,512]{3,2,1,0:T(8,128)(2,1)S(1)} %shard_map.90), channel_id=1, source_target_pairs={{0,64},{64,0},{1,65},{65,1},{2,66},{66,2},{3,67},{67,3},{4,68},{68... | collective-permute-start | bytes 1179656 | tf_op jit(solution)/shard_map/ppermute | solution.py:311
  60.8 6.9 %collective-permute-start.2 = (bf16[512,256]{1,0:T(8,128)(2,1)S(1)}, bf16[512,256]{1,0:T(8,128)(2,1)S(1)}, u32[]{:S(2)}, u32[]{:S(2)}) collective-permute-start(bf16[512,256]{1,0:T(8,128)(2,1)S(1)} %bitcast.12), channel_id=1, source_target_pairs={{0,64},{64,0},{1,65},{65,1},{2,66},{66,2},{3,67},{67,3},{4,68},{68... | collective-permute-start | bytes 786440 | tf_op jit(solution)/shard_map/ppermute | solution.py:311
  69.4 26.0 %all-to-all-start.2 = ((bf16[64,8,256]{2,1,0:T(8,128)(2,1)}), bf16[64,8,256]{2,1,0:T(8,128)(2,1)S(1)}, u32[]{:S(2)}, u32[]{:S(2)}) async-start(bf16[64,8,256]{2,1,0:T(8,128)(2,1)} %bitcast.5), calls=%async_computation.2 | async-start | bytes 524288 | tf_op jit(solution)/shard_map/all_to_all | solution.py:298
  76.4 7.4 %collective-permute-start.5 = (bf16[2,2,64,512]{3,2,1,0:T(8,128)(2,1)S(1)}, bf16[2,2,64,512]{3,2,1,0:T(8,128)(2,1)S(1)}, u32[]{:S(2)}, u32[]{:S(2)}) collective-permute-start(bf16[2,2,64,512]{3,2,1,0:T(8,128)(2,1)S(1)} %get-tuple-element.66), channel_id=1, source_target_pairs={{0,128},{128,256},{256,384},{384,0},{64,448},{192,64},{320,192},{4... | collective-permute-start | bytes 786440 | tf_op jit(solution)/shard_map/ppermute | solution.py:423
  80.2 15.2 %collective-permute-start.6 = (bf16[2,64,512]{2,1,0:T(8,128)(2,1)S(1)}, bf16[2,64,512]{2,1,0:T(8,128)(2,1)S(1)}, u32[]{:S(2)}, u32[]{:S(2)}) collective-permute-start(bf16[2,64,512]{2,1,0:T(8,128)(2,1)S(1)} %get-tuple-element.67), channel_id=1, source_target_pairs={{0,256},{128,384},{256,0},{384,128},{1,257},{129,385},{257,1},{385... | collective-permute-start | bytes 393224 | tf_op jit(solution)/shard_map/ppermute | solution.py:307
  83.9 11.6 %collective-permute-start.7 = (bf16[2,64,512]{2,1,0:T(8,128)(2,1)S(1)}, bf16[2,64,512]{2,1,0:T(8,128)(2,1)S(1)}, u32[]{:S(2)}, u32[]{:S(2)}) collective-permute-start(bf16[2,64,512]{2,1,0:T(8,128)(2,1)S(1)} %dynamic-slice_bitcast_fusion), channel_id=1, source_target_pairs={{0,64},{64,0},{1,65},{65,1},{2,66},{66,2},{3,67},{67,3},{4,68},{68... | collective-permute-start | bytes 393224 | tf_op jit(solution)/shard_map/ppermute | solution.py:311
  105.5 5.8 %copy-start = (f32[4,64,512]{2,1,0:T(8,128)S(1)}, f32[4,64,512]{2,1,0:T(8,128)}, u32[]{:S(2)}) copy-start(f32[4,64,512]{2,1,0:T(8,128)} %left.1) | copy-start | bytes 1572868
  105.5 5.8 %copy-start.1 = (f32[4,64,512]{2,1,0:T(8,128)S(1)}, f32[4,64,512]{2,1,0:T(8,128)}, u32[]{:S(2)}) copy-start(f32[4,64,512]{2,1,0:T(8,128)} %right.1) | copy-start | bytes 1572868
  105.7 7.1 %collective-permute-start.8 = (bf16[128,8,256]{2,1,0:T(8,128)(2,1)S(1)}, bf16[128,8,256]{2,1,0:T(8,128)(2,1)S(1)}, u32[]{:S(2)}, u32[]{:S(2)}) collective-permute-start(bf16[128,8,256]{2,1,0:T(8,128)(2,1)S(1)} %shard_map.96.near), channel_id=1, source_target_pairs={{0,64},{64,0},{1,65},{65,1},{2,66},{66,2},{3,67},{67,3},{4,68},{68... | collective-permute-start | bytes 1572872 | tf_op jit(solution)/shard_map/ppermute | solution.py:311

commit v12 on v11

--- a/solution.py
+++ b/solution.py
@@ -379,7 +379,7 @@
         [pltpu.VMEM((depth + 1, shard_rows, half), BF16)],
     )(place, parts)
 
-    outgoing, late_other, beside, across = lax.optimization_barrier((outgoing, other, beside, across))
+    outgoing, late_other, across = lax.optimization_barrier((outgoing, other, across))
     own = exchange(outgoing, ("y", "z"))
     across = turn(across, 2)
     stacked = call(

time: 114 us -> 114 us (level)
  blocking collectives: 10.1 us -> 21.9 us
  waiting for transfers between devices: 23.8 us -> 17.1 us
  starting transfers between devices: 67.9 us -> 63.8 us
    all_to_all x1 -> x2, blocking collectives: 10.1 us -> 21.9 us  [exchange(): return lax.all_to_all(value, axis, 0, 0, tiled=True)]
    all_to_all x3 -> x2, waiting for transfers between devices: 17.8 us -> 7.57 us  [exchange(): return lax.all_to_all(value, axis, 0, 0, tiled=True)]
    ppermute x2, starting transfers between devices: 8.31 us -> 5.65 us  [local(): beside = lax.ppermute(beside, ('x', 'core'), ways)]
    ppermute x2, waiting for transfers between devices: 1.8 us -> 4.12 us  [local(): beside = lax.ppermute(beside, ('x', 'core'), ways)]
    ppermute x2, starting transfers between devices: 6.65 us -> 5.01 us  [turn(): lax.ppermute(value, 'x', [(i, (i + k) % chips) for i in range(chips)])]
    ppermute x2, waiting for transfers between devices: 3.2 us -> 4.42 us  [turn(): lax.ppermute(value, 'x', [(i, (i + k) % chips) for i in range(chips)])]
    all_to_all x3 -> x2, starting transfers between devices: 23.3 us -> 23.4 us  [exchange(): return lax.all_to_all(value, axis, 0, 0, tiled=True)]
  transfers between devices with their start and end apart: 12 -> 11, of which waited for: 8 -> 7; matrix products, arithmetic and copies ran while one was open for 0% -> 0% of each run, Pallas kernels for 5% -> 5%
where the time goes in v12:
time: 114 us
  starting transfers between devices  63.8 us (56%)
  blocking collectives  21.9 us (19%)
  waiting for transfers between devices  17.1 us (15%)
  Pallas kernels  10.2 us (9%)
    ppermute x5, starting transfers between devices, swap_cores(): return lax.ppermute(value, 'core', [(0, 1), (1, 0)])  29.7 us
    all_to_all x2, starting transfers between devices, exchange(): return lax.all_to_all(value, axis, 0, 0, tiled=True)  23.4 us
    all_to_all x2, blocking collectives, exchange(): return lax.all_to_all(value, axis, 0, 0, tiled=True)  21.9 us
    all_to_all x2, waiting for transfers between devices, exchange(): return lax.all_to_all(value, axis, 0, 0, tiled=True)  7.57 us
    ppermute x2, starting transfers between devices, local(): beside = lax.ppermute(beside, ('x', 'core'), ways)  5.65 us
    ppermute x2, starting transfers between devices, turn(): lax.ppermute(value, 'x', [(i, (i + k) % chips) for i in range(chips)])  5.01 us
    ppermute x2, waiting for transfers between devices, turn(): lax.ppermute(value, 'x', [(i, (i + k) % chips) for i in range(chips)])  4.42 us
    ppermute x2, waiting for transfers between devices, local(): beside = lax.ppermute(beside, ('x', 'core'), ways)  4.12 us
  transfers between devices with their start and end apart: 11, of which 7 were waited for; matrix products, arithmetic and copies ran while one was open for 0% of the time, Pallas kernels for 5%

profile of v12, /device:TPU:1, one launch (start us, length us, event | category | flops | bytes accessed | tf_op | source)
XLA Modules:
  0.0 113.8 jit_solution(5149861484426180318)
XLA Ops:
  0.6 1.2 %shard_map.85 = bf16[32,64,256]{2,1,0:T(8,128)(2,1)S(1)} custom-call(bf16[16,64,512]{2,1,0:T(8,128)(2,1)} %bitcast.15, bf16[4,64,512]{2,1,0:T(8,128)(2,1)} %left_root.3, bf16[4,64,512]{2,1,0:T(8,128)(2,1)} %right_root.3), custom_call_target="tpu_custom_call" | custom-call | tf_op jit(solution)/shard_map/pallas_call | solution.py:333
  1.9 8.8 %collective-permute-start = (bf16[32,64,256]{2,1,0:T(8,128)(2,1)S(1)}, bf16[32,64,256]{2,1,0:T(8,128)(2,1)S(1)}, u32[]{:S(2)}, u32[]{:S(2)}) collective-permute-start(bf16[32,64,256]{2,1,0:T(8,128)(2,1)S(1)} %shard_map.85), channel_id=1, source_target_pairs={{0,64},{64,0},{1,65},{65,1},{2,66},{66,2},{3,67},{67,3},{4,68},{68... | collective-permute-start | bytes 3145736 | tf_op jit(solution)/shard_map/ppermute | solution.py:311
  10.7 2.6 %shard_map.86 = (bf16[16,64,256]{2,1,0:T(8,128)(2,1)S(1)}, bf16[2,64,512]{2,1,0:T(8,128)(2,1)S(1)}, bf16[2,64,512]{2,1,0:T(8,128)(2,1)S(1)}, bf16[2,64,512]{2,1,...) custom-call(s32[1,128]{1,0:T(1,128)} %bitcast.17, ...), custom_call_target="tpu_custom_call" | custom-call | bytes 4000000 | tf_op jit(solution)/shard_map/pallas_call | solution.py:341
  13.3 0.0 collective-permute-done.other
  13.3 0.2 shard_map.87
  13.5 11.7 %all_to_all.20.parts = bf16[4,32,8,256]{3,2,1,0:T(8,128)(2,1)S(1)} all-to-all(bf16[4,32,8,256]{3,2,1,0:T(8,128)(2,1)S(1)} %shard_map.87), channel_id=1, replica_groups=mesh['x'=4,'core'=2,'y'=4,'z'=16] {'x'}, dimensions={0} | all-to-all | bytes 1048576 | tf_op jit(solution)/shard_map/all_to_all | solution.py:298
  25.2 0.9 shard_map.88
  26.1 14.5 %all-to-all-start.1 = ((bf16[64,8,256]{2,1,0:T(8,128)(2,1)}), bf16[64,8,256]{2,1,0:T(8,128)(2,1)S(1)}, u32[]{:S(2)}, u32[]{:S(2)}) async-start(bf16[64,8,256]{2,1,0:T(8,128)(2,1)} %shard_map.88), calls=%async_computation.1 | async-start | bytes 524288 | tf_op jit(solution)/shard_map/all_to_all | solution.py:298
  40.6 2.8 %collective-permute-start.2 = (bf16[2,2,64,512]{3,2,1,0:T(8,128)(2,1)S(1)}, bf16[2,2,64,512]{3,2,1,0:T(8,128)(2,1)S(1)}, u32[]{:S(2)}, u32[]{:S(2)}) collective-permute-start(bf16[2,2,64,512]{3,2,1,0:T(8,128)(2,1)S(1)} %shard_map.89), channel_id=1, source_target_pairs={{0,128},{128,256},{256,384},{384,0},{64,448},{192,64},{320,192},{4... | collective-permute-start | bytes 786440 | tf_op jit(solution)/shard_map/ppermute | solution.py:374
  43.4 3.1 %collective-permute-start.3 = (bf16[2,64,512]{2,1,0:T(8,128)(2,1)S(1)}, bf16[2,64,512]{2,1,0:T(8,128)(2,1)S(1)}, u32[]{:S(2)}, u32[]{:S(2)}) collective-permute-start(bf16[2,64,512]{2,1,0:T(8,128)(2,1)S(1)} %get-tuple-element.56), channel_id=1, source_target_pairs={{0,256},{128,384},{256,0},{384,128},{1,257},{129,385},{257,1},{385... | collective-permute-start | bytes 393224 | tf_op jit(solution)/shard_map/ppermute | solution.py:307
  46.5 1.5 %collective-permute-done.2.beside = bf16[2,2,64,512]{3,2,1,0:T(8,128)(2,1)S(1)} collective-permute-done((bf16[2,2,64,512]{3,2,1,0:T(8,128)(2,1)S(1)}, bf16[2,2,64,512]{3,2,1,0:T(8,128)(2,1)S(1)}, u32[]{:S(2)}, u32[]{:S(2)}) %collective-permute-start.2) | collective-permute-done | bytes 262176 | tf_op jit(solution)/shard_map/ppermute | solution.py:374
  48.0 4.4 %collective-permute-done.3.across = bf16[2,64,512]{2,1,0:T(8,128)(2,1)S(1)} collective-permute-done((bf16[2,64,512]{2,1,0:T(8,128)(2,1)S(1)}, bf16[2,64,512]{2,1,0:T(8,128)(2,1)S(1)}, u32[]{:S(2)}, u32[]{:S(2)}) %collective-permute-start.3) | collective-permute-done | bytes 131104 | tf_op jit(solution)/shard_map/ppermute | solution.py:307
  52.5 3.8 %collective-permute-start.4 = (bf16[3,2,64,512]{3,2,1,0:T(8,128)(2,1)S(1)}, bf16[3,2,64,512]{3,2,1,0:T(8,128)(2,1)S(1)}, u32[]{:S(2)}, u32[]{:S(2)}) collective-permute-start(bf16[3,2,64,512]{3,2,1,0:T(8,128)(2,1)S(1)} %shard_map.90), channel_id=1, source_target_pairs={{0,64},{64,0},{1,65},{65,1},{2,66},{66,2},{3,67},{67,3},{4,68},{68... | collective-permute-start | bytes 1179656 | tf_op jit(solution)/shard_map/ppermute | solution.py:311
  56.3 2.9 %all-to-all-done.1 = bf16[64,8,256]{2,1,0:T(8,128)(2,1)S(1)} async-done(((bf16[64,8,256]{2,1,0:T(8,128)(2,1)}), bf16[64,8,256]{2,1,0:T(8,128)(2,1)S(1)}, u32[]{:S(2)}, u32[]{:S(2)}) %all-to-all-start.1) | async-done | bytes 262176 | tf_op jit(solution)/shard_map/all_to_all | solution.py:298
  59.2 5.2 %collective-permute-start.1 = (bf16[512,256]{1,0:T(8,128)(2,1)S(1)}, bf16[512,256]{1,0:T(8,128)(2,1)S(1)}, u32[]{:S(2)}, u32[]{:S(2)}) collective-permute-start(bf16[512,256]{1,0:T(8,128)(2,1)S(1)} %bitcast.12), channel_id=1, source_target_pairs={{0,64},{64,0},{1,65},{65,1},{2,66},{66,2},{3,67},{67,3},{4,68},{68... | collective-permute-start | bytes 786440 | tf_op jit(solution)/shard_map/ppermute | solution.py:311
  64.5 0.0 collective-permute-done.4.others
  64.5 0.1 shard_map.91
  64.6 0.3 shard_map.92
  64.9 0.7 collective-permute-done.1.other
  65.6 1.6 %shard_map.93 = bf16[512,256]{1,0:T(8,128)(2,1)} custom-call(bf16[512,256]{1,0:T(8,128)(2,1)S(1)} %collective-permute-done.1.other, f32[512,512]{1,0:T(8,128)S(1)} %get-tuple-element.58.partial, bf16[8,64,512]{2,1,0:T(8,128)(2,1)S(1)} %get-tuple-element.59.left, bf16[8,64,512]{2,1,0:T(8,128)(2,1)S(1)} %get-tuple-element.57.right, ...), custom_call_target="tpu_custom_call" | custom-call | tf_op jit(solution)/shard_map/pallas_call | solution.py:407
  67.2 8.9 %all-to-all-start.2 = ((bf16[64,8,256]{2,1,0:T(8,128)(2,1)}), bf16[64,8,256]{2,1,0:T(8,128)(2,1)S(1)}, u32[]{:S(2)}, u32[]{:S(2)}) async-start(bf16[64,8,256]{2,1,0:T(8,128)(2,1)} %bitcast.5), calls=%async_computation.2 | async-start | bytes 524288 | tf_op jit(solution)/shard_map/all_to_all | solution.py:298
  76.2 0.9 shard_map.95
  77.1 2.9 %collective-permute-start.5 = (bf16[2,2,64,512]{3,2,1,0:T(8,128)(2,1)S(1)}, bf16[2,2,64,512]{3,2,1,0:T(8,128)(2,1)S(1)}, u32[]{:S(2)}, u32[]{:S(2)}) collective-permute-start(bf16[2,2,64,512]{3,2,1,0:T(8,128)(2,1)S(1)} %get-tuple-element.64), channel_id=1, source_target_pairs={{0,128},{128,256},{256,384},{384,0},{64,448},{192,64},{320,192},{4... | collective-permute-start | bytes 786440 | tf_op jit(solution)/shard_map/ppermute | solution.py:423
  79.9 1.9 %collective-permute-start.6 = (bf16[2,64,512]{2,1,0:T(8,128)(2,1)S(1)}, bf16[2,64,512]{2,1,0:T(8,128)(2,1)S(1)}, u32[]{:S(2)}, u32[]{:S(2)}) collective-permute-start(bf16[2,64,512]{2,1,0:T(8,128)(2,1)S(1)} %get-tuple-element.65), channel_id=1, source_target_pairs={{0,256},{128,384},{256,0},{384,128},{1,257},{129,385},{257,1},{385... | collective-permute-start | bytes 393224 | tf_op jit(solution)/shard_map/ppermute | solution.py:307
  81.9 2.6 %collective-permute-done.5.beside = bf16[2,2,64,512]{3,2,1,0:T(8,128)(2,1)S(1)} collective-permute-done((bf16[2,2,64,512]{3,2,1,0:T(8,128)(2,1)S(1)}, bf16[2,2,64,512]{3,2,1,0:T(8,128)(2,1)S(1)}, u32[]{:S(2)}, u32[]{:S(2)}) %collective-permute-start.5) | collective-permute-done | bytes 262176 | tf_op jit(solution)/shard_map/ppermute | solution.py:423
  84.5 7.2 %collective-permute-start.7 = (bf16[2,64,512]{2,1,0:T(8,128)(2,1)S(1)}, bf16[2,64,512]{2,1,0:T(8,128)(2,1)S(1)}, u32[]{:S(2)}, u32[]{:S(2)}) collective-permute-start(bf16[2,64,512]{2,1,0:T(8,128)(2,1)S(1)} %dynamic-slice_bitcast_fusion), channel_id=1, source_target_pairs={{0,64},{64,0},{1,65},{65,1},{2,66},{66,2},{3,67},{67,3},{4,68},{68... | collective-permute-start | bytes 393224 | tf_op jit(solution)/shard_map/ppermute | solution.py:311
  91.7 4.6 %all-to-all-done.2.rows = bf16[64,8,256]{2,1,0:T(8,128)(2,1)S(1)} async-done(((bf16[64,8,256]{2,1,0:T(8,128)(2,1)}), bf16[64,8,256]{2,1,0:T(8,128)(2,1)S(1)}, u32[]{:S(2)}, u32[]{:S(2)}) %all-to-all-start.2) | async-done | bytes 262176 | tf_op jit(solution)/shard_map/all_to_all | solution.py:298
  96.4 0.0 collective-permute-done.6.across
  96.4 0.0 collective-permute-done.7.passed
  96.4 10.2 %all_to_all.21 = bf16[4,32,8,256]{3,2,1,0:T(8,128)(2,1)S(1)} all-to-all(bf16[4,32,8,256]{3,2,1,0:T(8,128)(2,1)S(1)} %shard_map.94), channel_id=1, replica_groups=mesh['x'=4,'core'=2,'y'=4,'z'=16] {'x'}, dimensions={0} | all-to-all | bytes 1048576 | tf_op jit(solution)/shard_map/all_to_all | solution.py:298
  106.6 0.0 copy-start
  106.6 0.0 copy-start.1
  106.6 0.2 shard_map.96.near
  106.8 4.7 %collective-permute-start.8 = (bf16[128,8,256]{2,1,0:T(8,128)(2,1)S(1)}, bf16[128,8,256]{2,1,0:T(8,128)(2,1)S(1)}, u32[]{:S(2)}, u32[]{:S(2)}) collective-permute-start(bf16[128,8,256]{2,1,0:T(8,128)(2,1)S(1)} %shard_map.96.near), channel_id=1, source_target_pairs={{0,64},{64,0},{1,65},{65,1},{2,66},{66,2},{3,67},{67,3},{4,68},{68... | collective-permute-start | bytes 1572872 | tf_op jit(solution)/shard_map/ppermute | solution.py:311
  111.5 0.0 copy-done
  111.5 0.0 copy-done.1
  111.5 1.2 %shard_map.97 = (bf16[128,8,512]{2,1,0:T(8,128)(2,1)}, f32[4,64,512]{2,1,0:T(8,128)}, f32[4,64,512]{2,1,0:T(8,128)}) custom-call(s32[1,128]{1,0:T(1,128)S(4)} %get-tuple-element.71.chip_of, bf16[128,8,256]{2,1,0:T(8,128)(2,1)S(1)} %shard_map.96.near, bf16[2,64,512]{2,1,0:T(8,128)(2,1)S(1)} %get-tuple-element.72.mine, ...), custom_call_target="tpu_custom_call" | custom-call | flops 10000000 | bytes 5000000 | tf_op jit(solution)/shard_map/pallas_call | solution.py:437
  112.8 0.3 collective-permute-done.8.rows
  113.0 0.8 shard_map.98
  (4 shorter events, 0.1 us)
Async XLA Ops:
  1.9 11.4 %collective-permute-start = (bf16[32,64,256]{2,1,0:T(8,128)(2,1)S(1)}, bf16[32,64,256]{2,1,0:T(8,128)(2,1)S(1)}, u32[]{:S(2)}, u32[]{:S(2)}) collective-permute-start(bf16[32,64,256]{2,1,0:T(8,128)(2,1)S(1)} %shard_map.85), channel_id=1, source_target_pairs={{0,64},{64,0},{1,65},{65,1},{2,66},{66,2},{3,67},{67,3},{4,68},{68... | collective-permute-start | bytes 3145736 | tf_op jit(solution)/shard_map/ppermute | solution.py:311
  26.1 33.1 %all-to-all-start.1 = ((bf16[64,8,256]{2,1,0:T(8,128)(2,1)}), bf16[64,8,256]{2,1,0:T(8,128)(2,1)S(1)}, u32[]{:S(2)}, u32[]{:S(2)}) async-start(bf16[64,8,256]{2,1,0:T(8,128)(2,1)} %shard_map.88), calls=%async_computation.1 | async-start | bytes 524288 | tf_op jit(solution)/shard_map/all_to_all | solution.py:298
  40.6 7.4 %collective-permute-start.2 = (bf16[2,2,64,512]{3,2,1,0:T(8,128)(2,1)S(1)}, bf16[2,2,64,512]{3,2,1,0:T(8,128)(2,1)S(1)}, u32[]{:S(2)}, u32[]{:S(2)}) collective-permute-start(bf16[2,2,64,512]{3,2,1,0:T(8,128)(2,1)S(1)} %shard_map.89), channel_id=1, source_target_pairs={{0,128},{128,256},{256,384},{384,0},{64,448},{192,64},{320,192},{4... | collective-permute-start | bytes 786440 | tf_op jit(solution)/shard_map/ppermute | solution.py:374
  43.4 9.0 %collective-permute-start.3 = (bf16[2,64,512]{2,1,0:T(8,128)(2,1)S(1)}, bf16[2,64,512]{2,1,0:T(8,128)(2,1)S(1)}, u32[]{:S(2)}, u32[]{:S(2)}) collective-permute-start(bf16[2,64,512]{2,1,0:T(8,128)(2,1)S(1)} %get-tuple-element.56), channel_id=1, source_target_pairs={{0,256},{128,384},{256,0},{384,128},{1,257},{129,385},{257,1},{385... | collective-permute-start | bytes 393224 | tf_op jit(solution)/shard_map/ppermute | solution.py:307
  52.5 12.0 %collective-permute-start.4 = (bf16[3,2,64,512]{3,2,1,0:T(8,128)(2,1)S(1)}, bf16[3,2,64,512]{3,2,1,0:T(8,128)(2,1)S(1)}, u32[]{:S(2)}, u32[]{:S(2)}) collective-permute-start(bf16[3,2,64,512]{3,2,1,0:T(8,128)(2,1)S(1)} %shard_map.90), channel_id=1, source_target_pairs={{0,64},{64,0},{1,65},{65,1},{2,66},{66,2},{3,67},{67,3},{4,68},{68... | collective-permute-start | bytes 1179656 | tf_op jit(solution)/shard_map/ppermute | solution.py:311
  59.2 6.4 %collective-permute-start.1 = (bf16[512,256]{1,0:T(8,128)(2,1)S(1)}, bf16[512,256]{1,0:T(8,128)(2,1)S(1)}, u32[]{:S(2)}, u32[]{:S(2)}) collective-permute-start(bf16[512,256]{1,0:T(8,128)(2,1)S(1)} %bitcast.12), channel_id=1, source_target_pairs={{0,64},{64,0},{1,65},{65,1},{2,66},{66,2},{3,67},{67,3},{4,68},{68... | collective-permute-start | bytes 786440 | tf_op jit(solution)/shard_map/ppermute | solution.py:311
  67.2 29.1 %all-to-all-start.2 = ((bf16[64,8,256]{2,1,0:T(8,128)(2,1)}), bf16[64,8,256]{2,1,0:T(8,128)(2,1)S(1)}, u32[]{:S(2)}, u32[]{:S(2)}) async-start(bf16[64,8,256]{2,1,0:T(8,128)(2,1)} %bitcast.5), calls=%async_computation.2 | async-start | bytes 524288 | tf_op jit(solution)/shard_map/all_to_all | solution.py:298
  77.1 7.4 %collective-permute-start.5 = (bf16[2,2,64,512]{3,2,1,0:T(8,128)(2,1)S(1)}, bf16[2,2,64,512]{3,2,1,0:T(8,128)(2,1)S(1)}, u32[]{:S(2)}, u32[]{:S(2)}) collective-permute-start(bf16[2,2,64,512]{3,2,1,0:T(8,128)(2,1)S(1)} %get-tuple-element.64), channel_id=1, source_target_pairs={{0,128},{128,256},{256,384},{384,0},{64,448},{192,64},{320,192},{4... | collective-permute-start | bytes 786440 | tf_op jit(solution)/shard_map/ppermute | solution.py:423
  79.9 16.5 %collective-permute-start.6 = (bf16[2,64,512]{2,1,0:T(8,128)(2,1)S(1)}, bf16[2,64,512]{2,1,0:T(8,128)(2,1)S(1)}, u32[]{:S(2)}, u32[]{:S(2)}) collective-permute-start(bf16[2,64,512]{2,1,0:T(8,128)(2,1)S(1)} %get-tuple-element.65), channel_id=1, source_target_pairs={{0,256},{128,384},{256,0},{384,128},{1,257},{129,385},{257,1},{385... | collective-permute-start | bytes 393224 | tf_op jit(solution)/shard_map/ppermute | solution.py:307
  84.5 11.9 %collective-permute-start.7 = (bf16[2,64,512]{2,1,0:T(8,128)(2,1)S(1)}, bf16[2,64,512]{2,1,0:T(8,128)(2,1)S(1)}, u32[]{:S(2)}, u32[]{:S(2)}) collective-permute-start(bf16[2,64,512]{2,1,0:T(8,128)(2,1)S(1)} %dynamic-slice_bitcast_fusion), channel_id=1, source_target_pairs={{0,64},{64,0},{1,65},{65,1},{2,66},{66,2},{3,67},{67,3},{4,68},{68... | collective-permute-start | bytes 393224 | tf_op jit(solution)/shard_map/ppermute | solution.py:311
  106.6 4.9 %copy-start = (f32[4,64,512]{2,1,0:T(8,128)S(1)}, f32[4,64,512]{2,1,0:T(8,128)}, u32[]{:S(2)}) copy-start(f32[4,64,512]{2,1,0:T(8,128)} %left.1) | copy-start | bytes 1572868
  106.6 4.9 %copy-start.1 = (f32[4,64,512]{2,1,0:T(8,128)S(1)}, f32[4,64,512]{2,1,0:T(8,128)}, u32[]{:S(2)}) copy-start(f32[4,64,512]{2,1,0:T(8,128)} %right.1) | copy-start | bytes 1572868
  106.8 6.2 %collective-permute-start.8 = (bf16[128,8,256]{2,1,0:T(8,128)(2,1)S(1)}, bf16[128,8,256]{2,1,0:T(8,128)(2,1)S(1)}, u32[]{:S(2)}, u32[]{:S(2)}) collective-permute-start(bf16[128,8,256]{2,1,0:T(8,128)(2,1)S(1)} %shard_map.96.near), channel_id=1, source_target_pairs={{0,64},{64,0},{1,65},{65,1},{2,66},{66,2},{3,67},{67,3},{4,68},{68... | collective-permute-start | bytes 1572872 | tf_op jit(solution)/shard_map/ppermute | solution.py:311
